TPU v7x, 32 devices: a whole 2x2x4 slice. The times are simulated.
32 devices in a mesh: narrow: 4 (over y, core), wide: 8 (over z, x).
Axes of the slice: x: 2, y: 2, z: 4, core: 2. Of those that a mesh axis runs over, the one named last changes fastest.
Arguments:
- layer_in: float32 [128, 384, 384], P(('narrow', 'wide')), may hold values from -6 to 6
- cotangent: float32 [128, 384, 384], P(('narrow', 'wide')), may hold values from -6 to 6
- qkv_master: float32 [1152, 384], P('wide'), may hold values from -0.3125 to 0.3125
- proj_master: float32 [384, 384], P('wide'), may hold values from -0.3125 to 0.3125
- up_master: float32 [1536, 384], P('wide'), may hold values from -0.3125 to 0.3125
- down_master: float32 [384, 1536], P('wide'), may hold values from -0.15625 to 0.15625
- vector_master: float32 [4608], P('wide'), may hold values from -0.3 to 1.4, as said below
- qkv_first: float32 [1152, 384], P('wide'), may hold values from -640 to 640
- proj_first: float32 [384, 384], P('wide'), may hold values from -640 to 640
- up_first: float32 [1536, 384], P('wide'), may hold values from -640 to 640
- down_first: float32 [384, 1536], P('wide'), may hold values from -640 to 640
- vector_first: float32 [4608], P('wide'), may hold values from -1280 to 1280
- qkv_second: float32 [1152, 384], P('wide'), may hold values from 12288 to 49152
- proj_second: float32 [384, 384], P('wide'), may hold values from 12288 to 49152
- up_second: float32 [1536, 384], P('wide'), may hold values from 12288 to 49152
- down_second: float32 [384, 1536], P('wide'), may hold values from 12288 to 49152
- vector_second: float32 [4608], P('wide'), may hold values from 49152 to 196608
Outputs:
- layer_out: float32 [128, 384, 384], P(('narrow', 'wide'))
- input_grad: float32 [128, 384, 384], P(('narrow', 'wide'))
- qkv_updated: float32 [1152, 384], P('wide')
- qkv_first_out: float32 [1152, 384], P('wide')
- qkv_second_out: float32 [1152, 384], P('wide')
- qkv_copy: bfloat16 [1152, 384], P('wide')
- proj_updated: float32 [384, 384], P('wide')
- proj_first_out: float32 [384, 384], P('wide')
- proj_second_out: float32 [384, 384], P('wide')
- proj_copy: bfloat16 [384, 384], P('wide')
- up_updated: float32 [1536, 384], P('wide')
- up_first_out: float32 [1536, 384], P('wide')
- up_second_out: float32 [1536, 384], P('wide')
- up_copy: bfloat16 [1536, 384], P('wide')
- down_updated: float32 [384, 1536], P('wide')
- down_first_out: float32 [384, 1536], P('wide')
- down_second_out: float32 [384, 1536], P('wide')
- down_copy: bfloat16 [384, 1536], P('wide')
- vector_updated: float32 [4608], P('wide')
- vector_first_out: float32 [4608], P('wide')
- vector_second_out: float32 [4608], P('wide')
- vector_copy: bfloat16 [4608], P('wide')
Inputs may be any that keep to these rules, and one draw needn't show every extreme that they name: `vector_master`: entries of gain_one and gain_two lie in 0.6 to 1.4; all other entries lie in -0.3 to 0.3.
All inputs are finite; a program needn't handle non-finite values.
Results may differ from a plain program's by a relative error of at most 0.015.
Values may be sent and summed in bfloat16 or wider, within the bound.
No kernel may reach another device: no remote copies, remote signals or barrier semaphores. Data moves between devices by JAX's collectives and lax.ppermute only.
A program may use at most 128 MiB of HBM per device.

v0:
```python
import jax
import jax.numpy as jnp
from jax import lax
from jax.sharding import PartitionSpec as P

D = 384
HEADS = 6
FF = 1536
STEP = 10


norm_eps = 1e-06
adam_eps = 1e-08
beta_first = 0.5
beta_second = 0.5
matrix_decay = 0.01
vector_rate = 0.3


def layer_norm(values, norm_gain, norm_shift):
    centred = values - jnp.mean(values, axis=-1, keepdims=True)
    variance = jnp.mean(centred * centred, axis=-1, keepdims=True)
    return centred * lax.rsqrt(variance + norm_eps) * norm_gain + norm_shift


def gelu_exact(values):
    return jax.nn.gelu(values, approximate=False)


def unpack(vector, model_width):
    pieces = [
        vector[position * model_width : (position + 1) * model_width] for position in range(8)
    ]
    return pieces + [vector[8 * model_width :]]


def project(operand, weight):
    return lax.dot_general(
        operand, weight, (((1,), (1,)), ((), ())), preferred_element_type=jnp.float32
    )


def weight_grad(grad_low, operand):
    return lax.dot_general(
        grad_low, operand, (((0,), (0,)), ((), ())), preferred_element_type=jnp.float32
    )


def forward_pass(inputs, weights):
    qkv_weight, proj_weight, up_weight, down_weight, vector = weights
    images, length, model_width = inputs.shape
    head_size = model_width // HEADS
    (
        gain_one,
        shift_one,
        gain_two,
        shift_two,
        query_bias,
        value_bias,
        proj_bias,
        down_bias,
        up_bias,
    ) = unpack(vector.astype(jnp.float32), model_width)
    token_rows = inputs.reshape(images * length, model_width)
    normed_one = layer_norm(token_rows, gain_one, shift_one).astype(jnp.bfloat16)
    joint_bias = jnp.concatenate([query_bias, jnp.zeros_like(query_bias), value_bias])
    qkv_joint = (project(normed_one, qkv_weight) + joint_bias).astype(jnp.bfloat16)
    qkv_joint = qkv_joint.reshape(images, length, 3, HEADS, head_size)
    scores = jnp.einsum(
        "bqhd,bkhd->bhqk",
        qkv_joint[:, :, 0],
        qkv_joint[:, :, 1],
        preferred_element_type=jnp.float32,
    )
    scores = scores * head_size ** (-0.5)
    row_max = jnp.max(scores, axis=-1, keepdims=True)
    log_total = row_max + jnp.log(jnp.sum(jnp.exp(scores - row_max), axis=-1, keepdims=True))
    probs_low = jnp.exp(scores - log_total).astype(jnp.bfloat16)
    heads_out = jnp.einsum(
        "bhqk,bkhd->bqhd", probs_low, qkv_joint[:, :, 2], preferred_element_type=jnp.float32
    )
    heads_out = heads_out.astype(jnp.bfloat16).reshape(images * length, model_width)
    middle = token_rows + (project(heads_out, proj_weight) + proj_bias)
    normed_two = layer_norm(middle, gain_two, shift_two).astype(jnp.bfloat16)
    upward = project(normed_two, up_weight) + up_bias
    activated = gelu_exact(upward).astype(jnp.bfloat16)
    layer_out = middle + (project(activated, down_weight) + down_bias)
    kept_state = (
        token_rows,
        normed_one,
        qkv_joint,
        log_total,
        heads_out,
        middle,
        normed_two,
        upward,
        activated,
    )
    return (layer_out.reshape(inputs.shape), kept_state)


def feed_back(cotangent, weights, kept_state):
    up_weight, down_weight, vector = (weights[2], weights[3], weights[4])
    token_rows, middle, normed_two, upward, activated = (
        kept_state[0],
        kept_state[5],
        kept_state[6],
        kept_state[7],
        kept_state[8],
    )
    model_width = token_rows.shape[1]
    norm_pieces = unpack(vector.astype(jnp.float32), model_width)
    gain_two, shift_two = (norm_pieces[2], norm_pieces[3])
    grad_out = cotangent.reshape(token_rows.shape)
    grad_low = grad_out.astype(jnp.bfloat16)
    down_grad = weight_grad(grad_low, activated)
    down_bias_grad = jnp.sum(grad_low, axis=0, dtype=jnp.float32)
    grad_act = jnp.dot(grad_low, down_weight, preferred_element_type=jnp.float32)
    gelu_back = jax.vjp(gelu_exact, upward)[1]
    grad_up = gelu_back(grad_act)[0].astype(jnp.bfloat16)
    up_grad = weight_grad(grad_up, normed_two)
    up_bias_grad = jnp.sum(grad_up, axis=0, dtype=jnp.float32)
    grad_normed = jnp.dot(grad_up, up_weight, preferred_element_type=jnp.float32)
    norm_back = jax.vjp(layer_norm, middle, gain_two, shift_two)[1]
    grad_middle, gain_two_grad, shift_two_grad = norm_back(grad_normed)
    grad_middle = grad_out + grad_middle
    return (
        grad_middle,
        up_grad,
        down_grad,
        (gain_two_grad, shift_two_grad, down_bias_grad, up_bias_grad),
    )


def attention_back(grad_middle, weights, kept_state, mlp_parts):
    qkv_weight, proj_weight, vector = (weights[0], weights[1], weights[4])
    token_rows, normed_one, qkv_joint, log_total, heads_out = (
        kept_state[0],
        kept_state[1],
        kept_state[2],
        kept_state[3],
        kept_state[4],
    )
    images, length, triple, head_count, head_size = qkv_joint.shape
    model_width = token_rows.shape[1]
    norm_pieces = unpack(vector.astype(jnp.float32), model_width)
    gain_one, shift_one = (norm_pieces[0], norm_pieces[1])
    grad_attn = grad_middle.astype(jnp.bfloat16)
    proj_grad = weight_grad(grad_attn, heads_out)
    proj_bias_grad = jnp.sum(grad_attn, axis=0, dtype=jnp.float32)
    grad_heads = jnp.dot(grad_attn, proj_weight, preferred_element_type=jnp.float32)
    grad_heads = grad_heads.astype(jnp.bfloat16).reshape(images, length, head_count, head_size)
    queries, keys_part, values_part = (qkv_joint[:, :, 0], qkv_joint[:, :, 1], qkv_joint[:, :, 2])
    scale_factor = head_size ** (-0.5)
    scores = (
        jnp.einsum("bqhd,bkhd->bhqk", queries, keys_part, preferred_element_type=jnp.float32)
        * scale_factor
    )
    attn_probs = jnp.exp(scores - log_total)
    grad_probs = jnp.einsum(
        "bqhd,bkhd->bhqk", grad_heads, values_part, preferred_element_type=jnp.float32
    )
    grad_values = jnp.einsum(
        "bhqk,bqhd->bkhd",
        attn_probs.astype(jnp.bfloat16),
        grad_heads,
        preferred_element_type=jnp.float32,
    )
    grad_scores = attn_probs * (
        grad_probs - jnp.sum(attn_probs * grad_probs, axis=-1, keepdims=True)
    )
    grad_scores = grad_scores.astype(jnp.bfloat16)
    grad_queries = (
        jnp.einsum("bhqk,bkhd->bqhd", grad_scores, keys_part, preferred_element_type=jnp.float32)
        * scale_factor
    )
    grad_keys = (
        jnp.einsum("bhqk,bqhd->bkhd", grad_scores, queries, preferred_element_type=jnp.float32)
        * scale_factor
    )
    grad_joint = jnp.stack([grad_queries, grad_keys, grad_values], axis=2).astype(jnp.bfloat16)
    grad_joint = grad_joint.reshape(images * length, triple * model_width)
    qkv_grad = weight_grad(grad_joint, normed_one)
    joint_sums = jnp.sum(grad_joint, axis=0, dtype=jnp.float32)
    grad_normed = jnp.dot(grad_joint, qkv_weight, preferred_element_type=jnp.float32)
    norm_back = jax.vjp(layer_norm, token_rows, gain_one, shift_one)[1]
    grad_rows, gain_one_grad, shift_one_grad = norm_back(grad_normed)
    gain_two_grad, shift_two_grad, down_bias_grad, up_bias_grad = mlp_parts
    vector_grad = jnp.concatenate(
        [
            gain_one_grad,
            shift_one_grad,
            gain_two_grad,
            shift_two_grad,
            joint_sums[:model_width],
            joint_sums[2 * model_width :],
            proj_bias_grad,
            down_bias_grad,
            up_bias_grad,
        ]
    )
    return (grad_middle + grad_rows, qkv_grad, proj_grad, vector_grad)


def adam_step(master, grad_sum, first_old, second_old, step_rate, weight_decay):
    first_new = beta_first * first_old + (1.0 - beta_first) * grad_sum
    second_new = beta_second * second_old + (1.0 - beta_second) * grad_sum * grad_sum
    first_hat = first_new / (1.0 - beta_first**STEP)
    second_hat = second_new / (1.0 - beta_second**STEP)
    updated = master - step_rate * (
        first_hat / (jnp.sqrt(second_hat) + adam_eps) + weight_decay * master
    )
    return (updated, first_new, second_new, updated.astype(jnp.bfloat16))


def per_device(
    layer_in,
    cotangent,
    qkv_master,
    proj_master,
    up_master,
    down_master,
    vector_master,
    qkv_first,
    proj_first,
    up_first,
    down_first,
    vector_first,
    qkv_second,
    proj_second,
    up_second,
    down_second,
    vector_second,
):
    qkv_copy = qkv_master.astype(jnp.bfloat16)
    proj_copy = proj_master.astype(jnp.bfloat16)
    up_copy = up_master.astype(jnp.bfloat16)
    down_copy = down_master.astype(jnp.bfloat16)
    vector_copy = vector_master.astype(jnp.bfloat16)
    gathered = (
        lax.all_gather(qkv_copy, "wide", axis=0, tiled=True),
        lax.all_gather(proj_copy, "wide", axis=0, tiled=True),
        lax.all_gather(up_copy, "wide", axis=0, tiled=True),
        lax.all_gather(down_copy, "wide", axis=0, tiled=True),
        lax.all_gather(vector_copy, "wide", axis=0, tiled=True),
    )
    layer_out, kept_state = forward_pass(layer_in, gathered)
    back_weights = (
        lax.all_gather(qkv_copy, "wide", axis=0, tiled=True),
        lax.all_gather(proj_copy, "wide", axis=0, tiled=True),
        lax.all_gather(up_copy, "wide", axis=0, tiled=True),
        lax.all_gather(down_copy, "wide", axis=0, tiled=True),
        lax.all_gather(vector_copy, "wide", axis=0, tiled=True),
    )
    kept_state = forward_pass(layer_in, back_weights)[1]
    grad_middle, up_grad, down_grad, mlp_parts = feed_back(cotangent, back_weights, kept_state)
    grad_inputs, qkv_grad, proj_grad, vector_grad = attention_back(
        grad_middle, back_weights, kept_state, mlp_parts
    )
    qkv_part, proj_part, up_part, down_part, vector_part = (
        lax.psum_scatter(qkv_grad, "wide", scatter_dimension=0, tiled=True),
        lax.psum_scatter(proj_grad, "wide", scatter_dimension=0, tiled=True),
        lax.psum_scatter(up_grad, "wide", scatter_dimension=0, tiled=True),
        lax.psum_scatter(down_grad, "wide", scatter_dimension=0, tiled=True),
        lax.psum_scatter(vector_grad, "wide", scatter_dimension=0, tiled=True),
    )
    qkv_sum, proj_sum, up_sum, down_sum, vector_sum = (
        lax.psum(qkv_part.astype(jnp.bfloat16), "narrow").astype(jnp.float32),
        lax.psum(proj_part.astype(jnp.bfloat16), "narrow").astype(jnp.float32),
        lax.psum(up_part.astype(jnp.bfloat16), "narrow").astype(jnp.float32),
        lax.psum(down_part.astype(jnp.bfloat16), "narrow").astype(jnp.float32),
        lax.psum(vector_part.astype(jnp.bfloat16), "narrow").astype(jnp.float32),
    )
    qkv_new = adam_step(qkv_master, qkv_sum, qkv_first, qkv_second, 0.6 * D ** (-0.5), matrix_decay)
    proj_new = adam_step(
        proj_master, proj_sum, proj_first, proj_second, 0.6 * D ** (-0.5), matrix_decay
    )
    up_new = adam_step(up_master, up_sum, up_first, up_second, 0.6 * D ** (-0.5), matrix_decay)
    down_new = adam_step(
        down_master, down_sum, down_first, down_second, 0.6 * FF ** (-0.5), matrix_decay
    )
    vector_new = adam_step(vector_master, vector_sum, vector_first, vector_second, vector_rate, 0.0)
    return (
        layer_out,
        grad_inputs.reshape(layer_in.shape),
        qkv_new[0],
        qkv_new[1],
        qkv_new[2],
        qkv_new[3],
        proj_new[0],
        proj_new[1],
        proj_new[2],
        proj_new[3],
        up_new[0],
        up_new[1],
        up_new[2],
        up_new[3],
        down_new[0],
        down_new[1],
        down_new[2],
        down_new[3],
        vector_new[0],
        vector_new[1],
        vector_new[2],
        vector_new[3],
    )


def solution(mesh):
    placed = (
        P(("narrow", "wide"), None, None),
        P(("narrow", "wide"), None, None),
        P("wide", None),
        P("wide", None),
        P("wide", None),
        P("wide", None),
        P("wide"),
        P("wide", None),
        P("wide", None),
        P("wide", None),
        P("wide", None),
        P("wide"),
        P("wide", None),
        P("wide", None),
        P("wide", None),
        P("wide", None),
        P("wide"),
    )
    return jax.shard_map(
        per_device,
        mesh=mesh,
        in_specs=placed,
        out_specs=(
            P(("narrow", "wide"), None, None),
            P(("narrow", "wide"), None, None),
            P("wide", None),
            P("wide", None),
            P("wide", None),
            P("wide", None),
            P("wide", None),
            P("wide", None),
            P("wide", None),
            P("wide", None),
            P("wide", None),
            P("wide", None),
            P("wide", None),
            P("wide", None),
            P("wide", None),
            P("wide", None),
            P("wide", None),
            P("wide", None),
            P("wide"),
            P("wide"),
            P("wide"),
            P("wide"),
        ),
        check_vma=False,
    )
```

profile of v0, /device:TPU:0, one launch (start us, length us, event | category | flops | bytes accessed | tf_op | source)
XLA Modules:
  0.0 569.0 jit_solution(18004616454230423842)
XLA Ops:
  7.2 1.8 convert_element_type.156
  9.1 1.6 convert_element_type.158
  10.9 2.0 reduce_sum.156
  13.5 0.6 fusion.45
  15.0 39.4 %all-reduce = bf16[4608]{0:T(1024)(128)(2,1)S(1)} all-reduce(bf16[4608]{0:T(1024)(128)(2,1)S(1)} %dynamic-update-slice), channel_id=1, replica_groups=mesh['narrow'=4,'wide'=8] {'wide'}, use_global_device_ids=true, to_apply=%add | all-reduce | flops 4608 | bytes 18432
  54.4 0.6 slice.90
  55.0 0.6 fusion.44
  55.7 33.2 %all_gather.22 = bf16[384,384]{1,0:T(8,128)(2,1)} all-gather(bf16[48,384]{1,0:T(8,128)(2,1)S(1)} %convert_element_type.154), channel_id=1, replica_groups=mesh['narrow'=4,'wide'=8] {'wide'}, dimensions={0}, use_global_device_ids=true | all-gather | bytes 331776 | tf_op jit(solution)/shard_map/all_gather | solution.py:242
  88.9 32.9 %all_gather.21 = bf16[1152,384]{1,0:T(8,128)(2,1)S(1)} all-gather(bf16[144,384]{1,0:T(8,128)(2,1)S(1)} %convert_element_type.149), channel_id=1, replica_groups=mesh['narrow'=4,'wide'=8] {'wide'}, dimensions={0}, use_global_device_ids=true | all-gather | bytes 995328 | tf_op jit(solution)/shard_map/all_gather | solution.py:241
  121.8 4.6 convert_reduce_fusion.2
  126.3 1.5 add_convert_fusion.1
  128.4 3.9 fusion.7
  132.3 5.9 %copy.98 = bf16[1536,1152]{0,1:T(8,128)(2,1)} copy(bf16[1536,1152]{1,0:T(8,128)(2,1)} %fusion.7) | data formatting | bytes 7077888 | tf_op jit(solution)/shard_map/convert_element_type | solution.py:67
  138.2 7.1 %reshape.198 = bf16[4,384,3,6,64]{1,0,4,3,2:T(4,128)(2,1)} reshape(bf16[1536,1152]{0,1:T(8,128)(2,1)} %copy.98) | data formatting | bytes 7077888 | tf_op jit(solution)/shard_map/reshape | solution.py:68
  145.4 3.2 fusion.42
  148.6 6.2 %multiply_reduce_fusion.1 = (f32[4,6,384]{2,1,0:T(8,128)S(1)}, f32[4,6,384,384]{2,3,1,0:T(8,128)}) fusion(bf16[4,384,1,6,64]{1,0,4,3,2:T(4,128)(2,1)S(1)} %get-tuple-element.129, bf16[4,384,1,6,64]{1,0,4,3,2:T(4,128)(2,1)S(1)} %get-tuple-element.130), kind=kOutput, calls=%fused_computation.5 | convolution fusion | flops 460053504 | bytes 16551936 | tf_op jit(solution)/shard_map/bqhd,bkhd->bhqk/dot_general | solution.py:69
  154.8 7.4 %exponential_reduce_fusion = f32[4,6,384]{2,1,0:T(8,128)S(1)} fusion(f32[4,6,384,384]{2,3,1,0:T(8,128)} %get-tuple-element.149, f32[4,6,384]{2,1,0:T(8,128)S(1)} %get-tuple-element.148), kind=kLoop, calls=%fused_computation.3 | loop fusion | flops 10607616 | bytes 14229504 | tf_op jit(solution)/shard_map/reduce_sum | solution.py:77
  162.2 7.7 %fusion.10 = bf16[4,384,6,64]{1,3,2,0:T(8,128)(2,1)S(1)} fusion(bf16[4,384,1,6,64]{1,0,4,3,2:T(4,128)(2,1)S(1)} %get-tuple-element.131, f32[4,6,384,384]{2,3,1,0:T(8,128)} %get-tuple-element.149, f32[4,6,384]{2,1,0:T(8,128)S(1)} %log_add_fusion), kind=kOutput, calls=%fused_computation.56 | convolution fusion | flops 464191488 | bytes 16551936 | tf_op jit(solution)/shard_map/bhqk,bkhd->bqhd/dot_general | solution.py:79
  170.0 0.9 copy.103
  171.1 1.1 fusion.46
  172.3 1.3 copy-done.4
  174.3 26.6 %multiply_convert_fusion.1 = (bf16[1536,1536]{1,0:T(8,128)(2,1)}, f32[1536,1536]{1,0:T(8,128)}, f32[1536,1536]{1,0:T(8,128)}) fusion(f32[1536]{0:T(1024)S(1)} %copy-done.58, bf16[1536,384]{1,0:T(8,128)(2,1)} %all-gather.3.cloned.1.call-done, f32[1536,384]{1,0:T(8,128)} %copy-done.4, f32[384]{0:T(512)S(1)} %copy-done.65, f32[384]{0:T(512)S(1)} %copy-done.59, ...), kind=kOutput, calls=%fused_computation.11 | convolution fusion | flops 1970601984 | bytes 27153408 | tf_op jit(solution)/shard_map/dot_general | solution.py:38
  200.9 11.4 %convert_reduce_fusion = (f32[1536]{0:T(1024)}, bf16[1536,1536]{1,0:T(8,128)(2,1)S(1)}) fusion(f32[1536,1536]{1,0:T(8,128)} %get-tuple-element.128, f32[1536,1536]{1,0:T(8,128)} %get-tuple-element.152, bf16[1536,384]{1,0:T(8,128)(2,1)} %get-tuple-element.133, bf16[384,1536]{1,0:T(8,128)(2,1)} %all-gather.5.cloned.1.call-done), kind=kOutput, calls=%fused_computation.9 | convolution fusion | flops 1849686528 | bytes 25958400 | tf_op jit(solution)/shard_map/dot_general | solution.py:118
  212.3 3.8 multiply_reduce_fusion.2
  216.1 1.3 fusion.40
  217.8 1.0 convert_reduce_fusion.3
  218.9 1.0 copy-done.17
  219.9 1.7 fusion.48
  221.5 3.2 convolution_convert_fusion
  224.7 2.4 copy.104
  227.1 3.4 reshape.202
  230.5 9.0 %convolution_bitcast_fusion.1 = bf16[4,384,1,6,64]{1,4,3,0,2:T(8,128)(2,1)} fusion(bf16[4,384,6,64]{1,0,3,2:T(4,128)(2,1)} %reshape.202, f32[4,6,384,384]{2,3,1,0:T(8,128)} %get-tuple-element.149, f32[4,6,384]{2,1,0:T(8,128)} %copy-done.20), kind=kOutput, calls=%fused_computation.54 | convolution fusion | flops 463601664 | bytes 16551936 | tf_op jit(solution)/shard_map/bhqk,bqhd->bkhd/dot_general | solution.py:163
  239.6 10.3 %multiply_reduce_fusion = (f32[4,6,384]{2,1,0:T(8,128)}, f32[4,6,384,384]{2,3,1,0:T(8,128)}) fusion(f32[4,6,384,384]{2,3,1,0:T(8,128)} %get-tuple-element.149, f32[4,6,384]{2,1,0:T(8,128)S(1)} %copy-done.21, bf16[4,384,1,6,64]{1,0,4,3,2:T(4,128)(2,1)S(1)} %get-tuple-element.131, bf16[4,384,6,64]{1,0,3,2:T(4,128)(2,1)S(1)} %copy-done.11), kind=kOutput, calls=%fused_computation.1 | convolution fusion | flops 467131392 | bytes 30744576 | tf_op jit(solution)/shard_map/bqhd,bkhd->bhqk/dot_general | solution.py:160
  250.0 10.4 %multiply_convert_fusion = bf16[4,6,384,384]{2,3,1,0:T(8,128)(2,1)S(1)} fusion(f32[4,6,384,384]{2,3,1,0:T(8,128)} %get-tuple-element.155, f32[4,6,384,384]{2,3,1,0:T(8,128)} %get-tuple-element.149, f32[4,6,384]{2,1,0:T(8,128)} %get-tuple-element.154, f32[4,6,384]{2,1,0:T(8,128)} %copy-done.20), kind=kLoop, calls=%fused_computation | loop fusion | flops 17694720 | bytes 35463168 | tf_op jit(solution)/shard_map/convert_element_type | solution.py:172
  260.4 2.6 multiply_bitcast_fusion
  263.0 1.3 multiply_bitcast_fusion.1
  264.3 1.5 convert_reduce_fusion.1
  265.8 3.0 copy.110
  268.9 0.6 copy.122
  269.5 1.7 copy-done.18
  271.3 3.3 fusion.47
  274.6 6.4 %convolution_bitcast_fusion = f32[384,1536]{0,1:T(8,128)} fusion(bf16[1536,1536]{1,0:T(8,128)(2,1)} %get-tuple-element.127, bf16[1536,384]{1,0:T(8,128)(2,1)S(1)} %copy-done.22), kind=kOutput, calls=%fused_computation.33 | convolution fusion | flops 1811939328 | bytes 8257536 | tf_op jit(solution)/shard_map/dot_general | solution.py:44
  281.0 3.2 copy.116
  284.9 6.6 %fusion.27 = f32[1536,384]{1,0:T(8,128)} fusion(bf16[1536,1536]{1,0:T(8,128)(2,1)} %copy-done.72, f32[1536,384]{1,0:T(8,128)S(1)} %copy-done.5, f32[384]{0:T(512)S(1)} %copy-done.66, f32[384]{0:T(512)S(1)} %copy-done.61, f32[1536]{0:T(1024)S(1)} %copy-done.52, f32[1536]{0:T(1024)S(1)} %broadcast_multiply_fusion), kind=kOutput, calls=%fused_computation.109 | convolution fusion | flops 1814888448 | bytes 9452544 | tf_op jit(solution)/shard_map/dot_general | solution.py:44
  292.6 0.6 copy-done.1
  293.3 6.0 %multiply_reduce_fusion.3 = (f32[384]{0:T(512)S(1)}, f32[1536]{0:T(1024)S(1)}, f32[384]{0:T(512)S(1)}, f32[1536,384]{1,0:T(8,128)}) fusion(f32[4,384,384]{2,1,0:T(8,128)S(1)} %copy-done.1, f32[1536]{0:T(1024)S(1)} %copy-done.46, f32[1536]{0:T(1024)S(1)} %copy-done.44, f32[384]{0:T(512)S(1)} %copy-done.49, bf16[1536,1152]{0,1:T(8,128)(2,1)} %bitcast.103, ...), kind=kOutput, calls=%fused_computation.43 | convolution fusion | flops 1363670784 | bytes 9165312 | tf_op jit(solution)/shard_map/dot_general | solution.py:185
  299.4 33.1 %all-reduce.1 = bf16[4608]{0:T(1024)(128)(2,1)S(1)} all-reduce(f32[4608]{0:T(1024)S(1)} %constant_dynamic-update-slice_fusion), channel_id=6, replica_groups=mesh['narrow'=4,'wide'=8] {'wide'}, use_global_device_ids=true, to_apply=%region_27.0.clone | all-reduce | flops 4608 | bytes 27648
  332.7 2.8 fusion.39
  335.5 6.6 %fusion.9 = f32[1536,384]{1,0:T(8,128)} fusion(f32[1536,384]{1,0:T(8,128)S(1)} %copy-done.6, bf16[1536,1536]{1,0:T(8,128)(2,1)} %get-tuple-element.127, bf16[384,1536]{1,0:T(8,128)(2,1)S(1)} %copy-done.70, f32[384]{0:T(512)S(1)} %copy-done.64), kind=kOutput, calls=%fused_computation.35 | convolution fusion | flops 1813118976 | bytes 10618368 | tf_op jit(solution)/shard_map/dot_general | solution.py:38
  342.2 1.9 add_add_fusion.2
  344.2 1.0 convert_element_type.171
  345.2 10.6 %all-reduce.2 = (bf16[48,384]{1,0:T(8,128)(2,1)S(1)}, bf16[576]{0:T(1024)(128)(2,1)S(1)}) all-reduce(bf16[48,384]{1,0:T(8,128)(2,1)S(1)} %convert_element_type.171, bf16[576]{0:T(1024)(128)(2,1)S(1)} %dynamic-slice.4), channel_id=1, replica_groups=mesh['narrow'=4,'wide'=8] {'narrow'}, use_global_device_ids=true, to_apply=%region_14.0 | all-reduce | flops 19008 | bytes 76032 | tf_op jit(solution)/shard_map/psum | solution.py:269
  355.8 0.7 fusion.34
  356.5 21.7 %reduce-scatter.7.cloned.1.call-done = f32[144,384]{1,0:T(8,128)} async-done(((f32[1152,384]{1,0:T(8,128)}), f32[144,384]{1,0:T(8,128)}) %reduce-scatter.7.cloned.1.call-update) | async-done | bytes 221200 | tf_op jit(solution)/shard_map/reduce_scatter | solution.py:261
  378.3 1.6 convert_element_type.168
  379.9 69.6 %reduce-scatter.13.cloned.1.call-done = f32[48,1536]{1,0:T(8,128)} async-done(((f32[384,1536]{1,0:T(8,128)}), f32[48,1536]{1,0:T(8,128)}) %reduce-scatter.13.cloned.1.call-update) | async-done | bytes 294928 | tf_op jit(solution)/shard_map/reduce_scatter | solution.py:264
  449.5 1.6 convert_element_type.177
  451.1 69.7 %reduce-scatter.11.cloned.1.call-done = f32[192,384]{1,0:T(8,128)} async-done(((f32[1536,384]{1,0:T(8,128)}), f32[192,384]{1,0:T(8,128)}) %reduce-scatter.11.cloned.1.call-update) | async-done | bytes 294928 | tf_op jit(solution)/shard_map/reduce_scatter | solution.py:263
  520.9 1.6 convert_element_type.174
  522.6 0.6 fusion.28
  523.2 33.7 %all-reduce.6.cloned.1.call-done = (bf16[144,384]{1,0:T(8,128)(2,1)}, bf16[192,384]{1,0:T(8,128)(2,1)}, bf16[48,1536]{1,0:T(8,128)(2,1)}) async-done(((bf16[144,384]{1,0:T(8,128)(2,1)}, bf16[192,384]{1,0:T(8,128)(2,1)}, bf16[48,1536]{1,0:T(8,128)(2,1)}), (bf16[144,384]{1,0:T(8,128)(2,1)}, bf16[192,384]{1,0:T(8,128)(2,1)}, bf16[48,1536]{1,0:T(8,128)(2,1)})) %all-reduce.6.cloned.1.call-update) | async-done | bytes 405520 | tf_op jit(solution)/shard_map/psum | solution.py:268
  556.9 1.9 fusion.37
  558.8 2.0 fusion.32
  560.8 1.1 fusion.30
  (196 shorter events, 4.2 us)
Async XLA Ops:
  7.2 5.7 %copy-start = (f32[4,384,384]{2,1,0:T(8,128)S(1)}, f32[4,384,384]{2,1,0:T(8,128)}, u32[]{:S(2)}) copy-start(f32[4,384,384]{2,1,0:T(8,128)} %param.17) | copy-start | bytes 7077892
  7.2 167.0 %all-gather.3.cloned.1.call-start = ((), (), s32[]{:S(2)}) async-start(), calls=%async_computation.4 | async-start | bytes 1327104 | tf_op jit(solution)/shard_map/all_gather | solution.py:243
  9.1 191.8 %all-gather.5.cloned.1.call-start = ((), (), s32[]{:S(2)}) async-start(), calls=%async_computation.5 | async-start | bytes 1327104 | tf_op jit(solution)/shard_map/all_gather | solution.py:244
  10.8 333.4 %reduce-scatter.9.cloned.1.call-start = ((), (), s32[]{:S(2)}) async-start(), calls=%async_computation.7 | async-start | bytes 663552 | tf_op jit(solution)/shard_map/reduce_scatter | solution.py:262
  10.8 2.6 copy-start.53
  10.9 2.6 copy-start.67
  10.9 44.8 %copy-start.30 = (f32[48,384]{1,0:T(8,128)S(1)}, f32[48,384]{1,0:T(8,128)}, u32[]{:S(2)}) copy-start(f32[48,384]{1,0:T(8,128)} %param.20) | copy-start | bytes 221188
  10.9 44.8 %copy-start.26 = (f32[144,384]{1,0:T(8,128)S(1)}, f32[144,384]{1,0:T(8,128)}, u32[]{:S(2)}) copy-start(f32[144,384]{1,0:T(8,128)} %param.19) | copy-start | bytes 663556
  13.4 114.4 %copy-start.43 = (f32[1536]{0:T(1024)}, f32[1536]{0:T(1024)S(1)}, u32[]{:S(2)}) copy-start(f32[1536]{0:T(1024)S(1)} %div.92) | copy-start | bytes 18436
  55.6 72.2 %copy-start.48 = (f32[384]{0:T(512)}, f32[384]{0:T(512)S(1)}, u32[]{:S(2)}) copy-start(f32[384]{0:T(512)S(1)} %get-tuple-element.142) | copy-start | bytes 4612
  55.6 70.7 %copy-start.39 = (f32[1536]{0:T(1024)}, f32[1536]{0:T(1024)S(1)}, u32[]{:S(2)}) copy-start(f32[1536]{0:T(1024)S(1)} %add.219) | copy-start | bytes 18436
  55.7 72.2 %copy-start.45 = (f32[1536]{0:T(1024)}, f32[1536]{0:T(1024)S(1)}, u32[]{:S(2)}) copy-start(f32[1536]{0:T(1024)S(1)} %rsqrt.27) | copy-start | bytes 18436
  121.8 6.6 %copy-start.28 = (bf16[1152,384]{1,0:T(8,128)(2,1)}, bf16[1152,384]{1,0:T(8,128)(2,1)S(1)}, u32[]{:S(2)}) copy-start(bf16[1152,384]{1,0:T(8,128)(2,1)S(1)} %all_gather.21) | copy-start | bytes 2654212
  148.6 6.2 %copy-start.9 = (bf16[4,384,1,6,64]{1,0,4,3,2:T(4,128)(2,1)}, bf16[4,384,1,6,64]{1,0,4,3,2:T(4,128)(2,1)S(1)}, u32[]{:S(2)}) copy-start(bf16[4,384,1,6,64]{1,0,4,3,2:T(4,128)(2,1)S(1)} %get-tuple-element.130) | copy-start | bytes 3538948
  148.6 6.2 %copy-start.12 = (bf16[4,384,1,6,64]{1,0,4,3,2:T(4,128)(2,1)}, bf16[4,384,1,6,64]{1,0,4,3,2:T(4,128)(2,1)S(1)}, u32[]{:S(2)}) copy-start(bf16[4,384,1,6,64]{1,0,4,3,2:T(4,128)(2,1)S(1)} %get-tuple-element.129) | copy-start | bytes 3538948
  162.2 7.7 %copy-start.20 = (f32[4,6,384]{2,1,0:T(8,128)}, f32[4,6,384]{2,1,0:T(8,128)S(1)}, u32[]{:S(2)}) copy-start(f32[4,6,384]{2,1,0:T(8,128)S(1)} %log_add_fusion) | copy-start | bytes 110596
  172.3 2.0 copy-start.58
  172.3 2.0 copy-start.59
  174.2 26.7 %copy-start.50 = (f32[1536]{0:T(1024)}, f32[1536]{0:T(1024)S(1)}, u32[]{:S(2)}) copy-start(f32[1536]{0:T(1024)S(1)} %fusion.22) | copy-start | bytes 18436
  200.9 11.4 %copy-start.5 = (f32[1536,384]{1,0:T(8,128)S(1)}, f32[1536,384]{1,0:T(8,128)}, u32[]{:S(2)}) copy-start(f32[1536,384]{1,0:T(8,128)} %copy-done.4) | copy-start | bytes 7077892
  200.9 11.4 %copy-start.51 = (f32[1536]{0:T(1024)S(1)}, f32[1536]{0:T(1024)}, u32[]{:S(2)}) copy-start(f32[1536]{0:T(1024)} %copy-done.50) | copy-start | bytes 18436
  200.9 11.4 %copy-start.60 = (f32[384]{0:T(512)S(1)}, f32[384]{0:T(512)}, u32[]{:S(2)}) copy-start(f32[384]{0:T(512)} %get-tuple-element.137) | copy-start | bytes 4612
  200.9 11.4 %copy-start.71 = (bf16[1536,384]{1,0:T(8,128)(2,1)S(1)}, bf16[1536,384]{1,0:T(8,128)(2,1)}, u32[]{:S(2)}) copy-start(bf16[1536,384]{1,0:T(8,128)(2,1)} %all-gather.3.cloned.1.call-done) | copy-start | bytes 3538948
  212.3 3.8 copy-start.72
  217.8 2.1 copy-start.16
  230.5 9.0 %copy-start.11 = (bf16[4,384,6,64]{1,0,3,2:T(4,128)(2,1)S(1)}, bf16[4,384,6,64]{1,0,3,2:T(4,128)(2,1)}, u32[]{:S(2)}) copy-start(bf16[4,384,6,64]{1,0,3,2:T(4,128)(2,1)} %reshape.202) | copy-start | bytes 3538948
  230.5 9.0 %copy-start.21 = (f32[4,6,384]{2,1,0:T(8,128)S(1)}, f32[4,6,384]{2,1,0:T(8,128)}, u32[]{:S(2)}) copy-start(f32[4,6,384]{2,1,0:T(8,128)} %copy-done.20) | copy-start | bytes 110596
  249.9 128.4 %reduce-scatter.7.cloned.1.call-start = ((), (), s32[]{:S(2)}) async-start(), calls=%async_computation.6 | async-start | bytes 1990656 | tf_op jit(solution)/shard_map/reduce_scatter | solution.py:261
  250.0 10.4 %copy-start.10 = (bf16[4,384,1,6,64]{1,0,4,3,2:T(4,128)(2,1)S(1)}, bf16[4,384,1,6,64]{1,0,4,3,2:T(4,128)(2,1)}, u32[]{:S(2)}) copy-start(bf16[4,384,1,6,64]{1,0,4,3,2:T(4,128)(2,1)} %copy-done.9) | copy-start | bytes 3538948
  260.4 2.6 copy-start.13
  268.9 2.4 copy-start.23
  271.3 3.3 copy-start.22
  274.5 174.9 %reduce-scatter.13.cloned.1.call-start = ((), (), s32[]{:S(2)}) async-start(), calls=%async_computation.9 | async-start | bytes 2654208 | tf_op jit(solution)/shard_map/reduce_scatter | solution.py:264
  284.3 236.6 %reduce-scatter.11.cloned.1.call-start = ((), (), s32[]{:S(2)}) async-start(), calls=%async_computation.8 | async-start | bytes 2654208 | tf_op jit(solution)/shard_map/reduce_scatter | solution.py:263
  284.9 7.5 %copy-start.47 = (f32[3,6,64]{2,1,0:T(8,128)S(1)}, f32[3,6,64]{2,1,0:T(8,128)}, u32[]{:S(2)}) copy-start(f32[3,6,64]{2,1,0:T(8,128)} %get-tuple-element.117) | copy-start | bytes 13828
  284.9 7.6 %copy-start.29 = (bf16[1152,384]{1,0:T(8,128)(2,1)S(1)}, bf16[1152,384]{1,0:T(8,128)(2,1)}, u32[]{:S(2)}) copy-start(bf16[1152,384]{1,0:T(8,128)(2,1)} %copy-done.28) | copy-start | bytes 2654212
  291.6 265.3 %all-reduce.6.cloned.1.call-start = ((), (), s32[]{:S(2)}) async-start(), calls=%async_computation.10 | async-start | bytes 811008 | tf_op jit(solution)/shard_map/psum | solution.py:268
  293.2 6.1 %copy-start.69 = (f32[384]{0:T(512)S(1)}, f32[384]{0:T(512)}, u32[]{:S(2)}) copy-start(f32[384]{0:T(512)} %get-tuple-element.88) | copy-start | bytes 4612
  293.2 6.1 %copy-start.68 = (f32[384]{0:T(512)S(1)}, f32[384]{0:T(512)}, u32[]{:S(2)}) copy-start(f32[384]{0:T(512)} %get-tuple-element.92) | copy-start | bytes 4612
  293.2 6.1 %copy-start.56 = (f32[384]{0:T(512)S(1)}, f32[384]{0:T(512)}, u32[]{:S(2)}) copy-start(f32[384]{0:T(512)} %get-tuple-element.115) | copy-start | bytes 4612
  293.2 6.1 %copy-start.55 = (f32[384]{0:T(512)S(1)}, f32[384]{0:T(512)}, u32[]{:S(2)}) copy-start(f32[384]{0:T(512)} %get-tuple-element.132) | copy-start | bytes 4612
  293.3 6.2 %copy-start.57 = (f32[1536]{0:T(1024)S(1)}, f32[1536]{0:T(1024)}, u32[]{:S(2)}) copy-start(f32[1536]{0:T(1024)} %get-tuple-element.157) | copy-start | bytes 18436
  293.3 39.4 %copy-start.40 = (f32[1536]{0:T(1024)S(1)}, f32[1536]{0:T(1024)}, u32[]{:S(2)}) copy-start(f32[1536]{0:T(1024)} %copy-done.39) | copy-start | bytes 18436
  332.7 2.8 copy-start.6
  332.7 2.8 copy-start.64
  332.7 2.8 copy-start.70
  335.5 6.7 %copy-start.3 = (f32[4,384,384]{2,1,0:T(8,128)S(1)}, f32[4,384,384]{2,1,0:T(8,128)}, u32[]{:S(2)}) copy-start(f32[4,384,384]{2,1,0:T(8,128)} %param.18) | copy-start | bytes 7077892
  335.5 6.7 %copy-start.8 = (f32[1536,384]{1,0:T(8,128)S(1)}, f32[1536,384]{1,0:T(8,128)}, u32[]{:S(2)}) copy-start(f32[1536,384]{1,0:T(8,128)} %copy-done.7) | copy-start | bytes 7077892
  342.2 13.6 %copy-start.31 = (f32[48,384]{1,0:T(8,128)S(1)}, f32[48,384]{1,0:T(8,128)}, u32[]{:S(2)}) copy-start(f32[48,384]{1,0:T(8,128)} %param.20) | copy-start | bytes 221188
  342.2 13.6 %copy-start.41 = (f32[48,384]{1,0:T(8,128)S(1)}, f32[48,384]{1,0:T(8,128)}, u32[]{:S(2)}) copy-start(f32[48,384]{1,0:T(8,128)} %param.25) | copy-start | bytes 221188
  342.2 13.6 %copy-start.42 = (f32[48,384]{1,0:T(8,128)S(1)}, f32[48,384]{1,0:T(8,128)}, u32[]{:S(2)}) copy-start(f32[48,384]{1,0:T(8,128)} %param.30) | copy-start | bytes 221188
  342.2 180.3 %copy-start.54 = (f32[576]{0:T(1024)S(1)}, f32[576]{0:T(1024)}, u32[]{:S(2)}) copy-start(f32[576]{0:T(1024)} %param.23) | copy-start | bytes 6916
  342.2 180.3 %copy-start.62 = (f32[576]{0:T(1024)S(1)}, f32[576]{0:T(1024)}, u32[]{:S(2)}) copy-start(f32[576]{0:T(1024)} %param.28) | copy-start | bytes 6916
  342.2 180.3 %copy-start.63 = (f32[576]{0:T(1024)S(1)}, f32[576]{0:T(1024)}, u32[]{:S(2)}) copy-start(f32[576]{0:T(1024)} %param.33) | copy-start | bytes 6916
  344.1 212.7 %copy-start.27 = (f32[144,384]{1,0:T(8,128)S(1)}, f32[144,384]{1,0:T(8,128)}, u32[]{:S(2)}) copy-start(f32[144,384]{1,0:T(8,128)} %param.19) | copy-start | bytes 663556
  344.1 212.7 %copy-start.36 = (f32[144,384]{1,0:T(8,128)S(1)}, f32[144,384]{1,0:T(8,128)}, u32[]{:S(2)}) copy-start(f32[144,384]{1,0:T(8,128)} %param.24) | copy-start | bytes 663556
  344.1 212.7 %copy-start.37 = (f32[144,384]{1,0:T(8,128)S(1)}, f32[144,384]{1,0:T(8,128)}, u32[]{:S(2)}) copy-start(f32[144,384]{1,0:T(8,128)} %param.29) | copy-start | bytes 663556
  344.1 214.6 %copy-start.24 = (f32[192,384]{1,0:T(8,128)S(1)}, f32[192,384]{1,0:T(8,128)}, u32[]{:S(2)}) copy-start(f32[192,384]{1,0:T(8,128)} %param.21) | copy-start | bytes 884740
  344.1 214.6 %copy-start.32 = (f32[192,384]{1,0:T(8,128)S(1)}, f32[192,384]{1,0:T(8,128)}, u32[]{:S(2)}) copy-start(f32[192,384]{1,0:T(8,128)} %param.26) | copy-start | bytes 884740
  344.1 214.6 %copy-start.33 = (f32[192,384]{1,0:T(8,128)S(1)}, f32[192,384]{1,0:T(8,128)}, u32[]{:S(2)}) copy-start(f32[192,384]{1,0:T(8,128)} %param.31) | copy-start | bytes 884740
  451.1 109.6 %copy-start.25 = (f32[48,1536]{1,0:T(8,128)S(1)}, f32[48,1536]{1,0:T(8,128)}, u32[]{:S(2)}) copy-start(f32[48,1536]{1,0:T(8,128)} %param.22) | copy-start | bytes 884740
  451.1 109.6 %copy-start.34 = (f32[48,1536]{1,0:T(8,128)S(1)}, f32[48,1536]{1,0:T(8,128)}, u32[]{:S(2)}) copy-start(f32[48,1536]{1,0:T(8,128)} %param.27) | copy-start | bytes 884740
  451.1 109.6 %copy-start.35 = (f32[48,1536]{1,0:T(8,128)S(1)}, f32[48,1536]{1,0:T(8,128)}, u32[]{:S(2)}) copy-start(f32[48,1536]{1,0:T(8,128)} %param.32) | copy-start | bytes 884740
  556.8 3.9 copy-start.38
  (16 other events, 21.7 us)
Sparse Core Ops, SparseCore 0:
  10.8 44.0 all-gather.2
  57.6 45.4 all-gather.4
  250.0 59.4 reduce-scatter.8
  313.2 65.0 reduce-scatter.6
  381.6 67.8 reduce-scatter.12
  452.8 67.9 reduce-scatter.10
  525.1 31.6 all-reduce.5
where the time goes:
time: 574 us; the launch traced here: 569 us
  waiting for transfers between devices  195 us (34%)
  blocking collectives  149 us (26%)
  matrix products  118 us (21%)
  other arithmetic  51.5 us (9%)
  local copies, waits for them, and re-layouts  38.3 us (7%)
  between operations  16.8 us (3%)
    unnamed x2, blocking collectives  72.6 us
    reduce_scatter x1, waiting for transfers between devices, per_device(): lax.psum_scatter(up_grad, 'wide', scatter_dimension=0, tiled=True)  69.7 us
    reduce_scatter x1, waiting for transfers between devices, per_device(): lax.psum_scatter(down_grad, 'wide', scatter_dimension=0, tiled=True)  69.6 us
    dot_general x4, matrix products, project(): lax.dot_general(operand, weight, (((1,), (1,)), ((), ())), preferred_elem...  38.3 us
    psum x1, waiting for transfers between devices, per_device(): lax.psum(qkv_part.astype(jnp.bfloat16), 'narrow').astype(jnp.float32)  33.7 us
    all_gather x1, blocking collectives, per_device(): lax.all_gather(proj_copy, 'wide', axis=0, tiled=True)  33.2 us
    all_gather x1, blocking collectives, per_device(): lax.all_gather(qkv_copy, 'wide', axis=0, tiled=True)  32.9 us
    reduce_scatter x1, waiting for transfers between devices, per_device(): lax.psum_scatter(qkv_grad, 'wide', scatter_dimension=0, tiled=True)  21.7 us
  transfers between devices with their start and end apart: 7, of which 4 were waited for; matrix products, arithmetic and copies ran while one was open for 26% of the time, Pallas kernels for 0%

commit v1 on v0

v1 whole, which is shorter than its diff:
```python
import functools
import jax, jax.numpy as jnp
from jax import lax
from jax.experimental import pallas as pl
from jax.experimental.pallas import tpu as pltpu
from jax.sharding import PartitionSpec as P

STEP = 10
beta_first = 0.5
beta_second = 0.5
adam_eps = 1e-08
matrix_decay = 0.01
vector_rate = 0.3
HEADS = 6
EPS = 1e-6
bf16, f32 = jnp.bfloat16, jnp.float32

def dot(a, b, ca, cb):
    return lax.dot_general(a, b, (((ca,), (cb,)), ((), ())), preferred_element_type=f32)

def norm_stats(v):
    mean = jnp.mean(v, axis=-1, keepdims=True)
    cen = v - mean
    var = jnp.mean(cen * cen, axis=-1, keepdims=True)
    rstd = lax.rsqrt(var + EPS)
    return cen * rstd, rstd

def attn_fwd(x_ref, w_ref, vrow_ref, vcol_ref, jt_ref, e_ref, il_ref, ot_ref, h_ref):
    xhat, _ = norm_stats(x_ref[0])
    h = (xhat * vrow_ref[0:1, :] + vrow_ref[1:2, :]).astype(bf16)
    h_ref[0] = h
    d = h.shape[1]
    hs = d // HEADS
    jt = dot(w_ref[...], h, 1, 1) + vcol_ref[:, 0:1]
    jt_ref[0] = jt.astype(bf16)
    for i in range(HEADS):
        qt = jt_ref[0, i * hs:(i + 1) * hs, :]
        kt = jt_ref[0, d + i * hs:d + (i + 1) * hs, :]
        vt = jt_ref[0, 2 * d + i * hs:2 * d + (i + 1) * hs, :]
        st = dot((kt * 0.125), qt, 0, 0)
        m = jnp.max(st, axis=0, keepdims=True)
        e = jnp.exp(st - m)
        l = jnp.sum(e, axis=0, keepdims=True)
        eb = e.astype(bf16)
        e_ref[0, i] = eb
        il = 1.0 / l
        il_ref[0, i:i + 1, :] = il
        ot = dot(vt, eb, 1, 0) * il
        ot_ref[0, i * hs:(i + 1) * hs, :] = ot.astype(bf16)

def call_attn_fwd(x, w, vrow, vcol):
    b, t, d = x.shape
    one = lambda *s: pl.BlockSpec((1,) + s, lambda i: (i,) + (0,) * len(s))
    full = lambda a: pl.BlockSpec(a.shape, lambda i: (0,) * a.ndim)
    return pl.pallas_call(
        attn_fwd, grid=(b,),
        in_specs=[one(t, d), full(w), full(vrow), full(vcol)],
        out_specs=[one(3 * d, t), one(HEADS, t, t), one(8, t), one(d, t), one(t, d)],
        out_shape=[jax.ShapeDtypeStruct((b, 3 * d, t), bf16), jax.ShapeDtypeStruct((b, HEADS, t, t), bf16),
                   jax.ShapeDtypeStruct((b, 8, t), f32), jax.ShapeDtypeStruct((b, d, t), bf16), jax.ShapeDtypeStruct((b, t, d), bf16)],
        compiler_params=pltpu.CompilerParams(vmem_limit_bytes=50 << 20), name="attn_fwd",
    )(x, w, vrow, vcol)

def gelu_pair(u):
    cdf = 0.5 + 0.5 * lax.erf(u * (0.5 ** 0.5))
    pdf = jnp.exp(u * u * -0.5) * 0.3989422804014327
    return u * cdf, cdf + u * pdf

def mlp(x_ref, ot_ref, cot_ref, wp_ref, wu_ref, wd_ref, vrow_ref, ub_ref,
        mid_ref, act_ref, dm_ref, dot_ref, dwp_ref, dwu_ref, dwd_ref, dv_ref, dub_ref):
    i = pl.program_id(0)
    @pl.when(i == 0)
    def _():
        dwp_ref[...] = jnp.zeros_like(dwp_ref)
        dwu_ref[...] = jnp.zeros_like(dwu_ref)
        dwd_ref[...] = jnp.zeros_like(dwd_ref)
        dv_ref[...] = jnp.zeros_like(dv_ref)
        dub_ref[...] = jnp.zeros_like(dub_ref)
    ot = ot_ref[0]
    mid = x_ref[0] + (dot(ot, wp_ref[...], 0, 1) + vrow_ref[6:7, :])
    mid_ref[0] = mid
    xhat, rstd = norm_stats(mid)
    h2 = (xhat * vrow_ref[2:3, :] + vrow_ref[3:4, :]).astype(bf16)
    u = dot(h2, wu_ref[...], 1, 1) + ub_ref[0:1, :]
    act, gp = gelu_pair(u)
    act = act.astype(bf16)
    act_ref[0] = act
    cot = cot_ref[0]
    g = cot.astype(bf16)
    dwd_ref[...] += dot(g, act, 0, 0)
    du = dot(g, wd_ref[...], 1, 0) * gp
    dul = du.astype(bf16)
    dwu_ref[...] += dot(dul, h2, 0, 0)
    dh2 = dot(dul, wu_ref[...], 1, 0)
    gy = dh2 * vrow_ref[2:3, :]
    m1 = jnp.mean(gy, axis=-1, keepdims=True)
    m2 = jnp.mean(gy * xhat, axis=-1, keepdims=True)
    dm = cot + rstd * (gy - m1 - xhat * m2)
    dm_ref[0] = dm
    dml = dm.astype(bf16)
    dwp_ref[...] += dot(dml, ot, 0, 1)
    dot_ref[0] = dot(wp_ref[...], dml, 0, 1).astype(bf16)
    dv_ref[2:3, :] += jnp.sum(dh2 * xhat, axis=0, keepdims=True)
    dv_ref[3:4, :] += jnp.sum(dh2, axis=0, keepdims=True)
    dv_ref[6:7, :] += jnp.sum(dml.astype(f32), axis=0, keepdims=True)
    dv_ref[7:8, :] += jnp.sum(g.astype(f32), axis=0, keepdims=True)
    dub_ref[0:1, :] += jnp.sum(dul.astype(f32), axis=0, keepdims=True)

def call_mlp(x, ot, cot, wp, wu, wd, vrow, ub):
    b, t, d = x.shape
    ff = wu.shape[0]
    one = lambda *s: pl.BlockSpec((1,) + s, lambda i: (i,) + (0,) * len(s))
    full = lambda a: pl.BlockSpec(a.shape, lambda i: (0,) * a.ndim)
    S = jax.ShapeDtypeStruct
    outs = [S((b, t, d), f32), S((b, t, ff), bf16), S((b, t, d), f32), S((b, d, t), bf16),
            S((d, d), f32), S((ff, d), f32), S((d, ff), f32), S((8, d), f32), S((8, ff), f32)]
    return pl.pallas_call(
        mlp, grid=(b,),
        in_specs=[one(t, d), one(d, t), one(t, d)] + [full(a) for a in (wp, wu, wd, vrow, ub)],
        out_specs=[one(t, d), one(t, ff), one(t, d), one(d, t)] + [full(a) for a in outs[4:]],
        out_shape=outs,
        compiler_params=pltpu.CompilerParams(vmem_limit_bytes=56 << 20), name="mlp",
    )(x, ot, cot, wp, wu, wd, vrow, ub)

def attn_bwd(jt_ref, e_ref, il_ref, ot_ref, dot_ref, h_ref, dj_ref, dw_ref):
    i = pl.program_id(0)
    @pl.when(i == 0)
    def _():
        dw_ref[...] = jnp.zeros_like(dw_ref)
    t, d = h_ref.shape[1:]
    hs = d // HEADS
    for i in range(HEADS):
        rows = slice(i * hs, (i + 1) * hs)
        qt = jt_ref[0, i * hs:(i + 1) * hs, :]
        kt = jt_ref[0, d + i * hs:d + (i + 1) * hs, :]
        vt = jt_ref[0, 2 * d + i * hs:2 * d + (i + 1) * hs, :]
        do = dot_ref[0, rows, :].astype(f32) * il_ref[0, i:i + 1, :]
        dd = jnp.sum(do * ot_ref[0, rows, :].astype(f32), axis=0, keepdims=True)
        dob = do.astype(bf16)
        eb = e_ref[0, i]
        dp = dot(vt, dob, 0, 0)
        ds = (eb.astype(f32) * (dp - dd)).astype(bf16)
        dj_ref[0, rows, :] = (dot(kt, ds, 1, 0) * 0.125).astype(bf16)
        dj_ref[0, d + i * hs:d + (i + 1) * hs, :] = (dot(qt, ds, 1, 1) * 0.125).astype(bf16)
        dj_ref[0, 2 * d + i * hs:2 * d + (i + 1) * hs, :] = dot(dob, eb, 1, 1).astype(bf16)
    hx = jnp.concatenate([h_ref[0], jnp.ones((t, 128), bf16)], axis=1)
    dw_ref[...] += dot(dj_ref[0], hx, 1, 0)

def call_attn_bwd(jt, e, il, ot, dot_, h):
    b, t, d = h.shape
    one = lambda *s: pl.BlockSpec((1,) + s, lambda i: (i,) + (0,) * len(s))
    S = jax.ShapeDtypeStruct
    return pl.pallas_call(
        attn_bwd, grid=(b,),
        in_specs=[one(3 * d, t), one(HEADS, t, t), one(8, t), one(d, t), one(d, t), one(t, d)],
        out_specs=[one(3 * d, t), pl.BlockSpec((3 * d, d + 128), lambda i: (0, 0))],
        out_shape=[S((b, 3 * d, t), bf16), S((3 * d, d + 128), f32)],
        compiler_params=pltpu.CompilerParams(vmem_limit_bytes=50 << 20), name="attn_bwd",
    )(jt, e, il, ot, dot_, h)

def tail(x_ref, dm_ref, dj_ref, w_ref, mid_ref, act_ref, wd_ref, vrow_ref, gx_ref, lo_ref):
    lo_ref[0] = mid_ref[0] + (dot(act_ref[0], wd_ref[...], 1, 1) + vrow_ref[7:8, :])
    dh = dot(dj_ref[0], w_ref[...], 0, 0)
    xhat, rstd = norm_stats(x_ref[0])
    gy = dh * vrow_ref[0:1, :]
    m1 = jnp.mean(gy, axis=-1, keepdims=True)
    m2 = jnp.mean(gy * xhat, axis=-1, keepdims=True)
    gx_ref[0] = dm_ref[0] + rstd * (gy - m1 - xhat * m2)

def call_tail(x, dm, dj, w, mid, act, wd, vrow):
    b, t, d = x.shape
    one = lambda *s: pl.BlockSpec((1,) + s, lambda i: (i,) + (0,) * len(s))
    full = lambda a: pl.BlockSpec(a.shape, lambda i: (0,) * a.ndim)
    S = jax.ShapeDtypeStruct
    return pl.pallas_call(
        tail, grid=(b,),
        in_specs=[one(t, d), one(t, d), one(3 * d, t), full(w), one(t, d), one(t, act.shape[2]), full(wd), full(vrow)],
        out_specs=[one(t, d), one(t, d)],
        out_shape=[S((b, t, d), f32), S((b, t, d), f32)],
        compiler_params=pltpu.CompilerParams(vmem_limit_bytes=50 << 20), name="tail",
    )(x, dm, dj, w, mid, act, wd, vrow)


class Links:
    def __init__(self, mesh):
        self.wide, self.narrow = mesh.shape["wide"], mesh.shape["narrow"]
        bits = [1 << k for k in range(self.wide.bit_length() - 1)]
        self.orders = (bits[::-1], bits[:1] + bits[:0:-1])
        self.masks = []
        for order in self.orders:
            masks = [0]
            for bit in order:
                masks = masks + [m ^ bit for m in masks]
            self.masks.append(masks)
        self.slots = [[masks.index(m) for m in range(self.wide)] for masks in self.masks]

    def permute(self, value, partner):
        pairs = []
        for n in range(self.narrow):
            for w in range(self.wide):
                n2, w2 = partner(n, w)
                pairs.append((n * self.wide + w, n2 * self.wide + w2))
        return lax.ppermute(value, ("narrow", "wide"), pairs)

    def core(self, value):
        return self.permute(value, lambda n, w: (n ^ 1, w))

    def step(self, value, k):
        return self.permute(value, lambda n, w: (n, w ^ self.orders[n % 2][k]))

    def others(self, value):
        total = value.astype(f32)
        bit = 2
        while bit < self.narrow:
            low = total.astype(bf16)
            total = low.astype(f32) + self.permute(low, lambda n, w, bit=bit: (n ^ bit, w)).astype(f32)
            bit *= 2
        return total

    def here(self):
        return lax.axis_index("wide"), lax.axis_index("narrow") % 2

    def gather(self, packed):
        me, core = self.here()
        rows, columns = packed.shape
        held = lax.dynamic_slice_in_dim(packed, core * (rows // 2), rows // 2)
        for k in range(len(self.orders[0])):
            held = jnp.concatenate([held, self.step(held, k)], axis=0)
        both = jnp.concatenate([held, self.core(held)], axis=0).reshape(2 * self.wide, rows // 2, columns)
        relative = jnp.arange(self.wide) ^ me
        first = jnp.take(jnp.array(self.slots[0]), relative) + core * self.wide
        second = jnp.take(jnp.array(self.slots[1]), relative) + (1 - core) * self.wide
        index = jnp.stack([first, second], axis=1).reshape(-1)
        return jnp.take(both, index, axis=0).reshape(self.wide, rows, columns)

    def reduce(self, packed):
        me, core = self.here()
        _, rows, columns = packed.shape
        halves = packed.reshape(2 * self.wide, rows // 2, columns)
        masks = jnp.array(self.masks)
        own = jnp.take(halves, (masks[core] ^ me) * 2 + core, axis=0)
        give = jnp.take(halves, (masks[1 - core] ^ me) * 2 + (1 - core), axis=0)
        held = own + self.core(give.astype(bf16)).astype(f32)
        for k in range(len(self.orders[0]) - 1, -1, -1):
            half = held.shape[0] // 2
            held = held[:half] + self.step(held[half:].astype(bf16), k).astype(f32)
        total = self.others(held[0])
        other = self.core(total)
        return jnp.where(core == 0, jnp.concatenate([total, other]), jnp.concatenate([other, total]))


def to_rows(block, columns):
    return jnp.concatenate([block[..., j:j + columns] for j in range(0, block.shape[-1], columns)], axis=-2)


def from_rows(block, count):
    return jnp.concatenate(jnp.split(block, count, axis=-2), axis=-1)


def padded(block, multiple):
    extra = -block.shape[-2] % multiple
    return jnp.pad(block, [(0, 0)] * (block.ndim - 2) + [(0, extra), (0, 0)])


def adam_step(master, grad_sum, first_old, second_old, step_rate, weight_decay):
    first_new = beta_first * first_old + (1.0 - beta_first) * grad_sum
    second_new = beta_second * second_old + (1.0 - beta_second) * grad_sum * grad_sum
    first_hat = first_new / (1.0 - beta_first**STEP)
    second_hat = second_new / (1.0 - beta_second**STEP)
    updated = master - step_rate * (
        first_hat / (jnp.sqrt(second_hat) + adam_eps) + weight_decay * master
    )
    return (updated, first_new, second_new, updated.astype(bf16))


def per_device(links, x, cot, qkv_m, proj_m, up_m, down_m, vec_m, qkv_f, proj_f, up_f, down_f, vec_f, qkv_s, proj_s, up_s, down_s, vec_s):
    n = links.wide
    d = x.shape[2]
    ff = down_m.shape[1]
    parts = ff // d
    q_rows, p_rows, u_rows, v_size = qkv_m.shape[0], proj_m.shape[0], up_m.shape[0], vec_m.shape[0]
    v_rows = -(-v_size // d)
    vec_block = jnp.pad(vec_m, (0, v_rows * d - v_size)).reshape(v_rows, d)
    first = padded(jnp.concatenate([qkv_m, vec_block]).astype(bf16), 32)
    second = padded(jnp.concatenate([proj_m, up_m, to_rows(down_m, d)]).astype(bf16), 32)
    first_all = links.gather(first)
    second_all = links.gather(second)
    wq = first_all[:, :q_rows].reshape(-1, d)
    vec = first_all[:, q_rows:q_rows + v_rows].reshape(n, v_rows * d)[:, :v_size].reshape(-1).astype(f32)
    wp = second_all[:, :p_rows].reshape(-1, d)
    wu = second_all[:, p_rows:p_rows + u_rows].reshape(-1, d)
    wd = from_rows(second_all[:, p_rows + u_rows:p_rows + u_rows + parts * p_rows], parts).reshape(-1, ff)
    vrow = vec[:8 * d].reshape(8, d)
    qkv_bias = jnp.concatenate([vrow[4], jnp.zeros_like(vrow[4]), vrow[5]])
    vcol = jnp.broadcast_to(qkv_bias[:, None], (3 * d, 8))
    ub = jnp.broadcast_to(vec[None, 8 * d:], (8, ff))

    jt, e, il, ot, h = call_attn_fwd(x, wq, vrow, vcol)
    mid, act, dm, dot_, dwp, dwu, dwd, dv, dub = call_mlp(x, ot, cot, wp, wu, wd, vrow, ub)
    grads = padded(jnp.concatenate([dwp.reshape(n, p_rows, d), dwu.reshape(n, u_rows, d), to_rows(dwd.reshape(n, p_rows, ff), d)], axis=1), 32)
    second_sum = links.reduce(grads)
    dj, dwx = call_attn_bwd(jt, e, il, ot, dot_, h)
    dwq, db = dwx[:, :d], dwx[:, d]
    wqf = wq.astype(f32)
    dg1 = jnp.sum(wqf * (dwq - db[:, None] * vrow[1]), axis=0) / vrow[0]
    ds1 = jnp.sum(wqf * db[:, None], axis=0)
    dvec = jnp.concatenate([dg1, ds1, dv[2], dv[3], db[:d], db[2 * d:], dv[6], dv[7], dub[0]]).reshape(n, v_size)
    dvec = jnp.pad(dvec, ((0, 0), (0, v_rows * d - v_size))).reshape(n, v_rows, d)
    first_sum = links.reduce(padded(jnp.concatenate([dwq.reshape(n, q_rows, d), dvec], axis=1), 32))
    gx, lo = call_tail(x, dm, dj, wq, mid, act, wd, vrow)

    g_q = first_sum[:q_rows]
    g_v = first_sum[q_rows:q_rows + v_rows].reshape(-1)[:v_size]
    g_p = second_sum[:p_rows]
    g_u = second_sum[p_rows:p_rows + u_rows]
    g_d = from_rows(second_sum[p_rows + u_rows:p_rows + u_rows + parts * p_rows], parts)
    return (
        lo, gx,
        *adam_step(qkv_m, g_q, qkv_f, qkv_s, 0.6 * d ** -0.5, matrix_decay),
        *adam_step(proj_m, g_p, proj_f, proj_s, 0.6 * d ** -0.5, matrix_decay),
        *adam_step(up_m, g_u, up_f, up_s, 0.6 * d ** -0.5, matrix_decay),
        *adam_step(down_m, g_d, down_f, down_s, 0.6 * ff ** -0.5, matrix_decay),
        *adam_step(vec_m, g_v, vec_f, vec_s, vector_rate, 0.0),
    )


def solution(mesh):
    tokens = P(("narrow", "wide"), None, None)
    matrix, vector = P("wide", None), P("wide")
    state = (matrix,) * 4 + (vector,)
    return jax.shard_map(
        functools.partial(per_device, Links(mesh)),
        mesh=mesh,
        in_specs=(tokens, tokens) + state * 3,
        out_specs=(tokens, tokens) + (matrix,) * 16 + (vector,) * 4,
        check_vma=False,
    )
```

time: 574 us -> 207 us (0.36)
  waiting for transfers between devices: 195 us -> 40.8 us
  blocking collectives: 149 us -> 0 us
  matrix products: 118 us -> 0 us
  Pallas kernels: 0 us -> 67.2 us
  starting transfers between devices: 0.5 us -> 26 us
  other arithmetic: 51.5 us -> 26.8 us
  between operations: 16.8 us -> 1.56 us
    reduce_scatter x4 -> x0, waiting for transfers between devices: 161 us -> none  [the longest x1 69.7 us: per_device(): lax.psum_scatter(up_grad, 'wide', scatter_dimension=0, tiled=True)]
    dot_general x18 -> x0, matrix products: 118 us -> none  [the longest x4 38.3 us: project(): lax.dot_general(operand, weight, (((1,), (1,)), ((), ())), preferred_elem...]
    unnamed x2 -> x0, blocking collectives: 72.6 us -> none
    pallas_call x0 -> x4, Pallas kernels: none -> 67.2 us  [the longest x1 24.4 us: call_mlp(): pl.pallas_call(mlp, grid=(b,), in_specs=[one(t, d), one(d, t), one(t, d)]...]
    all_gather x2 -> x0, blocking collectives: 66 us -> none  [the longest x1 33.2 us: per_device(): lax.all_gather(proj_copy, 'wide', axis=0, tiled=True)]
    ppermute x0 -> x20, waiting for transfers between devices: none -> 40.8 us  [permute(): return lax.ppermute(value, ('narrow', 'wide'), pairs)]
    psum x1 -> x0, waiting for transfers between devices: 33.7 us -> none  [per_device(): lax.psum(qkv_part.astype(jnp.bfloat16), 'narrow').astype(jnp.float32)]
    ppermute x0 -> x20, starting transfers between devices: none -> 26 us  [permute(): return lax.ppermute(value, ('narrow', 'wide'), pairs)]
  transfers between devices with their start and end apart: 7 -> 20, of which waited for: 4 -> 10; matrix products, arithmetic and copies ran while one was open for 26% -> 15% of each run, Pallas kernels for 0% -> 12%
where the time goes in v1:
time: 207 us; the launch traced here: 206 us
  Pallas kernels  67.2 us (32%)
  local copies, waits for them, and re-layouts  43.4 us (21%)
  waiting for transfers between devices  40.8 us (20%)
  other arithmetic  26.8 us (13%)
  starting transfers between devices  26 us (13%)
    ppermute x20, waiting for transfers between devices, permute(): return lax.ppermute(value, ('narrow', 'wide'), pairs)  40.8 us
    ppermute x20, starting transfers between devices, permute(): return lax.ppermute(value, ('narrow', 'wide'), pairs)  26 us
    pallas_call x1, Pallas kernels, call_mlp(): pl.pallas_call(mlp, grid=(b,), in_specs=[one(t, d), one(d, t), one(t, d)]...  24.4 us
    pallas_call x1, Pallas kernels, call_attn_bwd(): pl.pallas_call(attn_bwd, grid=(b,), in_specs=[one(3 * d, t), one(HEADS, t...  17 us
    pallas_call x1, Pallas kernels, call_attn_fwd(): pl.pallas_call(attn_fwd, grid=(b,), in_specs=[one(t, d), full(w), full(vr...  15.7 us
    pallas_call x1, Pallas kernels, call_tail(): pl.pallas_call(tail, grid=(b,), in_specs=[one(t, d), one(t, d), one(3 * d...  10.1 us
    unnamed x102, local copies, waits for them, and re-layouts  9.8 us
    gather x2, local copies, waits for them, and re-layouts, reduce(): give = jnp.take(halves, (masks[1 - core] ^ me) * 2 + (1 - core), axis=0)  6.66 us
  transfers between devices with their start and end apart: 20, of which 10 were waited for; matrix products, arithmetic and copies ran while one was open for 15% of the time, Pallas kernels for 12%

profile of v1, /device:TPU:0, one launch (start us, length us, event | category | flops | bytes accessed | tf_op | source)
XLA Modules:
  0.0 205.9 jit_solution(3044917760510241386)
XLA Ops:
  0.7 0.7 convert.47
  1.4 0.9 convert.46
  2.4 4.1 %collective-permute-start = (bf16[80,384]{1,0:T(8,128)(2,1)S(1)}, bf16[80,384]{1,0:T(8,128)(2,1)S(1)}, u32[]{:S(2)}, u32[]{:S(2)}) collective-permute-start(bf16[80,384]{1,0:T(8,128)(2,1)S(1)} %get-tuple-element.94), channel_id=1, source_target_pairs={{0,4},{1,5},{2,6},{3,7},{4,0},{5,1},{6,2},{7,3},{8,9},{9,8},{10,11... | collective-permute-start | bytes 184328 | tf_op jit(solution)/shard_map/ppermute | solution.py:203
  6.5 0.9 constant_dynamic-update-slice_fusion.9
  7.4 1.0 convert.50
  8.4 1.0 convert_dynamic-update-slice_fusion
  9.5 0.7 constant_dynamic-update-slice_fusion.14
  10.2 0.6 gather_fusion.3
  10.9 0.6 gather_fusion.2
  11.8 2.0 collective-permute-start.1
  14.2 2.5 %collective-permute-done.1 = bf16[160,384]{1,0:T(8,128)(2,1)S(1)} collective-permute-done((bf16[160,384]{1,0:T(8,128)(2,1)S(1)}, bf16[160,384]{1,0:T(8,128)(2,1)S(1)}, u32[]{:S(2)}, u32[]{:S(2)}) %collective-permute-start.1) | collective-permute-done | bytes 122912 | tf_op jit(solution)/shard_map/ppermute | solution.py:203
  16.7 1.9 collective-permute-start.2
  18.6 1.7 collective-permute-done.4
  21.0 2.1 collective-permute-done.2
  23.1 6.7 %collective-permute-start.3 = (bf16[640,384]{1,0:T(8,128)(2,1)S(1)}, bf16[640,384]{1,0:T(8,128)(2,1)S(1)}, u32[]{:S(2)}, u32[]{:S(2)}) collective-permute-start(bf16[640,384]{1,0:T(8,128)(2,1)S(1)} %pad_maximum_fusion.3), channel_id=1, source_target_pairs={{0,8},{1,9},{2,10},{3,11},{4,12},{5,13},{6,14},{7,15},{8,0},{9,1},... | collective-permute-start | bytes 1474568 | tf_op jit(solution)/shard_map/ppermute | solution.py:203
  29.8 2.1 %collective-permute-done.5 = bf16[448,384]{1,0:T(8,128)(2,1)S(1)} collective-permute-done((bf16[448,384]{1,0:T(8,128)(2,1)S(1)}, bf16[448,384]{1,0:T(8,128)(2,1)S(1)}, u32[]{:S(2)}, u32[]{:S(2)}) %collective-permute-start.5) | collective-permute-done | bytes 344096 | tf_op jit(solution)/shard_map/ppermute | solution.py:203
  32.0 1.7 collective-permute-start.6
  33.7 0.7 constant_dynamic-update-slice_fusion.13
  34.4 0.8 constant_dynamic-update-slice_fusion.12
  35.3 0.9 copy-done.16
  36.3 2.0 gather_fusion
  38.2 4.8 %collective-permute-done.6 = bf16[896,384]{1,0:T(8,128)(2,1)S(1)} collective-permute-done((bf16[896,384]{1,0:T(8,128)(2,1)S(1)}, bf16[896,384]{1,0:T(8,128)(2,1)S(1)}, u32[]{:S(2)}, u32[]{:S(2)}) %collective-permute-start.6) | collective-permute-done | bytes 688160 | tf_op jit(solution)/shard_map/ppermute | solution.py:203
  43.0 1.3 pad_maximum_fusion
  45.1 15.7 %attn_fwd.1 = (bf16[4,1152,384]{2,1,0:T(8,128)(2,1)}, bf16[4,6,384,384]{3,2,1,0:T(8,128)(2,1)}, f32[4,8,384]{2,1,0:T(8,128)S(1)}, bf16[4,384,384]{2,1,0:T(8,128)(2,1)S(1)}, bf16[4,384,384]{2,1,0:T(8,128)(2,1)S(1)}) custom-call(f32[4,384,384]{2,1,0:T(8,128)} %x_ref.5, bf16[1152,384]{1,0:T(8,128)(2,1)S(1)} %bitcast.42, ...), custom_call_target="tpu_custom_call" | custom-call | tf_op jit(solution)/shard_map/attn_fwd/pallas_call | solution.py:55
  60.8 1.1 copy-done.1
  61.9 2.1 %constant_dynamic-update-slice_fusion.11 = bf16[3584,384]{1,0:T(8,128)(2,1)} fusion(bf16[3584,384]{1,0:T(8,128)(2,1)} %constant_dynamic-update-slice_fusion.12, bf16[896,384]{1,0:T(8,128)(2,1)} %copy-done.11), kind=kLoop, calls=%fused_computation.88 | loop fusion | bytes 1376256
  64.0 2.5 %constant_dynamic-update-slice_fusion.10 = bf16[3584,384]{1,0:T(8,128)(2,1)} fusion(bf16[3584,384]{1,0:T(8,128)(2,1)} %constant_dynamic-update-slice_fusion.11, bf16[1792,384]{1,0:T(8,128)(2,1)} %collective-permute-done.7), kind=kLoop, calls=%fused_computation.87 | loop fusion | bytes 2752512 | tf_op jit(solution)/shard_map/concatenate | solution.py:229
  66.6 4.2 %gather_fusion.1 = bf16[16,224,384]{2,1,0:T(8,128)(2,1)} fusion(bf16[16,224,384]{2,1,0:T(8,128)(2,1)} %bitcast.6, s32[1024]{0:T(1024)S(1)} %pad_clamp_fusion.2), kind=kCustom, calls=%fused_computation.7 | custom fusion | bytes 5505088 | tf_op jit(solution)/shard_map/jit(_take)/gather | solution.py:234
  70.8 2.2 %bitcast_select_fusion = bf16[8,448,384]{2,1,0:T(8,128)(2,1)S(1)} fusion(pred[8,448]{1,0:T(8,128)(4,1)S(1)} %broadcast_in_dim.71, bf16[8,448,384]{2,1,0:T(8,128)(2,1)} %bitcast.48), kind=kLoop, calls=%fused_computation.8 | loop fusion | flops 1376256 | bytes 5508608 | tf_op jit(solution)/shard_map/jit(_take)/select_n | solution.py:234
  73.0 0.9 fusion.34
  73.9 1.2 slice.250
  75.1 1.1 pad_maximum_fusion.1
  76.2 0.6 broadcast_in_dim.74.ub_ref
  76.9 24.4 %mlp.1 = (f32[4,384,384]{2,1,0:T(8,128)}, bf16[4,384,1536]{2,1,0:T(8,128)(2,1)}, f32[4,384,384]{2,1,0:T(8,128)}, bf16[4,384,384]{2,1,0:T(8,128)(2,1)}, f32[384,3...) custom-call(f32[4,384,384]{2,1,0:T(8,128)} %x_ref.5, ...), custom_call_target="tpu_custom_call" | custom-call | tf_op jit(solution)/shard_map/mlp/pallas_call | solution.py:117
  101.3 1.3 copy-done.3
  102.6 17.0 %attn_bwd.1 = (bf16[4,1152,384]{2,1,0:T(8,128)(2,1)}, f32[1152,512]{1,0:T(8,128)}) custom-call(bf16[4,1152,384]{2,1,0:T(8,128)(2,1)} %get-tuple-element.45.jt_ref, bf16[4,6,384,384]{3,2,1,0:T(8,128)(2,1)} %get-tuple-element.46.e_ref, f32[4,8,384]{2,1,0:T(8,128)S(1)} %get-tuple-element.47.il_ref, bf16[4,384,384]{2,1,0:T(8,128)(2,1)S(1)} %copy-done.2, ...), custom_call_target="tpu_custom_call" | custom-call | tf_op jit(solution)/shard_map/attn_bwd/pallas_call | solution.py:153
  119.6 1.3 slice_reduce_fusion
  121.0 3.2 %fusion.35 = (f32[1152,384]{1,0:T(8,128)}, f32[384]{0:T(512)S(1)}) fusion(f32[1152,512]{1,0:T(8,128)} %get-tuple-element.55, f32[384]{0:T(512)S(1)} %get-tuple-element.110, f32[1152]{0:T(1024)S(1)} %slice_reduce_fusion, bf16[8,144,384]{2,1,0:T(8,128)(2,1)S(1)} %slice.239), kind=kLoop, calls=%fused_computation.152 | loop fusion | flops 2211456 | bytes 4431360 | tf_op jit(solution)/shard_map/slice | solution.py:303
  124.8 1.5 copy-done.12
  126.5 2.9 %pad.30 = f32[8,448,384]{2,1,0:T(8,128)} pad(f32[8,432,384]{2,1,0:T(8,128)S(1)} %slice_dynamic-update-slice_fusion, f32[]{:T(128)} %constant.95.clone.1), padding=0_0x0_16x0_0 | pad | bytes 10813444 | tf_op jit(solution)/shard_map/jit(_pad)/pad | solution.py:262
  129.4 4.3 %gather_fusion.7 = bf16[8,224,384]{2,1,0:T(8,128)(2,1)} fusion(f32[16,224,384]{2,1,0:T(8,128)} %bitcast.46, s32[1024]{0:T(1024)S(1)} %pad_clamp_fusion), kind=kCustom, calls=%fused_computation.5.clone | custom fusion | bytes 2752544 | tf_op jit(solution)/shard_map/jit(_take)/gather | solution.py:242
  133.7 3.0 %select_convert_fusion = bf16[8,224,384]{2,1,0:T(8,128)(2,1)} fusion(bf16[8,224,384]{2,1,0:T(8,128)(2,1)} %gather_fusion.7, pred[8]{0:T(512)(128)(4,1)S(1)} %copy-done.32), kind=kLoop, calls=%fused_computation.9 | loop fusion | flops 688128 | bytes 2752520 | tf_op jit(solution)/shard_map/convert_element_type | solution.py:243
  137.3 1.2 slice_reduce_fusion.1
  138.5 0.8 slice_reduce_fusion.3
  139.5 1.4 select_maximum_fusion
  140.9 2.3 %gather_fusion.5 = bf16[8,80,384]{2,1,0:T(8,128)(2,1)S(1)} fusion(f32[16,80,384]{2,1,0:T(8,128)} %bitcast.50, s32[1024]{0:T(1024)S(1)} %pad_clamp_fusion), kind=kCustom, calls=%fused_computation.4.clone | custom fusion | bytes 983072 | tf_op jit(solution)/shard_map/jit(_take)/gather | solution.py:242
  143.2 0.9 select_convert_fusion.1
  144.2 1.6 gather_fusion.4
  145.7 4.8 %gather_fusion.6 = f32[8,224,384]{2,1,0:T(8,128)} fusion(f32[16,224,384]{2,1,0:T(8,128)} %bitcast.47, s32[1024]{0:T(1024)S(1)} %pad_clamp_fusion.1), kind=kCustom, calls=%fused_computation.2.clone | custom fusion | bytes 5505056 | tf_op jit(solution)/shard_map/jit(_take)/gather | solution.py:241
  150.6 2.6 %select_add_fusion = f32[8,224,384]{2,1,0:T(8,128)S(1)} fusion(f32[8,224,384]{2,1,0:T(8,128)} %gather_fusion.6, bf16[8,224,384]{2,1,0:T(8,128)(2,1)} %collective-permute-done.14, pred[8]{0:T(512)(128)(4,1)S(1)} %copy-done.33), kind=kLoop, calls=%fused_computation.10 | loop fusion | flops 2064384 | bytes 6881288 | tf_op jit(solution)/shard_map/add | solution.py:243
  153.3 1.7 collective-permute-start.15
  155.7 11.3 %collective-permute-done.9 = bf16[4,80,384]{2,1,0:T(8,128)(2,1)S(1)} collective-permute-done((bf16[4,80,384]{2,1,0:T(8,128)(2,1)S(1)}, bf16[4,80,384]{2,1,0:T(8,128)(2,1)S(1)}, u32[]{:S(2)}, u32[]{:S(2)}) %collective-permute-start.9) | collective-permute-done | bytes 245792 | tf_op jit(solution)/shard_map/ppermute | solution.py:203
  167.3 2.1 %collective-permute-start.16 = (bf16[2,224,384]{2,1,0:T(8,128)(2,1)S(1)}, bf16[2,224,384]{2,1,0:T(8,128)(2,1)S(1)}, u32[]{:S(2)}, u32[]{:S(2)}) collective-permute-start(bf16[2,224,384]{2,1,0:T(8,128)(2,1)S(1)} %slice.328), channel_id=1, source_target_pairs={{0,2},{1,3},{2,0},{3,1},{4,6},{5,7},{6,4},{7,5},{8,12},{9,13},{10,... | collective-permute-start | bytes 1032200 | tf_op jit(solution)/shard_map/ppermute | solution.py:203
  169.3 4.0 %collective-permute-done.10 = bf16[2,80,384]{2,1,0:T(8,128)(2,1)S(1)} collective-permute-done((bf16[2,80,384]{2,1,0:T(8,128)(2,1)S(1)}, bf16[2,80,384]{2,1,0:T(8,128)(2,1)S(1)}, u32[]{:S(2)}, u32[]{:S(2)}) %collective-permute-start.10) | collective-permute-done | bytes 122912 | tf_op jit(solution)/shard_map/ppermute | solution.py:203
  173.7 6.4 %collective-permute-done.11 = bf16[1,80,384]{2,1,0:T(8,128)(2,1)S(1)} collective-permute-done((bf16[1,80,384]{2,1,0:T(8,128)(2,1)S(1)}, bf16[1,80,384]{2,1,0:T(8,128)(2,1)S(1)}, u32[]{:S(2)}, u32[]{:S(2)}) %collective-permute-start.11) | collective-permute-done | bytes 61472 | tf_op jit(solution)/shard_map/ppermute | solution.py:203
  180.2 1.8 collective-permute-start.12
  182.1 2.1 %collective-permute-start.17 = (bf16[1,224,384]{2,1,0:T(8,128)(2,1)S(1)}, bf16[1,224,384]{2,1,0:T(8,128)(2,1)S(1)}, u32[]{:S(2)}, u32[]{:S(2)}) collective-permute-start(bf16[1,224,384]{2,1,0:T(8,128)(2,1)S(1)} %slice.330), channel_id=1, source_target_pairs={{0,4},{1,5},{2,6},{3,7},{4,0},{5,1},{6,2},{7,3},{8,9},{9,8},{10,11... | collective-permute-start | bytes 516104 | tf_op jit(solution)/shard_map/ppermute | solution.py:203
  184.5 5.7 %collective-permute-done.17 = bf16[1,224,384]{2,1,0:T(8,128)(2,1)S(1)} collective-permute-done((bf16[1,224,384]{2,1,0:T(8,128)(2,1)S(1)}, bf16[1,224,384]{2,1,0:T(8,128)(2,1)S(1)}, u32[]{:S(2)}, u32[]{:S(2)}) %collective-permute-start.17) | collective-permute-done | bytes 172064 | tf_op jit(solution)/shard_map/ppermute | solution.py:203
  190.8 10.1 %tail.1 = (f32[4,384,384]{2,1,0:T(8,128)}, f32[4,384,384]{2,1,0:T(8,128)}) custom-call(f32[4,384,384]{2,1,0:T(8,128)} %x_ref.5, f32[4,384,384]{2,1,0:T(8,128)} %get-tuple-element.44.dm_ref, bf16[4,1152,384]{2,1,0:T(8,128)(2,1)} %get-tuple-element.50.dj_ref, bf16[1152,384]{1,0:T(8,128)(2,1)S(1)} %bitcast.43, f32[4,384,384]{2,1,0:T(8,128)} %get-tuple-element.51.mid_ref, ...), custom_call_target="tpu_custom_call" | custom-call | tf_op jit(solution)/shard_map/tail/pallas_call | solution.py:175
  201.2 0.6 fusion.23
  201.8 1.0 fusion.31
  202.9 0.7 fusion.36
  203.6 1.1 fusion.27
  204.7 1.1 fusion.25
  (184 shorter events, 6.8 us)
Async XLA Ops:
  0.7 9.6 %copy-start.7 = (s32[8]{0:T(128)S(1)}, s32[8]{0:T(128)}, u32[]{:S(2)}) copy-start(s32[8]{0:T(128)} %constant.155.clone2.1) | copy-start | bytes 100
  0.7 10.2 %copy-start.6 = (s32[8]{0:T(128)S(1)}, s32[8]{0:T(128)}, u32[]{:S(2)}) copy-start(s32[8]{0:T(128)} %constant.154.clone2.1) | copy-start | bytes 100
  2.4 18.0 %copy-start.38 = (s32[2,8]{1,0:T(2,128)S(1)}, s32[2,8]{1,0:T(2,128)}, u32[]{:S(2)}) copy-start(s32[2,8]{1,0:T(2,128)} %constant.156.clone) | copy-start | bytes 196
  2.4 9.3 %collective-permute-start = (bf16[80,384]{1,0:T(8,128)(2,1)S(1)}, bf16[80,384]{1,0:T(8,128)(2,1)S(1)}, u32[]{:S(2)}, u32[]{:S(2)}) collective-permute-start(bf16[80,384]{1,0:T(8,128)(2,1)S(1)} %get-tuple-element.94), channel_id=1, source_target_pairs={{0,4},{1,5},{2,6},{3,7},{4,0},{5,1},{6,2},{7,3},{8,9},{9,8},{10,11... | collective-permute-start | bytes 184328 | tf_op jit(solution)/shard_map/ppermute | solution.py:203
  10.2 10.1 %collective-permute-start.4 = (bf16[224,384]{1,0:T(8,128)(2,1)S(1)}, bf16[224,384]{1,0:T(8,128)(2,1)S(1)}, u32[]{:S(2)}, u32[]{:S(2)}) collective-permute-start(bf16[224,384]{1,0:T(8,128)(2,1)S(1)} %get-tuple-element.92), channel_id=1, source_target_pairs={{0,4},{1,5},{2,6},{3,7},{4,0},{5,1},{6,2},{7,3},{8,9},{9,8},{10,11... | collective-permute-start | bytes 516104 | tf_op jit(solution)/shard_map/ppermute | solution.py:203
  11.8 4.9 %collective-permute-start.1 = (bf16[160,384]{1,0:T(8,128)(2,1)S(1)}, bf16[160,384]{1,0:T(8,128)(2,1)S(1)}, u32[]{:S(2)}, u32[]{:S(2)}) collective-permute-start(bf16[160,384]{1,0:T(8,128)(2,1)S(1)} %pad_maximum_fusion.7), channel_id=1, source_target_pairs={{0,2},{1,3},{2,0},{3,1},{4,6},{5,7},{6,4},{7,5},{8,12},{9,13},{10,... | collective-permute-start | bytes 368648 | tf_op jit(solution)/shard_map/ppermute | solution.py:203
  16.7 6.3 %collective-permute-start.2 = (bf16[320,384]{1,0:T(8,128)(2,1)S(1)}, bf16[320,384]{1,0:T(8,128)(2,1)S(1)}, u32[]{:S(2)}, u32[]{:S(2)}) collective-permute-start(bf16[320,384]{1,0:T(8,128)(2,1)S(1)} %pad_maximum_fusion.6), channel_id=1, source_target_pairs={{0,1},{1,0},{2,3},{3,2},{4,5},{5,4},{6,7},{7,6},{8,10},{9,11},{10,... | collective-permute-start | bytes 737288 | tf_op jit(solution)/shard_map/ppermute | solution.py:203
  20.3 11.6 %collective-permute-start.5 = (bf16[448,384]{1,0:T(8,128)(2,1)S(1)}, bf16[448,384]{1,0:T(8,128)(2,1)S(1)}, u32[]{:S(2)}, u32[]{:S(2)}) collective-permute-start(bf16[448,384]{1,0:T(8,128)(2,1)S(1)} %pad_maximum_fusion.4), channel_id=1, source_target_pairs={{0,2},{1,3},{2,0},{3,1},{4,6},{5,7},{6,4},{7,5},{8,12},{9,13},{10,... | collective-permute-start | bytes 1032200 | tf_op jit(solution)/shard_map/ppermute | solution.py:203
  23.1 12.2 %collective-permute-start.3 = (bf16[640,384]{1,0:T(8,128)(2,1)S(1)}, bf16[640,384]{1,0:T(8,128)(2,1)S(1)}, u32[]{:S(2)}, u32[]{:S(2)}) collective-permute-start(bf16[640,384]{1,0:T(8,128)(2,1)S(1)} %pad_maximum_fusion.3), channel_id=1, source_target_pairs={{0,8},{1,9},{2,10},{3,11},{4,12},{5,13},{6,14},{7,15},{8,0},{9,1},... | collective-permute-start | bytes 1474568 | tf_op jit(solution)/shard_map/ppermute | solution.py:203
  32.0 11.0 %collective-permute-start.6 = (bf16[896,384]{1,0:T(8,128)(2,1)S(1)}, bf16[896,384]{1,0:T(8,128)(2,1)S(1)}, u32[]{:S(2)}, u32[]{:S(2)}) collective-permute-start(bf16[896,384]{1,0:T(8,128)(2,1)S(1)} %pad_maximum_fusion.2), channel_id=1, source_target_pairs={{0,1},{1,0},{2,3},{3,2},{4,5},{5,4},{6,7},{7,6},{8,10},{9,11},{10,... | collective-permute-start | bytes 2064392 | tf_op jit(solution)/shard_map/ppermute | solution.py:203
  35.3 0.9 copy-start.16
  43.0 1.3 copy-start.11
  44.3 19.7 %collective-permute-start.7 = (bf16[1792,384]{1,0:T(8,128)(2,1)}, bf16[1792,384]{1,0:T(8,128)(2,1)}, u32[]{:S(2)}, u32[]{:S(2)}) collective-permute-start(bf16[1792,384]{1,0:T(8,128)(2,1)} %pad_maximum_fusion), channel_id=1, source_target_pairs={{0,8},{1,9},{2,10},{3,11},{4,12},{5,13},{6,14},{7,15},{8,0},{9,1},... | collective-permute-start | bytes 4128776 | tf_op jit(solution)/shard_map/ppermute | solution.py:203
  44.9 19.1 %copy-start.28 = (f32[4608]{0:T(1024)}, f32[4608]{0:T(1024)S(1)}, u32[]{:S(2)}) copy-start(f32[4608]{0:T(1024)S(1)} %reshape.265) | copy-start | bytes 55300
  44.9 19.1 %copy-start.4 = (f32[8,384]{1,0:T(8,128)}, f32[8,384]{1,0:T(8,128)S(1)}, u32[]{:S(2)}) copy-start(f32[8,384]{1,0:T(8,128)S(1)} %slice_convert_fusion.6.vrow_ref) | copy-start | bytes 36868
  60.8 1.1 copy-start.1
  73.9 2.4 %slice-start = ((f32[4608]{0:T(1024)}), f32[1536]{0:T(1024)S(1)}, s32[]{:S(2)}) async-start(f32[4608]{0:T(1024)} %copy-done.28), calls=%async_computation | async-start | bytes 16384 | tf_op jit(solution)/shard_map/slice | solution.py:296
  76.9 24.4 %copy-start.2 = (bf16[4,384,384]{2,1,0:T(8,128)(2,1)S(1)}, bf16[4,384,384]{2,1,0:T(8,128)(2,1)}, u32[]{:S(2)}) copy-start(bf16[4,384,384]{2,1,0:T(8,128)(2,1)} %copy-done.1) | copy-start | bytes 3538948
  101.3 1.3 copy-start.3
  121.0 3.5 %copy-start.36 = (f32[8,384]{1,0:T(8,128)S(1)}, f32[8,384]{1,0:T(8,128)}, u32[]{:S(2)}) copy-start(f32[8,384]{1,0:T(8,128)} %get-tuple-element.56) | copy-start | bytes 36868
  121.0 3.5 %copy-start.18 = (f32[384,384]{1,0:T(8,128)S(1)}, f32[384,384]{1,0:T(8,128)}, u32[]{:S(2)}) copy-start(f32[384,384]{1,0:T(8,128)} %get-tuple-element.58) | copy-start | bytes 1769476
  121.0 3.6 %copy-start.13 = (f32[1536,384]{1,0:T(8,128)S(1)}, f32[1536,384]{1,0:T(8,128)}, u32[]{:S(2)}) copy-start(f32[1536,384]{1,0:T(8,128)} %get-tuple-element.59) | copy-start | bytes 7077892
  124.6 1.7 copy-start.12
  129.4 4.4 %copy-start.32 = (pred[8]{0:T(512)(128)(4,1)S(1)}, pred[8]{0:T(512)(128)(4,1)}, u32[]{:S(2)}) copy-start(pred[8]{0:T(512)(128)(4,1)} %get-tuple-element.89) | copy-start | bytes 28
  129.4 7.8 %copy-start.29 = (f32[4608]{0:T(1024)S(1)}, f32[4608]{0:T(1024)}, u32[]{:S(2)}) copy-start(f32[4608]{0:T(1024)} %copy-done.28) | copy-start | bytes 55300
  129.4 7.8 %copy-start.30 = (f32[4608]{0:T(1024)S(1)}, f32[4608]{0:T(1024)}, u32[]{:S(2)}) copy-start(f32[4608]{0:T(1024)} %custom-call.1) | copy-start | bytes 55300
  133.7 5.7 %copy-start.8 = (f32[1152,384]{1,0:T(8,128)S(1)}, f32[1152,384]{1,0:T(8,128)}, u32[]{:S(2)}) copy-start(f32[1152,384]{1,0:T(8,128)} %get-tuple-element.100) | copy-start | bytes 5308420
  136.7 13.9 %collective-permute-start.14 = (bf16[8,224,384]{2,1,0:T(8,128)(2,1)}, bf16[8,224,384]{2,1,0:T(8,128)(2,1)}, u32[]{:S(2)}, u32[]{:S(2)}) collective-permute-start(bf16[8,224,384]{2,1,0:T(8,128)(2,1)} %select_convert_fusion), channel_id=1, source_target_pairs={{0,8},{1,9},{2,10},{3,11},{4,12},{5,13},{6,14},{7,15},{8,0},{9,1},... | collective-permute-start | bytes 4128776 | tf_op jit(solution)/shard_map/ppermute | solution.py:203
  139.5 4.7 %copy-start.37 = (s32[8]{0:T(128)S(1)}, s32[8]{0:T(128)}, u32[]{:S(2)}) copy-start(s32[8]{0:T(128)} %get-tuple-element.116) | copy-start | bytes 100
  140.9 3.3 %copy-start.9 = (f32[8,160,384]{2,1,0:T(8,128)S(1)}, f32[8,160,384]{2,1,0:T(8,128)}, u32[]{:S(2)}) copy-start(f32[8,160,384]{2,1,0:T(8,128)} %select_maximum_fusion) | copy-start | bytes 5898244
  144.2 10.8 %collective-permute-start.8 = (bf16[8,80,384]{2,1,0:T(8,128)(2,1)}, bf16[8,80,384]{2,1,0:T(8,128)(2,1)S(1)}, u32[]{:S(2)}, u32[]{:S(2)}) collective-permute-start(bf16[8,80,384]{2,1,0:T(8,128)(2,1)} %select_convert_fusion.1), channel_id=1, source_target_pairs={{0,8},{1,9},{2,10},{3,11},{4,12},{5,13},{6,14},{7,15},{8,0},{9,1},... | collective-permute-start | bytes 1474568 | tf_op jit(solution)/shard_map/ppermute | solution.py:203
  145.7 4.8 %copy-start.33 = (pred[8]{0:T(512)(128)(4,1)S(1)}, pred[8]{0:T(512)(128)(4,1)}, u32[]{:S(2)}) copy-start(pred[8]{0:T(512)(128)(4,1)} %get-tuple-element.115) | copy-start | bytes 28
  150.6 4.4 %copy-start.10 = (f32[8,80,384]{2,1,0:T(8,128)S(1)}, f32[8,80,384]{2,1,0:T(8,128)}, u32[]{:S(2)}) copy-start(f32[8,80,384]{2,1,0:T(8,128)} %gather_fusion.4) | copy-start | bytes 2949124
  153.3 13.8 %collective-permute-start.15 = (bf16[4,224,384]{2,1,0:T(8,128)(2,1)S(1)}, bf16[4,224,384]{2,1,0:T(8,128)(2,1)S(1)}, u32[]{:S(2)}, u32[]{:S(2)}) collective-permute-start(bf16[4,224,384]{2,1,0:T(8,128)(2,1)S(1)} %slice.327), channel_id=1, source_target_pairs={{0,1},{1,0},{2,3},{3,2},{4,5},{5,4},{6,7},{7,6},{8,10},{9,11},{10,... | collective-permute-start | bytes 2064392 | tf_op jit(solution)/shard_map/ppermute | solution.py:203
  155.2 11.7 %collective-permute-start.9 = (bf16[4,80,384]{2,1,0:T(8,128)(2,1)S(1)}, bf16[4,80,384]{2,1,0:T(8,128)(2,1)S(1)}, u32[]{:S(2)}, u32[]{:S(2)}) collective-permute-start(bf16[4,80,384]{2,1,0:T(8,128)(2,1)S(1)} %slice.329), channel_id=1, source_target_pairs={{0,1},{1,0},{2,3},{3,2},{4,5},{5,4},{6,7},{7,6},{8,10},{9,11},{10,... | collective-permute-start | bytes 737288 | tf_op jit(solution)/shard_map/ppermute | solution.py:203
  167.0 6.3 %collective-permute-start.10 = (bf16[2,80,384]{2,1,0:T(8,128)(2,1)S(1)}, bf16[2,80,384]{2,1,0:T(8,128)(2,1)S(1)}, u32[]{:S(2)}, u32[]{:S(2)}) collective-permute-start(bf16[2,80,384]{2,1,0:T(8,128)(2,1)S(1)} %slice.331), channel_id=1, source_target_pairs={{0,2},{1,3},{2,0},{3,1},{4,6},{5,7},{6,4},{7,5},{8,12},{9,13},{10,... | collective-permute-start | bytes 368648 | tf_op jit(solution)/shard_map/ppermute | solution.py:203
  167.2 23.6 %copy-start = (bf16[8,48,1536]{2,1,0:T(8,128)(2,1)S(1)}, bf16[8,48,1536]{2,1,0:T(8,128)(2,1)}, u32[]{:S(2)}) copy-start(bf16[8,48,1536]{2,1,0:T(8,128)(2,1)} %pad_maximum_fusion.1) | copy-start | bytes 3538948
  167.2 23.6 %copy-start.5 = (f32[8,384]{1,0:T(8,128)S(1)}, f32[8,384]{1,0:T(8,128)}, u32[]{:S(2)}) copy-start(f32[8,384]{1,0:T(8,128)} %copy-done.4) | copy-start | bytes 36868
  167.3 14.7 %collective-permute-start.16 = (bf16[2,224,384]{2,1,0:T(8,128)(2,1)S(1)}, bf16[2,224,384]{2,1,0:T(8,128)(2,1)S(1)}, u32[]{:S(2)}, u32[]{:S(2)}) collective-permute-start(bf16[2,224,384]{2,1,0:T(8,128)(2,1)S(1)} %slice.328), channel_id=1, source_target_pairs={{0,2},{1,3},{2,0},{3,1},{4,6},{5,7},{6,4},{7,5},{8,12},{9,13},{10,... | collective-permute-start | bytes 1032200 | tf_op jit(solution)/shard_map/ppermute | solution.py:203
  173.4 6.8 %collective-permute-start.11 = (bf16[1,80,384]{2,1,0:T(8,128)(2,1)S(1)}, bf16[1,80,384]{2,1,0:T(8,128)(2,1)S(1)}, u32[]{:S(2)}, u32[]{:S(2)}) collective-permute-start(bf16[1,80,384]{2,1,0:T(8,128)(2,1)S(1)} %slice.332), channel_id=1, source_target_pairs={{0,4},{1,5},{2,6},{3,7},{4,0},{5,1},{6,2},{7,3},{8,9},{9,8},{10,11... | collective-permute-start | bytes 184328 | tf_op jit(solution)/shard_map/ppermute | solution.py:203
  180.2 4.3 %collective-permute-start.12 = (bf16[80,384]{1,0:T(8,128)(2,1)S(1)}, bf16[80,384]{1,0:T(8,128)(2,1)S(1)}, u32[]{:S(2)}, u32[]{:S(2)}) collective-permute-start(bf16[80,384]{1,0:T(8,128)(2,1)S(1)} %fusion.10), channel_id=1, source_target_pairs={{0,16},{1,17},{2,18},{3,19},{4,20},{5,21},{6,22},{7,23},{8,24},{9,... | collective-permute-start | bytes 184328 | tf_op jit(solution)/shard_map/ppermute | solution.py:203
  182.1 8.2 %collective-permute-start.17 = (bf16[1,224,384]{2,1,0:T(8,128)(2,1)S(1)}, bf16[1,224,384]{2,1,0:T(8,128)(2,1)S(1)}, u32[]{:S(2)}, u32[]{:S(2)}) collective-permute-start(bf16[1,224,384]{2,1,0:T(8,128)(2,1)S(1)} %slice.330), channel_id=1, source_target_pairs={{0,4},{1,5},{2,6},{3,7},{4,0},{5,1},{6,2},{7,3},{8,9},{9,8},{10,11... | collective-permute-start | bytes 516104 | tf_op jit(solution)/shard_map/ppermute | solution.py:203
  184.5 16.4 %collective-permute-start.13 = (f32[80,384]{1,0:T(8,128)S(1)}, f32[80,384]{1,0:T(8,128)S(1)}, u32[]{:S(2)}, u32[]{:S(2)}) collective-permute-start(f32[80,384]{1,0:T(8,128)S(1)} %convert_add_fusion.1), channel_id=1, source_target_pairs={{0,8},{1,9},{2,10},{3,11},{4,12},{5,13},{6,14},{7,15},{8,0},{9,1},... | collective-permute-start | bytes 368648 | tf_op jit(solution)/shard_map/ppermute | solution.py:203
  190.3 10.7 %collective-permute-start.18 = (bf16[224,384]{1,0:T(8,128)(2,1)S(1)}, bf16[224,384]{1,0:T(8,128)(2,1)S(1)}, u32[]{:S(2)}, u32[]{:S(2)}) collective-permute-start(bf16[224,384]{1,0:T(8,128)(2,1)S(1)} %fusion.4), channel_id=1, source_target_pairs={{0,16},{1,17},{2,18},{3,19},{4,20},{5,21},{6,22},{7,23},{8,24},{9,... | collective-permute-start | bytes 516104 | tf_op jit(solution)/shard_map/ppermute | solution.py:203
  190.8 10.4 %copy-start.31 = (f32[576]{0:T(1024)S(1)}, f32[576]{0:T(1024)}, u32[]{:S(2)}) copy-start(f32[576]{0:T(1024)} %param.35) | copy-start | bytes 6916
  190.8 10.4 %copy-start.34 = (f32[576]{0:T(1024)S(1)}, f32[576]{0:T(1024)}, u32[]{:S(2)}) copy-start(f32[576]{0:T(1024)} %param.40) | copy-start | bytes 6916
  190.8 10.4 %copy-start.35 = (f32[576]{0:T(1024)S(1)}, f32[576]{0:T(1024)}, u32[]{:S(2)}) copy-start(f32[576]{0:T(1024)} %param.45) | copy-start | bytes 6916
  190.8 11.0 %copy-start.17 = (f32[144,384]{1,0:T(8,128)S(1)}, f32[144,384]{1,0:T(8,128)}, u32[]{:S(2)}) copy-start(f32[144,384]{1,0:T(8,128)} %param.31) | copy-start | bytes 663556
  190.8 11.0 %copy-start.24 = (f32[144,384]{1,0:T(8,128)S(1)}, f32[144,384]{1,0:T(8,128)}, u32[]{:S(2)}) copy-start(f32[144,384]{1,0:T(8,128)} %param.36) | copy-start | bytes 663556
  190.8 11.0 %copy-start.25 = (f32[144,384]{1,0:T(8,128)S(1)}, f32[144,384]{1,0:T(8,128)}, u32[]{:S(2)}) copy-start(f32[144,384]{1,0:T(8,128)} %param.41) | copy-start | bytes 663556
  200.9 2.0 copy-start.23
  200.9 2.0 copy-start.26
  200.9 2.0 copy-start.27
  201.0 2.6 %copy-start.14 = (f32[192,384]{1,0:T(8,128)S(1)}, f32[192,384]{1,0:T(8,128)}, u32[]{:S(2)}) copy-start(f32[192,384]{1,0:T(8,128)} %param.33) | copy-start | bytes 884740
  201.0 2.6 %copy-start.19 = (f32[192,384]{1,0:T(8,128)S(1)}, f32[192,384]{1,0:T(8,128)}, u32[]{:S(2)}) copy-start(f32[192,384]{1,0:T(8,128)} %param.38) | copy-start | bytes 884740
  201.0 2.6 %copy-start.20 = (f32[192,384]{1,0:T(8,128)S(1)}, f32[192,384]{1,0:T(8,128)}, u32[]{:S(2)}) copy-start(f32[192,384]{1,0:T(8,128)} %param.43) | copy-start | bytes 884740
  201.1 1.7 collective-permute-start.19
  202.8 1.9 copy-start.15
  202.8 1.9 copy-start.21
  202.8 1.9 copy-start.22

commit v2 on v1

v2 whole, which is shorter than its diff:
```python
import functools

import jax
import jax.numpy as jnp
from jax import lax
from jax.experimental import pallas as pl
from jax.experimental.pallas import tpu as pltpu
from jax.sharding import PartitionSpec as P

STEP = 10
HEADS = 6
EPS = 1e-6
OWNERS = 8
beta_first = 0.5
beta_second = 0.5
adam_eps = 1e-08
matrix_decay = 0.01
vector_rate = 0.3
bf16, f32 = jnp.bfloat16, jnp.float32
S = jax.ShapeDtypeStruct
ANY = pl.BlockSpec(memory_space=pl.ANY)
HBM = pl.BlockSpec(memory_space=pltpu.HBM)


def dot(a, b, ca, cb):
    return lax.dot_general(a, b, (((ca,), (cb,)), ((), ())), preferred_element_type=f32)


def norm_stats(v):
    mean = jnp.mean(v, axis=-1, keepdims=True)
    cen = v - mean
    var = jnp.mean(cen * cen, axis=-1, keepdims=True)
    rstd = lax.rsqrt(var + EPS)
    return cen * rstd, rstd


def one(*shape, off=0):
    return pl.BlockSpec((1,) + shape, lambda i: (i + off,) + (0,) * len(shape))


def full(a):
    return pl.BlockSpec(a.shape, lambda i: (0,) * len(a.shape))


def whole(a):
    return pl.BlockSpec(a.shape, lambda: (0,) * len(a.shape))


def params(mib):
    return pltpu.CompilerParams(vmem_limit_bytes=mib << 20)


def cost(us):
    return pl.CostEstimate(flops=int(us * 1.0e9), bytes_accessed=1 << 20, transcendentals=0)


class Layout:
    def __init__(self, d, ff, masks, position):
        self.d, self.ff, self.cols = d, ff, ff // d
        self.masks, self.position = masks, position
        self.q, self.p, self.u = 3 * d // OWNERS, d // OWNERS, ff // OWNERS
        q0 = (self.q // 2 + 15) // 16 * 16
        self.first = ((("q", 0, q0, 0, 0),), (("q", q0, self.q - q0, 0, 0), ("v", 0, 16, 0, self.q - q0)))
        self.first_rows = max(q0, self.q - q0 + 16)
        p0 = 16
        down = tuple(("d", 0, self.p, j, j * self.p) for j in range(self.cols))
        self.second = (
            (("u", 0, self.u, 0, 0), ("p", 0, p0, 0, self.u)),
            down + (("p", p0, self.p - p0, 0, self.cols * self.p),),
        )
        self.second_rows = max(self.u + p0, self.cols * self.p + self.p - p0)
        self.piece = (8 * d + ff) // (3 * OWNERS)


def place(lay, piece, owner):
    name, start, rows, col, _ = piece
    size = {"q": lay.q, "p": lay.p, "u": lay.u, "d": lay.p, "v": 16}[name]
    at = owner * size + start
    if not isinstance(at, int):
        at = pl.multiple_of(at, 16)
    return pl.ds(at, rows), pl.ds(col * lay.d, lay.d)


def pack(lay, q_hbm, p_hbm, u_hbm, d_hbm, v_hbm, first_ref, second_ref, q_ref, p_ref, u_ref, d_ref, v_ref, sems):
    refs = {"q": q_ref, "p": p_ref, "u": u_ref, "d": d_ref}
    moves = [pltpu.make_async_copy(a, b, sems.at[i]) for i, (a, b) in enumerate(
        ((q_hbm, q_ref), (v_hbm, v_ref), (p_hbm, p_ref), (u_hbm, u_ref), (d_hbm, d_ref)))]
    for move in moves:
        move.start()
    for move in moves:
        move.wait()
    core = lay.position()[1]
    v = v_ref[...].reshape(1, v_ref.shape[0])

    def fill(halves, out_ref):
        end = 0
        for name, start, rows, col, at in halves:
            if name == "v":
                out_ref[at:at + rows, :] = jnp.zeros((rows, lay.d), bf16)
                for k in range(3):
                    out_ref[at + k:at + k + 1, :lay.piece] = v[:, k * lay.piece:(k + 1) * lay.piece].astype(bf16)
            else:
                out_ref[at:at + rows, :] = refs[name][start:start + rows, col * lay.d:(col + 1) * lay.d].astype(bf16)
            end = at + rows
        if end < out_ref.shape[0]:
            out_ref[end:, :] = jnp.zeros((out_ref.shape[0] - end, lay.d), bf16)

    for half in range(2):
        @pl.when(core == half)
        def _():
            fill(lay.first[half], first_ref)
            fill(lay.second[half], second_ref)


def call_pack(lay, q, p, u, d, v):
    outs = [S((lay.first_rows, lay.d), bf16), S((lay.second_rows, lay.d), bf16)]
    return pl.pallas_call(
        functools.partial(pack, lay), in_specs=[HBM] * 5,
        out_specs=[whole(a) for a in outs], out_shape=outs,
        scratch_shapes=[pltpu.VMEM(a.shape, f32) for a in (q, p, u, d, v)] + [pltpu.SemaphoreType.DMA((5,))],
        compiler_params=params(60), name="pack",
    )(q, p, u, d, v)


def fetch(lay, halves, mine_ref, other_ref, dests, sems):
    me, core = lay.position()

    def copies(half, src_ref, base):
        out = []
        for j in range(OWNERS):
            for piece in halves[half]:
                name, _, rows, _, at = piece
                r, c = place(lay, piece, me ^ lay.masks[half][j])
                dst = dests[name].at[r] if name != "d" else dests[name].at[r, c]
                out.append(pltpu.make_async_copy(src_ref.at[j, pl.ds(at, rows)], dst, sems.at[base + len(out)]))
        return out

    for half in range(2):
        @pl.when(core == half)
        def _():
            first = copies(half, mine_ref, 0)
            both = first + copies(1 - half, other_ref, len(first))
            for c in both:
                c.start()
            for c in both:
                c.wait()


def emit(lay, halves, arrays, keep_ref, give_ref):
    me, core = lay.position()

    def fill(half, out_ref):
        for j in range(OWNERS):
            end = 0
            for piece in halves[half]:
                name, _, rows, _, at = piece
                r, c = place(lay, piece, me ^ lay.masks[half][j])
                out_ref[j, at:at + rows, :] = arrays[name][r, c].astype(out_ref.dtype)
                end = at + rows
            if end < out_ref.shape[1]:
                out_ref[j, end:, :] = jnp.zeros((out_ref.shape[1] - end, lay.d), out_ref.dtype)

    for half in range(2):
        @pl.when(core == half)
        def _():
            fill(half, keep_ref)
            fill(1 - half, give_ref)


def attn_fwd_image(x_ref, w_ref, vrow_ref, vcol_ref, jt_ref, e_ref, il_ref, ot_ref, h_ref):
    xhat, _ = norm_stats(x_ref[0])
    h = (xhat * vrow_ref[0:1, :] + vrow_ref[1:2, :]).astype(bf16)
    h_ref[0] = h
    d = h.shape[1]
    hs = d // HEADS
    jt = dot(w_ref[...], h, 1, 1) + vcol_ref[:, 0:1]
    jt_ref[0] = jt.astype(bf16)
    for i in range(HEADS):
        qt = jt_ref[0, i * hs:(i + 1) * hs, :]
        kt = jt_ref[0, d + i * hs:d + (i + 1) * hs, :]
        vt = jt_ref[0, 2 * d + i * hs:2 * d + (i + 1) * hs, :]
        st = dot((kt * 0.125), qt, 0, 0)
        m = jnp.max(st, axis=0, keepdims=True)
        e = jnp.exp(st - m)
        l = jnp.sum(e, axis=0, keepdims=True)
        eb = e.astype(bf16)
        e_ref[0, i] = eb
        il = 1.0 / l
        il_ref[0, i:i + 1, :] = il
        ot = dot(vt, eb, 1, 0) * il
        ot_ref[0, i * hs:(i + 1) * hs, :] = ot.astype(bf16)


def attn_fwd_first(lay, mine_ref, other_ref, x_ref, jt_ref, e_ref, il_ref, ot_ref, h_ref, w_ref, vrow_ref, vcol_ref, vec_scr, sems):
    @pl.when(pl.program_id(0) == 0)
    def _():
        fetch(lay, lay.first, mine_ref, other_ref, {"q": w_ref, "v": vec_scr}, sems)
        d, s = lay.d, lay.piece
        vrow_ref[...] = jnp.zeros_like(vrow_ref)
        for r in range(8 + lay.cols):
            for k in range(2):
                g = 2 * r + k
                row = vec_scr[g // 3 * 16:g // 3 * 16 + 16, :].astype(f32)[g % 3:g % 3 + 1, :s]
                vrow_ref[r:r + 1, k * s:(k + 1) * s] = row
        cols = jnp.transpose(vrow_ref[0:8, :])
        vcol_ref[...] = jnp.zeros_like(vcol_ref)
        vcol_ref[0:d, 0:1] = cols[:, 4:5]
        vcol_ref[2 * d:3 * d, 0:1] = cols[:, 5:6]
    attn_fwd_image(x_ref, w_ref, vrow_ref, vcol_ref, jt_ref, e_ref, il_ref, ot_ref, h_ref)


def attn_fwd_rest(x_ref, w_ref, vrow_ref, vcol_ref, a, b, c, d, e, jt_ref, e_ref, il_ref, ot_ref, h_ref):
    attn_fwd_image(x_ref, w_ref, vrow_ref, vcol_ref, jt_ref, e_ref, il_ref, ot_ref, h_ref)


def fwd_outs(b, t, d):
    return [S((b, 3 * d, t), bf16), S((b, HEADS, t, t), bf16), S((b, 8, t), f32), S((b, d, t), bf16), S((b, t, d), bf16)]


def fwd_blocks(t, d, off):
    return [one(3 * d, t, off=off), one(HEADS, t, t, off=off), one(8, t, off=off), one(d, t, off=off), one(t, d, off=off)]


def call_attn_fwd_first(lay, mine, other, x, count):
    b, t, d = x.shape
    extra = [S((3 * d, d), bf16), S((16, d), f32), S((3 * d, 8), f32)]
    n_copies = OWNERS * (len(lay.first[0]) + len(lay.first[1]))
    return pl.pallas_call(
        functools.partial(attn_fwd_first, lay), grid=(count,),
        in_specs=[HBM, HBM, one(t, d)],
        out_specs=fwd_blocks(t, d, 0) + [full(a) for a in extra],
        out_shape=fwd_outs(b, t, d) + extra,
        scratch_shapes=[pltpu.VMEM((OWNERS * 16, d), bf16), pltpu.SemaphoreType.DMA((n_copies,))],
        compiler_params=params(60), cost_estimate=cost(4 * count), name="attn_fwd_first",
    )(mine, other, x)


def call_attn_fwd_rest(x, w, vrow, vcol, outs, off, count):
    b, t, d = x.shape
    return pl.pallas_call(
        attn_fwd_rest, grid=(count,),
        in_specs=[one(t, d, off=off), full(w), full(vrow), full(vcol)] + [ANY] * 5,
        out_specs=fwd_blocks(t, d, off), out_shape=fwd_outs(b, t, d),
        input_output_aliases={4 + k: k for k in range(5)},
        compiler_params=params(60), cost_estimate=cost(4 * count), name="attn_fwd_rest",
    )(x, w, vrow, vcol, *outs)


def gelu_pair(u):
    cdf = 0.5 + 0.5 * lax.erf(u * (0.5 ** 0.5))
    pdf = jnp.exp(u * u * -0.5) * 0.3989422804014327
    return u * cdf, cdf + u * pdf


def mlp(lay, count, mine_ref, other_ref, x_ref, ot_ref, cot_ref, vrow_ref,
        mid_ref, act_ref, dm_ref, dot_ref, wd_ref, dv_ref, keep_ref, give_ref,
        wp_ref, wu_ref, dwp_ref, dwu_ref, dwd_ref, sems):
    i = pl.program_id(0)
    d, cols = lay.d, lay.cols

    @pl.when(i == 0)
    def _():
        fetch(lay, lay.second, mine_ref, other_ref, {"p": wp_ref, "u": wu_ref, "d": wd_ref}, sems)
        dwp_ref[...] = jnp.zeros_like(dwp_ref)
        dwu_ref[...] = jnp.zeros_like(dwu_ref)
        dwd_ref[...] = jnp.zeros_like(dwd_ref)
        dv_ref[...] = jnp.zeros_like(dv_ref)

    ot = ot_ref[0]
    mid = x_ref[0] + (dot(ot, wp_ref[...], 0, 1) + vrow_ref[6:7, :])
    mid_ref[0] = mid
    xhat, rstd = norm_stats(mid)
    h2 = (xhat * vrow_ref[2:3, :] + vrow_ref[3:4, :]).astype(bf16)
    ub = jnp.concatenate([vrow_ref[8 + j:9 + j, :] for j in range(cols)], axis=1)
    u = dot(h2, wu_ref[...], 1, 1) + ub
    act, gp = gelu_pair(u)
    act = act.astype(bf16)
    act_ref[0] = act
    cot = cot_ref[0]
    g = cot.astype(bf16)
    dwd_ref[...] += dot(g, act, 0, 0)
    du = dot(g, wd_ref[...], 1, 0) * gp
    dul = du.astype(bf16)
    dwu_ref[...] += dot(dul, h2, 0, 0)
    dh2 = dot(dul, wu_ref[...], 1, 0)
    gy = dh2 * vrow_ref[2:3, :]
    m1 = jnp.mean(gy, axis=-1, keepdims=True)
    m2 = jnp.mean(gy * xhat, axis=-1, keepdims=True)
    dm = cot + rstd * (gy - m1 - xhat * m2)
    dm_ref[0] = dm
    dml = dm.astype(bf16)
    dwp_ref[...] += dot(dml, ot, 0, 1)
    dot_ref[0] = dot(wp_ref[...], dml, 0, 1).astype(bf16)
    dv_ref[2:3, :] += jnp.sum(dh2 * xhat, axis=0, keepdims=True)
    dv_ref[3:4, :] += jnp.sum(dh2, axis=0, keepdims=True)
    dv_ref[6:7, :] += jnp.sum(dml.astype(f32), axis=0, keepdims=True)
    dv_ref[7:8, :] += jnp.sum(g.astype(f32), axis=0, keepdims=True)
    dub = jnp.sum(dul.astype(f32), axis=0, keepdims=True)
    for j in range(cols):
        dv_ref[8 + j:9 + j, :] += dub[:, j * d:(j + 1) * d]

    @pl.when(i == count - 1)
    def _():
        emit(lay, lay.second, {"p": dwp_ref, "u": dwu_ref, "d": dwd_ref}, keep_ref, give_ref)


def call_mlp(lay, mine, other, x, ot, cot, vrow):
    b, t, d = x.shape
    ff = lay.ff
    acc = [S((d, ff), bf16), S((16, d), f32), S((OWNERS, lay.second_rows, d), f32), S((OWNERS, lay.second_rows, d), bf16)]
    outs = [S((b, t, d), f32), S((b, t, ff), bf16), S((b, t, d), f32), S((b, d, t), bf16)] + acc
    n_copies = OWNERS * (len(lay.second[0]) + len(lay.second[1]))
    return pl.pallas_call(
        functools.partial(mlp, lay, b), grid=(b,),
        in_specs=[HBM, HBM, one(t, d), one(d, t), one(t, d), full(vrow)],
        out_specs=[one(t, d), one(t, ff), one(t, d), one(d, t)] + [full(a) for a in acc],
        out_shape=outs,
        scratch_shapes=[pltpu.VMEM((d, d), bf16), pltpu.VMEM((ff, d), bf16), pltpu.VMEM((d, d), f32), pltpu.VMEM((ff, d), f32),
                        pltpu.VMEM((d, ff), f32), pltpu.SemaphoreType.DMA((n_copies,))],
        compiler_params=params(60), cost_estimate=cost(24), name="mlp",
    )(mine, other, x, ot, cot, vrow)


def attn_bwd_image(jt_ref, e_ref, il_ref, ot_ref, dot_ref, h_ref, dj_ref, dw_ref):
    t, d = h_ref.shape[1:]
    hs = d // HEADS
    for i in range(HEADS):
        rows = slice(i * hs, (i + 1) * hs)
        qt = jt_ref[0, i * hs:(i + 1) * hs, :]
        kt = jt_ref[0, d + i * hs:d + (i + 1) * hs, :]
        vt = jt_ref[0, 2 * d + i * hs:2 * d + (i + 1) * hs, :]
        do = dot_ref[0, rows, :].astype(f32) * il_ref[0, i:i + 1, :]
        dd = jnp.sum(do * ot_ref[0, rows, :].astype(f32), axis=0, keepdims=True)
        dob = do.astype(bf16)
        eb = e_ref[0, i]
        dp = dot(vt, dob, 0, 0)
        ds = (eb.astype(f32) * (dp - dd)).astype(bf16)
        dj_ref[0, rows, :] = (dot(kt, ds, 1, 0) * 0.125).astype(bf16)
        dj_ref[0, d + i * hs:d + (i + 1) * hs, :] = (dot(qt, ds, 1, 1) * 0.125).astype(bf16)
        dj_ref[0, 2 * d + i * hs:2 * d + (i + 1) * hs, :] = dot(dob, eb, 1, 1).astype(bf16)
    hx = jnp.concatenate([h_ref[0], jnp.ones((t, 128), bf16)], axis=1)
    dw_ref[...] += dot(dj_ref[0], hx, 1, 0)


def attn_bwd_first(jt_ref, e_ref, il_ref, ot_ref, dot_ref, h_ref, dj_ref, dw_ref):
    @pl.when(pl.program_id(0) == 0)
    def _():
        dw_ref[...] = jnp.zeros_like(dw_ref)
    attn_bwd_image(jt_ref, e_ref, il_ref, ot_ref, dot_ref, h_ref, dj_ref, dw_ref)


def attn_bwd_last(lay, count, jt_ref, e_ref, il_ref, ot_ref, dot_ref, h_ref, dw_in_ref, w_ref, vrow_ref, dv_ref, dj_in_ref,
                  dj_ref, keep_ref, give_ref, dw_ref, vec_scr):
    i = pl.program_id(0)

    @pl.when(i == 0)
    def _():
        dw_ref[...] = dw_in_ref[...]
    attn_bwd_image(jt_ref, e_ref, il_ref, ot_ref, dot_ref, h_ref, dj_ref, dw_ref)

    @pl.when(i == count - 1)
    def _():
        d, s = lay.d, lay.piece
        w = w_ref[...].astype(f32)
        db = dw_ref[:, d:d + 1]
        gain = jnp.sum(w * (dw_ref[:, 0:d] - db * vrow_ref[1:2, :]), axis=0, keepdims=True) / vrow_ref[0:1, :]
        shift = jnp.sum(w * db, axis=0, keepdims=True)
        biases = jnp.transpose(dw_ref[:, d:d + 8])
        rows = [gain, shift, dv_ref[2:3, :], dv_ref[3:4, :], biases[0:1, 0:d], biases[0:1, 2 * d:3 * d]]
        rows += [dv_ref[k:k + 1, :] for k in range(6, 8 + lay.cols)]
        vec_scr[...] = jnp.zeros_like(vec_scr)
        for g in range(3 * OWNERS):
            at = g // 3 * 16 + g % 3
            vec_scr[at:at + 1, 0:s] = rows[g // 2][:, g % 2 * s:(g % 2 + 1) * s]
        emit(lay, lay.first, {"q": dw_ref, "v": vec_scr}, keep_ref, give_ref)


def bwd_blocks(t, d, off):
    return [one(3 * d, t, off=off), one(HEADS, t, t, off=off), one(8, t, off=off), one(d, t, off=off), one(d, t, off=off), one(t, d, off=off)]


def call_attn_bwd_first(acts, count):
    b, t, d = acts[-1].shape
    dw = S((3 * d, d + 128), f32)
    return pl.pallas_call(
        attn_bwd_first, grid=(count,), in_specs=bwd_blocks(t, d, 0),
        out_specs=[one(3 * d, t), full(dw)], out_shape=[S((b, 3 * d, t), bf16), dw],
        compiler_params=params(60), cost_estimate=cost(4 * count), name="attn_bwd_first",
    )(*acts)


def call_attn_bwd_last(lay, acts, dw, w, vrow, dv, dj, off, count):
    b, t, d = acts[-1].shape
    slots = [S((OWNERS, lay.first_rows, d), f32), S((OWNERS, lay.first_rows, d), bf16)]
    return pl.pallas_call(
        functools.partial(attn_bwd_last, lay, count), grid=(count,),
        in_specs=bwd_blocks(t, d, off) + [full(dw), full(w), full(vrow), full(dv), ANY],
        out_specs=[one(3 * d, t, off=off)] + [full(a) for a in slots], out_shape=[S((b, 3 * d, t), bf16)] + slots,
        scratch_shapes=[pltpu.VMEM(dw.shape, f32), pltpu.VMEM((OWNERS * 16, d), f32)],
        input_output_aliases={10: 0},
        compiler_params=params(60), cost_estimate=cost(4 * count + 2), name="attn_bwd_last",
    )(*acts, dw, w, vrow, dv, dj)


def tail(x_ref, dm_ref, dj_ref, w_ref, mid_ref, act_ref, wd_ref, vrow_ref, gx_ref, lo_ref):
    lo_ref[0] = mid_ref[0] + (dot(act_ref[0], wd_ref[...], 1, 1) + vrow_ref[7:8, :])
    dh = dot(dj_ref[0], w_ref[...], 0, 0)
    xhat, rstd = norm_stats(x_ref[0])
    gy = dh * vrow_ref[0:1, :]
    m1 = jnp.mean(gy, axis=-1, keepdims=True)
    m2 = jnp.mean(gy * xhat, axis=-1, keepdims=True)
    gx_ref[0] = dm_ref[0] + rstd * (gy - m1 - xhat * m2)


def call_tail(x, dm, dj, w, mid, act, wd, vrow):
    b, t, d = x.shape
    return pl.pallas_call(
        tail, grid=(b,),
        in_specs=[one(t, d), one(t, d), one(3 * d, t), full(w), one(t, d), one(t, act.shape[2]), full(wd), full(vrow)],
        out_specs=[one(t, d), one(t, d)],
        out_shape=[S((b, t, d), f32), S((b, t, d), f32)],
        compiler_params=params(60), cost_estimate=cost(10), name="tail",
    )(x, dm, dj, w, mid, act, wd, vrow)


def adam_values(master, first, second, grad, rate, decay):
    first_new = beta_first * first + (1.0 - beta_first) * grad
    second_new = beta_second * second + (1.0 - beta_second) * grad * grad
    first_hat = first_new * (1.0 / (1.0 - beta_first ** STEP))
    second_hat = second_new * (1.0 / (1.0 - beta_second ** STEP))
    new = master - rate * (first_hat / (jnp.sqrt(second_hat) + adam_eps) + decay * master)
    return new, first_new, second_new, new.astype(bf16)


def adam_rows(refs, outs, rows, grad, rate, decay):
    for out, value in zip(outs, adam_values(*(r[rows] for r in refs), grad, rate, decay)):
        out[rows] = value


def adam(lay, halves, names, mine_ref, other_ref, *refs):
    core = lay.position()[1]
    count = len(names)
    states = {name: refs[3 * k:3 * k + 3] for k, name in enumerate(names)}
    outs = {name: refs[3 * count + 4 * k:3 * count + 4 * k + 4] for k, name in enumerate(names)}
    rates = {"q": 0.6 * lay.d ** -0.5, "p": 0.6 * lay.d ** -0.5, "u": 0.6 * lay.d ** -0.5, "d": 0.6 * lay.ff ** -0.5, "v": vector_rate}

    def step(half, src_ref):
        for name, start, rows, col, at in halves[half]:
            if name == "v":
                grad = jnp.concatenate([src_ref[at + k:at + k + 1, :lay.piece] for k in range(3)], axis=1)
                size = 3 * lay.piece
                new = adam_values(*(r[...].reshape(1, size) for r in states[name]), grad, rates[name], 0.0)
                for out, value in zip(outs[name], new):
                    out[...] = value.reshape(size)
            else:
                span = (slice(start, start + rows), slice(col * lay.d, (col + 1) * lay.d))
                adam_rows(states[name], outs[name], span, src_ref[at:at + rows, :], rates[name], matrix_decay)

    for half in range(2):
        @pl.when(core == half)
        def _():
            step(half, mine_ref)
            step(1 - half, other_ref)


def call_adam(lay, halves, mine, other, states):
    names = tuple(states)
    flat = [a for name in names for a in states[name]]
    outs = [S(states[name][0].shape, t) for name in names for t in (f32, f32, f32, bf16)]
    got = pl.pallas_call(
        functools.partial(adam, lay, halves, names),
        in_specs=[whole(a) for a in (mine, other, *flat)], out_specs=[whole(a) for a in outs], out_shape=outs,
        compiler_params=params(60), cost_estimate=cost(3), name="adam",
    )(mine, other, *flat)
    return {name: got[4 * k:4 * k + 4] for k, name in enumerate(names)}


class Links:
    def __init__(self, mesh):
        self.wide, self.narrow = mesh.shape["wide"], mesh.shape["narrow"]
        bits = [1 << k for k in range(self.wide.bit_length() - 1)]
        self.orders = (bits[::-1], bits[:1] + bits[:0:-1])
        self.rounds = len(bits)
        self.masks = []
        for order in self.orders:
            masks = [0]
            for bit in order:
                masks = masks + [m ^ bit for m in masks]
            self.masks.append(masks)
        self.slots = [[masks.index(m) for m in range(self.wide)] for masks in self.masks]

    def permute(self, value, partner):
        pairs = []
        for n in range(self.narrow):
            for w in range(self.wide):
                n2, w2 = partner(n, w)
                pairs.append((n * self.wide + w, n2 * self.wide + w2))
        return lax.ppermute(value, ("narrow", "wide"), pairs)

    def core(self, value):
        return self.permute(value, lambda n, w: (n ^ 1, w))

    def step(self, value, k):
        return self.permute(value, lambda n, w: (n, w ^ self.orders[n % 2][k]))

    def others(self, value):
        total = value.astype(f32)
        bit = 2
        while bit < self.narrow:
            low = total.astype(bf16)
            total = low.astype(f32) + self.permute(low, lambda n, w, bit=bit: (n ^ bit, w)).astype(f32)
            bit *= 2
        return total

    def here(self):
        return lax.axis_index("wide"), lax.axis_index("narrow") % 2

    def gather(self, half):
        moving = Gather(self, half)
        for _ in range(self.rounds):
            moving.round()
        return moving.core()

    def reduce(self, keep, give):
        moving = Reduce(self, keep, give)
        moving.core()
        for _ in range(self.rounds):
            moving.round()
        moving.others()
        return moving.finish()


    def gather_rows(self, packed):
        me, core = self.here()
        rows, columns = packed.shape
        mine, other = self.gather(lax.dynamic_slice_in_dim(packed, core * (rows // 2), rows // 2))
        both = jnp.concatenate([mine, other], axis=0)
        relative = jnp.arange(self.wide) ^ me
        first = jnp.take(jnp.array(self.slots[0]), relative) + core * self.wide
        second = jnp.take(jnp.array(self.slots[1]), relative) + (1 - core) * self.wide
        index = jnp.stack([first, second], axis=1).reshape(-1)
        return jnp.take(both, index, axis=0).reshape(self.wide, rows, columns)

    def reduce_rows(self, packed):
        me, core = self.here()
        _, rows, columns = packed.shape
        halves = packed.reshape(2 * self.wide, rows // 2, columns)
        masks = jnp.array(self.masks)
        keep = jnp.take(halves, (masks[core] ^ me) * 2 + core, axis=0)
        give = jnp.take(halves, (masks[1 - core] ^ me) * 2 + (1 - core), axis=0)
        total, other = self.reduce(keep, give.astype(bf16))
        return jnp.where(core == 0, jnp.concatenate([total, other]), jnp.concatenate([other, total]))


class Gather:
    def __init__(self, links, half):
        self.links, self.held, self.k = links, half[None], 0

    def round(self):
        self.held = jnp.concatenate([self.held, self.links.step(self.held, self.k)], axis=0)
        self.k += 1

    def core(self):
        return self.held, self.links.core(self.held)


class Reduce:
    def __init__(self, links, keep, give):
        self.links, self.held, self.give, self.k = links, keep, give, links.rounds

    def core(self):
        self.held = self.held + self.links.core(self.give).astype(f32)

    def round(self):
        self.k -= 1
        half = self.held.shape[0] // 2
        self.held = self.held[:half] + self.links.step(self.held[half:].astype(bf16), self.k).astype(f32)

    def others(self):
        self.held = self.links.others(self.held[0])

    def finish(self):
        return self.held, self.links.core(self.held)


class Here:
    def __init__(self, held, other):
        self.held, self.other = held, other

    def round(self):
        pass

    def others(self):
        pass

    def core(self):
        return self.held, self.other

    finish = core


def to_rows(block, columns):
    return jnp.concatenate([block[..., j:j + columns] for j in range(0, block.shape[-1], columns)], axis=-2)


def from_rows(block, count):
    return jnp.concatenate(jnp.split(block, count, axis=-2), axis=-1)


def padded(block, multiple):
    extra = -block.shape[-2] % multiple
    return jnp.pad(block, [(0, 0)] * (block.ndim - 2) + [(0, extra), (0, 0)])


def to_slots(lay, halves, rows, arrays):
    out = []
    for half in halves:
        parts = []
        for name, start, count, col, _ in half:
            block = arrays[name].reshape(OWNERS, -1, arrays[name].shape[-1])
            parts.append(block[:, start:start + count, col * lay.d:(col + 1) * lay.d])
        block = jnp.concatenate(parts, axis=1)
        out.append(jnp.pad(block, ((0, 0), (0, rows - block.shape[1]), (0, 0))))
    return out


def from_slots(halves, both):
    found = {}
    for half, block in zip(halves, both):
        for name, start, count, col, at in half:
            found.setdefault(name, {})[(start, col)] = block[:, at:at + count].astype(f32)
    out = {}
    for name, parts in found.items():
        axis = 2 if max(col for _, col in parts) else 1
        block = jnp.concatenate([parts[key] for key in sorted(parts)], axis=axis)
        out[name] = block.reshape(-1, block.shape[-1])
    return out


FIRST_IMAGES = 2


def after(value, *earlier):
    return lax.optimization_barrier((value, *earlier))[0]


def compute(lay, x, cot, gather, reduce, rounds):
    b = x.shape[0]
    k = min(FIRST_IMAGES, b - 1)
    one, two = gather
    one.round()
    two.held = after(two.held, one.held)
    two.round()
    one.round()
    one.held, two.held = lax.optimization_barrier((one.held, two.held))
    for _ in range(rounds - 2):
        one.round()
    first = one.core()
    two.held, *first = lax.optimization_barrier((two.held, *first))
    *outs, wq, vrow, vcol = call_attn_fwd_first(lay, *first, x, k)
    for _ in range(rounds - 2):
        two.round()
    *outs, two.held = lax.optimization_barrier((*outs, two.held))
    jt, e, il, ot, h = call_attn_fwd_rest(x, wq, vrow, vcol, outs, k, b - k)
    two.round()
    ot, two.held = lax.optimization_barrier((ot, two.held))
    second = two.core()
    mid, act, dm, dot_, wd, dv, keep, give = call_mlp(lay, *second, x, ot, cot, vrow)
    down = reduce(keep, give)
    down.core()
    acts = (jt, e, il, ot, after(dot_, down.held), h)
    dj, dw = call_attn_bwd_first(acts, k)
    down.round()
    dw = after(dw, down.held)
    dj, keep, give = call_attn_bwd_last(lay, acts, dw, wq, vrow, dv, dj, k, b - k)
    for _ in range(rounds - 2):
        down.round()
    up = reduce(keep, give)
    up.core()
    dj, up.held = lax.optimization_barrier((dj, up.held))
    up.round()
    gx, lo = call_tail(x, dm, dj, wq, mid, act, wd, vrow)
    up.held = after(up.held, gx)
    for _ in range(rounds - 1):
        up.round()
    down.round()
    down.others()
    second_sum = down.finish()
    up.others()
    return lo, gx, up.finish(), second_sum


def eight_owners(links, lay, x, cot, states):
    masters = {name: s[0] for name, s in states.items()}
    first, second = call_pack(lay, *(masters[name] for name in "qpudv"))
    gather = Gather(links, first), Gather(links, second)
    lo, gx, first_sum, second_sum = compute(lay, x, cot, gather, functools.partial(Reduce, links), links.rounds)
    new = call_adam(lay, lay.second, *second_sum, {name: states[name] for name in "pud"})
    new |= call_adam(lay, lay.first, *first_sum, {name: states[name] for name in "qv"})
    return lo, gx, new


def any_owners(links, lay, x, cot, states):
    n, d = links.wide, lay.d
    masters = {name: s[0] for name, s in states.items()}
    v_size = masters["v"].shape[0]
    v_rows = -(-v_size // d)

    def vec_rows(v):
        return jnp.pad(v, ((0, 0), (0, v_rows * d - v_size))).reshape(-1, v_rows, d)

    def split(block):
        at, out = 0, {}
        for name in "qpu":
            rows = masters[name].shape[0]
            out[name] = block[:, at:at + rows]
            at += rows
        rows = masters["d"].shape[0]
        out["d"] = from_rows(block[:, at:at + rows * lay.cols], lay.cols)
        at += rows * lay.cols
        out["v"] = block[:, at:at + v_rows].reshape(-1, 1, v_rows * d)[:, :, :v_size]
        return {name: a.reshape(-1, a.shape[2]) for name, a in out.items()}

    def join(a, lead):
        blocks = [a[name].reshape(lead, -1, d) for name in "qpu"]
        blocks += [to_rows(a["d"].reshape(lead, -1, lay.ff), d), vec_rows(a["v"].reshape(lead, v_size))]
        return padded(jnp.concatenate(blocks, axis=1), 32)

    def eighths(v):
        return jnp.pad(v.reshape(OWNERS, 3, lay.piece), ((0, 0), (0, 13), (0, d - lay.piece))).reshape(-1, d)

    got = split(links.gather_rows(join(masters, 1)[0].astype(bf16)))
    got["v"] = eighths(got["v"])
    gather = Here(*to_slots(lay, lay.first, lay.first_rows, got)), Here(*to_slots(lay, lay.second, lay.second_rows, got))
    lo, gx, first_sum, second_sum = compute(lay, x, cot, gather, Here, 3)
    grads = from_slots(lay.first, first_sum) | from_slots(lay.second, second_sum)
    grads["v"] = grads["v"].reshape(OWNERS, 16, d)[:, :3, :lay.piece]
    mine = split(links.reduce_rows(join(grads, n))[None])
    rates = {"q": 0.6 * d ** -0.5, "p": 0.6 * d ** -0.5, "u": 0.6 * d ** -0.5, "d": 0.6 * lay.ff ** -0.5, "v": vector_rate}
    new = {}
    for name, refs in states.items():
        new[name] = adam_values(*refs, mine[name].reshape(refs[0].shape), rates[name], 0.0 if name == "v" else matrix_decay)
    return lo, gx, new


def per_device(links, x, cot, *arrays):
    if links.wide == OWNERS:
        run, masks, position = eight_owners, links.masks, links.here
    else:
        run, masks, position = any_owners, [list(range(OWNERS))] * 2, lambda: (0, 0)
    lay = Layout(x.shape[2], arrays[3].shape[1], masks, position)
    names = "qpudv"
    states = {name: arrays[k::5] for k, name in enumerate(names)}
    lo, gx, new = run(links, lay, x, cot, states)
    return (lo, gx, *(a for name in names for a in new[name]))


def solution(mesh):
    tokens = P(("narrow", "wide"), None, None)
    matrix, vector = P("wide", None), P("wide")
    state = (matrix,) * 4 + (vector,)
    return jax.shard_map(
        functools.partial(per_device, Links(mesh)),
        mesh=mesh,
        in_specs=(tokens, tokens) + state * 3,
        out_specs=(tokens, tokens) + (matrix,) * 16 + (vector,) * 4,
        check_vma=False,
    )
```

time: 207 us -> 156 us (0.75)
  local copies, waits for them, and re-layouts: 43.4 us -> 3.52 us
  Pallas kernels: 67.2 us -> 90.7 us
  other arithmetic: 26.8 us -> 6.55 us
  waiting for transfers between devices: 40.8 us -> 28.7 us
    pallas_call x3 -> x8, Pallas kernels: 57.1 us -> 79.8 us  [the longest x1 27.7 us: call_mlp(): pl.pallas_call(functools.partial(mlp, lay, b), grid=(b,), in_specs=[HBM,...]
    gather x8 -> x0, local copies, waits for them, and re-layouts: 20.5 us -> none  [the longest x2 6.66 us: reduce(): give = jnp.take(halves, (masks[1 - core] ^ me) * 2 + (1 - core), axis=0)]
    ppermute x20, waiting for transfers between devices: 40.8 us -> 28.7 us  [permute(): return lax.ppermute(value, ('narrow', 'wide'), pairs)]
    convert_element_type x7 -> x0, other arithmetic: 7.75 us -> none  [the longest x2 3.92 us: reduce(): held = own + self.core(give.astype(bf16)).astype(f32)]
    unnamed x102 -> x19, local copies, waits for them, and re-layouts: 9.8 us -> 3.28 us
    slice x16 -> x6, local copies, waits for them, and re-layouts: 4.89 us -> 0.2 us  [round(): self.held[half:].astype(bf16)]
    slice x2 -> x0, other arithmetic: 3.18 us -> none  [the longest x1 3.18 us: per_device(): dwq, db = (dwx[:, :d], dwx[:, d])]
    pad x3 -> x0, local copies, waits for them, and re-layouts: 2.87 us -> none  [the longest x1 2.86 us: padded(): return jnp.pad(block, [(0, 0)] * (block.ndim - 2) + [(0, extra), (0, 0)])]
  transfers between devices with their start and end apart: 20 -> 20, of which waited for: 10 -> 11; matrix products, arithmetic and copies ran while one was open for 15% -> 1% of each run, Pallas kernels for 12% -> 38%
where the time goes in v2:
time: 156 us
  Pallas kernels  90.7 us (58%)
  waiting for transfers between devices  28.7 us (18%)
  starting transfers between devices  25.1 us (16%)
  other arithmetic  6.55 us (4%)
  local copies, waits for them, and re-layouts  3.52 us (2%)
    ppermute x20, waiting for transfers between devices, permute(): return lax.ppermute(value, ('narrow', 'wide'), pairs)  28.7 us
    pallas_call x1, Pallas kernels, call_mlp(): pl.pallas_call(functools.partial(mlp, lay, b), grid=(b,), in_specs=[HBM,...  27.7 us
    ppermute x20, starting transfers between devices, permute(): return lax.ppermute(value, ('narrow', 'wide'), pairs)  25.1 us
    pallas_call x1, Pallas kernels, call_attn_bwd_last(): pl.pallas_call(functools.partial(attn_bwd_last, lay, count), grid=(count,...  12.9 us
    pallas_call x1, Pallas kernels, call_attn_fwd_first(): pl.pallas_call(functools.partial(attn_fwd_first, lay), grid=(count,), in_...  11.3 us
    pallas_call x1, Pallas kernels, call_tail(): pl.pallas_call(tail, grid=(b,), in_specs=[one(t, d), one(t, d), one(3 * d...  10.9 us
    pallas_call x1, Pallas kernels, call_attn_bwd_first(): pl.pallas_call(attn_bwd_first, grid=(count,), in_specs=bwd_blocks(t, d, 0...  10.3 us
    pallas_call x1, Pallas kernels, call_attn_fwd_rest(): pl.pallas_call(attn_fwd_rest, grid=(count,), in_specs=[one(t, d, off=off)...  9.57 us
  transfers between devices with their start and end apart: 20, of which 11 were waited for; matrix products, arithmetic and copies ran while one was open for 1% of the time, Pallas kernels for 38%

profile of v2, /device:TPU:0, one launch (start us, length us, event | category | flops | bytes accessed | tf_op | source)
XLA Modules:
  0.0 155.7 jit_solution(9452994512075897071)
XLA Ops:
  0.7 2.0 %pack.1 = (bf16[80,384]{1,0:T(8,128)(2,1)}, bf16[224,384]{1,0:T(8,128)(2,1)}) custom-call(f32[144,384]{1,0:T(8,128)} %refs_0_.2, f32[48,384]{1,0:T(8,128)} %refs_0_.3, f32[192,384]{1,0:T(8,128)} %refs_3_.3, f32[48,1536]{1,0:T(8,128)} %refs_6_.1, f32[576]{0:T(1024)} %refs_3_.2), custom_call_target="tpu_custom_call" | custom-call | tf_op jit(solution)/shard_map/pack/pallas_call | solution.py:117
  2.6 4.1 %collective-permute-start = (bf16[1,80,384]{2,1,0:T(8,128)(2,1)}, bf16[1,80,384]{2,1,0:T(8,128)(2,1)S(1)}, u32[]{:S(2)}, u32[]{:S(2)}) collective-permute-start(bf16[1,80,384]{2,1,0:T(8,128)(2,1)} %bitcast.6), channel_id=1, source_target_pairs={{0,4},{1,5},{2,6},{3,7},{4,0},{5,1},{6,2},{7,3},{8,9},{9,8},{10,11... | collective-permute-start | bytes 184328 | tf_op jit(solution)/shard_map/ppermute | solution.py:498
  6.7 2.4 %collective-permute-done = bf16[1,80,384]{2,1,0:T(8,128)(2,1)S(1)} collective-permute-done((bf16[1,80,384]{2,1,0:T(8,128)(2,1)}, bf16[1,80,384]{2,1,0:T(8,128)(2,1)S(1)}, u32[]{:S(2)}, u32[]{:S(2)}) %collective-permute-start) | collective-permute-done | bytes 61472 | tf_op jit(solution)/shard_map/ppermute | solution.py:498
  9.2 0.8 pad_maximum_fusion.4
  10.0 2.0 %collective-permute-start.1 = (bf16[2,80,384]{2,1,0:T(8,128)(2,1)S(1)}, bf16[2,80,384]{2,1,0:T(8,128)(2,1)S(1)}, u32[]{:S(2)}, u32[]{:S(2)}) collective-permute-start(bf16[2,80,384]{2,1,0:T(8,128)(2,1)S(1)} %pad_maximum_fusion.4), channel_id=1, source_target_pairs={{0,2},{1,3},{2,0},{3,1},{4,6},{5,7},{6,4},{7,5},{8,12},{9,13},{10,... | collective-permute-start | bytes 368648 | tf_op jit(solution)/shard_map/ppermute | solution.py:498
  12.0 3.1 %collective-permute-start.2 = (bf16[1,224,384]{2,1,0:T(8,128)(2,1)}, bf16[1,224,384]{2,1,0:T(8,128)(2,1)S(1)}, u32[]{:S(2)}, u32[]{:S(2)}) collective-permute-start(bf16[1,224,384]{2,1,0:T(8,128)(2,1)} %bitcast.9), channel_id=1, source_target_pairs={{0,4},{1,5},{2,6},{3,7},{4,0},{5,1},{6,2},{7,3},{8,9},{9,8},{10,11... | collective-permute-start | bytes 516104 | tf_op jit(solution)/shard_map/ppermute | solution.py:498
  15.1 0.0 collective-permute-done.1
  15.1 0.9 pad_maximum_fusion.3
  16.0 4.7 %collective-permute-done.2 = bf16[1,224,384]{2,1,0:T(8,128)(2,1)S(1)} collective-permute-done((bf16[1,224,384]{2,1,0:T(8,128)(2,1)}, bf16[1,224,384]{2,1,0:T(8,128)(2,1)S(1)}, u32[]{:S(2)}, u32[]{:S(2)}) %collective-permute-start.2) | collective-permute-done | bytes 172064 | tf_op jit(solution)/shard_map/ppermute | solution.py:498
  20.7 1.0 pad_maximum_fusion.2
  21.6 1.6 collective-permute-start.3
  23.2 4.7 %collective-permute-done.3 = bf16[4,80,384]{2,1,0:T(8,128)(2,1)S(1)} collective-permute-done((bf16[4,80,384]{2,1,0:T(8,128)(2,1)S(1)}, bf16[4,80,384]{2,1,0:T(8,128)(2,1)S(1)}, u32[]{:S(2)}, u32[]{:S(2)}) %collective-permute-start.3) | collective-permute-done | bytes 245792 | tf_op jit(solution)/shard_map/ppermute | solution.py:498
  27.9 0.0 copy-start.3
  27.9 0.1 collective-permute-start.4
  28.0 1.9 %collective-permute-done.4.other_ref = bf16[8,80,384]{2,1,0:T(8,128)(2,1)S(1)} collective-permute-done((bf16[8,80,384]{2,1,0:T(8,128)(2,1)S(1)}, bf16[8,80,384]{2,1,0:T(8,128)(2,1)S(1)}, u32[]{:S(2)}, u32[]{:S(2)}) %collective-permute-start.4) | collective-permute-done | bytes 491552 | tf_op jit(solution)/shard_map/ppermute | solution.py:498
  29.9 0.0 collective-permute-start.5
  29.9 0.8 copy-done.6
  30.7 11.3 %attn_fwd_first.1 = (bf16[4,1152,384]{2,1,0:T(8,128)(2,1)}, bf16[4,6,384,384]{3,2,1,0:T(8,128)(2,1)}, f32[4,8,384]{2,1,0:T(8,128)}, bf16[4,384,384]{2,1,0:T(8,12...) custom-call(bf16[8,80,384]{2,1,0:T(8,128)(2,1)} %copy-done.3, ...), custom_call_target="tpu_custom_call" | custom-call | flops 8000000000 | bytes 1048576 | tf_op jit(solution)/shard_map/attn_fwd_first/pallas_call | solution.py:228
  41.9 0.0 collective-permute-done.5
  41.9 0.1 pad_maximum_fusion.1
  42.0 1.6 collective-permute-start.6
  43.6 9.6 %attn_fwd_rest.1 = (bf16[4,1152,384]{2,1,0:T(8,128)(2,1)}, bf16[4,6,384,384]{3,2,1,0:T(8,128)(2,1)}, f32[4,8,384]{2,1,0:T(8,128)}, bf16[4,384,384]{2,1,0:T(8,128)(2,1)}, bf16[4,384,384]{2,1,0:T(8,128)(2,1)}) custom-call(f32[4,384,384]{2,1,0:T(8,128)} %x_ref.7, ...), custom_call_target="tpu_custom_call", output_to_operand_aliasing={{0}: (4, {}), {1}: (5, {}), {2}: (6, {}), {3}: (7, {}), {4}... | custom-call | flops 8000000000 | bytes 1048576 | tf_op jit(solution)/shard_map/attn_fwd_rest/pallas_call | solution.py:240
  53.2 0.0 collective-permute-done.6
  53.2 0.2 pad_maximum_fusion.mine_ref
  53.3 0.0 copy-start
  53.3 0.5 collective-permute-start.7
  53.8 2.8 %collective-permute-done.7.other_ref = bf16[8,224,384]{2,1,0:T(8,128)(2,1)S(1)} collective-permute-done((bf16[8,224,384]{2,1,0:T(8,128)(2,1)S(1)}, bf16[8,224,384]{2,1,0:T(8,128)(2,1)S(1)}, u32[]{:S(2)}, u32[]{:S(2)}) %collective-permute-start.7) | collective-permute-done | bytes 1376288 | tf_op jit(solution)/shard_map/ppermute | solution.py:498
  56.6 1.1 copy-done.5
  57.7 27.7 %mlp.1 = (f32[4,384,384]{2,1,0:T(8,128)}, bf16[4,384,1536]{2,1,0:T(8,128)(2,1)}, f32[4,384,384]{2,1,0:T(8,128)}, bf16[4,384,384]{2,1,0:T(8,128)(2,1)}, bf16[384,...) custom-call(bf16[8,224,384]{2,1,0:T(8,128)(2,1)} %copy-done, ...), custom_call_target="tpu_custom_call" | custom-call | flops 24000000000 | bytes 1048576 | tf_op jit(solution)/shard_map/mlp/pallas_call | solution.py:313
  85.4 0.6 collective-permute-start.8
  86.0 3.0 %collective-permute-done.8 = bf16[8,224,384]{2,1,0:T(8,128)(2,1)S(1)} collective-permute-done((bf16[8,224,384]{2,1,0:T(8,128)(2,1)}, bf16[8,224,384]{2,1,0:T(8,128)(2,1)S(1)}, u32[]{:S(2)}, u32[]{:S(2)}) %collective-permute-start.8) | collective-permute-done | bytes 1376288 | tf_op jit(solution)/shard_map/ppermute | solution.py:498
  88.9 2.1 %convert_add_fusion = f32[8,224,384]{2,1,0:T(8,128)S(1)} fusion(f32[8,224,384]{2,1,0:T(8,128)} %get-tuple-element.121, bf16[8,224,384]{2,1,0:T(8,128)(2,1)S(1)} %collective-permute-done.8), kind=kLoop, calls=%fused_computation | loop fusion | flops 1376256 | bytes 6881280 | tf_op jit(solution)/shard_map/add | solution.py:572
  91.0 0.1 slice.84
  91.1 1.6 %collective-permute-start.9 = (bf16[4,224,384]{2,1,0:T(8,128)(2,1)S(1)}, bf16[4,224,384]{2,1,0:T(8,128)(2,1)}, u32[]{:S(2)}, u32[]{:S(2)}) collective-permute-start(bf16[4,224,384]{2,1,0:T(8,128)(2,1)S(1)} %slice.84), channel_id=1, source_target_pairs={{0,1},{1,0},{2,3},{3,2},{4,5},{5,4},{6,7},{7,6},{8,10},{9,11},{10,... | collective-permute-start | bytes 2064392 | tf_op jit(solution)/shard_map/ppermute | solution.py:498
  92.7 10.3 %attn_bwd_first.1 = (bf16[4,1152,384]{2,1,0:T(8,128)(2,1)}, f32[1152,512]{1,0:T(8,128)}) custom-call(bf16[4,1152,384]{2,1,0:T(8,128)(2,1)} %get-tuple-element.117.jt_ref, bf16[4,6,384,384]{3,2,1,0:T(8,128)(2,1)} %get-tuple-element.118.e_ref, f32[4,8,384]{2,1,0:T(8,128)} %get-tuple-element.119.il_ref, bf16[4,384,384]{2,1,0:T(8,128)(2,1)} %get-tuple-element.115.ot_ref, ...), custom_call_target="tpu_custom_call" | custom-call | flops 8000000000 | bytes 1048576 | tf_op jit(solution)/shard_map/attn_bwd_first/pallas_call | solution.py:385
  103.0 1.2 slice_add_fusion
  104.3 1.0 collective-permute-start.16
  105.3 12.9 %attn_bwd_last.1 = (bf16[4,1152,384]{2,1,0:T(8,128)(2,1)}, f32[8,80,384]{2,1,0:T(8,128)}, bf16[8,80,384]{2,1,0:T(8,128)(2,1)}) custom-call(bf16[4,1152,384]{2,1,0:T(8,128)(2,1)} %get-tuple-element.117.jt_ref, bf16[4,6,384,384]{3,2,1,0:T(8,128)(2,1)} %get-tuple-element.118.e_ref, ...), custom_call_target="tpu_custom_call", output_to_operand_aliasing={{0}: (10, {})} | custom-call | flops 10000000000 | bytes 1048576 | tf_op jit(solution)/shard_map/attn_bwd_last/pallas_call | solution.py:395
  118.2 0.0 copy-start.1
  118.3 0.2 collective-permute-start.10
  118.5 0.0 collective-permute-done.16
  118.5 0.1 slice_add_fusion.1
  118.6 1.7 %collective-permute-start.17 = (bf16[1,224,384]{2,1,0:T(8,128)(2,1)S(1)}, bf16[1,224,384]{2,1,0:T(8,128)(2,1)S(1)}, u32[]{:S(2)}, u32[]{:S(2)}) collective-permute-start(bf16[1,224,384]{2,1,0:T(8,128)(2,1)S(1)} %slice.87), channel_id=1, source_target_pairs={{0,4},{1,5},{2,6},{3,7},{4,0},{5,1},{6,2},{7,3},{8,9},{9,8},{10,11... | collective-permute-start | bytes 516104 | tf_op jit(solution)/shard_map/ppermute | solution.py:498
  120.3 0.1 collective-permute-done.10
  120.4 0.1 convert_add_fusion.1
  120.5 1.2 collective-permute-start.11
  121.7 10.9 %tail.1 = (f32[4,384,384]{2,1,0:T(8,128)}, f32[4,384,384]{2,1,0:T(8,128)}) custom-call(f32[4,384,384]{2,1,0:T(8,128)} %x_ref.7, f32[4,384,384]{2,1,0:T(8,128)} %get-tuple-element.116.dm_ref, bf16[4,1152,384]{2,1,0:T(8,128)(2,1)} %get-tuple-element.132.dj_ref, bf16[1152,384]{1,0:T(8,128)(2,1)} %get-tuple-element.98.w_ref, ...), custom_call_target="tpu_custom_call" | custom-call | flops 10000000000 | bytes 1048576 | tf_op jit(solution)/shard_map/tail/pallas_call | solution.py:417
  132.6 0.0 collective-permute-done.11
  132.7 1.3 collective-permute-start.12
  134.1 1.6 %collective-permute-start.18 = (bf16[224,384]{1,0:T(8,128)(2,1)S(1)}, bf16[224,384]{1,0:T(8,128)(2,1)S(1)}, u32[]{:S(2)}, u32[]{:S(2)}) collective-permute-start(bf16[224,384]{1,0:T(8,128)(2,1)S(1)} %fusion.1), channel_id=1, source_target_pairs={{0,16},{1,17},{2,18},{3,19},{4,20},{5,21},{6,22},{7,23},{8,24},{9,... | collective-permute-start | bytes 516104 | tf_op jit(solution)/shard_map/ppermute | solution.py:498
  135.7 2.8 %collective-permute-done.12 = bf16[2,80,384]{2,1,0:T(8,128)(2,1)S(1)} collective-permute-done((bf16[2,80,384]{2,1,0:T(8,128)(2,1)S(1)}, bf16[2,80,384]{2,1,0:T(8,128)(2,1)S(1)}, u32[]{:S(2)}, u32[]{:S(2)}) %collective-permute-start.12) | collective-permute-done | bytes 122912 | tf_op jit(solution)/shard_map/ppermute | solution.py:498
  138.5 1.3 collective-permute-start.13
  139.8 0.9 collective-permute-done.18
  140.7 0.1 collective-permute-start.19
  140.8 2.9 %collective-permute-done.13 = bf16[1,80,384]{2,1,0:T(8,128)(2,1)S(1)} collective-permute-done((bf16[1,80,384]{2,1,0:T(8,128)(2,1)S(1)}, bf16[1,80,384]{2,1,0:T(8,128)(2,1)S(1)}, u32[]{:S(2)}, u32[]{:S(2)}) %collective-permute-start.13) | collective-permute-done | bytes 61472 | tf_op jit(solution)/shard_map/ppermute | solution.py:498
  143.7 1.6 %collective-permute-start.14 = (bf16[80,384]{1,0:T(8,128)(2,1)S(1)}, bf16[80,384]{1,0:T(8,128)(2,1)S(1)}, u32[]{:S(2)}, u32[]{:S(2)}) collective-permute-start(bf16[80,384]{1,0:T(8,128)(2,1)S(1)} %fusion.3), channel_id=1, source_target_pairs={{0,16},{1,17},{2,18},{3,19},{4,20},{5,21},{6,22},{7,23},{8,24},{9,... | collective-permute-start | bytes 184328 | tf_op jit(solution)/shard_map/ppermute | solution.py:498
  145.3 2.7 %collective-permute-done.14 = bf16[80,384]{1,0:T(8,128)(2,1)S(1)} collective-permute-done((bf16[80,384]{1,0:T(8,128)(2,1)S(1)}, bf16[80,384]{1,0:T(8,128)(2,1)S(1)}, u32[]{:S(2)}, u32[]{:S(2)}) %collective-permute-start.14) | collective-permute-done | bytes 61472 | tf_op jit(solution)/shard_map/ppermute | solution.py:498
  148.0 0.1 collective-permute-start.15
  148.1 0.0 collective-permute-done.19.other_ref
  148.1 0.7 copy-done.7
  148.9 3.6 %adam.3 = (f32[48,384]{1,0:T(8,128)}, f32[48,384]{1,0:T(8,128)}, f32[48,384]{1,0:T(8,128)}, bf16[48,384]{1,0:T(8,128)(2,1)}, f32[192,384]{1,0:T(8,128)}, /*index...) custom-call(f32[224,384]{1,0:T(8,128)} %copy-done.2, ...), custom_call_target="tpu_custom_call" | custom-call | flops 3000000000 | bytes 1048576 | tf_op jit(solution)/shard_map/adam/pallas_call | solution.py:470
  152.4 0.0 collective-permute-done.15.other_ref
  152.5 0.6 copy-done.8
  153.1 2.5 %adam.2 = (f32[144,384]{1,0:T(8,128)}, f32[144,384]{1,0:T(8,128)}, f32[144,384]{1,0:T(8,128)}, bf16[144,384]{1,0:T(8,128)(2,1)}, f32[576]{0:T(1024)}, /*index=5*...) custom-call(f32[80,384]{1,0:T(8,128)} %copy-done.4, f32[80,384]{1,0:T(8,128)} %copy-done.8, f32[144,384]{1,0:T(8,128)} %refs_0_.2, ...), custom_call_target="tpu_custom_call" | custom-call | flops 3000000000 | bytes 1048576 | tf_op jit(solution)/shard_map/adam/pallas_call | solution.py:470
  (26 shorter events, 0.4 us)
Async XLA Ops:
  2.6 6.5 %collective-permute-start = (bf16[1,80,384]{2,1,0:T(8,128)(2,1)}, bf16[1,80,384]{2,1,0:T(8,128)(2,1)S(1)}, u32[]{:S(2)}, u32[]{:S(2)}) collective-permute-start(bf16[1,80,384]{2,1,0:T(8,128)(2,1)} %bitcast.6), channel_id=1, source_target_pairs={{0,4},{1,5},{2,6},{3,7},{4,0},{5,1},{6,2},{7,3},{8,9},{9,8},{10,11... | collective-permute-start | bytes 184328 | tf_op jit(solution)/shard_map/ppermute | solution.py:498
  10.0 5.1 %collective-permute-start.1 = (bf16[2,80,384]{2,1,0:T(8,128)(2,1)S(1)}, bf16[2,80,384]{2,1,0:T(8,128)(2,1)S(1)}, u32[]{:S(2)}, u32[]{:S(2)}) collective-permute-start(bf16[2,80,384]{2,1,0:T(8,128)(2,1)S(1)} %pad_maximum_fusion.4), channel_id=1, source_target_pairs={{0,2},{1,3},{2,0},{3,1},{4,6},{5,7},{6,4},{7,5},{8,12},{9,13},{10,... | collective-permute-start | bytes 368648 | tf_op jit(solution)/shard_map/ppermute | solution.py:498
  12.0 8.7 %collective-permute-start.2 = (bf16[1,224,384]{2,1,0:T(8,128)(2,1)}, bf16[1,224,384]{2,1,0:T(8,128)(2,1)S(1)}, u32[]{:S(2)}, u32[]{:S(2)}) collective-permute-start(bf16[1,224,384]{2,1,0:T(8,128)(2,1)} %bitcast.9), channel_id=1, source_target_pairs={{0,4},{1,5},{2,6},{3,7},{4,0},{5,1},{6,2},{7,3},{8,9},{9,8},{10,11... | collective-permute-start | bytes 516104 | tf_op jit(solution)/shard_map/ppermute | solution.py:498
  21.6 6.3 %collective-permute-start.3 = (bf16[4,80,384]{2,1,0:T(8,128)(2,1)S(1)}, bf16[4,80,384]{2,1,0:T(8,128)(2,1)S(1)}, u32[]{:S(2)}, u32[]{:S(2)}) collective-permute-start(bf16[4,80,384]{2,1,0:T(8,128)(2,1)S(1)} %pad_maximum_fusion.3), channel_id=1, source_target_pairs={{0,1},{1,0},{2,3},{3,2},{4,5},{5,4},{6,7},{7,6},{8,10},{9,11},{10,... | collective-permute-start | bytes 737288 | tf_op jit(solution)/shard_map/ppermute | solution.py:498
  27.9 1.9 %copy-start.3 = (bf16[8,80,384]{2,1,0:T(8,128)(2,1)}, bf16[8,80,384]{2,1,0:T(8,128)(2,1)S(1)}, u32[]{:S(2)}) copy-start(bf16[8,80,384]{2,1,0:T(8,128)(2,1)S(1)} %constant_dynamic-update-slice_fusion.mine_ref) | copy-start | bytes 1474564
  27.9 1.9 %collective-permute-start.4 = (bf16[8,80,384]{2,1,0:T(8,128)(2,1)S(1)}, bf16[8,80,384]{2,1,0:T(8,128)(2,1)S(1)}, u32[]{:S(2)}, u32[]{:S(2)}) collective-permute-start(bf16[8,80,384]{2,1,0:T(8,128)(2,1)S(1)} %constant_dynamic-update-slice_fusion.mine_ref), channel_id=1, source_target_pairs={{0,8},{1,9},{2,10},{3,11},{4,12},{5,13},{6,14},{7,15},{8,0},{9,1},... | collective-permute-start | bytes 1474568 | tf_op jit(solution)/shard_map/ppermute | solution.py:498
  29.9 0.8 copy-start.6
  29.9 12.1 %collective-permute-start.5 = (bf16[2,224,384]{2,1,0:T(8,128)(2,1)S(1)}, bf16[2,224,384]{2,1,0:T(8,128)(2,1)S(1)}, u32[]{:S(2)}, u32[]{:S(2)}) collective-permute-start(bf16[2,224,384]{2,1,0:T(8,128)(2,1)S(1)} %pad_maximum_fusion.2), channel_id=1, source_target_pairs={{0,2},{1,3},{2,0},{3,1},{4,6},{5,7},{6,4},{7,5},{8,12},{9,13},{10,... | collective-permute-start | bytes 1032200 | tf_op jit(solution)/shard_map/ppermute | solution.py:498
  42.0 11.1 %collective-permute-start.6 = (bf16[4,224,384]{2,1,0:T(8,128)(2,1)S(1)}, bf16[4,224,384]{2,1,0:T(8,128)(2,1)S(1)}, u32[]{:S(2)}, u32[]{:S(2)}) collective-permute-start(bf16[4,224,384]{2,1,0:T(8,128)(2,1)S(1)} %pad_maximum_fusion.1), channel_id=1, source_target_pairs={{0,1},{1,0},{2,3},{3,2},{4,5},{5,4},{6,7},{7,6},{8,10},{9,11},{10,... | collective-permute-start | bytes 2064392 | tf_op jit(solution)/shard_map/ppermute | solution.py:498
  53.3 3.3 %copy-start = (bf16[8,224,384]{2,1,0:T(8,128)(2,1)}, bf16[8,224,384]{2,1,0:T(8,128)(2,1)S(1)}, u32[]{:S(2)}) copy-start(bf16[8,224,384]{2,1,0:T(8,128)(2,1)S(1)} %pad_maximum_fusion.mine_ref) | copy-start | bytes 4128772
  53.3 3.3 %collective-permute-start.7 = (bf16[8,224,384]{2,1,0:T(8,128)(2,1)S(1)}, bf16[8,224,384]{2,1,0:T(8,128)(2,1)S(1)}, u32[]{:S(2)}, u32[]{:S(2)}) collective-permute-start(bf16[8,224,384]{2,1,0:T(8,128)(2,1)S(1)} %pad_maximum_fusion.mine_ref), channel_id=1, source_target_pairs={{0,8},{1,9},{2,10},{3,11},{4,12},{5,13},{6,14},{7,15},{8,0},{9,1},... | collective-permute-start | bytes 4128776 | tf_op jit(solution)/shard_map/ppermute | solution.py:498
  56.6 1.1 copy-start.5
  85.4 3.5 %collective-permute-start.8 = (bf16[8,224,384]{2,1,0:T(8,128)(2,1)}, bf16[8,224,384]{2,1,0:T(8,128)(2,1)S(1)}, u32[]{:S(2)}, u32[]{:S(2)}) collective-permute-start(bf16[8,224,384]{2,1,0:T(8,128)(2,1)} %get-tuple-element.122), channel_id=1, source_target_pairs={{0,8},{1,9},{2,10},{3,11},{4,12},{5,13},{6,14},{7,15},{8,0},{9,1},... | collective-permute-start | bytes 4128776 | tf_op jit(solution)/shard_map/ppermute | solution.py:498
  91.1 11.9 %collective-permute-start.9 = (bf16[4,224,384]{2,1,0:T(8,128)(2,1)S(1)}, bf16[4,224,384]{2,1,0:T(8,128)(2,1)}, u32[]{:S(2)}, u32[]{:S(2)}) collective-permute-start(bf16[4,224,384]{2,1,0:T(8,128)(2,1)S(1)} %slice.84), channel_id=1, source_target_pairs={{0,1},{1,0},{2,3},{3,2},{4,5},{5,4},{6,7},{7,6},{8,10},{9,11},{10,... | collective-permute-start | bytes 2064392 | tf_op jit(solution)/shard_map/ppermute | solution.py:498
  104.3 14.2 %collective-permute-start.16 = (bf16[2,224,384]{2,1,0:T(8,128)(2,1)S(1)}, bf16[2,224,384]{2,1,0:T(8,128)(2,1)S(1)}, u32[]{:S(2)}, u32[]{:S(2)}) collective-permute-start(bf16[2,224,384]{2,1,0:T(8,128)(2,1)S(1)} %slice.85), channel_id=1, source_target_pairs={{0,2},{1,3},{2,0},{3,1},{4,6},{5,7},{6,4},{7,5},{8,12},{9,13},{10,... | collective-permute-start | bytes 1032200 | tf_op jit(solution)/shard_map/ppermute | solution.py:498
  118.2 2.2 %copy-start.1 = (f32[8,80,384]{2,1,0:T(8,128)S(1)}, f32[8,80,384]{2,1,0:T(8,128)}, u32[]{:S(2)}) copy-start(f32[8,80,384]{2,1,0:T(8,128)} %get-tuple-element.130) | copy-start | bytes 2949124
  118.3 2.1 %collective-permute-start.10 = (bf16[8,80,384]{2,1,0:T(8,128)(2,1)}, bf16[8,80,384]{2,1,0:T(8,128)(2,1)S(1)}, u32[]{:S(2)}, u32[]{:S(2)}) collective-permute-start(bf16[8,80,384]{2,1,0:T(8,128)(2,1)} %get-tuple-element.131), channel_id=1, source_target_pairs={{0,8},{1,9},{2,10},{3,11},{4,12},{5,13},{6,14},{7,15},{8,0},{9,1},... | collective-permute-start | bytes 1474568 | tf_op jit(solution)/shard_map/ppermute | solution.py:498
  118.6 15.5 %collective-permute-start.17 = (bf16[1,224,384]{2,1,0:T(8,128)(2,1)S(1)}, bf16[1,224,384]{2,1,0:T(8,128)(2,1)S(1)}, u32[]{:S(2)}, u32[]{:S(2)}) collective-permute-start(bf16[1,224,384]{2,1,0:T(8,128)(2,1)S(1)} %slice.87), channel_id=1, source_target_pairs={{0,4},{1,5},{2,6},{3,7},{4,0},{5,1},{6,2},{7,3},{8,9},{9,8},{10,11... | collective-permute-start | bytes 516104 | tf_op jit(solution)/shard_map/ppermute | solution.py:498
  120.5 12.1 %collective-permute-start.11 = (bf16[4,80,384]{2,1,0:T(8,128)(2,1)S(1)}, bf16[4,80,384]{2,1,0:T(8,128)(2,1)S(1)}, u32[]{:S(2)}, u32[]{:S(2)}) collective-permute-start(bf16[4,80,384]{2,1,0:T(8,128)(2,1)S(1)} %slice.86), channel_id=1, source_target_pairs={{0,1},{1,0},{2,3},{3,2},{4,5},{5,4},{6,7},{7,6},{8,10},{9,11},{10,... | collective-permute-start | bytes 737288 | tf_op jit(solution)/shard_map/ppermute | solution.py:498
  132.7 5.7 %collective-permute-start.12 = (bf16[2,80,384]{2,1,0:T(8,128)(2,1)S(1)}, bf16[2,80,384]{2,1,0:T(8,128)(2,1)S(1)}, u32[]{:S(2)}, u32[]{:S(2)}) collective-permute-start(bf16[2,80,384]{2,1,0:T(8,128)(2,1)S(1)} %slice.88), channel_id=1, source_target_pairs={{0,2},{1,3},{2,0},{3,1},{4,6},{5,7},{6,4},{7,5},{8,12},{9,13},{10,... | collective-permute-start | bytes 368648 | tf_op jit(solution)/shard_map/ppermute | solution.py:498
  134.1 6.6 %collective-permute-start.18 = (bf16[224,384]{1,0:T(8,128)(2,1)S(1)}, bf16[224,384]{1,0:T(8,128)(2,1)S(1)}, u32[]{:S(2)}, u32[]{:S(2)}) collective-permute-start(bf16[224,384]{1,0:T(8,128)(2,1)S(1)} %fusion.1), channel_id=1, source_target_pairs={{0,16},{1,17},{2,18},{3,19},{4,20},{5,21},{6,22},{7,23},{8,24},{9,... | collective-permute-start | bytes 516104 | tf_op jit(solution)/shard_map/ppermute | solution.py:498
  138.5 5.2 %collective-permute-start.13 = (bf16[1,80,384]{2,1,0:T(8,128)(2,1)S(1)}, bf16[1,80,384]{2,1,0:T(8,128)(2,1)S(1)}, u32[]{:S(2)}, u32[]{:S(2)}) collective-permute-start(bf16[1,80,384]{2,1,0:T(8,128)(2,1)S(1)} %slice.89), channel_id=1, source_target_pairs={{0,4},{1,5},{2,6},{3,7},{4,0},{5,1},{6,2},{7,3},{8,9},{9,8},{10,11... | collective-permute-start | bytes 184328 | tf_op jit(solution)/shard_map/ppermute | solution.py:498
  140.7 7.4 %copy-start.2 = (f32[224,384]{1,0:T(8,128)}, f32[224,384]{1,0:T(8,128)S(1)}, u32[]{:S(2)}) copy-start(f32[224,384]{1,0:T(8,128)S(1)} %convert_add_fusion.3.mine_ref) | copy-start | bytes 1032196
  140.7 7.4 %collective-permute-start.19 = (f32[224,384]{1,0:T(8,128)S(1)}, f32[224,384]{1,0:T(8,128)S(1)}, u32[]{:S(2)}, u32[]{:S(2)}) collective-permute-start(f32[224,384]{1,0:T(8,128)S(1)} %convert_add_fusion.3.mine_ref), channel_id=1, source_target_pairs={{0,8},{1,9},{2,10},{3,11},{4,12},{5,13},{6,14},{7,15},{8,0},{9,1},... | collective-permute-start | bytes 1032200 | tf_op jit(solution)/shard_map/ppermute | solution.py:498
  143.7 4.3 %collective-permute-start.14 = (bf16[80,384]{1,0:T(8,128)(2,1)S(1)}, bf16[80,384]{1,0:T(8,128)(2,1)S(1)}, u32[]{:S(2)}, u32[]{:S(2)}) collective-permute-start(bf16[80,384]{1,0:T(8,128)(2,1)S(1)} %fusion.3), channel_id=1, source_target_pairs={{0,16},{1,17},{2,18},{3,19},{4,20},{5,21},{6,22},{7,23},{8,24},{9,... | collective-permute-start | bytes 184328 | tf_op jit(solution)/shard_map/ppermute | solution.py:498
  148.0 4.4 %copy-start.4 = (f32[80,384]{1,0:T(8,128)}, f32[80,384]{1,0:T(8,128)S(1)}, u32[]{:S(2)}) copy-start(f32[80,384]{1,0:T(8,128)S(1)} %convert_add_fusion.5.mine_ref) | copy-start | bytes 368644
  148.0 4.4 %collective-permute-start.15 = (f32[80,384]{1,0:T(8,128)S(1)}, f32[80,384]{1,0:T(8,128)S(1)}, u32[]{:S(2)}, u32[]{:S(2)}) collective-permute-start(f32[80,384]{1,0:T(8,128)S(1)} %convert_add_fusion.5.mine_ref), channel_id=1, source_target_pairs={{0,8},{1,9},{2,10},{3,11},{4,12},{5,13},{6,14},{7,15},{8,0},{9,1},... | collective-permute-start | bytes 368648 | tf_op jit(solution)/shard_map/ppermute | solution.py:498
  148.1 0.7 copy-start.7
  152.4 0.6 copy-start.8

commit v3 on v2

--- a/solution.py
+++ b/solution.py
@@ -11,6 +11,7 @@
 HEADS = 6
 EPS = 1e-6
 OWNERS = 8
+MLP_MIB = 26
 beta_first = 0.5
 beta_second = 0.5
 adam_eps = 1e-08
@@ -55,9 +56,10 @@
 
 
 class Layout:
-    def __init__(self, d, ff, masks, position):
+    def __init__(self, d, ff, orders, position):
         self.d, self.ff, self.cols = d, ff, ff // d
-        self.masks, self.position = masks, position
+        self.position = position
+        self.masks = [[sum(bit for k, bit in enumerate(order) if j >> k & 1) for j in range(OWNERS)] for order in orders]
         self.q, self.p, self.u = 3 * d // OWNERS, d // OWNERS, ff // OWNERS
         q0 = (self.q // 2 + 15) // 16 * 16
         self.first = ((("q", 0, q0, 0, 0),), (("q", q0, self.q - q0, 0, 0), ("v", 0, 16, 0, self.q - q0)))
@@ -231,7 +233,7 @@
         out_specs=fwd_blocks(t, d, 0) + [full(a) for a in extra],
         out_shape=fwd_outs(b, t, d) + extra,
         scratch_shapes=[pltpu.VMEM((OWNERS * 16, d), bf16), pltpu.SemaphoreType.DMA((n_copies,))],
-        compiler_params=params(60), cost_estimate=cost(4 * count), name="attn_fwd_first",
+        compiler_params=params(24), cost_estimate=cost(4 * count), name="attn_fwd_first",
     )(mine, other, x)
 
 
@@ -242,7 +244,7 @@
         in_specs=[one(t, d, off=off), full(w), full(vrow), full(vcol)] + [ANY] * 5,
         out_specs=fwd_blocks(t, d, off), out_shape=fwd_outs(b, t, d),
         input_output_aliases={4 + k: k for k in range(5)},
-        compiler_params=params(60), cost_estimate=cost(4 * count), name="attn_fwd_rest",
+        compiler_params=params(24), cost_estimate=cost(4 * count), name="attn_fwd_rest",
     )(x, w, vrow, vcol, *outs)
 
 
@@ -307,8 +309,9 @@
 def call_mlp(lay, mine, other, x, ot, cot, vrow):
     b, t, d = x.shape
     ff = lay.ff
-    acc = [S((d, ff), bf16), S((16, d), f32), S((OWNERS, lay.second_rows, d), f32), S((OWNERS, lay.second_rows, d), bf16)]
-    outs = [S((b, t, d), f32), S((b, t, ff), bf16), S((b, t, d), f32), S((b, d, t), bf16)] + acc
+    hbm = pltpu.HBM
+    acc = [hbm((d, ff), bf16), S((16, d), f32), hbm((OWNERS, lay.second_rows, d), f32), S((OWNERS, lay.second_rows, d), bf16)]
+    outs = [hbm((b, t, d), f32), hbm((b, t, ff), bf16), hbm((b, t, d), f32), S((b, d, t), bf16)] + acc
     n_copies = OWNERS * (len(lay.second[0]) + len(lay.second[1]))
     return pl.pallas_call(
         functools.partial(mlp, lay, b), grid=(b,),
@@ -317,7 +320,7 @@
         out_shape=outs,
         scratch_shapes=[pltpu.VMEM((d, d), bf16), pltpu.VMEM((ff, d), bf16), pltpu.VMEM((d, d), f32), pltpu.VMEM((ff, d), f32),
                         pltpu.VMEM((d, ff), f32), pltpu.SemaphoreType.DMA((n_copies,))],
-        compiler_params=params(60), cost_estimate=cost(24), name="mlp",
+        compiler_params=params(MLP_MIB), cost_estimate=cost(24), name="mlp",
     )(mine, other, x, ot, cot, vrow)
 
 
@@ -385,7 +388,7 @@
     return pl.pallas_call(
         attn_bwd_first, grid=(count,), in_specs=bwd_blocks(t, d, 0),
         out_specs=[one(3 * d, t), full(dw)], out_shape=[S((b, 3 * d, t), bf16), dw],
-        compiler_params=params(60), cost_estimate=cost(4 * count), name="attn_bwd_first",
+        compiler_params=params(24), cost_estimate=cost(4 * count), name="attn_bwd_first",
     )(*acts)
 
 
@@ -398,12 +401,24 @@
         out_specs=[one(3 * d, t, off=off)] + [full(a) for a in slots], out_shape=[S((b, 3 * d, t), bf16)] + slots,
         scratch_shapes=[pltpu.VMEM(dw.shape, f32), pltpu.VMEM((OWNERS * 16, d), f32)],
         input_output_aliases={10: 0},
-        compiler_params=params(60), cost_estimate=cost(4 * count + 2), name="attn_bwd_last",
+        compiler_params=params(28), cost_estimate=cost(4 * count + 2), name="attn_bwd_last",
     )(*acts, dw, w, vrow, dv, dj)
 
 
-def tail(x_ref, dm_ref, dj_ref, w_ref, mid_ref, act_ref, wd_ref, vrow_ref, gx_ref, lo_ref):
+def layer_end(mid_ref, act_ref, wd_ref, vrow_ref, lo_ref):
     lo_ref[0] = mid_ref[0] + (dot(act_ref[0], wd_ref[...], 1, 1) + vrow_ref[7:8, :])
+
+
+def call_layer_end(mid, act, wd, vrow):
+    b, t, d = mid.shape
+    return pl.pallas_call(
+        layer_end, grid=(b,), in_specs=[one(t, d), one(t, act.shape[2]), full(wd), full(vrow)],
+        out_specs=one(t, d), out_shape=S((b, t, d), f32),
+        compiler_params=params(16), cost_estimate=cost(4), name="layer_end",
+    )(mid, act, wd, vrow)
+
+
+def input_end(x_ref, dm_ref, dj_ref, w_ref, vrow_ref, gx_ref):
     dh = dot(dj_ref[0], w_ref[...], 0, 0)
     xhat, rstd = norm_stats(x_ref[0])
     gy = dh * vrow_ref[0:1, :]
@@ -412,15 +427,13 @@
     gx_ref[0] = dm_ref[0] + rstd * (gy - m1 - xhat * m2)
 
 
-def call_tail(x, dm, dj, w, mid, act, wd, vrow):
+def call_input_end(x, dm, dj, w, vrow):
     b, t, d = x.shape
     return pl.pallas_call(
-        tail, grid=(b,),
-        in_specs=[one(t, d), one(t, d), one(3 * d, t), full(w), one(t, d), one(t, act.shape[2]), full(wd), full(vrow)],
-        out_specs=[one(t, d), one(t, d)],
-        out_shape=[S((b, t, d), f32), S((b, t, d), f32)],
-        compiler_params=params(60), cost_estimate=cost(10), name="tail",
-    )(x, dm, dj, w, mid, act, wd, vrow)
+        input_end, grid=(b,), in_specs=[one(t, d), one(t, d), one(3 * d, t), full(w), full(vrow)],
+        out_specs=one(t, d), out_shape=S((b, t, d), f32),
+        compiler_params=params(16), cost_estimate=cost(4), name="input_end",
+    )(x, dm, dj, w, vrow)
 
 
 def adam_values(master, first, second, grad, rate, decay):
@@ -470,7 +483,7 @@
     got = pl.pallas_call(
         functools.partial(adam, lay, halves, names),
         in_specs=[whole(a) for a in (mine, other, *flat)], out_specs=[whole(a) for a in outs], out_shape=outs,
-        compiler_params=params(60), cost_estimate=cost(3), name="adam",
+        compiler_params=params(16), cost_estimate=cost(3), name="adam",
     )(mine, other, *flat)
     return {name: got[4 * k:4 * k + 4] for k, name in enumerate(names)}
 
@@ -644,17 +657,16 @@
     return lax.optimization_barrier((value, *earlier))[0]
 
 
-def compute(lay, x, cot, gather, reduce, rounds):
+def compute(lay, x, cot, gather, reduce, finish_second, rounds):
     b = x.shape[0]
     k = min(FIRST_IMAGES, b - 1)
     one, two = gather
     one.round()
     two.held = after(two.held, one.held)
     two.round()
-    one.round()
+    for _ in range(rounds - 1):
+        one.round()
     one.held, two.held = lax.optimization_barrier((one.held, two.held))
-    for _ in range(rounds - 2):
-        one.round()
     first = one.core()
     two.held, *first = lax.optimization_barrier((two.held, *first))
     *outs, wq, vrow, vcol = call_attn_fwd_first(lay, *first, x, k)
@@ -671,7 +683,7 @@
     acts = (jt, e, il, ot, after(dot_, down.held), h)
     dj, dw = call_attn_bwd_first(acts, k)
     down.round()
-    dw = after(dw, down.held)
+    dw, down.held = lax.optimization_barrier((dw, down.held))
     dj, keep, give = call_attn_bwd_last(lay, acts, dw, wq, vrow, dv, dj, k, b - k)
     for _ in range(rounds - 2):
         down.round()
@@ -679,23 +691,29 @@
     up.core()
     dj, up.held = lax.optimization_barrier((dj, up.held))
     up.round()
-    gx, lo = call_tail(x, dm, dj, wq, mid, act, wd, vrow)
-    up.held = after(up.held, gx)
-    for _ in range(rounds - 1):
+    gx = call_input_end(x, dm, dj, wq, vrow)
+    gx, up.held = lax.optimization_barrier((gx, up.held))
+    lo = call_layer_end(after(mid, gx), act, wd, vrow)
+    up.round()
+    lo, up.held = lax.optimization_barrier((lo, up.held))
+    for _ in range(rounds - 2):
         up.round()
     down.round()
     down.others()
-    second_sum = down.finish()
+    second_new = finish_second(*down.finish())
     up.others()
-    return lo, gx, up.finish(), second_sum
+    return lo, gx, up.finish(), second_new
 
 
 def eight_owners(links, lay, x, cot, states):
     masters = {name: s[0] for name, s in states.items()}
     first, second = call_pack(lay, *(masters[name] for name in "qpudv"))
     gather = Gather(links, first), Gather(links, second)
-    lo, gx, first_sum, second_sum = compute(lay, x, cot, gather, functools.partial(Reduce, links), links.rounds)
-    new = call_adam(lay, lay.second, *second_sum, {name: states[name] for name in "pud"})
+
+    def finish_second(mine, other):
+        return call_adam(lay, lay.second, mine, other, {name: states[name] for name in "pud"})
+
+    lo, gx, first_sum, new = compute(lay, x, cot, gather, functools.partial(Reduce, links), finish_second, links.rounds)
     new |= call_adam(lay, lay.first, *first_sum, {name: states[name] for name in "qv"})
     return lo, gx, new
 
@@ -732,7 +750,7 @@
     got = split(links.gather_rows(join(masters, 1)[0].astype(bf16)))
     got["v"] = eighths(got["v"])
     gather = Here(*to_slots(lay, lay.first, lay.first_rows, got)), Here(*to_slots(lay, lay.second, lay.second_rows, got))
-    lo, gx, first_sum, second_sum = compute(lay, x, cot, gather, Here, 3)
+    lo, gx, first_sum, second_sum = compute(lay, x, cot, gather, Here, lambda *both: both, 3)
     grads = from_slots(lay.first, first_sum) | from_slots(lay.second, second_sum)
     grads["v"] = grads["v"].reshape(OWNERS, 16, d)[:, :3, :lay.piece]
     mine = split(links.reduce_rows(join(grads, n))[None])
@@ -745,10 +763,10 @@
 
 def per_device(links, x, cot, *arrays):
     if links.wide == OWNERS:
-        run, masks, position = eight_owners, links.masks, links.here
+        run, orders, position = eight_owners, links.orders, links.here
     else:
-        run, masks, position = any_owners, [list(range(OWNERS))] * 2, lambda: (0, 0)
-    lay = Layout(x.shape[2], arrays[3].shape[1], masks, position)
+        run, orders, position = any_owners, [[1, 2, 4]] * 2, lambda: (0, 0)
+    lay = Layout(x.shape[2], arrays[3].shape[1], orders, position)
     names = "qpudv"
     states = {name: arrays[k::5] for k, name in enumerate(names)}
     lo, gx, new = run(links, lay, x, cot, states)

time: 156 us -> 137 us (0.88)
  Pallas kernels: 90.7 us -> 69.7 us
  starting transfers between devices: 25.1 us -> 32.4 us
  local copies, waits for them, and re-layouts: 3.52 us -> 0.33 us
  waiting for transfers between devices: 28.7 us -> 26.3 us
    ppermute x20, starting transfers between devices: 25.1 us -> 32.4 us  [permute(): return lax.ppermute(value, ('narrow', 'wide'), pairs)]
    pallas_call x1, Pallas kernels: 12.9 us -> 7.64 us  [call_attn_bwd_last(): pl.pallas_call(functools.partial(attn_bwd_last, lay, count), grid=(count,...]
    pallas_call x1, Pallas kernels: 10.3 us -> 6.96 us  [call_attn_bwd_first(): pl.pallas_call(attn_bwd_first, grid=(count,), in_specs=bwd_blocks(t, d, 0...]
    unnamed x19 -> x48, local copies, waits for them, and re-layouts: 3.28 us -> 0.13 us
    pallas_call x1, Pallas kernels: 9.57 us -> 6.51 us  [call_attn_fwd_rest(): pl.pallas_call(attn_fwd_rest, grid=(count,), in_specs=[one(t, d, off=off)...]
    pallas_call x2, Pallas kernels: 6.01 us -> 3.11 us  [call_adam(): pl.pallas_call(functools.partial(adam, lay, halves, names), in_specs=[who...]
    pallas_call x1, Pallas kernels: 11.3 us -> 8.69 us  [call_attn_fwd_first(): pl.pallas_call(functools.partial(attn_fwd_first, lay), grid=(count,), in_...]
    pallas_call x1 -> x2, Pallas kernels: 10.9 us -> 8.38 us  [the longest x1 4.3 us: call_input_end(): pl.pallas_call(input_end, grid=(b,), in_specs=[one(t, d), one(t, d), one(...]
  transfers between devices with their start and end apart: 20 -> 20, of which waited for: 11 -> 11; matrix products, arithmetic and copies ran while one was open for 1% -> 2% of each run, Pallas kernels for 38% -> 29%
where the time goes in v3:
time: 137 us; the launch traced here: 136 us
  Pallas kernels  69.7 us (51%)
  starting transfers between devices  32.4 us (24%)
  waiting for transfers between devices  26.3 us (19%)
  other arithmetic  6.25 us (5%)
    ppermute x20, starting transfers between devices, permute(): return lax.ppermute(value, ('narrow', 'wide'), pairs)  32.4 us
    ppermute x20, waiting for transfers between devices, permute(): return lax.ppermute(value, ('narrow', 'wide'), pairs)  26.3 us
    pallas_call x1, Pallas kernels, call_mlp(): pl.pallas_call(functools.partial(mlp, lay, b), grid=(b,), in_specs=[HBM,...  26.3 us
    pallas_call x1, Pallas kernels, call_attn_fwd_first(): pl.pallas_call(functools.partial(attn_fwd_first, lay), grid=(count,), in_...  8.69 us
    pallas_call x1, Pallas kernels, call_attn_bwd_last(): pl.pallas_call(functools.partial(attn_bwd_last, lay, count), grid=(count,...  7.64 us
    pallas_call x1, Pallas kernels, call_attn_bwd_first(): pl.pallas_call(attn_bwd_first, grid=(count,), in_specs=bwd_blocks(t, d, 0...  6.96 us
    pallas_call x1, Pallas kernels, call_attn_fwd_rest(): pl.pallas_call(attn_fwd_rest, grid=(count,), in_specs=[one(t, d, off=off)...  6.51 us
    pallas_call x1, Pallas kernels, call_input_end(): pl.pallas_call(input_end, grid=(b,), in_specs=[one(t, d), one(t, d), one(...  4.3 us
  transfers between devices with their start and end apart: 20, of which 11 were waited for; matrix products, arithmetic and copies ran while one was open for 2% of the time, Pallas kernels for 29%

profile of v3, /device:TPU:0, one launch (start us, length us, event | category | flops | bytes accessed | tf_op | source)
XLA Modules:
  0.0 136.2 jit_solution(11473003060899599381)
XLA Ops:
  0.7 2.1 %pack.1 = (bf16[80,384]{1,0:T(8,128)(2,1)}, bf16[224,384]{1,0:T(8,128)(2,1)}) custom-call(f32[144,384]{1,0:T(8,128)} %refs_0_.2, f32[48,384]{1,0:T(8,128)} %refs_0_.3, f32[192,384]{1,0:T(8,128)} %refs_3_.3, f32[48,1536]{1,0:T(8,128)} %refs_6_.1, f32[576]{0:T(1024)} %refs_3_.2), custom_call_target="tpu_custom_call" | custom-call | tf_op jit(solution)/shard_map/pack/pallas_call | solution.py:119
  2.8 4.1 %collective-permute-start = (bf16[1,80,384]{2,1,0:T(8,128)(2,1)}, bf16[1,80,384]{2,1,0:T(8,128)(2,1)S(1)}, u32[]{:S(2)}, u32[]{:S(2)}) collective-permute-start(bf16[1,80,384]{2,1,0:T(8,128)(2,1)} %bitcast.8), channel_id=1, source_target_pairs={{0,4},{1,5},{2,6},{3,7},{4,0},{5,1},{6,2},{7,3},{8,9},{9,8},{10,11... | collective-permute-start | bytes 184328 | tf_op jit(solution)/shard_map/ppermute | solution.py:511
  6.9 2.4 %collective-permute-done = bf16[1,80,384]{2,1,0:T(8,128)(2,1)S(1)} collective-permute-done((bf16[1,80,384]{2,1,0:T(8,128)(2,1)}, bf16[1,80,384]{2,1,0:T(8,128)(2,1)S(1)}, u32[]{:S(2)}, u32[]{:S(2)}) %collective-permute-start) | collective-permute-done | bytes 61472 | tf_op jit(solution)/shard_map/ppermute | solution.py:511
  9.3 0.8 pad_maximum_fusion.5
  10.2 2.0 %collective-permute-start.1 = (bf16[2,80,384]{2,1,0:T(8,128)(2,1)S(1)}, bf16[2,80,384]{2,1,0:T(8,128)(2,1)S(1)}, u32[]{:S(2)}, u32[]{:S(2)}) collective-permute-start(bf16[2,80,384]{2,1,0:T(8,128)(2,1)S(1)} %pad_maximum_fusion.5), channel_id=1, source_target_pairs={{0,2},{1,3},{2,0},{3,1},{4,6},{5,7},{6,4},{7,5},{8,12},{9,13},{10,... | collective-permute-start | bytes 368648 | tf_op jit(solution)/shard_map/ppermute | solution.py:511
  12.1 3.1 %collective-permute-start.3 = (bf16[1,224,384]{2,1,0:T(8,128)(2,1)}, bf16[1,224,384]{2,1,0:T(8,128)(2,1)S(1)}, u32[]{:S(2)}, u32[]{:S(2)}) collective-permute-start(bf16[1,224,384]{2,1,0:T(8,128)(2,1)} %bitcast.12), channel_id=1, source_target_pairs={{0,4},{1,5},{2,6},{3,7},{4,0},{5,1},{6,2},{7,3},{8,9},{9,8},{10,11... | collective-permute-start | bytes 516104 | tf_op jit(solution)/shard_map/ppermute | solution.py:511
  15.3 0.9 pad_maximum_fusion.4
  16.1 1.9 %collective-permute-start.2 = (bf16[4,80,384]{2,1,0:T(8,128)(2,1)S(1)}, bf16[4,80,384]{2,1,0:T(8,128)(2,1)S(1)}, u32[]{:S(2)}, u32[]{:S(2)}) collective-permute-start(bf16[4,80,384]{2,1,0:T(8,128)(2,1)S(1)} %pad_maximum_fusion.4), channel_id=1, source_target_pairs={{0,1},{1,0},{2,3},{3,2},{4,5},{5,4},{6,7},{7,6},{8,10},{9,11},{10,... | collective-permute-start | bytes 737288 | tf_op jit(solution)/shard_map/ppermute | solution.py:511
  18.1 2.7 %collective-permute-done.3 = bf16[1,224,384]{2,1,0:T(8,128)(2,1)S(1)} collective-permute-done((bf16[1,224,384]{2,1,0:T(8,128)(2,1)}, bf16[1,224,384]{2,1,0:T(8,128)(2,1)S(1)}, u32[]{:S(2)}, u32[]{:S(2)}) %collective-permute-start.3) | collective-permute-done | bytes 172064 | tf_op jit(solution)/shard_map/ppermute | solution.py:511
  20.8 1.0 pad_maximum_fusion.3
  21.8 0.6 collective-permute-done.2
  22.4 0.9 pad_maximum_fusion.2.mine_ref
  23.3 0.1 collective-permute-start.4
  23.4 1.9 %collective-permute-done.4.other_ref = bf16[8,80,384]{2,1,0:T(8,128)(2,1)S(1)} collective-permute-done((bf16[8,80,384]{2,1,0:T(8,128)(2,1)S(1)}, bf16[8,80,384]{2,1,0:T(8,128)(2,1)S(1)}, u32[]{:S(2)}, u32[]{:S(2)}) %collective-permute-start.4) | collective-permute-done | bytes 491552 | tf_op jit(solution)/shard_map/ppermute | solution.py:511
  25.2 1.7 %collective-permute-start.5 = (bf16[2,224,384]{2,1,0:T(8,128)(2,1)S(1)}, bf16[2,224,384]{2,1,0:T(8,128)(2,1)S(1)}, u32[]{:S(2)}, u32[]{:S(2)}) collective-permute-start(bf16[2,224,384]{2,1,0:T(8,128)(2,1)S(1)} %pad_maximum_fusion.3), channel_id=1, source_target_pairs={{0,2},{1,3},{2,0},{3,1},{4,6},{5,7},{6,4},{7,5},{8,12},{9,13},{10,... | collective-permute-start | bytes 1032200 | tf_op jit(solution)/shard_map/ppermute | solution.py:511
  27.0 8.7 %attn_fwd_first.1 = (bf16[4,1152,384]{2,1,0:T(8,128)(2,1)S(1)}, bf16[4,6,384,384]{3,2,1,0:T(8,128)(2,1)S(1)}, f32[4,8,384]{2,1,0:T(8,128)S(1)}, bf16[4,384,384]{...) custom-call(bf16[8,80,384]{2,1,0:T(8,128)(2,1)S(1)} %pad_maximum_fus, ...), custom_call_target="tpu_custom_call" | custom-call | flops 8000000000 | bytes 1048576 | tf_op jit(solution)/shard_map/attn_fwd_first/pallas_call | solution.py:230
  35.7 0.5 collective-permute-done.5
  36.2 0.1 pad_maximum_fusion.1
  36.2 1.9 %collective-permute-start.6 = (bf16[4,224,384]{2,1,0:T(8,128)(2,1)S(1)}, bf16[4,224,384]{2,1,0:T(8,128)(2,1)S(1)}, u32[]{:S(2)}, u32[]{:S(2)}) collective-permute-start(bf16[4,224,384]{2,1,0:T(8,128)(2,1)S(1)} %pad_maximum_fusion.1), channel_id=1, source_target_pairs={{0,1},{1,0},{2,3},{3,2},{4,5},{5,4},{6,7},{7,6},{8,10},{9,11},{10,... | collective-permute-start | bytes 2064392 | tf_op jit(solution)/shard_map/ppermute | solution.py:511
  38.2 6.5 %attn_fwd_rest.1 = (bf16[4,1152,384]{2,1,0:T(8,128)(2,1)S(1)}, bf16[4,6,384,384]{3,2,1,0:T(8,128)(2,1)S(1)}, f32[4,8,384]{2,1,0:T(8,128)S(1)}, bf16[4,384,384]{2,1,0:T(8,128)(2,1)S(1)}, bf16[4,384,384]{2,1,0:T(8,128)(2,1)S(1)}) custom-call(f32[4,384,384]{2,1,0:T(8,128)S(1)} %copy-done.6, ...), custom_call_target="tpu_custom_call", output_to_operand_aliasing={{0}: (4, {}), {1}: (5, {}), {2}: (6, {}), {3}: (7, {}), {4}... | custom-call | flops 8000000000 | bytes 1048576 | tf_op jit(solution)/shard_map/attn_fwd_rest/pallas_call | solution.py:242
  44.7 0.0 copy-start.5
  44.7 2.5 %collective-permute-done.6 = bf16[4,224,384]{2,1,0:T(8,128)(2,1)S(1)} collective-permute-done((bf16[4,224,384]{2,1,0:T(8,128)(2,1)S(1)}, bf16[4,224,384]{2,1,0:T(8,128)(2,1)S(1)}, u32[]{:S(2)}, u32[]{:S(2)}) %collective-permute-start.6) | collective-permute-done | bytes 688160 | tf_op jit(solution)/shard_map/ppermute | solution.py:511
  47.2 0.2 pad_maximum_fusion.mine_ref
  47.4 1.1 collective-permute-start.7
  48.5 2.8 %collective-permute-done.7.other_ref = bf16[8,224,384]{2,1,0:T(8,128)(2,1)S(1)} collective-permute-done((bf16[8,224,384]{2,1,0:T(8,128)(2,1)S(1)}, bf16[8,224,384]{2,1,0:T(8,128)(2,1)S(1)}, u32[]{:S(2)}, u32[]{:S(2)}) %collective-permute-start.7) | collective-permute-done | bytes 1376288 | tf_op jit(solution)/shard_map/ppermute | solution.py:511
  51.3 26.3 %mlp.1 = (f32[4,384,384]{2,1,0:T(8,128)}, bf16[4,384,1536]{2,1,0:T(8,128)(2,1)}, f32[4,384,384]{2,1,0:T(8,128)}, bf16[4,384,384]{2,1,0:T(8,128)(2,1)S(1)}, bf16[...) custom-call(bf16[8,224,384]{2,1,0:T(8,128)(2,1)S(1)} %pad_maximum_fusio, ...), custom_call_target="tpu_custom_call" | custom-call | flops 24000000000 | bytes 1048576 | tf_op jit(solution)/shard_map/mlp/pallas_call | solution.py:316
  77.6 0.7 collective-permute-start.8
  78.2 2.8 %collective-permute-done.8 = bf16[8,224,384]{2,1,0:T(8,128)(2,1)S(1)} collective-permute-done((bf16[8,224,384]{2,1,0:T(8,128)(2,1)S(1)}, bf16[8,224,384]{2,1,0:T(8,128)(2,1)S(1)}, u32[]{:S(2)}, u32[]{:S(2)}) %collective-permute-start.8) | collective-permute-done | bytes 1376288 | tf_op jit(solution)/shard_map/ppermute | solution.py:511
  81.0 2.0 %convert_add_fusion = f32[8,224,384]{2,1,0:T(8,128)S(1)} fusion(f32[8,224,384]{2,1,0:T(8,128)} %get-tuple-element.125, bf16[8,224,384]{2,1,0:T(8,128)(2,1)S(1)} %collective-permute-done.8), kind=kLoop, calls=%fused_computation | loop fusion | flops 1376256 | bytes 6881280 | tf_op jit(solution)/shard_map/add | solution.py:585
  83.0 0.1 slice.80
  83.1 1.6 %collective-permute-start.9 = (bf16[4,224,384]{2,1,0:T(8,128)(2,1)S(1)}, bf16[4,224,384]{2,1,0:T(8,128)(2,1)S(1)}, u32[]{:S(2)}, u32[]{:S(2)}) collective-permute-start(bf16[4,224,384]{2,1,0:T(8,128)(2,1)S(1)} %slice.80), channel_id=1, source_target_pairs={{0,1},{1,0},{2,3},{3,2},{4,5},{5,4},{6,7},{7,6},{8,10},{9,11},{10,... | collective-permute-start | bytes 2064392 | tf_op jit(solution)/shard_map/ppermute | solution.py:511
  84.7 7.0 %attn_bwd_first.1 = (bf16[4,1152,384]{2,1,0:T(8,128)(2,1)S(1)}, f32[1152,512]{1,0:T(8,128)S(1)}) custom-call(bf16[4,1152,384]{2,1,0:T(8,128)(2,1)S(1)} %get-tuple-element.121.jt_ref, bf16[4,6,384,384]{3,2,1,0:T(8,128)(2,1)S(1)} %get-tuple-element.122.e_ref, f32[4,8,384]{2,1,0:T(8,128)S(1)} %get-tuple-element.123.il_ref, ...), custom_call_target="tpu_custom_call" | custom-call | flops 8000000000 | bytes 1048576 | tf_op jit(solution)/shard_map/attn_bwd_first/pallas_call | solution.py:388
  91.6 2.5 %collective-permute-done.9 = bf16[4,224,384]{2,1,0:T(8,128)(2,1)S(1)} collective-permute-done((bf16[4,224,384]{2,1,0:T(8,128)(2,1)S(1)}, bf16[4,224,384]{2,1,0:T(8,128)(2,1)S(1)}, u32[]{:S(2)}, u32[]{:S(2)}) %collective-permute-start.9) | collective-permute-done | bytes 688160 | tf_op jit(solution)/shard_map/ppermute | solution.py:511
  94.1 0.1 slice_add_fusion
  94.3 1.8 %collective-permute-start.16 = (bf16[2,224,384]{2,1,0:T(8,128)(2,1)S(1)}, bf16[2,224,384]{2,1,0:T(8,128)(2,1)S(1)}, u32[]{:S(2)}, u32[]{:S(2)}) collective-permute-start(bf16[2,224,384]{2,1,0:T(8,128)(2,1)S(1)} %slice.81), channel_id=1, source_target_pairs={{0,2},{1,3},{2,0},{3,1},{4,6},{5,7},{6,4},{7,5},{8,12},{9,13},{10,... | collective-permute-start | bytes 1032200 | tf_op jit(solution)/shard_map/ppermute | solution.py:511
  96.1 7.6 %attn_bwd_last.1 = (bf16[4,1152,384]{2,1,0:T(8,128)(2,1)S(1)}, f32[8,80,384]{2,1,0:T(8,128)S(1)}, bf16[8,80,384]{2,1,0:T(8,128)(2,1)S(1)}) custom-call(bf16[4,1152,384]{2,1,0:T(8,128)(2,1)S(1)} %copy-done.21, bf16[4,6,384,384]{3,2,1,0:T(8,128)(2,1)S(1)} %get-tuple-element.122.e_ref, ...), custom_call_target="tpu_custom_call", output_to_operand_aliasing={{0}: (10, {})} | custom-call | flops 10000000000 | bytes 1048576 | tf_op jit(solution)/shard_map/attn_bwd_last/pallas_call | solution.py:398
  103.7 0.0 copy-start.17
  103.7 1.3 collective-permute-start.10
  105.0 0.1 convert_add_fusion.2
  105.1 3.0 %collective-permute-start.17 = (bf16[1,224,384]{2,1,0:T(8,128)(2,1)S(1)}, bf16[1,224,384]{2,1,0:T(8,128)(2,1)S(1)}, u32[]{:S(2)}, u32[]{:S(2)}) collective-permute-start(bf16[1,224,384]{2,1,0:T(8,128)(2,1)S(1)} %slice.83), channel_id=1, source_target_pairs={{0,4},{1,5},{2,6},{3,7},{4,0},{5,1},{6,2},{7,3},{8,9},{9,8},{10,11... | collective-permute-start | bytes 516104 | tf_op jit(solution)/shard_map/ppermute | solution.py:511
  108.1 0.1 convert_add_fusion.1
  108.3 1.6 %collective-permute-start.11 = (bf16[4,80,384]{2,1,0:T(8,128)(2,1)S(1)}, bf16[4,80,384]{2,1,0:T(8,128)(2,1)S(1)}, u32[]{:S(2)}, u32[]{:S(2)}) collective-permute-start(bf16[4,80,384]{2,1,0:T(8,128)(2,1)S(1)} %slice.82), channel_id=1, source_target_pairs={{0,1},{1,0},{2,3},{3,2},{4,5},{5,4},{6,7},{7,6},{8,10},{9,11},{10,... | collective-permute-start | bytes 737288 | tf_op jit(solution)/shard_map/ppermute | solution.py:511
  109.8 4.3 %input_end.1 = f32[4,384,384]{2,1,0:T(8,128)} custom-call(f32[4,384,384]{2,1,0:T(8,128)S(1)} %copy-done.6, f32[4,384,384]{2,1,0:T(8,128)S(1)} %copy-done.17, bf16[4,1152,384]{2,1,0:T(8,128)(2,1)S(1)} %get-tuple-element.136.dj_ref, bf16[1152,384]{1,0:T(8,128)(2,1)S(1)} %get-tuple-element.101.w_ref, f32[16,384]{1,0:T(8,128)S(1)} %get-tuple-element.102.vrow_ref), custom_call_target="tpu_custom_call" | custom-call | flops 4000000000 | bytes 1048576 | tf_op jit(solution)/shard_map/input_end/pallas_call | solution.py:432
  114.2 1.6 %collective-permute-start.18 = (bf16[224,384]{1,0:T(8,128)(2,1)S(1)}, bf16[224,384]{1,0:T(8,128)(2,1)S(1)}, u32[]{:S(2)}, u32[]{:S(2)}) collective-permute-start(bf16[224,384]{1,0:T(8,128)(2,1)S(1)} %fusion.1), channel_id=1, source_target_pairs={{0,16},{1,17},{2,18},{3,19},{4,20},{5,21},{6,22},{7,23},{8,24},{9,... | collective-permute-start | bytes 516104 | tf_op jit(solution)/shard_map/ppermute | solution.py:511
  115.8 2.5 %collective-permute-start.12 = (bf16[2,80,384]{2,1,0:T(8,128)(2,1)S(1)}, bf16[2,80,384]{2,1,0:T(8,128)(2,1)S(1)}, u32[]{:S(2)}, u32[]{:S(2)}) collective-permute-start(bf16[2,80,384]{2,1,0:T(8,128)(2,1)S(1)} %slice.84), channel_id=1, source_target_pairs={{0,2},{1,3},{2,0},{3,1},{4,6},{5,7},{6,4},{7,5},{8,12},{9,13},{10,... | collective-permute-start | bytes 368648 | tf_op jit(solution)/shard_map/ppermute | solution.py:511
  118.4 0.0 copy-start
  118.4 0.0 copy-start.1
  118.4 0.0 copy-start.3
  118.4 0.0 copy-start.7
  118.4 0.0 copy-start.8
  118.4 0.0 copy-start.10
  118.4 0.0 copy-start.13
  118.5 4.1 %layer_end.1 = f32[4,384,384]{2,1,0:T(8,128)} custom-call(f32[4,384,384]{2,1,0:T(8,128)S(1)} %copy-done.18, bf16[4,384,1536]{2,1,0:T(8,128)(2,1)S(1)} %bitcast.7, bf16[384,1536]{1,0:T(8,128)(2,1)S(1)} %copy-done.19, f32[16,384]{1,0:T(8,128)S(1)} %get-tuple-element.102.vrow_ref), custom_call_target="tpu_custom_call" | custom-call | flops 4000000000 | bytes 1048576 | tf_op jit(solution)/shard_map/layer_end/pallas_call | solution.py:414
  122.6 1.8 %collective-permute-start.13 = (bf16[1,80,384]{2,1,0:T(8,128)(2,1)S(1)}, bf16[1,80,384]{2,1,0:T(8,128)(2,1)S(1)}, u32[]{:S(2)}, u32[]{:S(2)}) collective-permute-start(bf16[1,80,384]{2,1,0:T(8,128)(2,1)S(1)} %slice.85), channel_id=1, source_target_pairs={{0,4},{1,5},{2,6},{3,7},{4,0},{5,1},{6,2},{7,3},{8,9},{9,8},{10,11... | collective-permute-start | bytes 184328 | tf_op jit(solution)/shard_map/ppermute | solution.py:511
  124.4 0.1 collective-permute-start.19
  124.5 3.9 %collective-permute-done.13 = bf16[1,80,384]{2,1,0:T(8,128)(2,1)S(1)} collective-permute-done((bf16[1,80,384]{2,1,0:T(8,128)(2,1)S(1)}, bf16[1,80,384]{2,1,0:T(8,128)(2,1)S(1)}, u32[]{:S(2)}, u32[]{:S(2)}) %collective-permute-start.13) | collective-permute-done | bytes 61472 | tf_op jit(solution)/shard_map/ppermute | solution.py:511
  128.5 0.6 collective-permute-start.14
  129.0 3.7 %collective-permute-done.14 = bf16[80,384]{1,0:T(8,128)(2,1)S(1)} collective-permute-done((bf16[80,384]{1,0:T(8,128)(2,1)S(1)}, bf16[80,384]{1,0:T(8,128)(2,1)S(1)}, u32[]{:S(2)}, u32[]{:S(2)}) %collective-permute-start.14) | collective-permute-done | bytes 61472 | tf_op jit(solution)/shard_map/ppermute | solution.py:511
  132.8 0.0 copy-start.11
  132.8 0.0 copy-start.12
  132.8 0.0 copy-start.16
  132.8 0.1 collective-permute-start.15
  133.0 1.9 %adam.3 = (f32[48,384]{1,0:T(8,128)}, f32[48,384]{1,0:T(8,128)}, f32[48,384]{1,0:T(8,128)}, bf16[48,384]{1,0:T(8,128)(2,1)}, f32[192,384]{1,0:T(8,128)}, /*index...) custom-call(f32[224,384]{1,0:T(8,128)S(1)} %convert_add_fusion.4.min, ...), custom_call_target="tpu_custom_call" | custom-call | flops 3000000000 | bytes 1048576 | tf_op jit(solution)/shard_map/adam/pallas_call | solution.py:483
  135.0 1.2 adam.2
  (57 shorter events, 0.4 us)
Async XLA Ops:
  0.7 26.3 %copy-start.6 = (f32[4,384,384]{2,1,0:T(8,128)S(1)}, f32[4,384,384]{2,1,0:T(8,128)}, u32[]{:S(2)}) copy-start(f32[4,384,384]{2,1,0:T(8,128)} %x_ref.7) | copy-start | bytes 7077892
  2.8 6.5 %collective-permute-start = (bf16[1,80,384]{2,1,0:T(8,128)(2,1)}, bf16[1,80,384]{2,1,0:T(8,128)(2,1)S(1)}, u32[]{:S(2)}, u32[]{:S(2)}) collective-permute-start(bf16[1,80,384]{2,1,0:T(8,128)(2,1)} %bitcast.8), channel_id=1, source_target_pairs={{0,4},{1,5},{2,6},{3,7},{4,0},{5,1},{6,2},{7,3},{8,9},{9,8},{10,11... | collective-permute-start | bytes 184328 | tf_op jit(solution)/shard_map/ppermute | solution.py:511
  10.2 5.1 %collective-permute-start.1 = (bf16[2,80,384]{2,1,0:T(8,128)(2,1)S(1)}, bf16[2,80,384]{2,1,0:T(8,128)(2,1)S(1)}, u32[]{:S(2)}, u32[]{:S(2)}) collective-permute-start(bf16[2,80,384]{2,1,0:T(8,128)(2,1)S(1)} %pad_maximum_fusion.5), channel_id=1, source_target_pairs={{0,2},{1,3},{2,0},{3,1},{4,6},{5,7},{6,4},{7,5},{8,12},{9,13},{10,... | collective-permute-start | bytes 368648 | tf_op jit(solution)/shard_map/ppermute | solution.py:511
  12.1 8.7 %collective-permute-start.3 = (bf16[1,224,384]{2,1,0:T(8,128)(2,1)}, bf16[1,224,384]{2,1,0:T(8,128)(2,1)S(1)}, u32[]{:S(2)}, u32[]{:S(2)}) collective-permute-start(bf16[1,224,384]{2,1,0:T(8,128)(2,1)} %bitcast.12), channel_id=1, source_target_pairs={{0,4},{1,5},{2,6},{3,7},{4,0},{5,1},{6,2},{7,3},{8,9},{9,8},{10,11... | collective-permute-start | bytes 516104 | tf_op jit(solution)/shard_map/ppermute | solution.py:511
  16.1 6.3 %collective-permute-start.2 = (bf16[4,80,384]{2,1,0:T(8,128)(2,1)S(1)}, bf16[4,80,384]{2,1,0:T(8,128)(2,1)S(1)}, u32[]{:S(2)}, u32[]{:S(2)}) collective-permute-start(bf16[4,80,384]{2,1,0:T(8,128)(2,1)S(1)} %pad_maximum_fusion.4), channel_id=1, source_target_pairs={{0,1},{1,0},{2,3},{3,2},{4,5},{5,4},{6,7},{7,6},{8,10},{9,11},{10,... | collective-permute-start | bytes 737288 | tf_op jit(solution)/shard_map/ppermute | solution.py:511
  23.3 1.9 %collective-permute-start.4 = (bf16[8,80,384]{2,1,0:T(8,128)(2,1)S(1)}, bf16[8,80,384]{2,1,0:T(8,128)(2,1)S(1)}, u32[]{:S(2)}, u32[]{:S(2)}) collective-permute-start(bf16[8,80,384]{2,1,0:T(8,128)(2,1)S(1)} %pad_maximum_fusion.2.mine_ref), channel_id=1, source_target_pairs={{0,8},{1,9},{2,10},{3,11},{4,12},{5,13},{6,14},{7,15},{8,0},{9,1},... | collective-permute-start | bytes 1474568 | tf_op jit(solution)/shard_map/ppermute | solution.py:511
  25.2 10.9 %collective-permute-start.5 = (bf16[2,224,384]{2,1,0:T(8,128)(2,1)S(1)}, bf16[2,224,384]{2,1,0:T(8,128)(2,1)S(1)}, u32[]{:S(2)}, u32[]{:S(2)}) collective-permute-start(bf16[2,224,384]{2,1,0:T(8,128)(2,1)S(1)} %pad_maximum_fusion.3), channel_id=1, source_target_pairs={{0,2},{1,3},{2,0},{3,1},{4,6},{5,7},{6,4},{7,5},{8,12},{9,13},{10,... | collective-permute-start | bytes 1032200 | tf_op jit(solution)/shard_map/ppermute | solution.py:511
  36.2 11.0 %collective-permute-start.6 = (bf16[4,224,384]{2,1,0:T(8,128)(2,1)S(1)}, bf16[4,224,384]{2,1,0:T(8,128)(2,1)S(1)}, u32[]{:S(2)}, u32[]{:S(2)}) collective-permute-start(bf16[4,224,384]{2,1,0:T(8,128)(2,1)S(1)} %pad_maximum_fusion.1), channel_id=1, source_target_pairs={{0,1},{1,0},{2,3},{3,2},{4,5},{5,4},{6,7},{7,6},{8,10},{9,11},{10,... | collective-permute-start | bytes 2064392 | tf_op jit(solution)/shard_map/ppermute | solution.py:511
  44.7 40.0 %copy-start.20 = (bf16[4,1152,384]{2,1,0:T(8,128)(2,1)}, bf16[4,1152,384]{2,1,0:T(8,128)(2,1)S(1)}, u32[]{:S(2)}) copy-start(bf16[4,1152,384]{2,1,0:T(8,128)(2,1)S(1)} %get-tuple-element.121.jt_ref) | copy-start | bytes 10616836
  44.7 6.6 %copy-start.5 = (f32[4,384,384]{2,1,0:T(8,128)S(1)}, f32[4,384,384]{2,1,0:T(8,128)}, u32[]{:S(2)}) copy-start(f32[4,384,384]{2,1,0:T(8,128)} %cot_ref.1) | copy-start | bytes 7077892
  47.4 3.9 %collective-permute-start.7 = (bf16[8,224,384]{2,1,0:T(8,128)(2,1)S(1)}, bf16[8,224,384]{2,1,0:T(8,128)(2,1)S(1)}, u32[]{:S(2)}, u32[]{:S(2)}) collective-permute-start(bf16[8,224,384]{2,1,0:T(8,128)(2,1)S(1)} %pad_maximum_fusion.mine_ref), channel_id=1, source_target_pairs={{0,8},{1,9},{2,10},{3,11},{4,12},{5,13},{6,14},{7,15},{8,0},{9,1},... | collective-permute-start | bytes 4128776 | tf_op jit(solution)/shard_map/ppermute | solution.py:511
  77.6 3.4 %collective-permute-start.8 = (bf16[8,224,384]{2,1,0:T(8,128)(2,1)S(1)}, bf16[8,224,384]{2,1,0:T(8,128)(2,1)S(1)}, u32[]{:S(2)}, u32[]{:S(2)}) collective-permute-start(bf16[8,224,384]{2,1,0:T(8,128)(2,1)S(1)} %get-tuple-element.126), channel_id=1, source_target_pairs={{0,8},{1,9},{2,10},{3,11},{4,12},{5,13},{6,14},{7,15},{8,0},{9,1},... | collective-permute-start | bytes 4128776 | tf_op jit(solution)/shard_map/ppermute | solution.py:511
  83.1 11.0 %collective-permute-start.9 = (bf16[4,224,384]{2,1,0:T(8,128)(2,1)S(1)}, bf16[4,224,384]{2,1,0:T(8,128)(2,1)S(1)}, u32[]{:S(2)}, u32[]{:S(2)}) collective-permute-start(bf16[4,224,384]{2,1,0:T(8,128)(2,1)S(1)} %slice.80), channel_id=1, source_target_pairs={{0,1},{1,0},{2,3},{3,2},{4,5},{5,4},{6,7},{7,6},{8,10},{9,11},{10,... | collective-permute-start | bytes 2064392 | tf_op jit(solution)/shard_map/ppermute | solution.py:511
  91.6 4.5 %copy-start.21 = (bf16[4,1152,384]{2,1,0:T(8,128)(2,1)S(1)}, bf16[4,1152,384]{2,1,0:T(8,128)(2,1)}, u32[]{:S(2)}) copy-start(bf16[4,1152,384]{2,1,0:T(8,128)(2,1)} %copy-done.20) | copy-start | bytes 10616836
  94.3 10.7 %collective-permute-start.16 = (bf16[2,224,384]{2,1,0:T(8,128)(2,1)S(1)}, bf16[2,224,384]{2,1,0:T(8,128)(2,1)S(1)}, u32[]{:S(2)}, u32[]{:S(2)}) collective-permute-start(bf16[2,224,384]{2,1,0:T(8,128)(2,1)S(1)} %slice.81), channel_id=1, source_target_pairs={{0,2},{1,3},{2,0},{3,1},{4,6},{5,7},{6,4},{7,5},{8,12},{9,13},{10,... | collective-permute-start | bytes 1032200 | tf_op jit(solution)/shard_map/ppermute | solution.py:511
  103.7 6.1 %copy-start.17 = (f32[4,384,384]{2,1,0:T(8,128)S(1)}, f32[4,384,384]{2,1,0:T(8,128)}, u32[]{:S(2)}) copy-start(f32[4,384,384]{2,1,0:T(8,128)} %get-tuple-element.120.dm_ref) | copy-start | bytes 7077892
  103.7 4.4 %collective-permute-start.10 = (bf16[8,80,384]{2,1,0:T(8,128)(2,1)S(1)}, bf16[8,80,384]{2,1,0:T(8,128)(2,1)S(1)}, u32[]{:S(2)}, u32[]{:S(2)}) collective-permute-start(bf16[8,80,384]{2,1,0:T(8,128)(2,1)S(1)} %get-tuple-element.135), channel_id=1, source_target_pairs={{0,8},{1,9},{2,10},{3,11},{4,12},{5,13},{6,14},{7,15},{8,0},{9,1},... | collective-permute-start | bytes 1474568 | tf_op jit(solution)/shard_map/ppermute | solution.py:511
  105.1 9.0 %collective-permute-start.17 = (bf16[1,224,384]{2,1,0:T(8,128)(2,1)S(1)}, bf16[1,224,384]{2,1,0:T(8,128)(2,1)S(1)}, u32[]{:S(2)}, u32[]{:S(2)}) collective-permute-start(bf16[1,224,384]{2,1,0:T(8,128)(2,1)S(1)} %slice.83), channel_id=1, source_target_pairs={{0,4},{1,5},{2,6},{3,7},{4,0},{5,1},{6,2},{7,3},{8,9},{9,8},{10,11... | collective-permute-start | bytes 516104 | tf_op jit(solution)/shard_map/ppermute | solution.py:511
  108.1 10.2 %slice-start = ((s8[4718592]{0:T(1024)(128)(4,1)}), s8[4194304]{0:T(1024)(128)(4,1)S(1)}, s32[]{:S(2)}) async-start(s8[4718592]{0:T(1024)(128)(4,1)} %bitcast.6), calls=%async_computation | async-start | bytes 8388608
  108.3 7.5 %collective-permute-start.11 = (bf16[4,80,384]{2,1,0:T(8,128)(2,1)S(1)}, bf16[4,80,384]{2,1,0:T(8,128)(2,1)S(1)}, u32[]{:S(2)}, u32[]{:S(2)}) collective-permute-start(bf16[4,80,384]{2,1,0:T(8,128)(2,1)S(1)} %slice.82), channel_id=1, source_target_pairs={{0,1},{1,0},{2,3},{3,2},{4,5},{5,4},{6,7},{7,6},{8,10},{9,11},{10,... | collective-permute-start | bytes 737288 | tf_op jit(solution)/shard_map/ppermute | solution.py:511
  109.8 8.5 %slice-start.1 = ((s8[4718592]{0:T(1024)(128)(4,1)}), s8[524288]{0:T(1024)(128)(4,1)S(1)}, s32[]{:S(2)}) async-start(s8[4718592]{0:T(1024)(128)(4,1)} %bitcast.6), calls=%async_computation.1 | async-start | bytes 1048576
  109.8 8.5 %copy-start.18 = (f32[4,384,384]{2,1,0:T(8,128)S(1)}, f32[4,384,384]{2,1,0:T(8,128)}, u32[]{:S(2)}) copy-start(f32[4,384,384]{2,1,0:T(8,128)} %get-tuple-element.139.mid_ref) | copy-start | bytes 7077892
  109.8 8.5 %copy-start.19 = (bf16[384,1536]{1,0:T(8,128)(2,1)S(1)}, bf16[384,1536]{1,0:T(8,128)(2,1)}, u32[]{:S(2)}) copy-start(bf16[384,1536]{1,0:T(8,128)(2,1)} %get-tuple-element.141.wd_ref) | copy-start | bytes 3538948
  114.2 10.2 %collective-permute-start.18 = (bf16[224,384]{1,0:T(8,128)(2,1)S(1)}, bf16[224,384]{1,0:T(8,128)(2,1)S(1)}, u32[]{:S(2)}, u32[]{:S(2)}) collective-permute-start(bf16[224,384]{1,0:T(8,128)(2,1)S(1)} %fusion.1), channel_id=1, source_target_pairs={{0,16},{1,17},{2,18},{3,19},{4,20},{5,21},{6,22},{7,23},{8,24},{9,... | collective-permute-start | bytes 516104 | tf_op jit(solution)/shard_map/ppermute | solution.py:511
  115.8 6.7 %collective-permute-start.12 = (bf16[2,80,384]{2,1,0:T(8,128)(2,1)S(1)}, bf16[2,80,384]{2,1,0:T(8,128)(2,1)S(1)}, u32[]{:S(2)}, u32[]{:S(2)}) collective-permute-start(bf16[2,80,384]{2,1,0:T(8,128)(2,1)S(1)} %slice.84), channel_id=1, source_target_pairs={{0,2},{1,3},{2,0},{3,1},{4,6},{5,7},{6,4},{7,5},{8,12},{9,13},{10,... | collective-permute-start | bytes 368648 | tf_op jit(solution)/shard_map/ppermute | solution.py:511
  118.4 14.6 %copy-start = (f32[192,384]{1,0:T(8,128)S(1)}, f32[192,384]{1,0:T(8,128)}, u32[]{:S(2)}) copy-start(f32[192,384]{1,0:T(8,128)} %refs_3_.3) | copy-start | bytes 884740
  118.4 14.6 %copy-start.1 = (f32[48,1536]{1,0:T(8,128)S(1)}, f32[48,1536]{1,0:T(8,128)}, u32[]{:S(2)}) copy-start(f32[48,1536]{1,0:T(8,128)} %refs_6_.1) | copy-start | bytes 884740
  118.4 14.6 %copy-start.3 = (f32[48,384]{1,0:T(8,128)S(1)}, f32[48,384]{1,0:T(8,128)}, u32[]{:S(2)}) copy-start(f32[48,384]{1,0:T(8,128)} %refs_0_.3) | copy-start | bytes 221188
  118.4 14.6 %copy-start.7 = (f32[192,384]{1,0:T(8,128)S(1)}, f32[192,384]{1,0:T(8,128)}, u32[]{:S(2)}) copy-start(f32[192,384]{1,0:T(8,128)} %refs_4_.3) | copy-start | bytes 884740
  118.4 14.6 %copy-start.8 = (f32[192,384]{1,0:T(8,128)S(1)}, f32[192,384]{1,0:T(8,128)}, u32[]{:S(2)}) copy-start(f32[192,384]{1,0:T(8,128)} %refs_5_.3) | copy-start | bytes 884740
  118.4 14.6 %copy-start.9 = (f32[48,1536]{1,0:T(8,128)S(1)}, f32[48,1536]{1,0:T(8,128)}, u32[]{:S(2)}) copy-start(f32[48,1536]{1,0:T(8,128)} %refs_7_.1) | copy-start | bytes 884740
  118.4 14.6 %copy-start.10 = (f32[48,1536]{1,0:T(8,128)S(1)}, f32[48,1536]{1,0:T(8,128)}, u32[]{:S(2)}) copy-start(f32[48,1536]{1,0:T(8,128)} %refs_8_.1) | copy-start | bytes 884740
  118.4 14.6 %copy-start.13 = (f32[48,384]{1,0:T(8,128)S(1)}, f32[48,384]{1,0:T(8,128)}, u32[]{:S(2)}) copy-start(f32[48,384]{1,0:T(8,128)} %refs_1_.3) | copy-start | bytes 221188
  118.5 14.6 %copy-start.14 = (f32[48,384]{1,0:T(8,128)S(1)}, f32[48,384]{1,0:T(8,128)}, u32[]{:S(2)}) copy-start(f32[48,384]{1,0:T(8,128)} %refs_2_.3) | copy-start | bytes 221188
  122.6 5.8 %collective-permute-start.13 = (bf16[1,80,384]{2,1,0:T(8,128)(2,1)S(1)}, bf16[1,80,384]{2,1,0:T(8,128)(2,1)S(1)}, u32[]{:S(2)}, u32[]{:S(2)}) collective-permute-start(bf16[1,80,384]{2,1,0:T(8,128)(2,1)S(1)} %slice.85), channel_id=1, source_target_pairs={{0,4},{1,5},{2,6},{3,7},{4,0},{5,1},{6,2},{7,3},{8,9},{9,8},{10,11... | collective-permute-start | bytes 184328 | tf_op jit(solution)/shard_map/ppermute | solution.py:511
  124.4 8.5 %collective-permute-start.19 = (f32[224,384]{1,0:T(8,128)S(1)}, f32[224,384]{1,0:T(8,128)S(1)}, u32[]{:S(2)}, u32[]{:S(2)}) collective-permute-start(f32[224,384]{1,0:T(8,128)S(1)} %convert_add_fusion.4.mine_ref), channel_id=1, source_target_pairs={{0,8},{1,9},{2,10},{3,11},{4,12},{5,13},{6,14},{7,15},{8,0},{9,1},... | collective-permute-start | bytes 1032200 | tf_op jit(solution)/shard_map/ppermute | solution.py:511
  128.5 4.3 %collective-permute-start.14 = (bf16[80,384]{1,0:T(8,128)(2,1)S(1)}, bf16[80,384]{1,0:T(8,128)(2,1)S(1)}, u32[]{:S(2)}, u32[]{:S(2)}) collective-permute-start(bf16[80,384]{1,0:T(8,128)(2,1)S(1)} %fusion.2), channel_id=1, source_target_pairs={{0,16},{1,17},{2,18},{3,19},{4,20},{5,21},{6,22},{7,23},{8,24},{9,... | collective-permute-start | bytes 184328 | tf_op jit(solution)/shard_map/ppermute | solution.py:511
  132.8 2.2 %copy-start.2 = (f32[144,384]{1,0:T(8,128)S(1)}, f32[144,384]{1,0:T(8,128)}, u32[]{:S(2)}) copy-start(f32[144,384]{1,0:T(8,128)} %refs_0_.2) | copy-start | bytes 663556
  132.8 2.2 %copy-start.4 = (f32[576]{0:T(1024)S(1)}, f32[576]{0:T(1024)}, u32[]{:S(2)}) copy-start(f32[576]{0:T(1024)} %refs_3_.2) | copy-start | bytes 6916
  132.8 2.2 %copy-start.11 = (f32[144,384]{1,0:T(8,128)S(1)}, f32[144,384]{1,0:T(8,128)}, u32[]{:S(2)}) copy-start(f32[144,384]{1,0:T(8,128)} %refs_1_.2) | copy-start | bytes 663556
  132.8 2.2 %copy-start.12 = (f32[144,384]{1,0:T(8,128)S(1)}, f32[144,384]{1,0:T(8,128)}, u32[]{:S(2)}) copy-start(f32[144,384]{1,0:T(8,128)} %refs_2_.2) | copy-start | bytes 663556
  132.8 2.2 %copy-start.15 = (f32[576]{0:T(1024)S(1)}, f32[576]{0:T(1024)}, u32[]{:S(2)}) copy-start(f32[576]{0:T(1024)} %refs_4_.2) | copy-start | bytes 6916
  132.8 2.2 %copy-start.16 = (f32[576]{0:T(1024)S(1)}, f32[576]{0:T(1024)}, u32[]{:S(2)}) copy-start(f32[576]{0:T(1024)} %refs_5_.2) | copy-start | bytes 6916
  132.8 2.1 %collective-permute-start.15 = (f32[80,384]{1,0:T(8,128)S(1)}, f32[80,384]{1,0:T(8,128)S(1)}, u32[]{:S(2)}, u32[]{:S(2)}) collective-permute-start(f32[80,384]{1,0:T(8,128)S(1)} %convert_add_fusion.6.mine_ref), channel_id=1, source_target_pairs={{0,8},{1,9},{2,10},{3,11},{4,12},{5,13},{6,14},{7,15},{8,0},{9,1},... | collective-permute-start | bytes 368648 | tf_op jit(solution)/shard_map/ppermute | solution.py:511

commit v4 on v3

--- a/solution.py
+++ b/solution.py
@@ -11,7 +11,7 @@
 HEADS = 6
 EPS = 1e-6
 OWNERS = 8
-MLP_MIB = 26
+MLP_MIB = 27
 beta_first = 0.5
 beta_second = 0.5
 adam_eps = 1e-08
@@ -177,11 +177,15 @@
     hs = d // HEADS
     jt = dot(w_ref[...], h, 1, 1) + vcol_ref[:, 0:1]
     jt_ref[0] = jt.astype(bf16)
+    def part(k, i):
+        return jt_ref[0, k * d + i * hs:k * d + (i + 1) * hs, :]
+
+    def scores(i):
+        return dot(part(1, i) * 0.125, part(0, i), 0, 0)
+
+    st = scores(0)
     for i in range(HEADS):
-        qt = jt_ref[0, i * hs:(i + 1) * hs, :]
-        kt = jt_ref[0, d + i * hs:d + (i + 1) * hs, :]
-        vt = jt_ref[0, 2 * d + i * hs:2 * d + (i + 1) * hs, :]
-        st = dot((kt * 0.125), qt, 0, 0)
+        later = scores(i + 1) if i + 1 < HEADS else None
         m = jnp.max(st, axis=0, keepdims=True)
         e = jnp.exp(st - m)
         l = jnp.sum(e, axis=0, keepdims=True)
@@ -189,8 +193,8 @@
         e_ref[0, i] = eb
         il = 1.0 / l
         il_ref[0, i:i + 1, :] = il
-        ot = dot(vt, eb, 1, 0) * il
-        ot_ref[0, i * hs:(i + 1) * hs, :] = ot.astype(bf16)
+        ot_ref[0, i * hs:(i + 1) * hs, :] = (dot(part(2, i), eb, 1, 0) * il).astype(bf16)
+        st = later
 
 
 def attn_fwd_first(lay, mine_ref, other_ref, x_ref, jt_ref, e_ref, il_ref, ot_ref, h_ref, w_ref, vrow_ref, vcol_ref, vec_scr, sems):
@@ -256,9 +260,11 @@
 
 def mlp(lay, count, mine_ref, other_ref, x_ref, ot_ref, cot_ref, vrow_ref,
         mid_ref, act_ref, dm_ref, dot_ref, wd_ref, dv_ref, keep_ref, give_ref,
-        wp_ref, wu_ref, dwp_ref, dwu_ref, dwd_ref, sems):
+        wp_ref, wu_ref, dwp_ref, dwu_ref, dwd_ref, h_ref, g_ref, xhat_ref, rstd_ref, du_ref, sems):
     i = pl.program_id(0)
-    d, cols = lay.d, lay.cols
+    cols = lay.cols
+    n, d, t = ot_ref.shape
+    images = [slice(k * t, (k + 1) * t) for k in range(n)]
 
     @pl.when(i == 0)
     def _():
@@ -268,38 +274,59 @@
         dwd_ref[...] = jnp.zeros_like(dwd_ref)
         dv_ref[...] = jnp.zeros_like(dv_ref)
 
-    ot = ot_ref[0]
-    mid = x_ref[0] + (dot(ot, wp_ref[...], 0, 1) + vrow_ref[6:7, :])
-    mid_ref[0] = mid
-    xhat, rstd = norm_stats(mid)
-    h2 = (xhat * vrow_ref[2:3, :] + vrow_ref[3:4, :]).astype(bf16)
-    ub = jnp.concatenate([vrow_ref[8 + j:9 + j, :] for j in range(cols)], axis=1)
-    u = dot(h2, wu_ref[...], 1, 1) + ub
-    act, gp = gelu_pair(u)
-    act = act.astype(bf16)
-    act_ref[0] = act
-    cot = cot_ref[0]
-    g = cot.astype(bf16)
-    dwd_ref[...] += dot(g, act, 0, 0)
-    du = dot(g, wd_ref[...], 1, 0) * gp
-    dul = du.astype(bf16)
-    dwu_ref[...] += dot(dul, h2, 0, 0)
-    dh2 = dot(dul, wu_ref[...], 1, 0)
-    gy = dh2 * vrow_ref[2:3, :]
-    m1 = jnp.mean(gy, axis=-1, keepdims=True)
-    m2 = jnp.mean(gy * xhat, axis=-1, keepdims=True)
-    dm = cot + rstd * (gy - m1 - xhat * m2)
-    dm_ref[0] = dm
-    dml = dm.astype(bf16)
-    dwp_ref[...] += dot(dml, ot, 0, 1)
-    dot_ref[0] = dot(wp_ref[...], dml, 0, 1).astype(bf16)
-    dv_ref[2:3, :] += jnp.sum(dh2 * xhat, axis=0, keepdims=True)
-    dv_ref[3:4, :] += jnp.sum(dh2, axis=0, keepdims=True)
-    dv_ref[6:7, :] += jnp.sum(dml.astype(f32), axis=0, keepdims=True)
-    dv_ref[7:8, :] += jnp.sum(g.astype(f32), axis=0, keepdims=True)
-    dub = jnp.sum(dul.astype(f32), axis=0, keepdims=True)
+    for k, rows in enumerate(images):
+        mid = x_ref[k] + (dot(ot_ref[k], wp_ref[...], 0, 1) + vrow_ref[6:7, :])
+        mid_ref[k] = mid
+        xhat, rstd = norm_stats(mid)
+        xhat_ref[rows] = xhat
+        rstd_ref[rows] = rstd
+        h_ref[rows] = (xhat * vrow_ref[2:3, :] + vrow_ref[3:4, :]).astype(bf16)
+        cot = cot_ref[k]
+        g_ref[rows] = cot.astype(bf16)
+        dv_ref[7:8, :] += jnp.sum(cot, axis=0, keepdims=True)
+    up_bias = jnp.concatenate([vrow_ref[8 + j:9 + j, :] for j in range(cols)], axis=1)
+    step = lay.ff // 3
+    spans = [slice(j * step, (j + 1) * step) for j in range(3)]
+    up_grads = []
+
+    def hidden(span):
+        total = jnp.zeros((1, step), f32)
+        for k, rows in enumerate(images):
+            u = dot(h_ref[rows], wu_ref[span], 1, 1) + up_bias[:, span]
+            act, slope = gelu_pair(u)
+            act_ref[k, :, span] = act.astype(bf16)
+            du = dot(g_ref[rows], wd_ref[:, span], 1, 0) * slope
+            du_ref[rows, span] = du.astype(bf16)
+            total += jnp.sum(du, axis=0, keepdims=True)
+        up_grads.append(total)
+
+    def weights(span):
+        act = jnp.concatenate([act_ref[k, :, span] for k in range(n)], axis=0)
+        dwd_ref[:, span] += dot(g_ref[...], act, 0, 0)
+        dwu_ref[span, :] += dot(du_ref[:, span], h_ref[...], 0, 0)
+
+    for j, span in enumerate(spans):
+        hidden(span)
+        if j:
+            weights(spans[j - 1])
+    weights(spans[-1])
+    up_grad = jnp.concatenate(up_grads, axis=1)
     for j in range(cols):
-        dv_ref[8 + j:9 + j, :] += dub[:, j * d:(j + 1) * d]
+        dv_ref[8 + j:9 + j, :] += up_grad[:, j * d:(j + 1) * d]
+    for k, rows in enumerate(images):
+        dh2 = dot(du_ref[rows], wu_ref[...], 1, 0)
+        xhat = xhat_ref[rows]
+        gy = dh2 * vrow_ref[2:3, :]
+        m1 = jnp.mean(gy, axis=-1, keepdims=True)
+        m2 = jnp.mean(gy * xhat, axis=-1, keepdims=True)
+        dm = cot_ref[k] + rstd_ref[rows] * (gy - m1 - xhat * m2)
+        dm_ref[k] = dm
+        dml = dm.astype(bf16)
+        dwp_ref[...] += dot(dml, ot_ref[k], 0, 1)
+        dot_ref[k] = dot(wp_ref[...], dml, 0, 1).astype(bf16)
+        dv_ref[2:3, :] += jnp.sum(dh2 * xhat, axis=0, keepdims=True)
+        dv_ref[3:4, :] += jnp.sum(dh2, axis=0, keepdims=True)
+        dv_ref[6:7, :] += jnp.sum(dm, axis=0, keepdims=True)
 
     @pl.when(i == count - 1)
     def _():
@@ -309,17 +336,23 @@
 def call_mlp(lay, mine, other, x, ot, cot, vrow):
     b, t, d = x.shape
     ff = lay.ff
+    n = 2 if b % 2 == 0 else 1
     hbm = pltpu.HBM
-    acc = [hbm((d, ff), bf16), S((16, d), f32), hbm((OWNERS, lay.second_rows, d), f32), S((OWNERS, lay.second_rows, d), bf16)]
+    acc = [hbm((d, ff), bf16), S((16, d), f32), S((OWNERS, lay.second_rows, d), bf16), S((OWNERS, lay.second_rows, d), bf16)]
     outs = [hbm((b, t, d), f32), hbm((b, t, ff), bf16), hbm((b, t, d), f32), S((b, d, t), bf16)] + acc
     n_copies = OWNERS * (len(lay.second[0]) + len(lay.second[1]))
+
+    def some(*shape):
+        return pl.BlockSpec((n,) + shape, lambda i: (i, 0, 0))
+
+    scratch = [S((d, d), bf16), S((ff, d), bf16), S((d, d), f32), S((ff, d), f32), S((d, ff), f32), S((n * t, d), bf16),
+               S((n * t, d), bf16), S((n * t, d), f32), S((n * t, 1), f32), S((n * t, ff), bf16)]
     return pl.pallas_call(
-        functools.partial(mlp, lay, b), grid=(b,),
-        in_specs=[HBM, HBM, one(t, d), one(d, t), one(t, d), full(vrow)],
-        out_specs=[one(t, d), one(t, ff), one(t, d), one(d, t)] + [full(a) for a in acc],
+        functools.partial(mlp, lay, b // n), grid=(b // n,),
+        in_specs=[HBM, HBM, some(t, d), some(d, t), some(t, d), full(vrow)],
+        out_specs=[some(t, d), some(t, ff), some(t, d), some(d, t)] + [full(a) for a in acc],
         out_shape=outs,
-        scratch_shapes=[pltpu.VMEM((d, d), bf16), pltpu.VMEM((ff, d), bf16), pltpu.VMEM((d, d), f32), pltpu.VMEM((ff, d), f32),
-                        pltpu.VMEM((d, ff), f32), pltpu.SemaphoreType.DMA((n_copies,))],
+        scratch_shapes=[pltpu.VMEM(a.shape, a.dtype) for a in scratch] + [pltpu.SemaphoreType.DMA((n_copies,))],
         compiler_params=params(MLP_MIB), cost_estimate=cost(24), name="mlp",
     )(mine, other, x, ot, cot, vrow)
 
@@ -327,20 +360,25 @@
 def attn_bwd_image(jt_ref, e_ref, il_ref, ot_ref, dot_ref, h_ref, dj_ref, dw_ref):
     t, d = h_ref.shape[1:]
     hs = d // HEADS
+    def part(k, i):
+        return jt_ref[0, k * d + i * hs:k * d + (i + 1) * hs, :]
+
+    def begin(i):
+        do = dot_ref[0, i * hs:(i + 1) * hs, :].astype(f32) * il_ref[0, i:i + 1, :]
+        dd = jnp.sum(do * ot_ref[0, i * hs:(i + 1) * hs, :].astype(f32), axis=0, keepdims=True)
+        dob = do.astype(bf16)
+        return dd, dob, dot(part(2, i), dob, 0, 0)
+
+    held = begin(0)
     for i in range(HEADS):
-        rows = slice(i * hs, (i + 1) * hs)
-        qt = jt_ref[0, i * hs:(i + 1) * hs, :]
-        kt = jt_ref[0, d + i * hs:d + (i + 1) * hs, :]
-        vt = jt_ref[0, 2 * d + i * hs:2 * d + (i + 1) * hs, :]
-        do = dot_ref[0, rows, :].astype(f32) * il_ref[0, i:i + 1, :]
-        dd = jnp.sum(do * ot_ref[0, rows, :].astype(f32), axis=0, keepdims=True)
-        dob = do.astype(bf16)
+        dd, dob, dp = held
+        if i + 1 < HEADS:
+            held = begin(i + 1)
         eb = e_ref[0, i]
-        dp = dot(vt, dob, 0, 0)
         ds = (eb.astype(f32) * (dp - dd)).astype(bf16)
-        dj_ref[0, rows, :] = (dot(kt, ds, 1, 0) * 0.125).astype(bf16)
-        dj_ref[0, d + i * hs:d + (i + 1) * hs, :] = (dot(qt, ds, 1, 1) * 0.125).astype(bf16)
         dj_ref[0, 2 * d + i * hs:2 * d + (i + 1) * hs, :] = dot(dob, eb, 1, 1).astype(bf16)
+        dj_ref[0, i * hs:(i + 1) * hs, :] = (dot(part(1, i), ds, 1, 0) * 0.125).astype(bf16)
+        dj_ref[0, d + i * hs:d + (i + 1) * hs, :] = (dot(part(0, i), ds, 1, 1) * 0.125).astype(bf16)
     hx = jnp.concatenate([h_ref[0], jnp.ones((t, 128), bf16)], axis=1)
     dw_ref[...] += dot(dj_ref[0], hx, 1, 0)
 
@@ -394,7 +432,7 @@
 
 def call_attn_bwd_last(lay, acts, dw, w, vrow, dv, dj, off, count):
     b, t, d = acts[-1].shape
-    slots = [S((OWNERS, lay.first_rows, d), f32), S((OWNERS, lay.first_rows, d), bf16)]
+    slots = [S((OWNERS, lay.first_rows, d), bf16), S((OWNERS, lay.first_rows, d), bf16)]
     return pl.pallas_call(
         functools.partial(attn_bwd_last, lay, count), grid=(count,),
         in_specs=bwd_blocks(t, d, off) + [full(dw), full(w), full(vrow), full(dv), ANY],
@@ -486,6 +524,10 @@
         compiler_params=params(16), cost_estimate=cost(3), name="adam",
     )(mine, other, *flat)
     return {name: got[4 * k:4 * k + 4] for k, name in enumerate(names)}
+
+
+def after(value, *earlier):
+    return lax.optimization_barrier((value, *earlier))[0] if earlier else value
 
 
 class Links:
@@ -569,8 +611,9 @@
     def __init__(self, links, half):
         self.links, self.held, self.k = links, half[None], 0
 
-    def round(self):
-        self.held = jnp.concatenate([self.held, self.links.step(self.held, self.k)], axis=0)
+    def round(self, *beside):
+        got = self.links.step(self.held, self.k)
+        self.held = jnp.concatenate([after(self.held, *beside), got], axis=0)
         self.k += 1
 
     def core(self):
@@ -581,13 +624,14 @@
     def __init__(self, links, keep, give):
         self.links, self.held, self.give, self.k = links, keep, give, links.rounds
 
-    def core(self):
-        self.held = self.held + self.links.core(self.give).astype(f32)
-
-    def round(self):
+    def core(self, *beside):
+        got = self.links.core(self.give)
+        self.held = after(self.held, *beside).astype(f32) + got.astype(f32)
+
+    def round(self, *beside):
         self.k -= 1
         half = self.held.shape[0] // 2
-        self.held = self.held[:half] + self.links.step(self.held[half:].astype(bf16), self.k).astype(f32)
+        self.held = after(self.held[:half], *beside) + self.links.step(self.held[half:].astype(bf16), self.k).astype(f32)
 
     def others(self):
         self.held = self.links.others(self.held[0])
@@ -600,13 +644,13 @@
     def __init__(self, held, other):
         self.held, self.other = held, other
 
-    def round(self):
+    def round(self, *beside):
         pass
 
     def others(self):
         pass
 
-    def core(self):
+    def core(self, *beside):
         return self.held, self.other
 
     finish = core
@@ -651,10 +695,7 @@
 
 
 FIRST_IMAGES = 2
-
-
-def after(value, *earlier):
-    return lax.optimization_barrier((value, *earlier))[0]
+BACK_IMAGES = 1
 
 
 def compute(lay, x, cot, gather, reduce, finish_second, rounds):
@@ -668,10 +709,9 @@
         one.round()
     one.held, two.held = lax.optimization_barrier((one.held, two.held))
     first = one.core()
-    two.held, *first = lax.optimization_barrier((two.held, *first))
     *outs, wq, vrow, vcol = call_attn_fwd_first(lay, *first, x, k)
     for _ in range(rounds - 2):
-        two.round()
+        two.round(vcol)
     *outs, two.held = lax.optimization_barrier((*outs, two.held))
     jt, e, il, ot, h = call_attn_fwd_rest(x, wq, vrow, vcol, outs, k, b - k)
     two.round()
@@ -679,16 +719,16 @@
     second = two.core()
     mid, act, dm, dot_, wd, dv, keep, give = call_mlp(lay, *second, x, ot, cot, vrow)
     down = reduce(keep, give)
-    down.core()
-    acts = (jt, e, il, ot, after(dot_, down.held), h)
-    dj, dw = call_attn_bwd_first(acts, k)
-    down.round()
+    acts = (jt, e, il, ot, dot_, h)
+    dj, dw = call_attn_bwd_first(acts, BACK_IMAGES)
+    down.core(dw)
     dw, down.held = lax.optimization_barrier((dw, down.held))
-    dj, keep, give = call_attn_bwd_last(lay, acts, dw, wq, vrow, dv, dj, k, b - k)
+    dj, keep, give = call_attn_bwd_last(lay, acts, dw, wq, vrow, dv, dj, BACK_IMAGES, b - BACK_IMAGES)
+    down.round(dj)
+    up = reduce(keep, give)
+    up.core(down.held)
     for _ in range(rounds - 2):
-        down.round()
-    up = reduce(keep, give)
-    up.core()
+        down.round(up.held)
     dj, up.held = lax.optimization_barrier((dj, up.held))
     up.round()
     gx = call_input_end(x, dm, dj, wq, vrow)

time: 137 us -> 127 us (0.927)
  Pallas kernels: 69.7 us -> 60.8 us
  starting transfers between devices: 32.4 us -> 30.3 us
  waiting for transfers between devices: 26.3 us -> 28.3 us
  other arithmetic: 6.25 us -> 4.52 us
    pallas_call x1, Pallas kernels: 6.96 us -> 2.59 us  [call_attn_bwd_first(): pl.pallas_call(attn_bwd_first, grid=(count,), in_specs=bwd_blocks(t, d, 0...]
    pallas_call x1, Pallas kernels: 26.3 us -> 24 us  [call_mlp(): pl.pallas_call(functools.partial(mlp, lay, b // n), grid=(b // n,), in_sp...]
    ppermute x20, starting transfers between devices: 32.4 us -> 30.3 us  [permute(): return lax.ppermute(value, ('narrow', 'wide'), pairs)]
    ppermute x20, waiting for transfers between devices: 26.3 us -> 28.3 us  [permute(): return lax.ppermute(value, ('narrow', 'wide'), pairs)]
    add x6, other arithmetic: 2.35 us -> 0.61 us  [the longest x2 0.37 us: core(): self.held = after(self.held, *beside).astype(f32) + got.astype(f32)]
    pallas_call x1, Pallas kernels: 8.69 us -> 7.09 us  [call_attn_fwd_first(): pl.pallas_call(functools.partial(attn_fwd_first, lay), grid=(count,), in_...]
    pallas_call x1, Pallas kernels: 6.51 us -> 4.92 us  [call_attn_fwd_rest(): pl.pallas_call(attn_fwd_rest, grid=(count,), in_specs=[one(t, d, off=off)...]
  transfers between devices with their start and end apart: 20 -> 20, of which waited for: 11 -> 14; matrix products, arithmetic and copies ran while one was open for 2% -> 2% of each run, Pallas kernels for 29% -> 26%
where the time goes in v4:
time: 127 us; the launch traced here: 126 us
  Pallas kernels  60.8 us (48%)
  starting transfers between devices  30.3 us (24%)
  waiting for transfers between devices  28.3 us (22%)
  other arithmetic  4.52 us (4%)
    ppermute x20, starting transfers between devices, permute(): return lax.ppermute(value, ('narrow', 'wide'), pairs)  30.3 us
    ppermute x20, waiting for transfers between devices, permute(): return lax.ppermute(value, ('narrow', 'wide'), pairs)  28.3 us
    pallas_call x1, Pallas kernels, call_mlp(): pl.pallas_call(functools.partial(mlp, lay, b // n), grid=(b // n,), in_sp...  24 us
    pallas_call x1, Pallas kernels, call_attn_bwd_last(): pl.pallas_call(functools.partial(attn_bwd_last, lay, count), grid=(count,...  8.7 us
    pallas_call x1, Pallas kernels, call_attn_fwd_first(): pl.pallas_call(functools.partial(attn_fwd_first, lay), grid=(count,), in_...  7.09 us
    pallas_call x1, Pallas kernels, call_attn_fwd_rest(): pl.pallas_call(attn_fwd_rest, grid=(count,), in_specs=[one(t, d, off=off)...  4.92 us
    pallas_call x1, Pallas kernels, call_input_end(): pl.pallas_call(input_end, grid=(b,), in_specs=[one(t, d), one(t, d), one(...  4.4 us
    pallas_call x1, Pallas kernels, call_layer_end(): pl.pallas_call(layer_end, grid=(b,), in_specs=[one(t, d), one(t, act.shap...  4.04 us
  transfers between devices with their start and end apart: 20, of which 14 were waited for; matrix products, arithmetic and copies ran while one was open for 2% of the time, Pallas kernels for 26%

profile of v4, /device:TPU:0, one launch (start us, length us, event | category | flops | bytes accessed | tf_op | source)
XLA Modules:
  0.0 126.2 jit_solution(1681532202389418594)
XLA Ops:
  0.7 2.0 %pack.1 = (bf16[80,384]{1,0:T(8,128)(2,1)}, bf16[224,384]{1,0:T(8,128)(2,1)}) custom-call(f32[144,384]{1,0:T(8,128)} %refs_0_.2, f32[48,384]{1,0:T(8,128)} %refs_0_.3, f32[192,384]{1,0:T(8,128)} %refs_3_.3, f32[48,1536]{1,0:T(8,128)} %refs_6_.1, f32[576]{0:T(1024)} %refs_3_.2), custom_call_target="tpu_custom_call" | custom-call | tf_op jit(solution)/shard_map/pack/pallas_call | solution.py:119
  2.7 4.1 %collective-permute-start = (bf16[1,80,384]{2,1,0:T(8,128)(2,1)}, bf16[1,80,384]{2,1,0:T(8,128)(2,1)S(1)}, u32[]{:S(2)}, u32[]{:S(2)}) collective-permute-start(bf16[1,80,384]{2,1,0:T(8,128)(2,1)} %bitcast.8), channel_id=1, source_target_pairs={{0,4},{1,5},{2,6},{3,7},{4,0},{5,1},{6,2},{7,3},{8,9},{9,8},{10,11... | collective-permute-start | bytes 184328 | tf_op jit(solution)/shard_map/ppermute | solution.py:553
  6.8 2.4 %collective-permute-done = bf16[1,80,384]{2,1,0:T(8,128)(2,1)S(1)} collective-permute-done((bf16[1,80,384]{2,1,0:T(8,128)(2,1)}, bf16[1,80,384]{2,1,0:T(8,128)(2,1)S(1)}, u32[]{:S(2)}, u32[]{:S(2)}) %collective-permute-start) | collective-permute-done | bytes 61472 | tf_op jit(solution)/shard_map/ppermute | solution.py:553
  9.2 0.8 pad_maximum_fusion.5
  10.0 2.0 %collective-permute-start.1 = (bf16[2,80,384]{2,1,0:T(8,128)(2,1)S(1)}, bf16[2,80,384]{2,1,0:T(8,128)(2,1)S(1)}, u32[]{:S(2)}, u32[]{:S(2)}) collective-permute-start(bf16[2,80,384]{2,1,0:T(8,128)(2,1)S(1)} %pad_maximum_fusion.5), channel_id=1, source_target_pairs={{0,2},{1,3},{2,0},{3,1},{4,6},{5,7},{6,4},{7,5},{8,12},{9,13},{10,... | collective-permute-start | bytes 368648 | tf_op jit(solution)/shard_map/ppermute | solution.py:553
  12.0 3.1 %collective-permute-start.3 = (bf16[1,224,384]{2,1,0:T(8,128)(2,1)}, bf16[1,224,384]{2,1,0:T(8,128)(2,1)S(1)}, u32[]{:S(2)}, u32[]{:S(2)}) collective-permute-start(bf16[1,224,384]{2,1,0:T(8,128)(2,1)} %bitcast.12), channel_id=1, source_target_pairs={{0,4},{1,5},{2,6},{3,7},{4,0},{5,1},{6,2},{7,3},{8,9},{9,8},{10,11... | collective-permute-start | bytes 516104 | tf_op jit(solution)/shard_map/ppermute | solution.py:553
  15.1 0.9 pad_maximum_fusion.4
  16.0 1.9 %collective-permute-start.2 = (bf16[4,80,384]{2,1,0:T(8,128)(2,1)S(1)}, bf16[4,80,384]{2,1,0:T(8,128)(2,1)S(1)}, u32[]{:S(2)}, u32[]{:S(2)}) collective-permute-start(bf16[4,80,384]{2,1,0:T(8,128)(2,1)S(1)} %pad_maximum_fusion.4), channel_id=1, source_target_pairs={{0,1},{1,0},{2,3},{3,2},{4,5},{5,4},{6,7},{7,6},{8,10},{9,11},{10,... | collective-permute-start | bytes 737288 | tf_op jit(solution)/shard_map/ppermute | solution.py:553
  17.9 2.7 %collective-permute-done.3 = bf16[1,224,384]{2,1,0:T(8,128)(2,1)S(1)} collective-permute-done((bf16[1,224,384]{2,1,0:T(8,128)(2,1)}, bf16[1,224,384]{2,1,0:T(8,128)(2,1)S(1)}, u32[]{:S(2)}, u32[]{:S(2)}) %collective-permute-start.3) | collective-permute-done | bytes 172064 | tf_op jit(solution)/shard_map/ppermute | solution.py:553
  20.7 1.0 pad_maximum_fusion.3
  21.6 0.6 collective-permute-done.2
  22.3 0.9 pad_maximum_fusion.2.mine_ref
  23.2 0.1 collective-permute-start.4
  23.2 1.8 %collective-permute-start.5 = (bf16[2,224,384]{2,1,0:T(8,128)(2,1)S(1)}, bf16[2,224,384]{2,1,0:T(8,128)(2,1)S(1)}, u32[]{:S(2)}, u32[]{:S(2)}) collective-permute-start(bf16[2,224,384]{2,1,0:T(8,128)(2,1)S(1)} %pad_maximum_fusion.3), channel_id=1, source_target_pairs={{0,2},{1,3},{2,0},{3,1},{4,6},{5,7},{6,4},{7,5},{8,12},{9,13},{10,... | collective-permute-start | bytes 1032200 | tf_op jit(solution)/shard_map/ppermute | solution.py:553
  25.0 0.0 collective-permute-done.4.other_ref
  25.1 7.1 %attn_fwd_first.1 = (bf16[4,1152,384]{2,1,0:T(8,128)(2,1)S(1)}, bf16[4,6,384,384]{3,2,1,0:T(8,128)(2,1)S(1)}, f32[4,8,384]{2,1,0:T(8,128)S(1)}, bf16[4,384,384]{...) custom-call(bf16[8,80,384]{2,1,0:T(8,128)(2,1)S(1)} %pad_maximum_fus, ...), custom_call_target="tpu_custom_call" | custom-call | flops 8000000000 | bytes 1048576 | tf_op jit(solution)/shard_map/attn_fwd_first/pallas_call | solution.py:234
  32.2 2.1 %collective-permute-done.5 = bf16[2,224,384]{2,1,0:T(8,128)(2,1)S(1)} collective-permute-done((bf16[2,224,384]{2,1,0:T(8,128)(2,1)S(1)}, bf16[2,224,384]{2,1,0:T(8,128)(2,1)S(1)}, u32[]{:S(2)}, u32[]{:S(2)}) %collective-permute-start.5) | collective-permute-done | bytes 344096 | tf_op jit(solution)/shard_map/ppermute | solution.py:553
  34.2 0.1 pad_maximum_fusion.1
  34.3 1.9 %collective-permute-start.6 = (bf16[4,224,384]{2,1,0:T(8,128)(2,1)S(1)}, bf16[4,224,384]{2,1,0:T(8,128)(2,1)S(1)}, u32[]{:S(2)}, u32[]{:S(2)}) collective-permute-start(bf16[4,224,384]{2,1,0:T(8,128)(2,1)S(1)} %pad_maximum_fusion.1), channel_id=1, source_target_pairs={{0,1},{1,0},{2,3},{3,2},{4,5},{5,4},{6,7},{7,6},{8,10},{9,11},{10,... | collective-permute-start | bytes 2064392 | tf_op jit(solution)/shard_map/ppermute | solution.py:553
  36.2 4.9 %attn_fwd_rest.1 = (bf16[4,1152,384]{2,1,0:T(8,128)(2,1)S(1)}, bf16[4,6,384,384]{3,2,1,0:T(8,128)(2,1)S(1)}, f32[4,8,384]{2,1,0:T(8,128)S(1)}, bf16[4,384,384]{2,1,0:T(8,128)(2,1)S(1)}, bf16[4,384,384]{2,1,0:T(8,128)(2,1)S(1)}) custom-call(f32[4,384,384]{2,1,0:T(8,128)S(1)} %copy-done.6, ...), custom_call_target="tpu_custom_call", output_to_operand_aliasing={{0}: (4, {}), {1}: (5, {}), {2}: (6, {}), {3}: (7, {}), {4}... | custom-call | flops 8000000000 | bytes 1048576 | tf_op jit(solution)/shard_map/attn_fwd_rest/pallas_call | solution.py:246
  41.2 0.0 copy-start.5
  41.2 4.1 %collective-permute-done.6 = bf16[4,224,384]{2,1,0:T(8,128)(2,1)S(1)} collective-permute-done((bf16[4,224,384]{2,1,0:T(8,128)(2,1)S(1)}, bf16[4,224,384]{2,1,0:T(8,128)(2,1)S(1)}, u32[]{:S(2)}, u32[]{:S(2)}) %collective-permute-start.6) | collective-permute-done | bytes 688160 | tf_op jit(solution)/shard_map/ppermute | solution.py:553
  45.3 0.2 pad_maximum_fusion.mine_ref
  45.5 0.8 collective-permute-start.7
  46.2 2.8 %collective-permute-done.7.other_ref = bf16[8,224,384]{2,1,0:T(8,128)(2,1)S(1)} collective-permute-done((bf16[8,224,384]{2,1,0:T(8,128)(2,1)S(1)}, bf16[8,224,384]{2,1,0:T(8,128)(2,1)S(1)}, u32[]{:S(2)}, u32[]{:S(2)}) %collective-permute-start.7) | collective-permute-done | bytes 1376288 | tf_op jit(solution)/shard_map/ppermute | solution.py:553
  49.0 24.0 %mlp.1 = (f32[4,384,384]{2,1,0:T(8,128)}, bf16[4,384,1536]{2,1,0:T(8,128)(2,1)}, f32[4,384,384]{2,1,0:T(8,128)}, bf16[4,384,384]{2,1,0:T(8,128)(2,1)S(1)}, bf16[...) custom-call(bf16[8,224,384]{2,1,0:T(8,128)(2,1)S(1)} %pad_maximum_fu, ...), custom_call_target="tpu_custom_call" | custom-call | flops 24000000000 | bytes 1048576 | tf_op jit(solution)/shard_map/mlp/pallas_call | solution.py:350
  73.0 0.7 collective-permute-start.8
  73.7 2.6 %attn_bwd_first.1 = (bf16[4,1152,384]{2,1,0:T(8,128)(2,1)S(1)}, f32[1152,512]{1,0:T(8,128)S(1)}) custom-call(bf16[4,1152,384]{2,1,0:T(8,128)(2,1)S(1)} %get-tuple-element.120.jt_ref, bf16[4,6,384,384]{3,2,1,0:T(8,128)(2,1)S(1)} %get-tuple-element.121.e_ref, f32[4,8,384]{2,1,0:T(8,128)S(1)} %get-tuple-element.122.il_ref, ...), custom_call_target="tpu_custom_call" | custom-call | flops 4000000000 | bytes 1048576 | tf_op jit(solution)/shard_map/attn_bwd_first/pallas_call | solution.py:426
  76.3 0.2 collective-permute-done.8
  76.4 0.3 convert_add_fusion
  76.7 0.1 slice.78
  76.8 1.6 %collective-permute-start.9 = (bf16[4,224,384]{2,1,0:T(8,128)(2,1)S(1)}, bf16[4,224,384]{2,1,0:T(8,128)(2,1)S(1)}, u32[]{:S(2)}, u32[]{:S(2)}) collective-permute-start(bf16[4,224,384]{2,1,0:T(8,128)(2,1)S(1)} %slice.78), channel_id=1, source_target_pairs={{0,1},{1,0},{2,3},{3,2},{4,5},{5,4},{6,7},{7,6},{8,10},{9,11},{10,... | collective-permute-start | bytes 2064392 | tf_op jit(solution)/shard_map/ppermute | solution.py:553
  78.4 8.7 %attn_bwd_last.1 = (bf16[4,1152,384]{2,1,0:T(8,128)(2,1)S(1)}, bf16[8,80,384]{2,1,0:T(8,128)(2,1)S(1)}, bf16[8,80,384]{2,1,0:T(8,128)(2,1)S(1)}) custom-call(bf16[4,1152,384]{2,1,0:T(8,128)(2,1)S(1)} %get-tuple-element.120.jt_ref, bf16[4,6,384,384]{3,2,1,0:T(8,128)(2,1)S(1)} %get-tuple-element.121.e_ref, ...), custom_call_target="tpu_custom_call", output_to_operand_aliasing={{0}: (10, {})} | custom-call | flops 14000000000 | bytes 1048576 | tf_op jit(solution)/shard_map/attn_bwd_last/pallas_call | solution.py:436
  87.1 0.4 collective-permute-start.10
  87.5 0.1 slice.42
  87.6 0.2 collective-permute-done.9
  87.8 0.1 convert_add_fusion.1
  88.0 1.0 collective-permute-done.10
  89.0 0.1 convert_add_fusion.2
  89.1 1.5 %collective-permute-start.11 = (bf16[4,80,384]{2,1,0:T(8,128)(2,1)S(1)}, bf16[4,80,384]{2,1,0:T(8,128)(2,1)S(1)}, u32[]{:S(2)}, u32[]{:S(2)}) collective-permute-start(bf16[4,80,384]{2,1,0:T(8,128)(2,1)S(1)} %slice.80), channel_id=1, source_target_pairs={{0,1},{1,0},{2,3},{3,2},{4,5},{5,4},{6,7},{7,6},{8,10},{9,11},{10,... | collective-permute-start | bytes 737288 | tf_op jit(solution)/shard_map/ppermute | solution.py:553
  90.7 1.7 %collective-permute-start.16 = (bf16[2,224,384]{2,1,0:T(8,128)(2,1)S(1)}, bf16[2,224,384]{2,1,0:T(8,128)(2,1)S(1)}, u32[]{:S(2)}, u32[]{:S(2)}) collective-permute-start(bf16[2,224,384]{2,1,0:T(8,128)(2,1)S(1)} %slice.79), channel_id=1, source_target_pairs={{0,2},{1,3},{2,0},{3,1},{4,6},{5,7},{6,4},{7,5},{8,12},{9,13},{10,... | collective-permute-start | bytes 1032200 | tf_op jit(solution)/shard_map/ppermute | solution.py:553
  92.4 4.4 %input_end.1 = f32[4,384,384]{2,1,0:T(8,128)} custom-call(f32[4,384,384]{2,1,0:T(8,128)S(1)} %copy-done.6, f32[4,384,384]{2,1,0:T(8,128)S(1)} %copy-done.17, bf16[4,1152,384]{2,1,0:T(8,128)(2,1)S(1)} %get-tuple-element.138.dj_ref, bf16[1152,384]{1,0:T(8,128)(2,1)S(1)} %get-tuple-element.99.w_ref, f32[16,384]{1,0:T(8,128)S(1)} %get-tuple-element.100.vrow_ref), custom_call_target="tpu_custom_call" | custom-call | flops 4000000000 | bytes 1048576 | tf_op jit(solution)/shard_map/input_end/pallas_call | solution.py:470
  96.8 0.4 collective-permute-start.12
  97.3 0.7 copy-done.19
  98.0 4.0 %layer_end.1 = f32[4,384,384]{2,1,0:T(8,128)} custom-call(f32[4,384,384]{2,1,0:T(8,128)S(1)} %copy-done.18, bf16[4,384,1536]{2,1,0:T(8,128)(2,1)S(1)} %bitcast.7, bf16[384,1536]{1,0:T(8,128)(2,1)S(1)} %copy-done.19, f32[16,384]{1,0:T(8,128)S(1)} %get-tuple-element.100.vrow_ref), custom_call_target="tpu_custom_call" | custom-call | flops 4000000000 | bytes 1048576 | tf_op jit(solution)/shard_map/layer_end/pallas_call | solution.py:452
  102.1 1.4 %collective-permute-done.12 = bf16[2,80,384]{2,1,0:T(8,128)(2,1)S(1)} collective-permute-done((bf16[2,80,384]{2,1,0:T(8,128)(2,1)S(1)}, bf16[2,80,384]{2,1,0:T(8,128)(2,1)S(1)}, u32[]{:S(2)}, u32[]{:S(2)}) %collective-permute-start.12) | collective-permute-done | bytes 122912 | tf_op jit(solution)/shard_map/ppermute | solution.py:553
  103.5 4.9 %collective-permute-start.13 = (bf16[1,80,384]{2,1,0:T(8,128)(2,1)S(1)}, bf16[1,80,384]{2,1,0:T(8,128)(2,1)S(1)}, u32[]{:S(2)}, u32[]{:S(2)}) collective-permute-start(bf16[1,80,384]{2,1,0:T(8,128)(2,1)S(1)} %slice.83), channel_id=1, source_target_pairs={{0,4},{1,5},{2,6},{3,7},{4,0},{5,1},{6,2},{7,3},{8,9},{9,8},{10,11... | collective-permute-start | bytes 184328 | tf_op jit(solution)/shard_map/ppermute | solution.py:553
  108.5 0.1 convert_add_fusion.3
  108.5 0.0 copy-start.2
  108.5 0.0 copy-start.4
  108.6 0.0 copy-start.15
  108.6 0.0 copy-start.16
  108.6 0.1 collective-permute-start.17
  108.7 2.6 %collective-permute-done.13 = bf16[1,80,384]{2,1,0:T(8,128)(2,1)S(1)} collective-permute-done((bf16[1,80,384]{2,1,0:T(8,128)(2,1)S(1)}, bf16[1,80,384]{2,1,0:T(8,128)(2,1)S(1)}, u32[]{:S(2)}, u32[]{:S(2)}) %collective-permute-start.13) | collective-permute-done | bytes 61472 | tf_op jit(solution)/shard_map/ppermute | solution.py:553
  111.3 1.6 %collective-permute-start.14 = (bf16[80,384]{1,0:T(8,128)(2,1)S(1)}, bf16[80,384]{1,0:T(8,128)(2,1)S(1)}, u32[]{:S(2)}, u32[]{:S(2)}) collective-permute-start(bf16[80,384]{1,0:T(8,128)(2,1)S(1)} %fusion.2), channel_id=1, source_target_pairs={{0,16},{1,17},{2,18},{3,19},{4,20},{5,21},{6,22},{7,23},{8,24},{9,... | collective-permute-start | bytes 184328 | tf_op jit(solution)/shard_map/ppermute | solution.py:553
  112.9 3.9 %collective-permute-done.17 = bf16[1,224,384]{2,1,0:T(8,128)(2,1)S(1)} collective-permute-done((bf16[1,224,384]{2,1,0:T(8,128)(2,1)S(1)}, bf16[1,224,384]{2,1,0:T(8,128)(2,1)S(1)}, u32[]{:S(2)}, u32[]{:S(2)}) %collective-permute-start.17) | collective-permute-done | bytes 172064 | tf_op jit(solution)/shard_map/ppermute | solution.py:553
  116.9 1.6 %collective-permute-start.18 = (bf16[224,384]{1,0:T(8,128)(2,1)S(1)}, bf16[224,384]{1,0:T(8,128)(2,1)S(1)}, u32[]{:S(2)}, u32[]{:S(2)}) collective-permute-start(bf16[224,384]{1,0:T(8,128)(2,1)S(1)} %fusion.1), channel_id=1, source_target_pairs={{0,16},{1,17},{2,18},{3,19},{4,20},{5,21},{6,22},{7,23},{8,24},{9,... | collective-permute-start | bytes 516104 | tf_op jit(solution)/shard_map/ppermute | solution.py:553
  118.5 0.1 collective-permute-start.15
  118.6 3.8 %collective-permute-done.18 = bf16[224,384]{1,0:T(8,128)(2,1)S(1)} collective-permute-done((bf16[224,384]{1,0:T(8,128)(2,1)S(1)}, bf16[224,384]{1,0:T(8,128)(2,1)S(1)}, u32[]{:S(2)}, u32[]{:S(2)}) %collective-permute-start.18) | collective-permute-done | bytes 172064 | tf_op jit(solution)/shard_map/ppermute | solution.py:553
  122.4 0.0 copy-start
  122.5 0.1 collective-permute-start.19
  122.7 1.2 adam.2
  123.8 0.4 collective-permute-done.19.other_ref
  124.3 1.9 %adam.3 = (f32[48,384]{1,0:T(8,128)}, f32[48,384]{1,0:T(8,128)}, f32[48,384]{1,0:T(8,128)}, bf16[48,384]{1,0:T(8,128)(2,1)}, f32[192,384]{1,0:T(8,128)}, /*index...) custom-call(f32[224,384]{1,0:T(8,128)S(1)} %convert_add_fusion.5.min, ...), custom_call_target="tpu_custom_call" | custom-call | flops 3000000000 | bytes 1048576 | tf_op jit(solution)/shard_map/adam/pallas_call | solution.py:521
  (58 shorter events, 0.4 us)
Async XLA Ops:
  2.6 22.4 %copy-start.6 = (f32[4,384,384]{2,1,0:T(8,128)S(1)}, f32[4,384,384]{2,1,0:T(8,128)}, u32[]{:S(2)}) copy-start(f32[4,384,384]{2,1,0:T(8,128)} %x_ref.7) | copy-start | bytes 7077892
  2.7 6.5 %collective-permute-start = (bf16[1,80,384]{2,1,0:T(8,128)(2,1)}, bf16[1,80,384]{2,1,0:T(8,128)(2,1)S(1)}, u32[]{:S(2)}, u32[]{:S(2)}) collective-permute-start(bf16[1,80,384]{2,1,0:T(8,128)(2,1)} %bitcast.8), channel_id=1, source_target_pairs={{0,4},{1,5},{2,6},{3,7},{4,0},{5,1},{6,2},{7,3},{8,9},{9,8},{10,11... | collective-permute-start | bytes 184328 | tf_op jit(solution)/shard_map/ppermute | solution.py:553
  10.0 5.1 %collective-permute-start.1 = (bf16[2,80,384]{2,1,0:T(8,128)(2,1)S(1)}, bf16[2,80,384]{2,1,0:T(8,128)(2,1)S(1)}, u32[]{:S(2)}, u32[]{:S(2)}) collective-permute-start(bf16[2,80,384]{2,1,0:T(8,128)(2,1)S(1)} %pad_maximum_fusion.5), channel_id=1, source_target_pairs={{0,2},{1,3},{2,0},{3,1},{4,6},{5,7},{6,4},{7,5},{8,12},{9,13},{10,... | collective-permute-start | bytes 368648 | tf_op jit(solution)/shard_map/ppermute | solution.py:553
  12.0 8.7 %collective-permute-start.3 = (bf16[1,224,384]{2,1,0:T(8,128)(2,1)}, bf16[1,224,384]{2,1,0:T(8,128)(2,1)S(1)}, u32[]{:S(2)}, u32[]{:S(2)}) collective-permute-start(bf16[1,224,384]{2,1,0:T(8,128)(2,1)} %bitcast.12), channel_id=1, source_target_pairs={{0,4},{1,5},{2,6},{3,7},{4,0},{5,1},{6,2},{7,3},{8,9},{9,8},{10,11... | collective-permute-start | bytes 516104 | tf_op jit(solution)/shard_map/ppermute | solution.py:553
  16.0 6.3 %collective-permute-start.2 = (bf16[4,80,384]{2,1,0:T(8,128)(2,1)S(1)}, bf16[4,80,384]{2,1,0:T(8,128)(2,1)S(1)}, u32[]{:S(2)}, u32[]{:S(2)}) collective-permute-start(bf16[4,80,384]{2,1,0:T(8,128)(2,1)S(1)} %pad_maximum_fusion.4), channel_id=1, source_target_pairs={{0,1},{1,0},{2,3},{3,2},{4,5},{5,4},{6,7},{7,6},{8,10},{9,11},{10,... | collective-permute-start | bytes 737288 | tf_op jit(solution)/shard_map/ppermute | solution.py:553
  23.2 1.9 %collective-permute-start.4 = (bf16[8,80,384]{2,1,0:T(8,128)(2,1)S(1)}, bf16[8,80,384]{2,1,0:T(8,128)(2,1)S(1)}, u32[]{:S(2)}, u32[]{:S(2)}) collective-permute-start(bf16[8,80,384]{2,1,0:T(8,128)(2,1)S(1)} %pad_maximum_fusion.2.mine_ref), channel_id=1, source_target_pairs={{0,8},{1,9},{2,10},{3,11},{4,12},{5,13},{6,14},{7,15},{8,0},{9,1},... | collective-permute-start | bytes 1474568 | tf_op jit(solution)/shard_map/ppermute | solution.py:553
  23.2 11.0 %collective-permute-start.5 = (bf16[2,224,384]{2,1,0:T(8,128)(2,1)S(1)}, bf16[2,224,384]{2,1,0:T(8,128)(2,1)S(1)}, u32[]{:S(2)}, u32[]{:S(2)}) collective-permute-start(bf16[2,224,384]{2,1,0:T(8,128)(2,1)S(1)} %pad_maximum_fusion.3), channel_id=1, source_target_pairs={{0,2},{1,3},{2,0},{3,1},{4,6},{5,7},{6,4},{7,5},{8,12},{9,13},{10,... | collective-permute-start | bytes 1032200 | tf_op jit(solution)/shard_map/ppermute | solution.py:553
  34.3 11.0 %collective-permute-start.6 = (bf16[4,224,384]{2,1,0:T(8,128)(2,1)S(1)}, bf16[4,224,384]{2,1,0:T(8,128)(2,1)S(1)}, u32[]{:S(2)}, u32[]{:S(2)}) collective-permute-start(bf16[4,224,384]{2,1,0:T(8,128)(2,1)S(1)} %pad_maximum_fusion.1), channel_id=1, source_target_pairs={{0,1},{1,0},{2,3},{3,2},{4,5},{5,4},{6,7},{7,6},{8,10},{9,11},{10,... | collective-permute-start | bytes 2064392 | tf_op jit(solution)/shard_map/ppermute | solution.py:553
  41.2 7.8 %copy-start.5 = (f32[4,384,384]{2,1,0:T(8,128)S(1)}, f32[4,384,384]{2,1,0:T(8,128)}, u32[]{:S(2)}) copy-start(f32[4,384,384]{2,1,0:T(8,128)} %cot_ref.1) | copy-start | bytes 7077892
  45.5 3.5 %collective-permute-start.7 = (bf16[8,224,384]{2,1,0:T(8,128)(2,1)S(1)}, bf16[8,224,384]{2,1,0:T(8,128)(2,1)S(1)}, u32[]{:S(2)}, u32[]{:S(2)}) collective-permute-start(bf16[8,224,384]{2,1,0:T(8,128)(2,1)S(1)} %pad_maximum_fusion.mine_ref), channel_id=1, source_target_pairs={{0,8},{1,9},{2,10},{3,11},{4,12},{5,13},{6,14},{7,15},{8,0},{9,1},... | collective-permute-start | bytes 4128776 | tf_op jit(solution)/shard_map/ppermute | solution.py:553
  73.0 3.4 %collective-permute-start.8 = (bf16[8,224,384]{2,1,0:T(8,128)(2,1)S(1)}, bf16[8,224,384]{2,1,0:T(8,128)(2,1)S(1)}, u32[]{:S(2)}, u32[]{:S(2)}) collective-permute-start(bf16[8,224,384]{2,1,0:T(8,128)(2,1)S(1)} %get-tuple-element.128), channel_id=1, source_target_pairs={{0,8},{1,9},{2,10},{3,11},{4,12},{5,13},{6,14},{7,15},{8,0},{9,1},... | collective-permute-start | bytes 4128776 | tf_op jit(solution)/shard_map/ppermute | solution.py:553
  76.8 11.0 %collective-permute-start.9 = (bf16[4,224,384]{2,1,0:T(8,128)(2,1)S(1)}, bf16[4,224,384]{2,1,0:T(8,128)(2,1)S(1)}, u32[]{:S(2)}, u32[]{:S(2)}) collective-permute-start(bf16[4,224,384]{2,1,0:T(8,128)(2,1)S(1)} %slice.78), channel_id=1, source_target_pairs={{0,1},{1,0},{2,3},{3,2},{4,5},{5,4},{6,7},{7,6},{8,10},{9,11},{10,... | collective-permute-start | bytes 2064392 | tf_op jit(solution)/shard_map/ppermute | solution.py:553
  87.1 1.9 %collective-permute-start.10 = (bf16[8,80,384]{2,1,0:T(8,128)(2,1)S(1)}, bf16[8,80,384]{2,1,0:T(8,128)(2,1)S(1)}, u32[]{:S(2)}, u32[]{:S(2)}) collective-permute-start(bf16[8,80,384]{2,1,0:T(8,128)(2,1)S(1)} %get-tuple-element.137), channel_id=1, source_target_pairs={{0,8},{1,9},{2,10},{3,11},{4,12},{5,13},{6,14},{7,15},{8,0},{9,1},... | collective-permute-start | bytes 1474568 | tf_op jit(solution)/shard_map/ppermute | solution.py:553
  87.9 1.2 copy-start.20
  88.0 4.4 %copy-start.17 = (f32[4,384,384]{2,1,0:T(8,128)S(1)}, f32[4,384,384]{2,1,0:T(8,128)}, u32[]{:S(2)}) copy-start(f32[4,384,384]{2,1,0:T(8,128)} %get-tuple-element.119.dm_ref) | copy-start | bytes 7077892
  89.0 8.3 %slice-start = ((s8[4718592]{0:T(1024)(128)(4,1)}), s8[4194304]{0:T(1024)(128)(4,1)S(1)}, s32[]{:S(2)}) async-start(s8[4718592]{0:T(1024)(128)(4,1)} %bitcast.6), calls=%async_computation | async-start | bytes 8388608
  89.1 7.6 %collective-permute-start.11 = (bf16[4,80,384]{2,1,0:T(8,128)(2,1)S(1)}, bf16[4,80,384]{2,1,0:T(8,128)(2,1)S(1)}, u32[]{:S(2)}, u32[]{:S(2)}) collective-permute-start(bf16[4,80,384]{2,1,0:T(8,128)(2,1)S(1)} %slice.80), channel_id=1, source_target_pairs={{0,1},{1,0},{2,3},{3,2},{4,5},{5,4},{6,7},{7,6},{8,10},{9,11},{10,... | collective-permute-start | bytes 737288 | tf_op jit(solution)/shard_map/ppermute | solution.py:553
  90.7 17.8 %collective-permute-start.16 = (bf16[2,224,384]{2,1,0:T(8,128)(2,1)S(1)}, bf16[2,224,384]{2,1,0:T(8,128)(2,1)S(1)}, u32[]{:S(2)}, u32[]{:S(2)}) collective-permute-start(bf16[2,224,384]{2,1,0:T(8,128)(2,1)S(1)} %slice.79), channel_id=1, source_target_pairs={{0,2},{1,3},{2,0},{3,1},{4,6},{5,7},{6,4},{7,5},{8,12},{9,13},{10,... | collective-permute-start | bytes 1032200 | tf_op jit(solution)/shard_map/ppermute | solution.py:553
  92.4 4.9 %slice-start.1 = ((s8[4718592]{0:T(1024)(128)(4,1)}), s8[524288]{0:T(1024)(128)(4,1)S(1)}, s32[]{:S(2)}) async-start(s8[4718592]{0:T(1024)(128)(4,1)} %bitcast.6), calls=%async_computation.1 | async-start | bytes 1048576
  92.4 4.9 %copy-start.18 = (f32[4,384,384]{2,1,0:T(8,128)S(1)}, f32[4,384,384]{2,1,0:T(8,128)}, u32[]{:S(2)}) copy-start(f32[4,384,384]{2,1,0:T(8,128)} %get-tuple-element.141.mid_ref) | copy-start | bytes 7077892
  96.8 1.3 %copy-start.19 = (bf16[384,1536]{1,0:T(8,128)(2,1)S(1)}, bf16[384,1536]{1,0:T(8,128)(2,1)}, u32[]{:S(2)}) copy-start(bf16[384,1536]{1,0:T(8,128)(2,1)} %get-tuple-element.143.wd_ref) | copy-start | bytes 3538948
  96.8 6.7 %collective-permute-start.12 = (bf16[2,80,384]{2,1,0:T(8,128)(2,1)S(1)}, bf16[2,80,384]{2,1,0:T(8,128)(2,1)S(1)}, u32[]{:S(2)}, u32[]{:S(2)}) collective-permute-start(bf16[2,80,384]{2,1,0:T(8,128)(2,1)S(1)} %slice.82), channel_id=1, source_target_pairs={{0,2},{1,3},{2,0},{3,1},{4,6},{5,7},{6,4},{7,5},{8,12},{9,13},{10,... | collective-permute-start | bytes 368648 | tf_op jit(solution)/shard_map/ppermute | solution.py:553
  98.0 10.4 %slice-start.2 = ((f32[4,224,384]{2,1,0:T(8,128)}), f32[2,224,384]{2,1,0:T(8,128)S(1)}, s32[]{:S(2)}) async-start(f32[4,224,384]{2,1,0:T(8,128)} %copy-done.20), calls=%async_computation.2 | async-start | bytes 1376256 | tf_op jit(solution)/shard_map/slice | solution.py:634
  103.5 7.8 %collective-permute-start.13 = (bf16[1,80,384]{2,1,0:T(8,128)(2,1)S(1)}, bf16[1,80,384]{2,1,0:T(8,128)(2,1)S(1)}, u32[]{:S(2)}, u32[]{:S(2)}) collective-permute-start(bf16[1,80,384]{2,1,0:T(8,128)(2,1)S(1)} %slice.83), channel_id=1, source_target_pairs={{0,4},{1,5},{2,6},{3,7},{4,0},{5,1},{6,2},{7,3},{8,9},{9,8},{10,11... | collective-permute-start | bytes 184328 | tf_op jit(solution)/shard_map/ppermute | solution.py:553
  108.5 14.1 %copy-start.2 = (f32[144,384]{1,0:T(8,128)S(1)}, f32[144,384]{1,0:T(8,128)}, u32[]{:S(2)}) copy-start(f32[144,384]{1,0:T(8,128)} %refs_0_.2) | copy-start | bytes 663556
  108.5 14.1 %copy-start.4 = (f32[576]{0:T(1024)S(1)}, f32[576]{0:T(1024)}, u32[]{:S(2)}) copy-start(f32[576]{0:T(1024)} %refs_3_.2) | copy-start | bytes 6916
  108.5 14.1 %copy-start.11 = (f32[144,384]{1,0:T(8,128)S(1)}, f32[144,384]{1,0:T(8,128)}, u32[]{:S(2)}) copy-start(f32[144,384]{1,0:T(8,128)} %refs_1_.2) | copy-start | bytes 663556
  108.6 14.1 %copy-start.12 = (f32[144,384]{1,0:T(8,128)S(1)}, f32[144,384]{1,0:T(8,128)}, u32[]{:S(2)}) copy-start(f32[144,384]{1,0:T(8,128)} %refs_2_.2) | copy-start | bytes 663556
  108.6 14.1 %copy-start.15 = (f32[576]{0:T(1024)S(1)}, f32[576]{0:T(1024)}, u32[]{:S(2)}) copy-start(f32[576]{0:T(1024)} %refs_4_.2) | copy-start | bytes 6916
  108.6 14.1 %copy-start.16 = (f32[576]{0:T(1024)S(1)}, f32[576]{0:T(1024)}, u32[]{:S(2)}) copy-start(f32[576]{0:T(1024)} %refs_5_.2) | copy-start | bytes 6916
  108.6 8.2 %collective-permute-start.17 = (bf16[1,224,384]{2,1,0:T(8,128)(2,1)S(1)}, bf16[1,224,384]{2,1,0:T(8,128)(2,1)S(1)}, u32[]{:S(2)}, u32[]{:S(2)}) collective-permute-start(bf16[1,224,384]{2,1,0:T(8,128)(2,1)S(1)} %slice.81), channel_id=1, source_target_pairs={{0,4},{1,5},{2,6},{3,7},{4,0},{5,1},{6,2},{7,3},{8,9},{9,8},{10,11... | collective-permute-start | bytes 516104 | tf_op jit(solution)/shard_map/ppermute | solution.py:553
  111.3 7.1 %collective-permute-start.14 = (bf16[80,384]{1,0:T(8,128)(2,1)S(1)}, bf16[80,384]{1,0:T(8,128)(2,1)S(1)}, u32[]{:S(2)}, u32[]{:S(2)}) collective-permute-start(bf16[80,384]{1,0:T(8,128)(2,1)S(1)} %fusion.2), channel_id=1, source_target_pairs={{0,16},{1,17},{2,18},{3,19},{4,20},{5,21},{6,22},{7,23},{8,24},{9,... | collective-permute-start | bytes 184328 | tf_op jit(solution)/shard_map/ppermute | solution.py:553
  116.9 5.5 %collective-permute-start.18 = (bf16[224,384]{1,0:T(8,128)(2,1)S(1)}, bf16[224,384]{1,0:T(8,128)(2,1)S(1)}, u32[]{:S(2)}, u32[]{:S(2)}) collective-permute-start(bf16[224,384]{1,0:T(8,128)(2,1)S(1)} %fusion.1), channel_id=1, source_target_pairs={{0,16},{1,17},{2,18},{3,19},{4,20},{5,21},{6,22},{7,23},{8,24},{9,... | collective-permute-start | bytes 516104 | tf_op jit(solution)/shard_map/ppermute | solution.py:553
  118.5 4.1 %collective-permute-start.15 = (f32[80,384]{1,0:T(8,128)S(1)}, f32[80,384]{1,0:T(8,128)S(1)}, u32[]{:S(2)}, u32[]{:S(2)}) collective-permute-start(f32[80,384]{1,0:T(8,128)S(1)} %convert_add_fusion.7.mine_ref), channel_id=1, source_target_pairs={{0,8},{1,9},{2,10},{3,11},{4,12},{5,13},{6,14},{7,15},{8,0},{9,1},... | collective-permute-start | bytes 368648 | tf_op jit(solution)/shard_map/ppermute | solution.py:553
  122.4 1.8 %copy-start = (f32[192,384]{1,0:T(8,128)S(1)}, f32[192,384]{1,0:T(8,128)}, u32[]{:S(2)}) copy-start(f32[192,384]{1,0:T(8,128)} %refs_3_.3) | copy-start | bytes 884740
  122.4 1.8 %copy-start.1 = (f32[48,1536]{1,0:T(8,128)S(1)}, f32[48,1536]{1,0:T(8,128)}, u32[]{:S(2)}) copy-start(f32[48,1536]{1,0:T(8,128)} %refs_6_.1) | copy-start | bytes 884740
  122.4 1.8 %copy-start.3 = (f32[48,384]{1,0:T(8,128)S(1)}, f32[48,384]{1,0:T(8,128)}, u32[]{:S(2)}) copy-start(f32[48,384]{1,0:T(8,128)} %refs_0_.3) | copy-start | bytes 221188
  122.4 1.8 %copy-start.7 = (f32[192,384]{1,0:T(8,128)S(1)}, f32[192,384]{1,0:T(8,128)}, u32[]{:S(2)}) copy-start(f32[192,384]{1,0:T(8,128)} %refs_4_.3) | copy-start | bytes 884740
  122.4 1.8 %copy-start.8 = (f32[192,384]{1,0:T(8,128)S(1)}, f32[192,384]{1,0:T(8,128)}, u32[]{:S(2)}) copy-start(f32[192,384]{1,0:T(8,128)} %refs_5_.3) | copy-start | bytes 884740
  122.5 1.8 %copy-start.9 = (f32[48,1536]{1,0:T(8,128)S(1)}, f32[48,1536]{1,0:T(8,128)}, u32[]{:S(2)}) copy-start(f32[48,1536]{1,0:T(8,128)} %refs_7_.1) | copy-start | bytes 884740
  122.5 1.8 %copy-start.10 = (f32[48,1536]{1,0:T(8,128)S(1)}, f32[48,1536]{1,0:T(8,128)}, u32[]{:S(2)}) copy-start(f32[48,1536]{1,0:T(8,128)} %refs_8_.1) | copy-start | bytes 884740
  122.5 1.8 %copy-start.13 = (f32[48,384]{1,0:T(8,128)S(1)}, f32[48,384]{1,0:T(8,128)}, u32[]{:S(2)}) copy-start(f32[48,384]{1,0:T(8,128)} %refs_1_.3) | copy-start | bytes 221188
  122.5 1.8 %copy-start.14 = (f32[48,384]{1,0:T(8,128)S(1)}, f32[48,384]{1,0:T(8,128)}, u32[]{:S(2)}) copy-start(f32[48,384]{1,0:T(8,128)} %refs_2_.3) | copy-start | bytes 221188
  122.5 1.7 %collective-permute-start.19 = (f32[224,384]{1,0:T(8,128)S(1)}, f32[224,384]{1,0:T(8,128)S(1)}, u32[]{:S(2)}, u32[]{:S(2)}) collective-permute-start(f32[224,384]{1,0:T(8,128)S(1)} %convert_add_fusion.5.mine_ref), channel_id=1, source_target_pairs={{0,8},{1,9},{2,10},{3,11},{4,12},{5,13},{6,14},{7,15},{8,0},{9,1},... | collective-permute-start | bytes 1032200 | tf_op jit(solution)/shard_map/ppermute | solution.py:553

commit v5 on v4

--- a/solution.py
+++ b/solution.py
@@ -124,28 +124,32 @@
     )(q, p, u, d, v)
 
 
-def fetch(lay, halves, mine_ref, other_ref, dests, sems):
+def fetch(lay, halves, mine_refs, other_refs, dests, sems, names, start=True, wait=True):
     me, core = lay.position()
-
-    def copies(half, src_ref, base):
-        out = []
+    each = OWNERS // 2
+
+    def copies(half, src_refs, base):
+        out, count = [], 0
         for j in range(OWNERS):
             for piece in halves[half]:
                 name, _, rows, _, at = piece
                 r, c = place(lay, piece, me ^ lay.masks[half][j])
                 dst = dests[name].at[r] if name != "d" else dests[name].at[r, c]
-                out.append(pltpu.make_async_copy(src_ref.at[j, pl.ds(at, rows)], dst, sems.at[base + len(out)]))
+                if name in names:
+                    out.append(pltpu.make_async_copy(src_refs[j // each].at[j % each, pl.ds(at, rows)], dst, sems.at[base + count]))
+                count += 1
         return out
 
     for half in range(2):
         @pl.when(core == half)
         def _():
-            first = copies(half, mine_ref, 0)
-            both = first + copies(1 - half, other_ref, len(first))
-            for c in both:
-                c.start()
-            for c in both:
-                c.wait()
+            both = copies(half, mine_refs, 0) + copies(1 - half, other_refs, OWNERS * len(halves[half]))
+            if start:
+                for c in both:
+                    c.start()
+            if wait:
+                for c in both:
+                    c.wait()
 
 
 def emit(lay, halves, arrays, keep_ref, give_ref):
@@ -197,10 +201,10 @@
         st = later
 
 
-def attn_fwd_first(lay, mine_ref, other_ref, x_ref, jt_ref, e_ref, il_ref, ot_ref, h_ref, w_ref, vrow_ref, vcol_ref, vec_scr, sems):
+def attn_fwd_first(lay, mine_a, mine_b, other_a, other_b, x_ref, jt_ref, e_ref, il_ref, ot_ref, h_ref, w_ref, vrow_ref, vcol_ref, vec_scr, sems):
     @pl.when(pl.program_id(0) == 0)
     def _():
-        fetch(lay, lay.first, mine_ref, other_ref, {"q": w_ref, "v": vec_scr}, sems)
+        fetch(lay, lay.first, (mine_a, mine_b), (other_a, other_b), {"q": w_ref, "v": vec_scr}, sems, "qv")
         d, s = lay.d, lay.piece
         vrow_ref[...] = jnp.zeros_like(vrow_ref)
         for r in range(8 + lay.cols):
@@ -227,18 +231,18 @@
     return [one(3 * d, t, off=off), one(HEADS, t, t, off=off), one(8, t, off=off), one(d, t, off=off), one(t, d, off=off)]
 
 
-def call_attn_fwd_first(lay, mine, other, x, count):
+def call_attn_fwd_first(lay, slots, x, count):
     b, t, d = x.shape
     extra = [S((3 * d, d), bf16), S((16, d), f32), S((3 * d, 8), f32)]
     n_copies = OWNERS * (len(lay.first[0]) + len(lay.first[1]))
     return pl.pallas_call(
         functools.partial(attn_fwd_first, lay), grid=(count,),
-        in_specs=[HBM, HBM, one(t, d)],
+        in_specs=[HBM] * 4 + [one(t, d)],
         out_specs=fwd_blocks(t, d, 0) + [full(a) for a in extra],
         out_shape=fwd_outs(b, t, d) + extra,
         scratch_shapes=[pltpu.VMEM((OWNERS * 16, d), bf16), pltpu.SemaphoreType.DMA((n_copies,))],
         compiler_params=params(24), cost_estimate=cost(4 * count), name="attn_fwd_first",
-    )(mine, other, x)
+    )(*slots, x)
 
 
 def call_attn_fwd_rest(x, w, vrow, vcol, outs, off, count):
@@ -258,7 +262,7 @@
     return u * cdf, cdf + u * pdf
 
 
-def mlp(lay, count, mine_ref, other_ref, x_ref, ot_ref, cot_ref, vrow_ref,
+def mlp(lay, count, mine_a, mine_b, other_a, other_b, x_ref, ot_ref, cot_ref, vrow_ref,
         mid_ref, act_ref, dm_ref, dot_ref, wd_ref, dv_ref, keep_ref, give_ref,
         wp_ref, wu_ref, dwp_ref, dwu_ref, dwd_ref, h_ref, g_ref, xhat_ref, rstd_ref, du_ref, sems):
     i = pl.program_id(0)
@@ -266,9 +270,11 @@
     n, d, t = ot_ref.shape
     images = [slice(k * t, (k + 1) * t) for k in range(n)]
 
+    weights_of = functools.partial(fetch, lay, lay.second, (mine_a, mine_b), (other_a, other_b), {"p": wp_ref, "u": wu_ref, "d": wd_ref}, sems)
+
     @pl.when(i == 0)
     def _():
-        fetch(lay, lay.second, mine_ref, other_ref, {"p": wp_ref, "u": wu_ref, "d": wd_ref}, sems)
+        weights_of("pud")
         dwp_ref[...] = jnp.zeros_like(dwp_ref)
         dwu_ref[...] = jnp.zeros_like(dwu_ref)
         dwd_ref[...] = jnp.zeros_like(dwd_ref)
@@ -333,7 +339,7 @@
         emit(lay, lay.second, {"p": dwp_ref, "u": dwu_ref, "d": dwd_ref}, keep_ref, give_ref)
 
 
-def call_mlp(lay, mine, other, x, ot, cot, vrow):
+def call_mlp(lay, slots, x, ot, cot, vrow):
     b, t, d = x.shape
     ff = lay.ff
     n = 2 if b % 2 == 0 else 1
@@ -349,12 +355,12 @@
                S((n * t, d), bf16), S((n * t, d), f32), S((n * t, 1), f32), S((n * t, ff), bf16)]
     return pl.pallas_call(
         functools.partial(mlp, lay, b // n), grid=(b // n,),
-        in_specs=[HBM, HBM, some(t, d), some(d, t), some(t, d), full(vrow)],
+        in_specs=[HBM] * 4 + [some(t, d), some(d, t), some(t, d), full(vrow)],
         out_specs=[some(t, d), some(t, ff), some(t, d), some(d, t)] + [full(a) for a in acc],
         out_shape=outs,
         scratch_shapes=[pltpu.VMEM(a.shape, a.dtype) for a in scratch] + [pltpu.SemaphoreType.DMA((n_copies,))],
         compiler_params=params(MLP_MIB), cost_estimate=cost(24), name="mlp",
-    )(mine, other, x, ot, cot, vrow)
+    )(*slots, x, ot, cot, vrow)
 
 
 def attn_bwd_image(jt_ref, e_ref, il_ref, ot_ref, dot_ref, h_ref, dj_ref, dw_ref):
@@ -619,6 +625,13 @@
     def core(self):
         return self.held, self.links.core(self.held)
 
+    def last(self):
+        self.got = self.links.step(self.held, self.k)
+        self.other = self.links.core(self.held)
+
+    def slots(self):
+        return self.held, self.got, self.other, self.links.core(self.got)
+
 
 class Reduce:
     def __init__(self, links, keep, give):
@@ -646,6 +659,13 @@
 
     def round(self, *beside):
         pass
+
+    def last(self):
+        self.got = None
+
+    def slots(self):
+        half = self.held.shape[0] // 2
+        return self.held[:half], self.held[half:], self.other[:half], self.other[half:]
 
     def others(self):
         pass
@@ -705,19 +725,22 @@
     one.round()
     two.held = after(two.held, one.held)
     two.round()
-    for _ in range(rounds - 1):
+    for _ in range(rounds - 2):
         one.round()
-    one.held, two.held = lax.optimization_barrier((one.held, two.held))
-    first = one.core()
-    *outs, wq, vrow, vcol = call_attn_fwd_first(lay, *first, x, k)
+    one.last()
+    if one.got is not None:
+        one.got, two.held = lax.optimization_barrier((one.got, two.held))
+    first = one.slots()
+    *outs, wq, vrow, vcol = call_attn_fwd_first(lay, first, x, k)
     for _ in range(rounds - 2):
         two.round(vcol)
     *outs, two.held = lax.optimization_barrier((*outs, two.held))
     jt, e, il, ot, h = call_attn_fwd_rest(x, wq, vrow, vcol, outs, k, b - k)
-    two.round()
-    ot, two.held = lax.optimization_barrier((ot, two.held))
-    second = two.core()
-    mid, act, dm, dot_, wd, dv, keep, give = call_mlp(lay, *second, x, ot, cot, vrow)
+    two.last()
+    if two.got is not None:
+        ot, two.got = lax.optimization_barrier((ot, two.got))
+    second = two.slots()
+    mid, act, dm, dot_, wd, dv, keep, give = call_mlp(lay, second, x, ot, cot, vrow)
     down = reduce(keep, give)
     acts = (jt, e, il, ot, dot_, h)
     dj, dw = call_attn_bwd_first(acts, BACK_IMAGES)
@@ -734,14 +757,14 @@
     gx = call_input_end(x, dm, dj, wq, vrow)
     gx, up.held = lax.optimization_barrier((gx, up.held))
     lo = call_layer_end(after(mid, gx), act, wd, vrow)
-    up.round()
-    lo, up.held = lax.optimization_barrier((lo, up.held))
+    up.round(lo, down.held)
+    down.round()
     for _ in range(rounds - 2):
-        up.round()
-    down.round()
+        up.round(down.held)
     down.others()
+    up.others()
+    up.held, down.held = lax.optimization_barrier((up.held, down.held))
     second_new = finish_second(*down.finish())
-    up.others()
     return lo, gx, up.finish(), second_new
 
 

time: 127 us -> 125 us (0.984)
    concatenate x6 -> x4, other arithmetic: 3.8 us -> 2.75 us  [round(): self.held = jnp.concatenate([after(self.held, *beside), got], axis=0)]
    ppermute x20 -> x22, starting transfers between devices: 30.3 us -> 29.3 us  [permute(): return lax.ppermute(value, ('narrow', 'wide'), pairs)]
    ppermute x20 -> x22, waiting for transfers between devices: 28.3 us -> 27.5 us  [permute(): return lax.ppermute(value, ('narrow', 'wide'), pairs)]
  transfers between devices with their start and end apart: 20 -> 22, of which waited for: 14 -> 15; matrix products, arithmetic and copies ran while one was open for 2% -> 2% of each run, Pallas kernels for 26% -> 26%
where the time goes in v5:
time: 125 us; the launch traced here: 124 us
  Pallas kernels  60.9 us (49%)
  starting transfers between devices  29.3 us (23%)
  waiting for transfers between devices  27.5 us (22%)
  other arithmetic  3.5 us (3%)
  local copies, waits for them, and re-layouts  2.1 us (2%)
    ppermute x22, starting transfers between devices, permute(): return lax.ppermute(value, ('narrow', 'wide'), pairs)  29.3 us
    ppermute x22, waiting for transfers between devices, permute(): return lax.ppermute(value, ('narrow', 'wide'), pairs)  27.5 us
    pallas_call x1, Pallas kernels, call_mlp(): pl.pallas_call(functools.partial(mlp, lay, b // n), grid=(b // n,), in_sp...  24.2 us
    pallas_call x1, Pallas kernels, call_attn_bwd_last(): pl.pallas_call(functools.partial(attn_bwd_last, lay, count), grid=(count,...  8.68 us
    pallas_call x1, Pallas kernels, call_attn_fwd_first(): pl.pallas_call(functools.partial(attn_fwd_first, lay), grid=(count,), in_...  7.09 us
    pallas_call x1, Pallas kernels, call_attn_fwd_rest(): pl.pallas_call(attn_fwd_rest, grid=(count,), in_specs=[one(t, d, off=off)...  4.93 us
    pallas_call x1, Pallas kernels, call_input_end(): pl.pallas_call(input_end, grid=(b,), in_specs=[one(t, d), one(t, d), one(...  4.31 us
    pallas_call x1, Pallas kernels, call_layer_end(): pl.pallas_call(layer_end, grid=(b,), in_specs=[one(t, d), one(t, act.shap...  4.07 us
  transfers between devices with their start and end apart: 22, of which 15 were waited for; matrix products, arithmetic and copies ran while one was open for 2% of the time, Pallas kernels for 26%

profile of v5, /device:TPU:0, one launch (start us, length us, event | category | flops | bytes accessed | tf_op | source)
XLA Modules:
  0.0 124.5 jit_solution(16907543362935702312)
XLA Ops:
  0.7 2.0 %pack.1 = (bf16[80,384]{1,0:T(8,128)(2,1)}, bf16[224,384]{1,0:T(8,128)(2,1)}) custom-call(f32[144,384]{1,0:T(8,128)} %refs_0_.2, f32[48,384]{1,0:T(8,128)} %refs_0_.3, f32[192,384]{1,0:T(8,128)} %refs_3_.3, f32[48,1536]{1,0:T(8,128)} %refs_6_.1, f32[576]{0:T(1024)} %refs_3_.2), custom_call_target="tpu_custom_call" | custom-call | tf_op jit(solution)/shard_map/pack/pallas_call | solution.py:119
  2.6 4.1 %collective-permute-start = (bf16[1,80,384]{2,1,0:T(8,128)(2,1)}, bf16[1,80,384]{2,1,0:T(8,128)(2,1)S(1)}, u32[]{:S(2)}, u32[]{:S(2)}) collective-permute-start(bf16[1,80,384]{2,1,0:T(8,128)(2,1)} %bitcast.11), channel_id=1, source_target_pairs={{0,4},{1,5},{2,6},{3,7},{4,0},{5,1},{6,2},{7,3},{8,9},{9,8},{10,11... | collective-permute-start | bytes 184328 | tf_op jit(solution)/shard_map/ppermute | solution.py:559
  6.7 2.4 %collective-permute-done = bf16[1,80,384]{2,1,0:T(8,128)(2,1)S(1)} collective-permute-done((bf16[1,80,384]{2,1,0:T(8,128)(2,1)}, bf16[1,80,384]{2,1,0:T(8,128)(2,1)S(1)}, u32[]{:S(2)}, u32[]{:S(2)}) %collective-permute-start) | collective-permute-done | bytes 61472 | tf_op jit(solution)/shard_map/ppermute | solution.py:559
  9.2 0.8 pad_maximum_fusion.3
  10.0 2.0 %collective-permute-start.1 = (bf16[2,80,384]{2,1,0:T(8,128)(2,1)S(1)}, bf16[2,80,384]{2,1,0:T(8,128)(2,1)S(1)}, u32[]{:S(2)}, u32[]{:S(2)}) collective-permute-start(bf16[2,80,384]{2,1,0:T(8,128)(2,1)S(1)} %pad_maximum_fusion.3), channel_id=1, source_target_pairs={{0,2},{1,3},{2,0},{3,1},{4,6},{5,7},{6,4},{7,5},{8,12},{9,13},{10,... | collective-permute-start | bytes 368648 | tf_op jit(solution)/shard_map/ppermute | solution.py:559
  12.0 3.1 %collective-permute-start.3 = (bf16[1,224,384]{2,1,0:T(8,128)(2,1)}, bf16[1,224,384]{2,1,0:T(8,128)(2,1)S(1)}, u32[]{:S(2)}, u32[]{:S(2)}) collective-permute-start(bf16[1,224,384]{2,1,0:T(8,128)(2,1)} %bitcast.14), channel_id=1, source_target_pairs={{0,4},{1,5},{2,6},{3,7},{4,0},{5,1},{6,2},{7,3},{8,9},{9,8},{10,11... | collective-permute-start | bytes 516104 | tf_op jit(solution)/shard_map/ppermute | solution.py:559
  15.1 0.9 pad_maximum_fusion.2.mine_a
  16.0 1.9 %collective-permute-start.2 = (bf16[4,80,384]{2,1,0:T(8,128)(2,1)S(1)}, bf16[4,80,384]{2,1,0:T(8,128)(2,1)S(1)}, u32[]{:S(2)}, u32[]{:S(2)}) collective-permute-start(bf16[4,80,384]{2,1,0:T(8,128)(2,1)S(1)} %pad_maximum_fusion.2.mine_a), channel_id=1, source_target_pairs={{0,1},{1,0},{2,3},{3,2},{4,5},{5,4},{6,7},{7,6},{8,10},{9,11},{10,... | collective-permute-start | bytes 737288 | tf_op jit(solution)/shard_map/ppermute | solution.py:559
  17.9 2.7 %collective-permute-done.3 = bf16[1,224,384]{2,1,0:T(8,128)(2,1)S(1)} collective-permute-done((bf16[1,224,384]{2,1,0:T(8,128)(2,1)}, bf16[1,224,384]{2,1,0:T(8,128)(2,1)S(1)}, u32[]{:S(2)}, u32[]{:S(2)}) %collective-permute-start.3) | collective-permute-done | bytes 172064 | tf_op jit(solution)/shard_map/ppermute | solution.py:559
  20.7 1.0 pad_maximum_fusion.1
  21.6 0.6 collective-permute-done.2.mine_b
  22.2 1.7 %collective-permute-start.6 = (bf16[2,224,384]{2,1,0:T(8,128)(2,1)S(1)}, bf16[2,224,384]{2,1,0:T(8,128)(2,1)S(1)}, u32[]{:S(2)}, u32[]{:S(2)}) collective-permute-start(bf16[2,224,384]{2,1,0:T(8,128)(2,1)S(1)} %pad_maximum_fusion.1), channel_id=1, source_target_pairs={{0,2},{1,3},{2,0},{3,1},{4,6},{5,7},{6,4},{7,5},{8,12},{9,13},{10,... | collective-permute-start | bytes 1032200 | tf_op jit(solution)/shard_map/ppermute | solution.py:559
  24.0 1.7 %copy-done.6 = f32[4,384,384]{2,1,0:T(8,128)S(1)} copy-done((f32[4,384,384]{2,1,0:T(8,128)S(1)}, f32[4,384,384]{2,1,0:T(8,128)}, u32[]{:S(2)}) %copy-start.6) | copy-done | bytes 2359320
  25.7 7.1 %attn_fwd_first.1 = (bf16[4,1152,384]{2,1,0:T(8,128)(2,1)S(1)}, bf16[4,6,384,384]{3,2,1,0:T(8,128)(2,1)S(1)}, f32[4,8,384]{2,1,0:T(8,128)S(1)}, bf16[4,384,384]{...) custom-call(bf16[4,80,384]{2,1,0:T(8,128)(2,1)S(1)} %pad_maximum_fus, ...), custom_call_target="tpu_custom_call" | custom-call | flops 8000000000 | bytes 1048576 | tf_op jit(solution)/shard_map/attn_fwd_first/pallas_call | solution.py:238
  32.8 0.4 collective-permute-done.6
  33.2 0.1 pad_maximum_fusion.mine_a
  33.3 1.0 collective-permute-start.8
  34.3 1.5 %collective-permute-start.7 = (bf16[4,224,384]{2,1,0:T(8,128)(2,1)S(1)}, bf16[4,224,384]{2,1,0:T(8,128)(2,1)S(1)}, u32[]{:S(2)}, u32[]{:S(2)}) collective-permute-start(bf16[4,224,384]{2,1,0:T(8,128)(2,1)S(1)} %pad_maximum_fusion.mine_a), channel_id=1, source_target_pairs={{0,1},{1,0},{2,3},{3,2},{4,5},{5,4},{6,7},{7,6},{8,10},{9,11},{10,... | collective-permute-start | bytes 2064392 | tf_op jit(solution)/shard_map/ppermute | solution.py:559
  35.8 4.9 %attn_fwd_rest.1 = (bf16[4,1152,384]{2,1,0:T(8,128)(2,1)S(1)}, bf16[4,6,384,384]{3,2,1,0:T(8,128)(2,1)S(1)}, f32[4,8,384]{2,1,0:T(8,128)S(1)}, bf16[4,384,384]{2,1,0:T(8,128)(2,1)S(1)}, bf16[4,384,384]{2,1,0:T(8,128)(2,1)S(1)}) custom-call(f32[4,384,384]{2,1,0:T(8,128)S(1)} %copy-done.7, ...), custom_call_target="tpu_custom_call", output_to_operand_aliasing={{0}: (4, {}), {1}: (5, {}), {2}: (6, {}), {3}: (7, {}), {4}... | custom-call | flops 8000000000 | bytes 1048576 | tf_op jit(solution)/shard_map/attn_fwd_rest/pallas_call | solution.py:250
  40.7 4.5 %collective-permute-done.7.mine_b = bf16[4,224,384]{2,1,0:T(8,128)(2,1)S(1)} collective-permute-done((bf16[4,224,384]{2,1,0:T(8,128)(2,1)S(1)}, bf16[4,224,384]{2,1,0:T(8,128)(2,1)S(1)}, u32[]{:S(2)}, u32[]{:S(2)}) %collective-permute-start.7) | collective-permute-done | bytes 688160 | tf_op jit(solution)/shard_map/ppermute | solution.py:559
  45.2 0.6 collective-permute-start.9
  45.8 1.8 %collective-permute-done.9.other_b = bf16[4,224,384]{2,1,0:T(8,128)(2,1)S(1)} collective-permute-done((bf16[4,224,384]{2,1,0:T(8,128)(2,1)S(1)}, bf16[4,224,384]{2,1,0:T(8,128)(2,1)S(1)}, u32[]{:S(2)}, u32[]{:S(2)}) %collective-permute-start.9) | collective-permute-done | bytes 688160 | tf_op jit(solution)/shard_map/ppermute | solution.py:559
  47.6 24.2 %mlp.1 = (f32[4,384,384]{2,1,0:T(8,128)}, bf16[4,384,1536]{2,1,0:T(8,128)(2,1)}, f32[4,384,384]{2,1,0:T(8,128)}, bf16[4,384,384]{2,1,0:T(8,128)(2,1)S(1)}, bf16[...) custom-call(bf16[4,224,384]{2,1,0:T(8,128)(2,1)S(1)} %pad_maximum_fu, ...), custom_call_target="tpu_custom_call" | custom-call | flops 24000000000 | bytes 1048576 | tf_op jit(solution)/shard_map/mlp/pallas_call | solution.py:356
  71.8 0.5 collective-permute-start.10
  72.3 2.6 %attn_bwd_first.1 = (bf16[4,1152,384]{2,1,0:T(8,128)(2,1)S(1)}, f32[1152,512]{1,0:T(8,128)S(1)}) custom-call(bf16[4,1152,384]{2,1,0:T(8,128)(2,1)S(1)} %get-tuple-element.122.jt_ref, bf16[4,6,384,384]{3,2,1,0:T(8,128)(2,1)S(1)} %get-tuple-element.123.e_ref, f32[4,8,384]{2,1,0:T(8,128)S(1)} %get-tuple-element.124.il_ref, ...), custom_call_target="tpu_custom_call" | custom-call | flops 4000000000 | bytes 1048576 | tf_op jit(solution)/shard_map/attn_bwd_first/pallas_call | solution.py:432
  74.9 0.2 collective-permute-done.10
  75.1 0.3 convert_add_fusion
  75.3 0.1 slice.71
  75.4 1.6 %collective-permute-start.11 = (bf16[4,224,384]{2,1,0:T(8,128)(2,1)S(1)}, bf16[4,224,384]{2,1,0:T(8,128)(2,1)S(1)}, u32[]{:S(2)}, u32[]{:S(2)}) collective-permute-start(bf16[4,224,384]{2,1,0:T(8,128)(2,1)S(1)} %slice.71), channel_id=1, source_target_pairs={{0,1},{1,0},{2,3},{3,2},{4,5},{5,4},{6,7},{7,6},{8,10},{9,11},{10,... | collective-permute-start | bytes 2064392 | tf_op jit(solution)/shard_map/ppermute | solution.py:559
  77.0 8.7 %attn_bwd_last.1 = (bf16[4,1152,384]{2,1,0:T(8,128)(2,1)S(1)}, bf16[8,80,384]{2,1,0:T(8,128)(2,1)S(1)}, bf16[8,80,384]{2,1,0:T(8,128)(2,1)S(1)}) custom-call(bf16[4,1152,384]{2,1,0:T(8,128)(2,1)S(1)} %get-tuple-element.122.jt_ref, bf16[4,6,384,384]{3,2,1,0:T(8,128)(2,1)S(1)} %get-tuple-element.123.e_ref, ...), custom_call_target="tpu_custom_call", output_to_operand_aliasing={{0}: (10, {})} | custom-call | flops 14000000000 | bytes 1048576 | tf_op jit(solution)/shard_map/attn_bwd_last/pallas_call | solution.py:442
  85.7 1.6 %collective-permute-start.12 = (bf16[8,80,384]{2,1,0:T(8,128)(2,1)S(1)}, bf16[8,80,384]{2,1,0:T(8,128)(2,1)S(1)}, u32[]{:S(2)}, u32[]{:S(2)}) collective-permute-start(bf16[8,80,384]{2,1,0:T(8,128)(2,1)S(1)} %get-tuple-element.139), channel_id=1, source_target_pairs={{0,8},{1,9},{2,10},{3,11},{4,12},{5,13},{6,14},{7,15},{8,0},{9,1},... | collective-permute-start | bytes 1474568 | tf_op jit(solution)/shard_map/ppermute | solution.py:559
  87.3 0.1 slice.42
  87.4 0.1 convert_add_fusion.1
  87.6 0.0 copy-start.18
  87.6 1.2 collective-permute-done.12
  88.8 0.1 convert_add_fusion.2
  89.0 1.6 %collective-permute-start.13 = (bf16[4,80,384]{2,1,0:T(8,128)(2,1)S(1)}, bf16[4,80,384]{2,1,0:T(8,128)(2,1)S(1)}, u32[]{:S(2)}, u32[]{:S(2)}) collective-permute-start(bf16[4,80,384]{2,1,0:T(8,128)(2,1)S(1)} %slice.73), channel_id=1, source_target_pairs={{0,1},{1,0},{2,3},{3,2},{4,5},{5,4},{6,7},{7,6},{8,10},{9,11},{10,... | collective-permute-start | bytes 737288 | tf_op jit(solution)/shard_map/ppermute | solution.py:559
  90.5 0.9 collective-permute-start.14
  91.5 4.3 %input_end.1 = f32[4,384,384]{2,1,0:T(8,128)} custom-call(f32[4,384,384]{2,1,0:T(8,128)S(1)} %copy-done.7, f32[4,384,384]{2,1,0:T(8,128)S(1)} %copy-done.18, bf16[4,1152,384]{2,1,0:T(8,128)(2,1)S(1)} %get-tuple-element.140.dj_ref, bf16[1152,384]{1,0:T(8,128)(2,1)S(1)} %get-tuple-element.110.w_ref, f32[16,384]{1,0:T(8,128)S(1)} %get-tuple-element.111.vrow_ref), custom_call_target="tpu_custom_call" | custom-call | flops 4000000000 | bytes 1048576 | tf_op jit(solution)/shard_map/input_end/pallas_call | solution.py:476
  95.9 1.4 %collective-permute-start.15 = (bf16[2,80,384]{2,1,0:T(8,128)(2,1)S(1)}, bf16[2,80,384]{2,1,0:T(8,128)(2,1)S(1)}, u32[]{:S(2)}, u32[]{:S(2)}) collective-permute-start(bf16[2,80,384]{2,1,0:T(8,128)(2,1)S(1)} %slice.75), channel_id=1, source_target_pairs={{0,2},{1,3},{2,0},{3,1},{4,6},{5,7},{6,4},{7,5},{8,12},{9,13},{10,... | collective-permute-start | bytes 368648 | tf_op jit(solution)/shard_map/ppermute | solution.py:559
  97.3 4.1 %layer_end.1 = f32[4,384,384]{2,1,0:T(8,128)} custom-call(f32[4,384,384]{2,1,0:T(8,128)S(1)} %copy-done.19, bf16[4,384,1536]{2,1,0:T(8,128)(2,1)S(1)} %bitcast.9, bf16[384,1536]{1,0:T(8,128)(2,1)S(1)} %copy-done.20, f32[16,384]{1,0:T(8,128)S(1)} %get-tuple-element.111.vrow_ref), custom_call_target="tpu_custom_call" | custom-call | flops 4000000000 | bytes 1048576 | tf_op jit(solution)/shard_map/layer_end/pallas_call | solution.py:458
  101.4 0.0 copy-start.16
  101.4 0.0 copy-start.17
  101.4 0.6 collective-permute-done.14
  102.0 0.1 convert_add_fusion.3
  102.1 1.6 %collective-permute-start.16 = (bf16[1,224,384]{2,1,0:T(8,128)(2,1)S(1)}, bf16[1,224,384]{2,1,0:T(8,128)(2,1)S(1)}, u32[]{:S(2)}, u32[]{:S(2)}) collective-permute-start(bf16[1,224,384]{2,1,0:T(8,128)(2,1)S(1)} %slice.74), channel_id=1, source_target_pairs={{0,4},{1,5},{2,6},{3,7},{4,0},{5,1},{6,2},{7,3},{8,9},{9,8},{10,11... | collective-permute-start | bytes 516104 | tf_op jit(solution)/shard_map/ppermute | solution.py:559
  103.7 0.9 collective-permute-done.15
  104.7 1.5 %collective-permute-start.17 = (bf16[1,80,384]{2,1,0:T(8,128)(2,1)S(1)}, bf16[1,80,384]{2,1,0:T(8,128)(2,1)S(1)}, u32[]{:S(2)}, u32[]{:S(2)}) collective-permute-start(bf16[1,80,384]{2,1,0:T(8,128)(2,1)S(1)} %slice.76), channel_id=1, source_target_pairs={{0,4},{1,5},{2,6},{3,7},{4,0},{5,1},{6,2},{7,3},{8,9},{9,8},{10,11... | collective-permute-start | bytes 184328 | tf_op jit(solution)/shard_map/ppermute | solution.py:559
  106.2 4.8 %collective-permute-done.16 = bf16[1,224,384]{2,1,0:T(8,128)(2,1)S(1)} collective-permute-done((bf16[1,224,384]{2,1,0:T(8,128)(2,1)S(1)}, bf16[1,224,384]{2,1,0:T(8,128)(2,1)S(1)}, u32[]{:S(2)}, u32[]{:S(2)}) %collective-permute-start.16) | collective-permute-done | bytes 172064 | tf_op jit(solution)/shard_map/ppermute | solution.py:559
  111.0 0.6 collective-permute-done.17
  111.7 1.6 %collective-permute-start.18 = (bf16[80,384]{1,0:T(8,128)(2,1)S(1)}, bf16[80,384]{1,0:T(8,128)(2,1)S(1)}, u32[]{:S(2)}, u32[]{:S(2)}) collective-permute-start(bf16[80,384]{1,0:T(8,128)(2,1)S(1)} %fusion), channel_id=1, source_target_pairs={{0,16},{1,17},{2,18},{3,19},{4,20},{5,21},{6,22},{7,23},{8,24},{9,... | collective-permute-start | bytes 184328 | tf_op jit(solution)/shard_map/ppermute | solution.py:559
  113.3 0.5 collective-permute-start.19
  113.8 2.2 %collective-permute-done.18 = bf16[80,384]{1,0:T(8,128)(2,1)S(1)} collective-permute-done((bf16[80,384]{1,0:T(8,128)(2,1)S(1)}, bf16[80,384]{1,0:T(8,128)(2,1)S(1)}, u32[]{:S(2)}, u32[]{:S(2)}) %collective-permute-start.18) | collective-permute-done | bytes 61472 | tf_op jit(solution)/shard_map/ppermute | solution.py:559
  116.0 3.7 %collective-permute-done.19 = bf16[224,384]{1,0:T(8,128)(2,1)S(1)} collective-permute-done((bf16[224,384]{1,0:T(8,128)(2,1)S(1)}, bf16[224,384]{1,0:T(8,128)(2,1)S(1)}, u32[]{:S(2)}, u32[]{:S(2)}) %collective-permute-start.19) | collective-permute-done | bytes 172064 | tf_op jit(solution)/shard_map/ppermute | solution.py:559
  119.7 0.0 copy-start
  119.8 0.0 copy-start.8
  119.8 0.0 copy-start.9
  119.8 0.0 copy-start.11
  119.8 0.0 copy-start.14
  119.8 0.1 collective-permute-start.20
  119.9 0.5 collective-permute-start.21
  120.4 0.8 collective-permute-done.20.other_ref
  121.3 1.2 adam.2
  122.6 1.9 %adam.3 = (f32[48,384]{1,0:T(8,128)}, f32[48,384]{1,0:T(8,128)}, f32[48,384]{1,0:T(8,128)}, bf16[48,384]{1,0:T(8,128)(2,1)}, f32[192,384]{1,0:T(8,128)}, /*index...) custom-call(f32[224,384]{1,0:T(8,128)S(1)} %convert_add_fusion.5.min, ...), custom_call_target="tpu_custom_call" | custom-call | flops 3000000000 | bytes 1048576 | tf_op jit(solution)/shard_map/adam/pallas_call | solution.py:527
  (64 shorter events, 0.4 us)
Async XLA Ops:
  2.6 6.5 %collective-permute-start = (bf16[1,80,384]{2,1,0:T(8,128)(2,1)}, bf16[1,80,384]{2,1,0:T(8,128)(2,1)S(1)}, u32[]{:S(2)}, u32[]{:S(2)}) collective-permute-start(bf16[1,80,384]{2,1,0:T(8,128)(2,1)} %bitcast.11), channel_id=1, source_target_pairs={{0,4},{1,5},{2,6},{3,7},{4,0},{5,1},{6,2},{7,3},{8,9},{9,8},{10,11... | collective-permute-start | bytes 184328 | tf_op jit(solution)/shard_map/ppermute | solution.py:559
  10.0 5.1 %collective-permute-start.1 = (bf16[2,80,384]{2,1,0:T(8,128)(2,1)S(1)}, bf16[2,80,384]{2,1,0:T(8,128)(2,1)S(1)}, u32[]{:S(2)}, u32[]{:S(2)}) collective-permute-start(bf16[2,80,384]{2,1,0:T(8,128)(2,1)S(1)} %pad_maximum_fusion.3), channel_id=1, source_target_pairs={{0,2},{1,3},{2,0},{3,1},{4,6},{5,7},{6,4},{7,5},{8,12},{9,13},{10,... | collective-permute-start | bytes 368648 | tf_op jit(solution)/shard_map/ppermute | solution.py:559
  12.0 8.7 %collective-permute-start.3 = (bf16[1,224,384]{2,1,0:T(8,128)(2,1)}, bf16[1,224,384]{2,1,0:T(8,128)(2,1)S(1)}, u32[]{:S(2)}, u32[]{:S(2)}) collective-permute-start(bf16[1,224,384]{2,1,0:T(8,128)(2,1)} %bitcast.14), channel_id=1, source_target_pairs={{0,4},{1,5},{2,6},{3,7},{4,0},{5,1},{6,2},{7,3},{8,9},{9,8},{10,11... | collective-permute-start | bytes 516104 | tf_op jit(solution)/shard_map/ppermute | solution.py:559
  16.0 6.3 %collective-permute-start.2 = (bf16[4,80,384]{2,1,0:T(8,128)(2,1)S(1)}, bf16[4,80,384]{2,1,0:T(8,128)(2,1)S(1)}, u32[]{:S(2)}, u32[]{:S(2)}) collective-permute-start(bf16[4,80,384]{2,1,0:T(8,128)(2,1)S(1)} %pad_maximum_fusion.2.mine_a), channel_id=1, source_target_pairs={{0,1},{1,0},{2,3},{3,2},{4,5},{5,4},{6,7},{7,6},{8,10},{9,11},{10,... | collective-permute-start | bytes 737288 | tf_op jit(solution)/shard_map/ppermute | solution.py:559
  17.9 6.1 %collective-permute-start.4 = (bf16[4,80,384]{2,1,0:T(8,128)(2,1)S(1)}, bf16[4,80,384]{2,1,0:T(8,128)(2,1)S(1)}, u32[]{:S(2)}, u32[]{:S(2)}) collective-permute-start(bf16[4,80,384]{2,1,0:T(8,128)(2,1)S(1)} %pad_maximum_fusion.2.mine_a), channel_id=1, source_target_pairs={{0,8},{1,9},{2,10},{3,11},{4,12},{5,13},{6,14},{7,15},{8,0},{9,1},... | collective-permute-start | bytes 737288 | tf_op jit(solution)/shard_map/ppermute | solution.py:559
  22.2 1.8 %collective-permute-start.5 = (bf16[4,80,384]{2,1,0:T(8,128)(2,1)S(1)}, bf16[4,80,384]{2,1,0:T(8,128)(2,1)S(1)}, u32[]{:S(2)}, u32[]{:S(2)}) collective-permute-start(bf16[4,80,384]{2,1,0:T(8,128)(2,1)S(1)} %collective-permute-done.2.mine_b), channel_id=1, source_target_pairs={{0,8},{1,9},{2,10},{3,11},{4,12},{5,13},{6,14},{7,15},{8,0},{9,1},... | collective-permute-start | bytes 737288 | tf_op jit(solution)/shard_map/ppermute | solution.py:559
  22.2 10.9 %collective-permute-start.6 = (bf16[2,224,384]{2,1,0:T(8,128)(2,1)S(1)}, bf16[2,224,384]{2,1,0:T(8,128)(2,1)S(1)}, u32[]{:S(2)}, u32[]{:S(2)}) collective-permute-start(bf16[2,224,384]{2,1,0:T(8,128)(2,1)S(1)} %pad_maximum_fusion.1), channel_id=1, source_target_pairs={{0,2},{1,3},{2,0},{3,1},{4,6},{5,7},{6,4},{7,5},{8,12},{9,13},{10,... | collective-permute-start | bytes 1032200 | tf_op jit(solution)/shard_map/ppermute | solution.py:559
  24.0 1.7 %copy-start.6 = (f32[4,384,384]{2,1,0:T(8,128)S(1)}, f32[4,384,384]{2,1,0:T(8,128)}, u32[]{:S(2)}) copy-start(f32[4,384,384]{2,1,0:T(8,128)} %x_ref.7) | copy-start | bytes 7077892
  25.7 10.1 %copy-start.7 = (f32[4,384,384]{2,1,0:T(8,128)S(1)}, f32[4,384,384]{2,1,0:T(8,128)}, u32[]{:S(2)}) copy-start(f32[4,384,384]{2,1,0:T(8,128)} %x_ref.7) | copy-start | bytes 7077892
  33.3 12.6 %collective-permute-start.8 = (bf16[4,224,384]{2,1,0:T(8,128)(2,1)S(1)}, bf16[4,224,384]{2,1,0:T(8,128)(2,1)S(1)}, u32[]{:S(2)}, u32[]{:S(2)}) collective-permute-start(bf16[4,224,384]{2,1,0:T(8,128)(2,1)S(1)} %pad_maximum_fusion.mine_a), channel_id=1, source_target_pairs={{0,8},{1,9},{2,10},{3,11},{4,12},{5,13},{6,14},{7,15},{8,0},{9,1},... | collective-permute-start | bytes 2064392 | tf_op jit(solution)/shard_map/ppermute | solution.py:559
  34.3 10.9 %collective-permute-start.7 = (bf16[4,224,384]{2,1,0:T(8,128)(2,1)S(1)}, bf16[4,224,384]{2,1,0:T(8,128)(2,1)S(1)}, u32[]{:S(2)}, u32[]{:S(2)}) collective-permute-start(bf16[4,224,384]{2,1,0:T(8,128)(2,1)S(1)} %pad_maximum_fusion.mine_a), channel_id=1, source_target_pairs={{0,1},{1,0},{2,3},{3,2},{4,5},{5,4},{6,7},{7,6},{8,10},{9,11},{10,... | collective-permute-start | bytes 2064392 | tf_op jit(solution)/shard_map/ppermute | solution.py:559
  35.8 11.8 %copy-start.5 = (f32[4,384,384]{2,1,0:T(8,128)S(1)}, f32[4,384,384]{2,1,0:T(8,128)}, u32[]{:S(2)}) copy-start(f32[4,384,384]{2,1,0:T(8,128)} %cot_ref.1) | copy-start | bytes 7077892
  45.2 2.4 %collective-permute-start.9 = (bf16[4,224,384]{2,1,0:T(8,128)(2,1)S(1)}, bf16[4,224,384]{2,1,0:T(8,128)(2,1)S(1)}, u32[]{:S(2)}, u32[]{:S(2)}) collective-permute-start(bf16[4,224,384]{2,1,0:T(8,128)(2,1)S(1)} %collective-permute-done.7.mine_b), channel_id=1, source_target_pairs={{0,8},{1,9},{2,10},{3,11},{4,12},{5,13},{6,14},{7,15},{8,0},{9,1},... | collective-permute-start | bytes 2064392 | tf_op jit(solution)/shard_map/ppermute | solution.py:559
  71.8 3.3 %collective-permute-start.10 = (bf16[8,224,384]{2,1,0:T(8,128)(2,1)S(1)}, bf16[8,224,384]{2,1,0:T(8,128)(2,1)S(1)}, u32[]{:S(2)}, u32[]{:S(2)}) collective-permute-start(bf16[8,224,384]{2,1,0:T(8,128)(2,1)S(1)} %get-tuple-element.130), channel_id=1, source_target_pairs={{0,8},{1,9},{2,10},{3,11},{4,12},{5,13},{6,14},{7,15},{8,0},{9,1},... | collective-permute-start | bytes 4128776 | tf_op jit(solution)/shard_map/ppermute | solution.py:559
  75.4 12.0 %collective-permute-start.11 = (bf16[4,224,384]{2,1,0:T(8,128)(2,1)S(1)}, bf16[4,224,384]{2,1,0:T(8,128)(2,1)S(1)}, u32[]{:S(2)}, u32[]{:S(2)}) collective-permute-start(bf16[4,224,384]{2,1,0:T(8,128)(2,1)S(1)} %slice.71), channel_id=1, source_target_pairs={{0,1},{1,0},{2,3},{3,2},{4,5},{5,4},{6,7},{7,6},{8,10},{9,11},{10,... | collective-permute-start | bytes 2064392 | tf_op jit(solution)/shard_map/ppermute | solution.py:559
  85.7 3.1 %collective-permute-start.12 = (bf16[8,80,384]{2,1,0:T(8,128)(2,1)S(1)}, bf16[8,80,384]{2,1,0:T(8,128)(2,1)S(1)}, u32[]{:S(2)}, u32[]{:S(2)}) collective-permute-start(bf16[8,80,384]{2,1,0:T(8,128)(2,1)S(1)} %get-tuple-element.139), channel_id=1, source_target_pairs={{0,8},{1,9},{2,10},{3,11},{4,12},{5,13},{6,14},{7,15},{8,0},{9,1},... | collective-permute-start | bytes 1474568 | tf_op jit(solution)/shard_map/ppermute | solution.py:559
  87.6 8.2 %copy-start.21 = (f32[4,224,384]{2,1,0:T(8,128)}, f32[4,224,384]{2,1,0:T(8,128)S(1)}, u32[]{:S(2)}) copy-start(f32[4,224,384]{2,1,0:T(8,128)S(1)} %convert_add_fusion.1) | copy-start | bytes 4128772
  87.6 3.9 %copy-start.18 = (f32[4,384,384]{2,1,0:T(8,128)S(1)}, f32[4,384,384]{2,1,0:T(8,128)}, u32[]{:S(2)}) copy-start(f32[4,384,384]{2,1,0:T(8,128)} %get-tuple-element.121.dm_ref) | copy-start | bytes 7077892
  88.8 8.5 %slice-start = ((s8[4718592]{0:T(1024)(128)(4,1)}), s8[4194304]{0:T(1024)(128)(4,1)S(1)}, s32[]{:S(2)}) async-start(s8[4718592]{0:T(1024)(128)(4,1)} %bitcast.8), calls=%async_computation | async-start | bytes 8388608
  89.0 6.8 %collective-permute-start.13 = (bf16[4,80,384]{2,1,0:T(8,128)(2,1)S(1)}, bf16[4,80,384]{2,1,0:T(8,128)(2,1)S(1)}, u32[]{:S(2)}, u32[]{:S(2)}) collective-permute-start(bf16[4,80,384]{2,1,0:T(8,128)(2,1)S(1)} %slice.73), channel_id=1, source_target_pairs={{0,1},{1,0},{2,3},{3,2},{4,5},{5,4},{6,7},{7,6},{8,10},{9,11},{10,... | collective-permute-start | bytes 737288 | tf_op jit(solution)/shard_map/ppermute | solution.py:559
  90.5 11.5 %collective-permute-start.14 = (bf16[2,224,384]{2,1,0:T(8,128)(2,1)S(1)}, bf16[2,224,384]{2,1,0:T(8,128)(2,1)S(1)}, u32[]{:S(2)}, u32[]{:S(2)}) collective-permute-start(bf16[2,224,384]{2,1,0:T(8,128)(2,1)S(1)} %slice.72), channel_id=1, source_target_pairs={{0,2},{1,3},{2,0},{3,1},{4,6},{5,7},{6,4},{7,5},{8,12},{9,13},{10,... | collective-permute-start | bytes 1032200 | tf_op jit(solution)/shard_map/ppermute | solution.py:559
  91.5 5.8 %slice-start.1 = ((s8[4718592]{0:T(1024)(128)(4,1)}), s8[524288]{0:T(1024)(128)(4,1)S(1)}, s32[]{:S(2)}) async-start(s8[4718592]{0:T(1024)(128)(4,1)} %bitcast.8), calls=%async_computation.1 | async-start | bytes 1048576
  91.5 5.8 %copy-start.19 = (f32[4,384,384]{2,1,0:T(8,128)S(1)}, f32[4,384,384]{2,1,0:T(8,128)}, u32[]{:S(2)}) copy-start(f32[4,384,384]{2,1,0:T(8,128)} %get-tuple-element.143.mid_ref) | copy-start | bytes 7077892
  91.5 5.8 %copy-start.20 = (bf16[384,1536]{1,0:T(8,128)(2,1)S(1)}, bf16[384,1536]{1,0:T(8,128)(2,1)}, u32[]{:S(2)}) copy-start(bf16[384,1536]{1,0:T(8,128)(2,1)} %get-tuple-element.145.wd_ref) | copy-start | bytes 3538948
  95.9 8.8 %collective-permute-start.15 = (bf16[2,80,384]{2,1,0:T(8,128)(2,1)S(1)}, bf16[2,80,384]{2,1,0:T(8,128)(2,1)S(1)}, u32[]{:S(2)}, u32[]{:S(2)}) collective-permute-start(bf16[2,80,384]{2,1,0:T(8,128)(2,1)S(1)} %slice.75), channel_id=1, source_target_pairs={{0,2},{1,3},{2,0},{3,1},{4,6},{5,7},{6,4},{7,5},{8,12},{9,13},{10,... | collective-permute-start | bytes 368648 | tf_op jit(solution)/shard_map/ppermute | solution.py:559
  97.3 4.7 %slice-start.2 = ((f32[4,224,384]{2,1,0:T(8,128)}), f32[2,224,384]{2,1,0:T(8,128)S(1)}, s32[]{:S(2)}) async-start(f32[4,224,384]{2,1,0:T(8,128)} %copy-done.21), calls=%async_computation.2 | async-start | bytes 1376256 | tf_op jit(solution)/shard_map/slice | solution.py:647
  101.4 19.9 %copy-start.2 = (f32[144,384]{1,0:T(8,128)S(1)}, f32[144,384]{1,0:T(8,128)}, u32[]{:S(2)}) copy-start(f32[144,384]{1,0:T(8,128)} %refs_0_.2) | copy-start | bytes 663556
  101.4 19.9 %copy-start.4 = (f32[576]{0:T(1024)S(1)}, f32[576]{0:T(1024)}, u32[]{:S(2)}) copy-start(f32[576]{0:T(1024)} %refs_3_.2) | copy-start | bytes 6916
  101.4 19.9 %copy-start.12 = (f32[144,384]{1,0:T(8,128)S(1)}, f32[144,384]{1,0:T(8,128)}, u32[]{:S(2)}) copy-start(f32[144,384]{1,0:T(8,128)} %refs_1_.2) | copy-start | bytes 663556
  101.4 19.9 %copy-start.13 = (f32[144,384]{1,0:T(8,128)S(1)}, f32[144,384]{1,0:T(8,128)}, u32[]{:S(2)}) copy-start(f32[144,384]{1,0:T(8,128)} %refs_2_.2) | copy-start | bytes 663556
  101.4 19.9 %copy-start.16 = (f32[576]{0:T(1024)S(1)}, f32[576]{0:T(1024)}, u32[]{:S(2)}) copy-start(f32[576]{0:T(1024)} %refs_4_.2) | copy-start | bytes 6916
  101.4 19.9 %copy-start.17 = (f32[576]{0:T(1024)S(1)}, f32[576]{0:T(1024)}, u32[]{:S(2)}) copy-start(f32[576]{0:T(1024)} %refs_5_.2) | copy-start | bytes 6916
  102.1 8.9 %collective-permute-start.16 = (bf16[1,224,384]{2,1,0:T(8,128)(2,1)S(1)}, bf16[1,224,384]{2,1,0:T(8,128)(2,1)S(1)}, u32[]{:S(2)}, u32[]{:S(2)}) collective-permute-start(bf16[1,224,384]{2,1,0:T(8,128)(2,1)S(1)} %slice.74), channel_id=1, source_target_pairs={{0,4},{1,5},{2,6},{3,7},{4,0},{5,1},{6,2},{7,3},{8,9},{9,8},{10,11... | collective-permute-start | bytes 516104 | tf_op jit(solution)/shard_map/ppermute | solution.py:559
  104.7 7.0 %collective-permute-start.17 = (bf16[1,80,384]{2,1,0:T(8,128)(2,1)S(1)}, bf16[1,80,384]{2,1,0:T(8,128)(2,1)S(1)}, u32[]{:S(2)}, u32[]{:S(2)}) collective-permute-start(bf16[1,80,384]{2,1,0:T(8,128)(2,1)S(1)} %slice.76), channel_id=1, source_target_pairs={{0,4},{1,5},{2,6},{3,7},{4,0},{5,1},{6,2},{7,3},{8,9},{9,8},{10,11... | collective-permute-start | bytes 184328 | tf_op jit(solution)/shard_map/ppermute | solution.py:559
  111.7 4.3 %collective-permute-start.18 = (bf16[80,384]{1,0:T(8,128)(2,1)S(1)}, bf16[80,384]{1,0:T(8,128)(2,1)S(1)}, u32[]{:S(2)}, u32[]{:S(2)}) collective-permute-start(bf16[80,384]{1,0:T(8,128)(2,1)S(1)} %fusion), channel_id=1, source_target_pairs={{0,16},{1,17},{2,18},{3,19},{4,20},{5,21},{6,22},{7,23},{8,24},{9,... | collective-permute-start | bytes 184328 | tf_op jit(solution)/shard_map/ppermute | solution.py:559
  113.3 6.4 %collective-permute-start.19 = (bf16[224,384]{1,0:T(8,128)(2,1)S(1)}, bf16[224,384]{1,0:T(8,128)(2,1)S(1)}, u32[]{:S(2)}, u32[]{:S(2)}) collective-permute-start(bf16[224,384]{1,0:T(8,128)(2,1)S(1)} %bitcast.10), channel_id=1, source_target_pairs={{0,16},{1,17},{2,18},{3,19},{4,20},{5,21},{6,22},{7,23},{8,24},{9,... | collective-permute-start | bytes 516104 | tf_op jit(solution)/shard_map/ppermute | solution.py:559
  119.7 2.7 %copy-start = (f32[192,384]{1,0:T(8,128)S(1)}, f32[192,384]{1,0:T(8,128)}, u32[]{:S(2)}) copy-start(f32[192,384]{1,0:T(8,128)} %refs_3_.3) | copy-start | bytes 884740
  119.7 2.7 %copy-start.1 = (f32[48,1536]{1,0:T(8,128)S(1)}, f32[48,1536]{1,0:T(8,128)}, u32[]{:S(2)}) copy-start(f32[48,1536]{1,0:T(8,128)} %refs_6_.1) | copy-start | bytes 884740
  119.8 2.7 %copy-start.3 = (f32[48,384]{1,0:T(8,128)S(1)}, f32[48,384]{1,0:T(8,128)}, u32[]{:S(2)}) copy-start(f32[48,384]{1,0:T(8,128)} %refs_0_.3) | copy-start | bytes 221188
  119.8 2.7 %copy-start.8 = (f32[192,384]{1,0:T(8,128)S(1)}, f32[192,384]{1,0:T(8,128)}, u32[]{:S(2)}) copy-start(f32[192,384]{1,0:T(8,128)} %refs_4_.3) | copy-start | bytes 884740
  119.8 2.7 %copy-start.9 = (f32[192,384]{1,0:T(8,128)S(1)}, f32[192,384]{1,0:T(8,128)}, u32[]{:S(2)}) copy-start(f32[192,384]{1,0:T(8,128)} %refs_5_.3) | copy-start | bytes 884740
  119.8 2.7 %copy-start.10 = (f32[48,1536]{1,0:T(8,128)S(1)}, f32[48,1536]{1,0:T(8,128)}, u32[]{:S(2)}) copy-start(f32[48,1536]{1,0:T(8,128)} %refs_7_.1) | copy-start | bytes 884740
  119.8 2.7 %copy-start.11 = (f32[48,1536]{1,0:T(8,128)S(1)}, f32[48,1536]{1,0:T(8,128)}, u32[]{:S(2)}) copy-start(f32[48,1536]{1,0:T(8,128)} %refs_8_.1) | copy-start | bytes 884740
  119.8 2.7 %copy-start.14 = (f32[48,384]{1,0:T(8,128)S(1)}, f32[48,384]{1,0:T(8,128)}, u32[]{:S(2)}) copy-start(f32[48,384]{1,0:T(8,128)} %refs_1_.3) | copy-start | bytes 221188
  119.8 2.7 %copy-start.15 = (f32[48,384]{1,0:T(8,128)S(1)}, f32[48,384]{1,0:T(8,128)}, u32[]{:S(2)}) copy-start(f32[48,384]{1,0:T(8,128)} %refs_2_.3) | copy-start | bytes 221188
  119.8 1.4 %collective-permute-start.20 = (f32[80,384]{1,0:T(8,128)S(1)}, f32[80,384]{1,0:T(8,128)S(1)}, u32[]{:S(2)}, u32[]{:S(2)}) collective-permute-start(f32[80,384]{1,0:T(8,128)S(1)} %convert_add_fusion.7.mine_ref), channel_id=1, source_target_pairs={{0,8},{1,9},{2,10},{3,11},{4,12},{5,13},{6,14},{7,15},{8,0},{9,1},... | collective-permute-start | bytes 368648 | tf_op jit(solution)/shard_map/ppermute | solution.py:559
  119.9 2.5 %collective-permute-start.21 = (f32[224,384]{1,0:T(8,128)S(1)}, f32[224,384]{1,0:T(8,128)S(1)}, u32[]{:S(2)}, u32[]{:S(2)}) collective-permute-start(f32[224,384]{1,0:T(8,128)S(1)} %convert_add_fusion.5.mine_ref), channel_id=1, source_target_pairs={{0,8},{1,9},{2,10},{3,11},{4,12},{5,13},{6,14},{7,15},{8,0},{9,1},... | collective-permute-start | bytes 1032200 | tf_op jit(solution)/shard_map/ppermute | solution.py:559

commit v6 on v5

--- a/solution.py
+++ b/solution.py
@@ -11,7 +11,7 @@
 HEADS = 6
 EPS = 1e-6
 OWNERS = 8
-MLP_MIB = 27
+MLP_MIB = 30
 beta_first = 0.5
 beta_second = 0.5
 adam_eps = 1e-08
@@ -280,8 +280,9 @@
         dwd_ref[...] = jnp.zeros_like(dwd_ref)
         dv_ref[...] = jnp.zeros_like(dv_ref)
 
+    attn = [dot(ot_ref[k], wp_ref[...], 0, 1) for k in range(n)]
     for k, rows in enumerate(images):
-        mid = x_ref[k] + (dot(ot_ref[k], wp_ref[...], 0, 1) + vrow_ref[6:7, :])
+        mid = x_ref[k] + (attn[k] + vrow_ref[6:7, :])
         mid_ref[k] = mid
         xhat, rstd = norm_stats(mid)
         xhat_ref[rows] = xhat
@@ -297,11 +298,12 @@
 
     def hidden(span):
         total = jnp.zeros((1, step), f32)
+        first = [dot(h_ref[rows], wu_ref[span], 1, 1) for rows in images]
+        backs = [dot(g_ref[rows], wd_ref[:, span], 1, 0) for rows in images]
         for k, rows in enumerate(images):
-            u = dot(h_ref[rows], wu_ref[span], 1, 1) + up_bias[:, span]
-            act, slope = gelu_pair(u)
+            act, slope = gelu_pair(first[k] + up_bias[:, span])
             act_ref[k, :, span] = act.astype(bf16)
-            du = dot(g_ref[rows], wd_ref[:, span], 1, 0) * slope
+            du = backs[k] * slope
             du_ref[rows, span] = du.astype(bf16)
             total += jnp.sum(du, axis=0, keepdims=True)
         up_grads.append(total)
@@ -319,8 +321,9 @@
     up_grad = jnp.concatenate(up_grads, axis=1)
     for j in range(cols):
         dv_ref[8 + j:9 + j, :] += up_grad[:, j * d:(j + 1) * d]
+    normed = [dot(du_ref[rows], wu_ref[...], 1, 0) for rows in images]
     for k, rows in enumerate(images):
-        dh2 = dot(du_ref[rows], wu_ref[...], 1, 0)
+        dh2 = normed[k]
         xhat = xhat_ref[rows]
         gy = dh2 * vrow_ref[2:3, :]
         m1 = jnp.mean(gy, axis=-1, keepdims=True)

time: 125 us -> 124 us (level)
  Pallas kernels: 60.9 us -> 59.6 us
    pallas_call x1, Pallas kernels: 24.2 us -> 22.9 us  [call_mlp(): pl.pallas_call(functools.partial(mlp, lay, b // n), grid=(b // n,), in_sp...]
  transfers between devices with their start and end apart: 22 -> 22, of which waited for: 15 -> 15; matrix products, arithmetic and copies ran while one was open for 2% -> 2% of each run, Pallas kernels for 26% -> 27%
where the time goes in v6:
time: 124 us; the launch traced here: 123 us
  Pallas kernels  59.6 us (48%)
  starting transfers between devices  29.3 us (24%)
  waiting for transfers between devices  27.6 us (22%)
  other arithmetic  3.5 us (3%)
  local copies, waits for them, and re-layouts  2.1 us (2%)
    ppermute x22, starting transfers between devices, permute(): return lax.ppermute(value, ('narrow', 'wide'), pairs)  29.3 us
    ppermute x22, waiting for transfers between devices, permute(): return lax.ppermute(value, ('narrow', 'wide'), pairs)  27.6 us
    pallas_call x1, Pallas kernels, call_mlp(): pl.pallas_call(functools.partial(mlp, lay, b // n), grid=(b // n,), in_sp...  22.9 us
    pallas_call x1, Pallas kernels, call_attn_bwd_last(): pl.pallas_call(functools.partial(attn_bwd_last, lay, count), grid=(count,...  8.67 us
    pallas_call x1, Pallas kernels, call_attn_fwd_first(): pl.pallas_call(functools.partial(attn_fwd_first, lay), grid=(count,), in_...  7.09 us
    pallas_call x1, Pallas kernels, call_attn_fwd_rest(): pl.pallas_call(attn_fwd_rest, grid=(count,), in_specs=[one(t, d, off=off)...  4.93 us
    pallas_call x1, Pallas kernels, call_input_end(): pl.pallas_call(input_end, grid=(b,), in_specs=[one(t, d), one(t, d), one(...  4.31 us
    pallas_call x1, Pallas kernels, call_layer_end(): pl.pallas_call(layer_end, grid=(b,), in_specs=[one(t, d), one(t, act.shap...  4.07 us
  transfers between devices with their start and end apart: 22, of which 15 were waited for; matrix products, arithmetic and copies ran while one was open for 2% of the time, Pallas kernels for 27%

profile of v6, /device:TPU:0, one launch (start us, length us, event | category | flops | bytes accessed | tf_op | source)
XLA Modules:
  0.0 123.3 jit_solution(3027697419597528847)
XLA Ops:
  0.7 2.0 %pack.1 = (bf16[80,384]{1,0:T(8,128)(2,1)}, bf16[224,384]{1,0:T(8,128)(2,1)}) custom-call(f32[144,384]{1,0:T(8,128)} %refs_0_.2, f32[48,384]{1,0:T(8,128)} %refs_0_.3, f32[192,384]{1,0:T(8,128)} %refs_3_.3, f32[48,1536]{1,0:T(8,128)} %refs_6_.1, f32[576]{0:T(1024)} %refs_3_.2), custom_call_target="tpu_custom_call" | custom-call | tf_op jit(solution)/shard_map/pack/pallas_call | solution.py:119
  2.6 4.1 %collective-permute-start = (bf16[1,80,384]{2,1,0:T(8,128)(2,1)}, bf16[1,80,384]{2,1,0:T(8,128)(2,1)S(1)}, u32[]{:S(2)}, u32[]{:S(2)}) collective-permute-start(bf16[1,80,384]{2,1,0:T(8,128)(2,1)} %bitcast.11), channel_id=1, source_target_pairs={{0,4},{1,5},{2,6},{3,7},{4,0},{5,1},{6,2},{7,3},{8,9},{9,8},{10,11... | collective-permute-start | bytes 184328 | tf_op jit(solution)/shard_map/ppermute | solution.py:562
  6.7 2.4 %collective-permute-done = bf16[1,80,384]{2,1,0:T(8,128)(2,1)S(1)} collective-permute-done((bf16[1,80,384]{2,1,0:T(8,128)(2,1)}, bf16[1,80,384]{2,1,0:T(8,128)(2,1)S(1)}, u32[]{:S(2)}, u32[]{:S(2)}) %collective-permute-start) | collective-permute-done | bytes 61472 | tf_op jit(solution)/shard_map/ppermute | solution.py:562
  9.2 0.8 pad_maximum_fusion.3
  10.0 2.0 %collective-permute-start.1 = (bf16[2,80,384]{2,1,0:T(8,128)(2,1)S(1)}, bf16[2,80,384]{2,1,0:T(8,128)(2,1)S(1)}, u32[]{:S(2)}, u32[]{:S(2)}) collective-permute-start(bf16[2,80,384]{2,1,0:T(8,128)(2,1)S(1)} %pad_maximum_fusion.3), channel_id=1, source_target_pairs={{0,2},{1,3},{2,0},{3,1},{4,6},{5,7},{6,4},{7,5},{8,12},{9,13},{10,... | collective-permute-start | bytes 368648 | tf_op jit(solution)/shard_map/ppermute | solution.py:562
  12.0 3.1 %collective-permute-start.3 = (bf16[1,224,384]{2,1,0:T(8,128)(2,1)}, bf16[1,224,384]{2,1,0:T(8,128)(2,1)S(1)}, u32[]{:S(2)}, u32[]{:S(2)}) collective-permute-start(bf16[1,224,384]{2,1,0:T(8,128)(2,1)} %bitcast.14), channel_id=1, source_target_pairs={{0,4},{1,5},{2,6},{3,7},{4,0},{5,1},{6,2},{7,3},{8,9},{9,8},{10,11... | collective-permute-start | bytes 516104 | tf_op jit(solution)/shard_map/ppermute | solution.py:562
  15.1 0.9 pad_maximum_fusion.2.mine_a
  16.0 1.9 %collective-permute-start.2 = (bf16[4,80,384]{2,1,0:T(8,128)(2,1)S(1)}, bf16[4,80,384]{2,1,0:T(8,128)(2,1)S(1)}, u32[]{:S(2)}, u32[]{:S(2)}) collective-permute-start(bf16[4,80,384]{2,1,0:T(8,128)(2,1)S(1)} %pad_maximum_fusion.2.mine_a), channel_id=1, source_target_pairs={{0,1},{1,0},{2,3},{3,2},{4,5},{5,4},{6,7},{7,6},{8,10},{9,11},{10,... | collective-permute-start | bytes 737288 | tf_op jit(solution)/shard_map/ppermute | solution.py:562
  17.9 2.7 %collective-permute-done.3 = bf16[1,224,384]{2,1,0:T(8,128)(2,1)S(1)} collective-permute-done((bf16[1,224,384]{2,1,0:T(8,128)(2,1)}, bf16[1,224,384]{2,1,0:T(8,128)(2,1)S(1)}, u32[]{:S(2)}, u32[]{:S(2)}) %collective-permute-start.3) | collective-permute-done | bytes 172064 | tf_op jit(solution)/shard_map/ppermute | solution.py:562
  20.7 1.0 pad_maximum_fusion.1
  21.6 0.6 collective-permute-done.2.mine_b
  22.2 1.7 %collective-permute-start.6 = (bf16[2,224,384]{2,1,0:T(8,128)(2,1)S(1)}, bf16[2,224,384]{2,1,0:T(8,128)(2,1)S(1)}, u32[]{:S(2)}, u32[]{:S(2)}) collective-permute-start(bf16[2,224,384]{2,1,0:T(8,128)(2,1)S(1)} %pad_maximum_fusion.1), channel_id=1, source_target_pairs={{0,2},{1,3},{2,0},{3,1},{4,6},{5,7},{6,4},{7,5},{8,12},{9,13},{10,... | collective-permute-start | bytes 1032200 | tf_op jit(solution)/shard_map/ppermute | solution.py:562
  24.0 1.7 %copy-done.6 = f32[4,384,384]{2,1,0:T(8,128)S(1)} copy-done((f32[4,384,384]{2,1,0:T(8,128)S(1)}, f32[4,384,384]{2,1,0:T(8,128)}, u32[]{:S(2)}) %copy-start.6) | copy-done | bytes 2359320
  25.7 7.1 %attn_fwd_first.1 = (bf16[4,1152,384]{2,1,0:T(8,128)(2,1)S(1)}, bf16[4,6,384,384]{3,2,1,0:T(8,128)(2,1)S(1)}, f32[4,8,384]{2,1,0:T(8,128)S(1)}, bf16[4,384,384]{...) custom-call(bf16[4,80,384]{2,1,0:T(8,128)(2,1)S(1)} %pad_maximum_fus, ...), custom_call_target="tpu_custom_call" | custom-call | flops 8000000000 | bytes 1048576 | tf_op jit(solution)/shard_map/attn_fwd_first/pallas_call | solution.py:238
  32.8 0.4 collective-permute-done.6
  33.2 0.1 pad_maximum_fusion.mine_a
  33.3 1.0 collective-permute-start.8
  34.3 1.5 %collective-permute-start.7 = (bf16[4,224,384]{2,1,0:T(8,128)(2,1)S(1)}, bf16[4,224,384]{2,1,0:T(8,128)(2,1)S(1)}, u32[]{:S(2)}, u32[]{:S(2)}) collective-permute-start(bf16[4,224,384]{2,1,0:T(8,128)(2,1)S(1)} %pad_maximum_fusion.mine_a), channel_id=1, source_target_pairs={{0,1},{1,0},{2,3},{3,2},{4,5},{5,4},{6,7},{7,6},{8,10},{9,11},{10,... | collective-permute-start | bytes 2064392 | tf_op jit(solution)/shard_map/ppermute | solution.py:562
  35.8 4.9 %attn_fwd_rest.1 = (bf16[4,1152,384]{2,1,0:T(8,128)(2,1)S(1)}, bf16[4,6,384,384]{3,2,1,0:T(8,128)(2,1)S(1)}, f32[4,8,384]{2,1,0:T(8,128)S(1)}, bf16[4,384,384]{2,1,0:T(8,128)(2,1)S(1)}, bf16[4,384,384]{2,1,0:T(8,128)(2,1)S(1)}) custom-call(f32[4,384,384]{2,1,0:T(8,128)S(1)} %copy-done.7, ...), custom_call_target="tpu_custom_call", output_to_operand_aliasing={{0}: (4, {}), {1}: (5, {}), {2}: (6, {}), {3}: (7, {}), {4}... | custom-call | flops 8000000000 | bytes 1048576 | tf_op jit(solution)/shard_map/attn_fwd_rest/pallas_call | solution.py:250
  40.7 4.5 %collective-permute-done.7.mine_b = bf16[4,224,384]{2,1,0:T(8,128)(2,1)S(1)} collective-permute-done((bf16[4,224,384]{2,1,0:T(8,128)(2,1)S(1)}, bf16[4,224,384]{2,1,0:T(8,128)(2,1)S(1)}, u32[]{:S(2)}, u32[]{:S(2)}) %collective-permute-start.7) | collective-permute-done | bytes 688160 | tf_op jit(solution)/shard_map/ppermute | solution.py:562
  45.2 0.6 collective-permute-start.9
  45.8 1.8 %collective-permute-done.9.other_b = bf16[4,224,384]{2,1,0:T(8,128)(2,1)S(1)} collective-permute-done((bf16[4,224,384]{2,1,0:T(8,128)(2,1)S(1)}, bf16[4,224,384]{2,1,0:T(8,128)(2,1)S(1)}, u32[]{:S(2)}, u32[]{:S(2)}) %collective-permute-start.9) | collective-permute-done | bytes 688160 | tf_op jit(solution)/shard_map/ppermute | solution.py:562
  47.6 22.9 %mlp.1 = (f32[4,384,384]{2,1,0:T(8,128)}, bf16[4,384,1536]{2,1,0:T(8,128)(2,1)}, f32[4,384,384]{2,1,0:T(8,128)}, bf16[4,384,384]{2,1,0:T(8,128)(2,1)S(1)}, bf16[...) custom-call(bf16[4,224,384]{2,1,0:T(8,128)(2,1)S(1)} %pad_maximum_fu, ...), custom_call_target="tpu_custom_call" | custom-call | flops 24000000000 | bytes 1048576 | tf_op jit(solution)/shard_map/mlp/pallas_call | solution.py:359
  70.5 0.5 collective-permute-start.10
  71.1 2.6 %attn_bwd_first.1 = (bf16[4,1152,384]{2,1,0:T(8,128)(2,1)S(1)}, f32[1152,512]{1,0:T(8,128)S(1)}) custom-call(bf16[4,1152,384]{2,1,0:T(8,128)(2,1)S(1)} %get-tuple-element.122.jt_ref, bf16[4,6,384,384]{3,2,1,0:T(8,128)(2,1)S(1)} %get-tuple-element.123.e_ref, f32[4,8,384]{2,1,0:T(8,128)S(1)} %get-tuple-element.124.il_ref, ...), custom_call_target="tpu_custom_call" | custom-call | flops 4000000000 | bytes 1048576 | tf_op jit(solution)/shard_map/attn_bwd_first/pallas_call | solution.py:435
  73.6 0.2 collective-permute-done.10
  73.8 0.3 convert_add_fusion
  74.1 0.1 slice.71
  74.2 1.6 %collective-permute-start.11 = (bf16[4,224,384]{2,1,0:T(8,128)(2,1)S(1)}, bf16[4,224,384]{2,1,0:T(8,128)(2,1)S(1)}, u32[]{:S(2)}, u32[]{:S(2)}) collective-permute-start(bf16[4,224,384]{2,1,0:T(8,128)(2,1)S(1)} %slice.71), channel_id=1, source_target_pairs={{0,1},{1,0},{2,3},{3,2},{4,5},{5,4},{6,7},{7,6},{8,10},{9,11},{10,... | collective-permute-start | bytes 2064392 | tf_op jit(solution)/shard_map/ppermute | solution.py:562
  75.7 8.7 %attn_bwd_last.1 = (bf16[4,1152,384]{2,1,0:T(8,128)(2,1)S(1)}, bf16[8,80,384]{2,1,0:T(8,128)(2,1)S(1)}, bf16[8,80,384]{2,1,0:T(8,128)(2,1)S(1)}) custom-call(bf16[4,1152,384]{2,1,0:T(8,128)(2,1)S(1)} %get-tuple-element.122.jt_ref, bf16[4,6,384,384]{3,2,1,0:T(8,128)(2,1)S(1)} %get-tuple-element.123.e_ref, ...), custom_call_target="tpu_custom_call", output_to_operand_aliasing={{0}: (10, {})} | custom-call | flops 14000000000 | bytes 1048576 | tf_op jit(solution)/shard_map/attn_bwd_last/pallas_call | solution.py:445
  84.4 1.6 %collective-permute-start.12 = (bf16[8,80,384]{2,1,0:T(8,128)(2,1)S(1)}, bf16[8,80,384]{2,1,0:T(8,128)(2,1)S(1)}, u32[]{:S(2)}, u32[]{:S(2)}) collective-permute-start(bf16[8,80,384]{2,1,0:T(8,128)(2,1)S(1)} %get-tuple-element.139), channel_id=1, source_target_pairs={{0,8},{1,9},{2,10},{3,11},{4,12},{5,13},{6,14},{7,15},{8,0},{9,1},... | collective-permute-start | bytes 1474568 | tf_op jit(solution)/shard_map/ppermute | solution.py:562
  86.1 0.1 slice.42
  86.2 0.1 convert_add_fusion.1
  86.3 0.0 copy-start.18
  86.4 1.2 collective-permute-done.12
  87.5 0.1 convert_add_fusion.2
  87.7 1.6 %collective-permute-start.13 = (bf16[4,80,384]{2,1,0:T(8,128)(2,1)S(1)}, bf16[4,80,384]{2,1,0:T(8,128)(2,1)S(1)}, u32[]{:S(2)}, u32[]{:S(2)}) collective-permute-start(bf16[4,80,384]{2,1,0:T(8,128)(2,1)S(1)} %slice.73), channel_id=1, source_target_pairs={{0,1},{1,0},{2,3},{3,2},{4,5},{5,4},{6,7},{7,6},{8,10},{9,11},{10,... | collective-permute-start | bytes 737288 | tf_op jit(solution)/shard_map/ppermute | solution.py:562
  89.2 0.9 collective-permute-start.14
  90.2 4.3 %input_end.1 = f32[4,384,384]{2,1,0:T(8,128)} custom-call(f32[4,384,384]{2,1,0:T(8,128)S(1)} %copy-done.7, f32[4,384,384]{2,1,0:T(8,128)S(1)} %copy-done.18, bf16[4,1152,384]{2,1,0:T(8,128)(2,1)S(1)} %get-tuple-element.140.dj_ref, bf16[1152,384]{1,0:T(8,128)(2,1)S(1)} %get-tuple-element.110.w_ref, f32[16,384]{1,0:T(8,128)S(1)} %get-tuple-element.111.vrow_ref), custom_call_target="tpu_custom_call" | custom-call | flops 4000000000 | bytes 1048576 | tf_op jit(solution)/shard_map/input_end/pallas_call | solution.py:479
  94.6 1.4 %collective-permute-start.15 = (bf16[2,80,384]{2,1,0:T(8,128)(2,1)S(1)}, bf16[2,80,384]{2,1,0:T(8,128)(2,1)S(1)}, u32[]{:S(2)}, u32[]{:S(2)}) collective-permute-start(bf16[2,80,384]{2,1,0:T(8,128)(2,1)S(1)} %slice.75), channel_id=1, source_target_pairs={{0,2},{1,3},{2,0},{3,1},{4,6},{5,7},{6,4},{7,5},{8,12},{9,13},{10,... | collective-permute-start | bytes 368648 | tf_op jit(solution)/shard_map/ppermute | solution.py:562
  96.0 4.1 %layer_end.1 = f32[4,384,384]{2,1,0:T(8,128)} custom-call(f32[4,384,384]{2,1,0:T(8,128)S(1)} %copy-done.19, bf16[4,384,1536]{2,1,0:T(8,128)(2,1)S(1)} %bitcast.9, bf16[384,1536]{1,0:T(8,128)(2,1)S(1)} %copy-done.20, f32[16,384]{1,0:T(8,128)S(1)} %get-tuple-element.111.vrow_ref), custom_call_target="tpu_custom_call" | custom-call | flops 4000000000 | bytes 1048576 | tf_op jit(solution)/shard_map/layer_end/pallas_call | solution.py:461
  100.1 0.0 copy-start.16
  100.1 0.0 copy-start.17
  100.1 0.6 collective-permute-done.14
  100.7 0.1 convert_add_fusion.3
  100.8 1.6 %collective-permute-start.16 = (bf16[1,224,384]{2,1,0:T(8,128)(2,1)S(1)}, bf16[1,224,384]{2,1,0:T(8,128)(2,1)S(1)}, u32[]{:S(2)}, u32[]{:S(2)}) collective-permute-start(bf16[1,224,384]{2,1,0:T(8,128)(2,1)S(1)} %slice.74), channel_id=1, source_target_pairs={{0,4},{1,5},{2,6},{3,7},{4,0},{5,1},{6,2},{7,3},{8,9},{9,8},{10,11... | collective-permute-start | bytes 516104 | tf_op jit(solution)/shard_map/ppermute | solution.py:562
  102.4 0.9 collective-permute-done.15
  103.4 1.4 %collective-permute-start.17 = (bf16[1,80,384]{2,1,0:T(8,128)(2,1)S(1)}, bf16[1,80,384]{2,1,0:T(8,128)(2,1)S(1)}, u32[]{:S(2)}, u32[]{:S(2)}) collective-permute-start(bf16[1,80,384]{2,1,0:T(8,128)(2,1)S(1)} %slice.76), channel_id=1, source_target_pairs={{0,4},{1,5},{2,6},{3,7},{4,0},{5,1},{6,2},{7,3},{8,9},{9,8},{10,11... | collective-permute-start | bytes 184328 | tf_op jit(solution)/shard_map/ppermute | solution.py:562
  104.8 4.9 %collective-permute-done.16 = bf16[1,224,384]{2,1,0:T(8,128)(2,1)S(1)} collective-permute-done((bf16[1,224,384]{2,1,0:T(8,128)(2,1)S(1)}, bf16[1,224,384]{2,1,0:T(8,128)(2,1)S(1)}, u32[]{:S(2)}, u32[]{:S(2)}) %collective-permute-start.16) | collective-permute-done | bytes 172064 | tf_op jit(solution)/shard_map/ppermute | solution.py:562
  109.8 0.6 collective-permute-done.17
  110.4 1.6 %collective-permute-start.18 = (bf16[80,384]{1,0:T(8,128)(2,1)S(1)}, bf16[80,384]{1,0:T(8,128)(2,1)S(1)}, u32[]{:S(2)}, u32[]{:S(2)}) collective-permute-start(bf16[80,384]{1,0:T(8,128)(2,1)S(1)} %fusion), channel_id=1, source_target_pairs={{0,16},{1,17},{2,18},{3,19},{4,20},{5,21},{6,22},{7,23},{8,24},{9,... | collective-permute-start | bytes 184328 | tf_op jit(solution)/shard_map/ppermute | solution.py:562
  112.0 0.5 collective-permute-start.19
  112.5 2.4 %collective-permute-done.18 = bf16[80,384]{1,0:T(8,128)(2,1)S(1)} collective-permute-done((bf16[80,384]{1,0:T(8,128)(2,1)S(1)}, bf16[80,384]{1,0:T(8,128)(2,1)S(1)}, u32[]{:S(2)}, u32[]{:S(2)}) %collective-permute-start.18) | collective-permute-done | bytes 61472 | tf_op jit(solution)/shard_map/ppermute | solution.py:562
  114.9 3.6 %collective-permute-done.19 = bf16[224,384]{1,0:T(8,128)(2,1)S(1)} collective-permute-done((bf16[224,384]{1,0:T(8,128)(2,1)S(1)}, bf16[224,384]{1,0:T(8,128)(2,1)S(1)}, u32[]{:S(2)}, u32[]{:S(2)}) %collective-permute-start.19) | collective-permute-done | bytes 172064 | tf_op jit(solution)/shard_map/ppermute | solution.py:562
  118.5 0.0 copy-start
  118.5 0.0 copy-start.1
  118.6 0.0 copy-start.9
  118.6 0.0 copy-start.10
  118.6 0.0 copy-start.15
  118.6 0.1 collective-permute-start.20
  118.7 0.5 collective-permute-start.21
  119.2 0.8 collective-permute-done.20.other_ref
  120.1 1.2 adam.2
  121.4 1.9 %adam.3 = (f32[48,384]{1,0:T(8,128)}, f32[48,384]{1,0:T(8,128)}, f32[48,384]{1,0:T(8,128)}, bf16[48,384]{1,0:T(8,128)(2,1)}, f32[192,384]{1,0:T(8,128)}, /*index...) custom-call(f32[224,384]{1,0:T(8,128)S(1)} %convert_add_fusion.5.min, ...), custom_call_target="tpu_custom_call" | custom-call | flops 3000000000 | bytes 1048576 | tf_op jit(solution)/shard_map/adam/pallas_call | solution.py:530
  (64 shorter events, 0.4 us)
Async XLA Ops:
  2.6 6.5 %collective-permute-start = (bf16[1,80,384]{2,1,0:T(8,128)(2,1)}, bf16[1,80,384]{2,1,0:T(8,128)(2,1)S(1)}, u32[]{:S(2)}, u32[]{:S(2)}) collective-permute-start(bf16[1,80,384]{2,1,0:T(8,128)(2,1)} %bitcast.11), channel_id=1, source_target_pairs={{0,4},{1,5},{2,6},{3,7},{4,0},{5,1},{6,2},{7,3},{8,9},{9,8},{10,11... | collective-permute-start | bytes 184328 | tf_op jit(solution)/shard_map/ppermute | solution.py:562
  10.0 5.1 %collective-permute-start.1 = (bf16[2,80,384]{2,1,0:T(8,128)(2,1)S(1)}, bf16[2,80,384]{2,1,0:T(8,128)(2,1)S(1)}, u32[]{:S(2)}, u32[]{:S(2)}) collective-permute-start(bf16[2,80,384]{2,1,0:T(8,128)(2,1)S(1)} %pad_maximum_fusion.3), channel_id=1, source_target_pairs={{0,2},{1,3},{2,0},{3,1},{4,6},{5,7},{6,4},{7,5},{8,12},{9,13},{10,... | collective-permute-start | bytes 368648 | tf_op jit(solution)/shard_map/ppermute | solution.py:562
  12.0 8.7 %collective-permute-start.3 = (bf16[1,224,384]{2,1,0:T(8,128)(2,1)}, bf16[1,224,384]{2,1,0:T(8,128)(2,1)S(1)}, u32[]{:S(2)}, u32[]{:S(2)}) collective-permute-start(bf16[1,224,384]{2,1,0:T(8,128)(2,1)} %bitcast.14), channel_id=1, source_target_pairs={{0,4},{1,5},{2,6},{3,7},{4,0},{5,1},{6,2},{7,3},{8,9},{9,8},{10,11... | collective-permute-start | bytes 516104 | tf_op jit(solution)/shard_map/ppermute | solution.py:562
  16.0 6.3 %collective-permute-start.2 = (bf16[4,80,384]{2,1,0:T(8,128)(2,1)S(1)}, bf16[4,80,384]{2,1,0:T(8,128)(2,1)S(1)}, u32[]{:S(2)}, u32[]{:S(2)}) collective-permute-start(bf16[4,80,384]{2,1,0:T(8,128)(2,1)S(1)} %pad_maximum_fusion.2.mine_a), channel_id=1, source_target_pairs={{0,1},{1,0},{2,3},{3,2},{4,5},{5,4},{6,7},{7,6},{8,10},{9,11},{10,... | collective-permute-start | bytes 737288 | tf_op jit(solution)/shard_map/ppermute | solution.py:562
  17.9 6.1 %collective-permute-start.4 = (bf16[4,80,384]{2,1,0:T(8,128)(2,1)S(1)}, bf16[4,80,384]{2,1,0:T(8,128)(2,1)S(1)}, u32[]{:S(2)}, u32[]{:S(2)}) collective-permute-start(bf16[4,80,384]{2,1,0:T(8,128)(2,1)S(1)} %pad_maximum_fusion.2.mine_a), channel_id=1, source_target_pairs={{0,8},{1,9},{2,10},{3,11},{4,12},{5,13},{6,14},{7,15},{8,0},{9,1},... | collective-permute-start | bytes 737288 | tf_op jit(solution)/shard_map/ppermute | solution.py:562
  22.2 1.8 %collective-permute-start.5 = (bf16[4,80,384]{2,1,0:T(8,128)(2,1)S(1)}, bf16[4,80,384]{2,1,0:T(8,128)(2,1)S(1)}, u32[]{:S(2)}, u32[]{:S(2)}) collective-permute-start(bf16[4,80,384]{2,1,0:T(8,128)(2,1)S(1)} %collective-permute-done.2.mine_b), channel_id=1, source_target_pairs={{0,8},{1,9},{2,10},{3,11},{4,12},{5,13},{6,14},{7,15},{8,0},{9,1},... | collective-permute-start | bytes 737288 | tf_op jit(solution)/shard_map/ppermute | solution.py:562
  22.2 10.9 %collective-permute-start.6 = (bf16[2,224,384]{2,1,0:T(8,128)(2,1)S(1)}, bf16[2,224,384]{2,1,0:T(8,128)(2,1)S(1)}, u32[]{:S(2)}, u32[]{:S(2)}) collective-permute-start(bf16[2,224,384]{2,1,0:T(8,128)(2,1)S(1)} %pad_maximum_fusion.1), channel_id=1, source_target_pairs={{0,2},{1,3},{2,0},{3,1},{4,6},{5,7},{6,4},{7,5},{8,12},{9,13},{10,... | collective-permute-start | bytes 1032200 | tf_op jit(solution)/shard_map/ppermute | solution.py:562
  24.0 1.7 %copy-start.6 = (f32[4,384,384]{2,1,0:T(8,128)S(1)}, f32[4,384,384]{2,1,0:T(8,128)}, u32[]{:S(2)}) copy-start(f32[4,384,384]{2,1,0:T(8,128)} %x_ref.7) | copy-start | bytes 7077892
  25.7 10.1 %copy-start.7 = (f32[4,384,384]{2,1,0:T(8,128)S(1)}, f32[4,384,384]{2,1,0:T(8,128)}, u32[]{:S(2)}) copy-start(f32[4,384,384]{2,1,0:T(8,128)} %x_ref.7) | copy-start | bytes 7077892
  33.3 12.6 %collective-permute-start.8 = (bf16[4,224,384]{2,1,0:T(8,128)(2,1)S(1)}, bf16[4,224,384]{2,1,0:T(8,128)(2,1)S(1)}, u32[]{:S(2)}, u32[]{:S(2)}) collective-permute-start(bf16[4,224,384]{2,1,0:T(8,128)(2,1)S(1)} %pad_maximum_fusion.mine_a), channel_id=1, source_target_pairs={{0,8},{1,9},{2,10},{3,11},{4,12},{5,13},{6,14},{7,15},{8,0},{9,1},... | collective-permute-start | bytes 2064392 | tf_op jit(solution)/shard_map/ppermute | solution.py:562
  34.3 10.9 %collective-permute-start.7 = (bf16[4,224,384]{2,1,0:T(8,128)(2,1)S(1)}, bf16[4,224,384]{2,1,0:T(8,128)(2,1)S(1)}, u32[]{:S(2)}, u32[]{:S(2)}) collective-permute-start(bf16[4,224,384]{2,1,0:T(8,128)(2,1)S(1)} %pad_maximum_fusion.mine_a), channel_id=1, source_target_pairs={{0,1},{1,0},{2,3},{3,2},{4,5},{5,4},{6,7},{7,6},{8,10},{9,11},{10,... | collective-permute-start | bytes 2064392 | tf_op jit(solution)/shard_map/ppermute | solution.py:562
  35.8 11.8 %copy-start.5 = (f32[4,384,384]{2,1,0:T(8,128)S(1)}, f32[4,384,384]{2,1,0:T(8,128)}, u32[]{:S(2)}) copy-start(f32[4,384,384]{2,1,0:T(8,128)} %cot_ref.1) | copy-start | bytes 7077892
  45.2 2.4 %collective-permute-start.9 = (bf16[4,224,384]{2,1,0:T(8,128)(2,1)S(1)}, bf16[4,224,384]{2,1,0:T(8,128)(2,1)S(1)}, u32[]{:S(2)}, u32[]{:S(2)}) collective-permute-start(bf16[4,224,384]{2,1,0:T(8,128)(2,1)S(1)} %collective-permute-done.7.mine_b), channel_id=1, source_target_pairs={{0,8},{1,9},{2,10},{3,11},{4,12},{5,13},{6,14},{7,15},{8,0},{9,1},... | collective-permute-start | bytes 2064392 | tf_op jit(solution)/shard_map/ppermute | solution.py:562
  70.5 3.3 %collective-permute-start.10 = (bf16[8,224,384]{2,1,0:T(8,128)(2,1)S(1)}, bf16[8,224,384]{2,1,0:T(8,128)(2,1)S(1)}, u32[]{:S(2)}, u32[]{:S(2)}) collective-permute-start(bf16[8,224,384]{2,1,0:T(8,128)(2,1)S(1)} %get-tuple-element.130), channel_id=1, source_target_pairs={{0,8},{1,9},{2,10},{3,11},{4,12},{5,13},{6,14},{7,15},{8,0},{9,1},... | collective-permute-start | bytes 4128776 | tf_op jit(solution)/shard_map/ppermute | solution.py:562
  74.2 12.0 %collective-permute-start.11 = (bf16[4,224,384]{2,1,0:T(8,128)(2,1)S(1)}, bf16[4,224,384]{2,1,0:T(8,128)(2,1)S(1)}, u32[]{:S(2)}, u32[]{:S(2)}) collective-permute-start(bf16[4,224,384]{2,1,0:T(8,128)(2,1)S(1)} %slice.71), channel_id=1, source_target_pairs={{0,1},{1,0},{2,3},{3,2},{4,5},{5,4},{6,7},{7,6},{8,10},{9,11},{10,... | collective-permute-start | bytes 2064392 | tf_op jit(solution)/shard_map/ppermute | solution.py:562
  84.4 3.1 %collective-permute-start.12 = (bf16[8,80,384]{2,1,0:T(8,128)(2,1)S(1)}, bf16[8,80,384]{2,1,0:T(8,128)(2,1)S(1)}, u32[]{:S(2)}, u32[]{:S(2)}) collective-permute-start(bf16[8,80,384]{2,1,0:T(8,128)(2,1)S(1)} %get-tuple-element.139), channel_id=1, source_target_pairs={{0,8},{1,9},{2,10},{3,11},{4,12},{5,13},{6,14},{7,15},{8,0},{9,1},... | collective-permute-start | bytes 1474568 | tf_op jit(solution)/shard_map/ppermute | solution.py:562
  86.3 8.2 %copy-start.21 = (f32[4,224,384]{2,1,0:T(8,128)}, f32[4,224,384]{2,1,0:T(8,128)S(1)}, u32[]{:S(2)}) copy-start(f32[4,224,384]{2,1,0:T(8,128)S(1)} %convert_add_fusion.1) | copy-start | bytes 4128772
  86.3 3.9 %copy-start.18 = (f32[4,384,384]{2,1,0:T(8,128)S(1)}, f32[4,384,384]{2,1,0:T(8,128)}, u32[]{:S(2)}) copy-start(f32[4,384,384]{2,1,0:T(8,128)} %get-tuple-element.121.dm_ref) | copy-start | bytes 7077892
  87.5 8.5 %slice-start = ((s8[4718592]{0:T(1024)(128)(4,1)}), s8[4194304]{0:T(1024)(128)(4,1)S(1)}, s32[]{:S(2)}) async-start(s8[4718592]{0:T(1024)(128)(4,1)} %bitcast.8), calls=%async_computation | async-start | bytes 8388608
  87.7 6.8 %collective-permute-start.13 = (bf16[4,80,384]{2,1,0:T(8,128)(2,1)S(1)}, bf16[4,80,384]{2,1,0:T(8,128)(2,1)S(1)}, u32[]{:S(2)}, u32[]{:S(2)}) collective-permute-start(bf16[4,80,384]{2,1,0:T(8,128)(2,1)S(1)} %slice.73), channel_id=1, source_target_pairs={{0,1},{1,0},{2,3},{3,2},{4,5},{5,4},{6,7},{7,6},{8,10},{9,11},{10,... | collective-permute-start | bytes 737288 | tf_op jit(solution)/shard_map/ppermute | solution.py:562
  89.2 11.5 %collective-permute-start.14 = (bf16[2,224,384]{2,1,0:T(8,128)(2,1)S(1)}, bf16[2,224,384]{2,1,0:T(8,128)(2,1)S(1)}, u32[]{:S(2)}, u32[]{:S(2)}) collective-permute-start(bf16[2,224,384]{2,1,0:T(8,128)(2,1)S(1)} %slice.72), channel_id=1, source_target_pairs={{0,2},{1,3},{2,0},{3,1},{4,6},{5,7},{6,4},{7,5},{8,12},{9,13},{10,... | collective-permute-start | bytes 1032200 | tf_op jit(solution)/shard_map/ppermute | solution.py:562
  90.2 5.8 %slice-start.1 = ((s8[4718592]{0:T(1024)(128)(4,1)}), s8[524288]{0:T(1024)(128)(4,1)S(1)}, s32[]{:S(2)}) async-start(s8[4718592]{0:T(1024)(128)(4,1)} %bitcast.8), calls=%async_computation.1 | async-start | bytes 1048576
  90.2 5.8 %copy-start.19 = (f32[4,384,384]{2,1,0:T(8,128)S(1)}, f32[4,384,384]{2,1,0:T(8,128)}, u32[]{:S(2)}) copy-start(f32[4,384,384]{2,1,0:T(8,128)} %get-tuple-element.143.mid_ref) | copy-start | bytes 7077892
  90.2 5.8 %copy-start.20 = (bf16[384,1536]{1,0:T(8,128)(2,1)S(1)}, bf16[384,1536]{1,0:T(8,128)(2,1)}, u32[]{:S(2)}) copy-start(bf16[384,1536]{1,0:T(8,128)(2,1)} %get-tuple-element.145.wd_ref) | copy-start | bytes 3538948
  94.6 8.7 %collective-permute-start.15 = (bf16[2,80,384]{2,1,0:T(8,128)(2,1)S(1)}, bf16[2,80,384]{2,1,0:T(8,128)(2,1)S(1)}, u32[]{:S(2)}, u32[]{:S(2)}) collective-permute-start(bf16[2,80,384]{2,1,0:T(8,128)(2,1)S(1)} %slice.75), channel_id=1, source_target_pairs={{0,2},{1,3},{2,0},{3,1},{4,6},{5,7},{6,4},{7,5},{8,12},{9,13},{10,... | collective-permute-start | bytes 368648 | tf_op jit(solution)/shard_map/ppermute | solution.py:562
  96.0 4.7 %slice-start.2 = ((f32[4,224,384]{2,1,0:T(8,128)}), f32[2,224,384]{2,1,0:T(8,128)S(1)}, s32[]{:S(2)}) async-start(f32[4,224,384]{2,1,0:T(8,128)} %copy-done.21), calls=%async_computation.2 | async-start | bytes 1376256 | tf_op jit(solution)/shard_map/slice | solution.py:650
  100.1 19.9 %copy-start.2 = (f32[144,384]{1,0:T(8,128)S(1)}, f32[144,384]{1,0:T(8,128)}, u32[]{:S(2)}) copy-start(f32[144,384]{1,0:T(8,128)} %refs_0_.2) | copy-start | bytes 663556
  100.1 19.9 %copy-start.4 = (f32[576]{0:T(1024)S(1)}, f32[576]{0:T(1024)}, u32[]{:S(2)}) copy-start(f32[576]{0:T(1024)} %refs_3_.2) | copy-start | bytes 6916
  100.1 19.9 %copy-start.12 = (f32[144,384]{1,0:T(8,128)S(1)}, f32[144,384]{1,0:T(8,128)}, u32[]{:S(2)}) copy-start(f32[144,384]{1,0:T(8,128)} %refs_1_.2) | copy-start | bytes 663556
  100.1 19.9 %copy-start.13 = (f32[144,384]{1,0:T(8,128)S(1)}, f32[144,384]{1,0:T(8,128)}, u32[]{:S(2)}) copy-start(f32[144,384]{1,0:T(8,128)} %refs_2_.2) | copy-start | bytes 663556
  100.1 19.9 %copy-start.16 = (f32[576]{0:T(1024)S(1)}, f32[576]{0:T(1024)}, u32[]{:S(2)}) copy-start(f32[576]{0:T(1024)} %refs_4_.2) | copy-start | bytes 6916
  100.1 19.9 %copy-start.17 = (f32[576]{0:T(1024)S(1)}, f32[576]{0:T(1024)}, u32[]{:S(2)}) copy-start(f32[576]{0:T(1024)} %refs_5_.2) | copy-start | bytes 6916
  100.8 8.9 %collective-permute-start.16 = (bf16[1,224,384]{2,1,0:T(8,128)(2,1)S(1)}, bf16[1,224,384]{2,1,0:T(8,128)(2,1)S(1)}, u32[]{:S(2)}, u32[]{:S(2)}) collective-permute-start(bf16[1,224,384]{2,1,0:T(8,128)(2,1)S(1)} %slice.74), channel_id=1, source_target_pairs={{0,4},{1,5},{2,6},{3,7},{4,0},{5,1},{6,2},{7,3},{8,9},{9,8},{10,11... | collective-permute-start | bytes 516104 | tf_op jit(solution)/shard_map/ppermute | solution.py:562
  103.4 7.0 %collective-permute-start.17 = (bf16[1,80,384]{2,1,0:T(8,128)(2,1)S(1)}, bf16[1,80,384]{2,1,0:T(8,128)(2,1)S(1)}, u32[]{:S(2)}, u32[]{:S(2)}) collective-permute-start(bf16[1,80,384]{2,1,0:T(8,128)(2,1)S(1)} %slice.76), channel_id=1, source_target_pairs={{0,4},{1,5},{2,6},{3,7},{4,0},{5,1},{6,2},{7,3},{8,9},{9,8},{10,11... | collective-permute-start | bytes 184328 | tf_op jit(solution)/shard_map/ppermute | solution.py:562
  110.4 4.5 %collective-permute-start.18 = (bf16[80,384]{1,0:T(8,128)(2,1)S(1)}, bf16[80,384]{1,0:T(8,128)(2,1)S(1)}, u32[]{:S(2)}, u32[]{:S(2)}) collective-permute-start(bf16[80,384]{1,0:T(8,128)(2,1)S(1)} %fusion), channel_id=1, source_target_pairs={{0,16},{1,17},{2,18},{3,19},{4,20},{5,21},{6,22},{7,23},{8,24},{9,... | collective-permute-start | bytes 184328 | tf_op jit(solution)/shard_map/ppermute | solution.py:562
  112.0 6.5 %collective-permute-start.19 = (bf16[224,384]{1,0:T(8,128)(2,1)S(1)}, bf16[224,384]{1,0:T(8,128)(2,1)S(1)}, u32[]{:S(2)}, u32[]{:S(2)}) collective-permute-start(bf16[224,384]{1,0:T(8,128)(2,1)S(1)} %bitcast.10), channel_id=1, source_target_pairs={{0,16},{1,17},{2,18},{3,19},{4,20},{5,21},{6,22},{7,23},{8,24},{9,... | collective-permute-start | bytes 516104 | tf_op jit(solution)/shard_map/ppermute | solution.py:562
  118.5 2.7 %copy-start = (f32[192,384]{1,0:T(8,128)S(1)}, f32[192,384]{1,0:T(8,128)}, u32[]{:S(2)}) copy-start(f32[192,384]{1,0:T(8,128)} %refs_3_.3) | copy-start | bytes 884740
  118.5 2.7 %copy-start.1 = (f32[48,1536]{1,0:T(8,128)S(1)}, f32[48,1536]{1,0:T(8,128)}, u32[]{:S(2)}) copy-start(f32[48,1536]{1,0:T(8,128)} %refs_6_.1) | copy-start | bytes 884740
  118.6 2.7 %copy-start.3 = (f32[48,384]{1,0:T(8,128)S(1)}, f32[48,384]{1,0:T(8,128)}, u32[]{:S(2)}) copy-start(f32[48,384]{1,0:T(8,128)} %refs_0_.3) | copy-start | bytes 221188
  118.6 2.7 %copy-start.8 = (f32[192,384]{1,0:T(8,128)S(1)}, f32[192,384]{1,0:T(8,128)}, u32[]{:S(2)}) copy-start(f32[192,384]{1,0:T(8,128)} %refs_4_.3) | copy-start | bytes 884740
  118.6 2.7 %copy-start.9 = (f32[192,384]{1,0:T(8,128)S(1)}, f32[192,384]{1,0:T(8,128)}, u32[]{:S(2)}) copy-start(f32[192,384]{1,0:T(8,128)} %refs_5_.3) | copy-start | bytes 884740
  118.6 2.7 %copy-start.10 = (f32[48,1536]{1,0:T(8,128)S(1)}, f32[48,1536]{1,0:T(8,128)}, u32[]{:S(2)}) copy-start(f32[48,1536]{1,0:T(8,128)} %refs_7_.1) | copy-start | bytes 884740
  118.6 2.7 %copy-start.11 = (f32[48,1536]{1,0:T(8,128)S(1)}, f32[48,1536]{1,0:T(8,128)}, u32[]{:S(2)}) copy-start(f32[48,1536]{1,0:T(8,128)} %refs_8_.1) | copy-start | bytes 884740
  118.6 2.7 %copy-start.14 = (f32[48,384]{1,0:T(8,128)S(1)}, f32[48,384]{1,0:T(8,128)}, u32[]{:S(2)}) copy-start(f32[48,384]{1,0:T(8,128)} %refs_1_.3) | copy-start | bytes 221188
  118.6 2.7 %copy-start.15 = (f32[48,384]{1,0:T(8,128)S(1)}, f32[48,384]{1,0:T(8,128)}, u32[]{:S(2)}) copy-start(f32[48,384]{1,0:T(8,128)} %refs_2_.3) | copy-start | bytes 221188
  118.6 1.4 %collective-permute-start.20 = (f32[80,384]{1,0:T(8,128)S(1)}, f32[80,384]{1,0:T(8,128)S(1)}, u32[]{:S(2)}, u32[]{:S(2)}) collective-permute-start(f32[80,384]{1,0:T(8,128)S(1)} %convert_add_fusion.7.mine_ref), channel_id=1, source_target_pairs={{0,8},{1,9},{2,10},{3,11},{4,12},{5,13},{6,14},{7,15},{8,0},{9,1},... | collective-permute-start | bytes 368648 | tf_op jit(solution)/shard_map/ppermute | solution.py:562
  118.7 2.5 %collective-permute-start.21 = (f32[224,384]{1,0:T(8,128)S(1)}, f32[224,384]{1,0:T(8,128)S(1)}, u32[]{:S(2)}, u32[]{:S(2)}) collective-permute-start(f32[224,384]{1,0:T(8,128)S(1)} %convert_add_fusion.5.mine_ref), channel_id=1, source_target_pairs={{0,8},{1,9},{2,10},{3,11},{4,12},{5,13},{6,14},{7,15},{8,0},{9,1},... | collective-permute-start | bytes 1032200 | tf_op jit(solution)/shard_map/ppermute | solution.py:562

commit v7 on v6

--- a/solution.py
+++ b/solution.py
@@ -628,9 +628,9 @@
     def core(self):
         return self.held, self.links.core(self.held)
 
-    def last(self):
+    def last(self, *before):
         self.got = self.links.step(self.held, self.k)
-        self.other = self.links.core(self.held)
+        self.other = self.links.core(after(self.held, *before))
 
     def slots(self):
         return self.held, self.got, self.other, self.links.core(self.got)
@@ -663,7 +663,7 @@
     def round(self, *beside):
         pass
 
-    def last(self):
+    def last(self, *before):
         self.got = None
 
     def slots(self):
@@ -739,7 +739,7 @@
         two.round(vcol)
     *outs, two.held = lax.optimization_barrier((*outs, two.held))
     jt, e, il, ot, h = call_attn_fwd_rest(x, wq, vrow, vcol, outs, k, b - k)
-    two.last()
+    two.last(ot)
     if two.got is not None:
         ot, two.got = lax.optimization_barrier((ot, two.got))
     second = two.slots()

time: 124 us -> 122 us (0.984)
  waiting for transfers between devices: 27.6 us -> 23.3 us
  starting transfers between devices: 29.3 us -> 32.6 us
    ppermute x22, waiting for transfers between devices: 27.6 us -> 23.3 us  [permute(): return lax.ppermute(value, ('narrow', 'wide'), pairs)]
    ppermute x22, starting transfers between devices: 29.3 us -> 32.6 us  [permute(): return lax.ppermute(value, ('narrow', 'wide'), pairs)]
where the time goes in v7:
time: 122 us
  Pallas kernels  59.6 us (49%)
  starting transfers between devices  32.6 us (27%)
  waiting for transfers between devices  23.3 us (19%)
  other arithmetic  3.5 us (3%)
  local copies, waits for them, and re-layouts  2.1 us (2%)
    ppermute x22, starting transfers between devices, permute(): return lax.ppermute(value, ('narrow', 'wide'), pairs)  32.6 us
    ppermute x22, waiting for transfers between devices, permute(): return lax.ppermute(value, ('narrow', 'wide'), pairs)  23.3 us
    pallas_call x1, Pallas kernels, call_mlp(): pl.pallas_call(functools.partial(mlp, lay, b // n), grid=(b // n,), in_sp...  22.9 us
    pallas_call x1, Pallas kernels, call_attn_bwd_last(): pl.pallas_call(functools.partial(attn_bwd_last, lay, count), grid=(count,...  8.67 us
    pallas_call x1, Pallas kernels, call_attn_fwd_first(): pl.pallas_call(functools.partial(attn_fwd_first, lay), grid=(count,), in_...  7.08 us
    pallas_call x1, Pallas kernels, call_attn_fwd_rest(): pl.pallas_call(attn_fwd_rest, grid=(count,), in_specs=[one(t, d, off=off)...  4.93 us
    pallas_call x1, Pallas kernels, call_input_end(): pl.pallas_call(input_end, grid=(b,), in_specs=[one(t, d), one(t, d), one(...  4.3 us
    pallas_call x1, Pallas kernels, call_layer_end(): pl.pallas_call(layer_end, grid=(b,), in_specs=[one(t, d), one(t, act.shap...  4.08 us
  transfers between devices with their start and end apart: 22, of which 15 were waited for; matrix products, arithmetic and copies ran while one was open for 2% of the time, Pallas kernels for 27%

profile of v7, /device:TPU:0, one launch (start us, length us, event | category | flops | bytes accessed | tf_op | source)
XLA Modules:
  0.0 122.2 jit_solution(1277211097002481768)
XLA Ops:
  0.7 2.0 %pack.1 = (bf16[80,384]{1,0:T(8,128)(2,1)}, bf16[224,384]{1,0:T(8,128)(2,1)}) custom-call(f32[144,384]{1,0:T(8,128)} %refs_0_.2, f32[48,384]{1,0:T(8,128)} %refs_0_.3, f32[192,384]{1,0:T(8,128)} %refs_3_.3, f32[48,1536]{1,0:T(8,128)} %refs_6_.1, f32[576]{0:T(1024)} %refs_3_.2), custom_call_target="tpu_custom_call" | custom-call | tf_op jit(solution)/shard_map/pack/pallas_call | solution.py:119
  2.6 4.1 %collective-permute-start = (bf16[1,80,384]{2,1,0:T(8,128)(2,1)}, bf16[1,80,384]{2,1,0:T(8,128)(2,1)S(1)}, u32[]{:S(2)}, u32[]{:S(2)}) collective-permute-start(bf16[1,80,384]{2,1,0:T(8,128)(2,1)} %bitcast.11), channel_id=1, source_target_pairs={{0,4},{1,5},{2,6},{3,7},{4,0},{5,1},{6,2},{7,3},{8,9},{9,8},{10,11... | collective-permute-start | bytes 184328 | tf_op jit(solution)/shard_map/ppermute | solution.py:562
  6.7 2.4 %collective-permute-done = bf16[1,80,384]{2,1,0:T(8,128)(2,1)S(1)} collective-permute-done((bf16[1,80,384]{2,1,0:T(8,128)(2,1)}, bf16[1,80,384]{2,1,0:T(8,128)(2,1)S(1)}, u32[]{:S(2)}, u32[]{:S(2)}) %collective-permute-start) | collective-permute-done | bytes 61472 | tf_op jit(solution)/shard_map/ppermute | solution.py:562
  9.2 0.8 pad_maximum_fusion.3
  10.0 2.0 %collective-permute-start.1 = (bf16[2,80,384]{2,1,0:T(8,128)(2,1)S(1)}, bf16[2,80,384]{2,1,0:T(8,128)(2,1)S(1)}, u32[]{:S(2)}, u32[]{:S(2)}) collective-permute-start(bf16[2,80,384]{2,1,0:T(8,128)(2,1)S(1)} %pad_maximum_fusion.3), channel_id=1, source_target_pairs={{0,2},{1,3},{2,0},{3,1},{4,6},{5,7},{6,4},{7,5},{8,12},{9,13},{10,... | collective-permute-start | bytes 368648 | tf_op jit(solution)/shard_map/ppermute | solution.py:562
  12.0 3.1 %collective-permute-start.3 = (bf16[1,224,384]{2,1,0:T(8,128)(2,1)}, bf16[1,224,384]{2,1,0:T(8,128)(2,1)S(1)}, u32[]{:S(2)}, u32[]{:S(2)}) collective-permute-start(bf16[1,224,384]{2,1,0:T(8,128)(2,1)} %bitcast.14), channel_id=1, source_target_pairs={{0,4},{1,5},{2,6},{3,7},{4,0},{5,1},{6,2},{7,3},{8,9},{9,8},{10,11... | collective-permute-start | bytes 516104 | tf_op jit(solution)/shard_map/ppermute | solution.py:562
  15.1 0.9 pad_maximum_fusion.2.mine_a
  16.0 1.9 %collective-permute-start.2 = (bf16[4,80,384]{2,1,0:T(8,128)(2,1)S(1)}, bf16[4,80,384]{2,1,0:T(8,128)(2,1)S(1)}, u32[]{:S(2)}, u32[]{:S(2)}) collective-permute-start(bf16[4,80,384]{2,1,0:T(8,128)(2,1)S(1)} %pad_maximum_fusion.2.mine_a), channel_id=1, source_target_pairs={{0,1},{1,0},{2,3},{3,2},{4,5},{5,4},{6,7},{7,6},{8,10},{9,11},{10,... | collective-permute-start | bytes 737288 | tf_op jit(solution)/shard_map/ppermute | solution.py:562
  17.9 2.7 %collective-permute-done.3 = bf16[1,224,384]{2,1,0:T(8,128)(2,1)S(1)} collective-permute-done((bf16[1,224,384]{2,1,0:T(8,128)(2,1)}, bf16[1,224,384]{2,1,0:T(8,128)(2,1)S(1)}, u32[]{:S(2)}, u32[]{:S(2)}) %collective-permute-start.3) | collective-permute-done | bytes 172064 | tf_op jit(solution)/shard_map/ppermute | solution.py:562
  20.7 1.0 pad_maximum_fusion.1
  21.6 0.6 collective-permute-done.2.mine_b
  22.2 1.7 %collective-permute-start.6 = (bf16[2,224,384]{2,1,0:T(8,128)(2,1)S(1)}, bf16[2,224,384]{2,1,0:T(8,128)(2,1)S(1)}, u32[]{:S(2)}, u32[]{:S(2)}) collective-permute-start(bf16[2,224,384]{2,1,0:T(8,128)(2,1)S(1)} %pad_maximum_fusion.1), channel_id=1, source_target_pairs={{0,2},{1,3},{2,0},{3,1},{4,6},{5,7},{6,4},{7,5},{8,12},{9,13},{10,... | collective-permute-start | bytes 1032200 | tf_op jit(solution)/shard_map/ppermute | solution.py:562
  24.0 1.7 %copy-done.6 = f32[4,384,384]{2,1,0:T(8,128)S(1)} copy-done((f32[4,384,384]{2,1,0:T(8,128)S(1)}, f32[4,384,384]{2,1,0:T(8,128)}, u32[]{:S(2)}) %copy-start.6) | copy-done | bytes 2359320
  25.7 7.1 %attn_fwd_first.1 = (bf16[4,1152,384]{2,1,0:T(8,128)(2,1)S(1)}, bf16[4,6,384,384]{3,2,1,0:T(8,128)(2,1)S(1)}, f32[4,8,384]{2,1,0:T(8,128)S(1)}, bf16[4,384,384]{...) custom-call(bf16[4,80,384]{2,1,0:T(8,128)(2,1)S(1)} %pad_maximum_fus, ...), custom_call_target="tpu_custom_call" | custom-call | flops 8000000000 | bytes 1048576 | tf_op jit(solution)/shard_map/attn_fwd_first/pallas_call | solution.py:238
  32.8 0.4 collective-permute-done.6
  33.2 0.1 pad_maximum_fusion.mine_a
  33.3 1.9 %collective-permute-start.7 = (bf16[4,224,384]{2,1,0:T(8,128)(2,1)S(1)}, bf16[4,224,384]{2,1,0:T(8,128)(2,1)S(1)}, u32[]{:S(2)}, u32[]{:S(2)}) collective-permute-start(bf16[4,224,384]{2,1,0:T(8,128)(2,1)S(1)} %pad_maximum_fusion.mine_a), channel_id=1, source_target_pairs={{0,1},{1,0},{2,3},{3,2},{4,5},{5,4},{6,7},{7,6},{8,10},{9,11},{10,... | collective-permute-start | bytes 2064392 | tf_op jit(solution)/shard_map/ppermute | solution.py:562
  35.2 4.9 %attn_fwd_rest.1 = (bf16[4,1152,384]{2,1,0:T(8,128)(2,1)S(1)}, bf16[4,6,384,384]{3,2,1,0:T(8,128)(2,1)S(1)}, f32[4,8,384]{2,1,0:T(8,128)S(1)}, bf16[4,384,384]{2,1,0:T(8,128)(2,1)S(1)}, bf16[4,384,384]{2,1,0:T(8,128)(2,1)S(1)}) custom-call(f32[4,384,384]{2,1,0:T(8,128)S(1)} %copy-done.7, ...), custom_call_target="tpu_custom_call", output_to_operand_aliasing={{0}: (4, {}), {1}: (5, {}), {2}: (6, {}), {3}: (7, {}), {4}... | custom-call | flops 8000000000 | bytes 1048576 | tf_op jit(solution)/shard_map/attn_fwd_rest/pallas_call | solution.py:250
  40.1 2.3 %collective-permute-start.8 = (bf16[4,224,384]{2,1,0:T(8,128)(2,1)S(1)}, bf16[4,224,384]{2,1,0:T(8,128)(2,1)S(1)}, u32[]{:S(2)}, u32[]{:S(2)}) collective-permute-start(bf16[4,224,384]{2,1,0:T(8,128)(2,1)S(1)} %pad_maximum_fusion.mine_a), channel_id=1, source_target_pairs={{0,8},{1,9},{2,10},{3,11},{4,12},{5,13},{6,14},{7,15},{8,0},{9,1},... | collective-permute-start | bytes 2064392 | tf_op jit(solution)/shard_map/ppermute | solution.py:562
  42.4 1.8 %collective-permute-done.7.mine_b = bf16[4,224,384]{2,1,0:T(8,128)(2,1)S(1)} collective-permute-done((bf16[4,224,384]{2,1,0:T(8,128)(2,1)S(1)}, bf16[4,224,384]{2,1,0:T(8,128)(2,1)S(1)}, u32[]{:S(2)}, u32[]{:S(2)}) %collective-permute-start.7) | collective-permute-done | bytes 688160 | tf_op jit(solution)/shard_map/ppermute | solution.py:562
  44.3 1.5 %collective-permute-start.9 = (bf16[4,224,384]{2,1,0:T(8,128)(2,1)S(1)}, bf16[4,224,384]{2,1,0:T(8,128)(2,1)S(1)}, u32[]{:S(2)}, u32[]{:S(2)}) collective-permute-start(bf16[4,224,384]{2,1,0:T(8,128)(2,1)S(1)} %collective-permute-done.7.mine_b), channel_id=1, source_target_pairs={{0,8},{1,9},{2,10},{3,11},{4,12},{5,13},{6,14},{7,15},{8,0},{9,1},... | collective-permute-start | bytes 2064392 | tf_op jit(solution)/shard_map/ppermute | solution.py:562
  45.8 1.8 %collective-permute-done.9.other_b = bf16[4,224,384]{2,1,0:T(8,128)(2,1)S(1)} collective-permute-done((bf16[4,224,384]{2,1,0:T(8,128)(2,1)S(1)}, bf16[4,224,384]{2,1,0:T(8,128)(2,1)S(1)}, u32[]{:S(2)}, u32[]{:S(2)}) %collective-permute-start.9) | collective-permute-done | bytes 688160 | tf_op jit(solution)/shard_map/ppermute | solution.py:562
  47.5 22.9 %mlp.1 = (f32[4,384,384]{2,1,0:T(8,128)}, bf16[4,384,1536]{2,1,0:T(8,128)(2,1)}, f32[4,384,384]{2,1,0:T(8,128)}, bf16[4,384,384]{2,1,0:T(8,128)(2,1)S(1)}, bf16[...) custom-call(bf16[4,224,384]{2,1,0:T(8,128)(2,1)S(1)} %pad_maximum_fu, ...), custom_call_target="tpu_custom_call" | custom-call | flops 24000000000 | bytes 1048576 | tf_op jit(solution)/shard_map/mlp/pallas_call | solution.py:359
  70.4 0.5 collective-permute-start.10
  71.0 2.6 %attn_bwd_first.1 = (bf16[4,1152,384]{2,1,0:T(8,128)(2,1)S(1)}, f32[1152,512]{1,0:T(8,128)S(1)}) custom-call(bf16[4,1152,384]{2,1,0:T(8,128)(2,1)S(1)} %get-tuple-element.124.jt_ref, bf16[4,6,384,384]{3,2,1,0:T(8,128)(2,1)S(1)} %get-tuple-element.125.e_ref, f32[4,8,384]{2,1,0:T(8,128)S(1)} %get-tuple-element.126.il_ref, ...), custom_call_target="tpu_custom_call" | custom-call | flops 4000000000 | bytes 1048576 | tf_op jit(solution)/shard_map/attn_bwd_first/pallas_call | solution.py:435
  73.6 0.2 collective-permute-done.10
  73.7 0.3 convert_add_fusion
  74.0 0.1 slice.71
  74.1 1.6 %collective-permute-start.11 = (bf16[4,224,384]{2,1,0:T(8,128)(2,1)S(1)}, bf16[4,224,384]{2,1,0:T(8,128)(2,1)S(1)}, u32[]{:S(2)}, u32[]{:S(2)}) collective-permute-start(bf16[4,224,384]{2,1,0:T(8,128)(2,1)S(1)} %slice.71), channel_id=1, source_target_pairs={{0,1},{1,0},{2,3},{3,2},{4,5},{5,4},{6,7},{7,6},{8,10},{9,11},{10,... | collective-permute-start | bytes 2064392 | tf_op jit(solution)/shard_map/ppermute | solution.py:562
  75.6 8.7 %attn_bwd_last.1 = (bf16[4,1152,384]{2,1,0:T(8,128)(2,1)S(1)}, bf16[8,80,384]{2,1,0:T(8,128)(2,1)S(1)}, bf16[8,80,384]{2,1,0:T(8,128)(2,1)S(1)}) custom-call(bf16[4,1152,384]{2,1,0:T(8,128)(2,1)S(1)} %get-tuple-element.124.jt_ref, bf16[4,6,384,384]{3,2,1,0:T(8,128)(2,1)S(1)} %get-tuple-element.125.e_ref, ...), custom_call_target="tpu_custom_call", output_to_operand_aliasing={{0}: (10, {})} | custom-call | flops 14000000000 | bytes 1048576 | tf_op jit(solution)/shard_map/attn_bwd_last/pallas_call | solution.py:445
  84.3 0.4 collective-permute-start.12
  84.7 0.1 slice.42
  84.8 0.3 collective-permute-done.11
  85.1 0.1 convert_add_fusion.1
  85.2 0.0 copy-start.18
  85.3 1.0 collective-permute-done.12
  86.2 0.1 convert_add_fusion.2
  86.4 1.5 %collective-permute-start.13 = (bf16[4,80,384]{2,1,0:T(8,128)(2,1)S(1)}, bf16[4,80,384]{2,1,0:T(8,128)(2,1)S(1)}, u32[]{:S(2)}, u32[]{:S(2)}) collective-permute-start(bf16[4,80,384]{2,1,0:T(8,128)(2,1)S(1)} %slice.73), channel_id=1, source_target_pairs={{0,1},{1,0},{2,3},{3,2},{4,5},{5,4},{6,7},{7,6},{8,10},{9,11},{10,... | collective-permute-start | bytes 737288 | tf_op jit(solution)/shard_map/ppermute | solution.py:562
  87.9 0.8 collective-permute-start.14
  88.7 4.3 %input_end.1 = f32[4,384,384]{2,1,0:T(8,128)} custom-call(f32[4,384,384]{2,1,0:T(8,128)S(1)} %copy-done.7, f32[4,384,384]{2,1,0:T(8,128)S(1)} %copy-done.18, bf16[4,1152,384]{2,1,0:T(8,128)(2,1)S(1)} %get-tuple-element.142.dj_ref, bf16[1152,384]{1,0:T(8,128)(2,1)S(1)} %get-tuple-element.111.w_ref, f32[16,384]{1,0:T(8,128)S(1)} %get-tuple-element.112.vrow_ref), custom_call_target="tpu_custom_call" | custom-call | flops 4000000000 | bytes 1048576 | tf_op jit(solution)/shard_map/input_end/pallas_call | solution.py:479
  93.1 1.4 %collective-permute-start.15 = (bf16[2,80,384]{2,1,0:T(8,128)(2,1)S(1)}, bf16[2,80,384]{2,1,0:T(8,128)(2,1)S(1)}, u32[]{:S(2)}, u32[]{:S(2)}) collective-permute-start(bf16[2,80,384]{2,1,0:T(8,128)(2,1)S(1)} %slice.75), channel_id=1, source_target_pairs={{0,2},{1,3},{2,0},{3,1},{4,6},{5,7},{6,4},{7,5},{8,12},{9,13},{10,... | collective-permute-start | bytes 368648 | tf_op jit(solution)/shard_map/ppermute | solution.py:562
  94.6 4.1 %layer_end.1 = f32[4,384,384]{2,1,0:T(8,128)} custom-call(f32[4,384,384]{2,1,0:T(8,128)S(1)} %copy-done.19, bf16[4,384,1536]{2,1,0:T(8,128)(2,1)S(1)} %bitcast.9, bf16[384,1536]{1,0:T(8,128)(2,1)S(1)} %copy-done.20, f32[16,384]{1,0:T(8,128)S(1)} %get-tuple-element.112.vrow_ref), custom_call_target="tpu_custom_call" | custom-call | flops 4000000000 | bytes 1048576 | tf_op jit(solution)/shard_map/layer_end/pallas_call | solution.py:461
  98.7 0.0 copy-start.16
  98.7 0.0 copy-start.17
  98.7 0.7 collective-permute-done.14
  99.4 0.1 convert_add_fusion.3
  99.5 2.8 %collective-permute-start.16 = (bf16[1,224,384]{2,1,0:T(8,128)(2,1)S(1)}, bf16[1,224,384]{2,1,0:T(8,128)(2,1)S(1)}, u32[]{:S(2)}, u32[]{:S(2)}) collective-permute-start(bf16[1,224,384]{2,1,0:T(8,128)(2,1)S(1)} %slice.74), channel_id=1, source_target_pairs={{0,4},{1,5},{2,6},{3,7},{4,0},{5,1},{6,2},{7,3},{8,9},{9,8},{10,11... | collective-permute-start | bytes 516104 | tf_op jit(solution)/shard_map/ppermute | solution.py:562
  102.4 2.3 %collective-permute-start.17 = (bf16[1,80,384]{2,1,0:T(8,128)(2,1)S(1)}, bf16[1,80,384]{2,1,0:T(8,128)(2,1)S(1)}, u32[]{:S(2)}, u32[]{:S(2)}) collective-permute-start(bf16[1,80,384]{2,1,0:T(8,128)(2,1)S(1)} %slice.76), channel_id=1, source_target_pairs={{0,4},{1,5},{2,6},{3,7},{4,0},{5,1},{6,2},{7,3},{8,9},{9,8},{10,11... | collective-permute-start | bytes 184328 | tf_op jit(solution)/shard_map/ppermute | solution.py:562
  104.7 3.7 %collective-permute-done.16 = bf16[1,224,384]{2,1,0:T(8,128)(2,1)S(1)} collective-permute-done((bf16[1,224,384]{2,1,0:T(8,128)(2,1)S(1)}, bf16[1,224,384]{2,1,0:T(8,128)(2,1)S(1)}, u32[]{:S(2)}, u32[]{:S(2)}) %collective-permute-start.16) | collective-permute-done | bytes 172064 | tf_op jit(solution)/shard_map/ppermute | solution.py:562
  108.4 1.3 %collective-permute-done.17 = bf16[1,80,384]{2,1,0:T(8,128)(2,1)S(1)} collective-permute-done((bf16[1,80,384]{2,1,0:T(8,128)(2,1)S(1)}, bf16[1,80,384]{2,1,0:T(8,128)(2,1)S(1)}, u32[]{:S(2)}, u32[]{:S(2)}) %collective-permute-start.17) | collective-permute-done | bytes 61472 | tf_op jit(solution)/shard_map/ppermute | solution.py:562
  109.7 1.6 %collective-permute-start.18 = (bf16[80,384]{1,0:T(8,128)(2,1)S(1)}, bf16[80,384]{1,0:T(8,128)(2,1)S(1)}, u32[]{:S(2)}, u32[]{:S(2)}) collective-permute-start(bf16[80,384]{1,0:T(8,128)(2,1)S(1)} %fusion), channel_id=1, source_target_pairs={{0,16},{1,17},{2,18},{3,19},{4,20},{5,21},{6,22},{7,23},{8,24},{9,... | collective-permute-start | bytes 184328 | tf_op jit(solution)/shard_map/ppermute | solution.py:562
  111.3 0.5 collective-permute-start.19
  111.8 2.8 %collective-permute-done.18 = bf16[80,384]{1,0:T(8,128)(2,1)S(1)} collective-permute-done((bf16[80,384]{1,0:T(8,128)(2,1)S(1)}, bf16[80,384]{1,0:T(8,128)(2,1)S(1)}, u32[]{:S(2)}, u32[]{:S(2)}) %collective-permute-start.18) | collective-permute-done | bytes 61472 | tf_op jit(solution)/shard_map/ppermute | solution.py:562
  114.7 2.7 %collective-permute-done.19 = bf16[224,384]{1,0:T(8,128)(2,1)S(1)} collective-permute-done((bf16[224,384]{1,0:T(8,128)(2,1)S(1)}, bf16[224,384]{1,0:T(8,128)(2,1)S(1)}, u32[]{:S(2)}, u32[]{:S(2)}) %collective-permute-start.19) | collective-permute-done | bytes 172064 | tf_op jit(solution)/shard_map/ppermute | solution.py:562
  117.4 0.0 copy-start
  117.5 0.0 copy-start.1
  117.5 0.0 copy-start.3
  117.5 0.0 copy-start.10
  117.5 0.0 copy-start.11
  117.6 0.1 collective-permute-start.20
  117.6 0.5 collective-permute-start.21
  118.1 0.8 collective-permute-done.20.other_ref
  119.0 1.2 adam.2
  120.3 1.9 %adam.3 = (f32[48,384]{1,0:T(8,128)}, f32[48,384]{1,0:T(8,128)}, f32[48,384]{1,0:T(8,128)}, bf16[48,384]{1,0:T(8,128)(2,1)}, f32[192,384]{1,0:T(8,128)}, /*index...) custom-call(f32[224,384]{1,0:T(8,128)S(1)} %convert_add_fusion.5.min, ...), custom_call_target="tpu_custom_call" | custom-call | flops 3000000000 | bytes 1048576 | tf_op jit(solution)/shard_map/adam/pallas_call | solution.py:530
  (64 shorter events, 0.4 us)
Async XLA Ops:
  2.6 6.5 %collective-permute-start = (bf16[1,80,384]{2,1,0:T(8,128)(2,1)}, bf16[1,80,384]{2,1,0:T(8,128)(2,1)S(1)}, u32[]{:S(2)}, u32[]{:S(2)}) collective-permute-start(bf16[1,80,384]{2,1,0:T(8,128)(2,1)} %bitcast.11), channel_id=1, source_target_pairs={{0,4},{1,5},{2,6},{3,7},{4,0},{5,1},{6,2},{7,3},{8,9},{9,8},{10,11... | collective-permute-start | bytes 184328 | tf_op jit(solution)/shard_map/ppermute | solution.py:562
  10.0 5.1 %collective-permute-start.1 = (bf16[2,80,384]{2,1,0:T(8,128)(2,1)S(1)}, bf16[2,80,384]{2,1,0:T(8,128)(2,1)S(1)}, u32[]{:S(2)}, u32[]{:S(2)}) collective-permute-start(bf16[2,80,384]{2,1,0:T(8,128)(2,1)S(1)} %pad_maximum_fusion.3), channel_id=1, source_target_pairs={{0,2},{1,3},{2,0},{3,1},{4,6},{5,7},{6,4},{7,5},{8,12},{9,13},{10,... | collective-permute-start | bytes 368648 | tf_op jit(solution)/shard_map/ppermute | solution.py:562
  12.0 8.7 %collective-permute-start.3 = (bf16[1,224,384]{2,1,0:T(8,128)(2,1)}, bf16[1,224,384]{2,1,0:T(8,128)(2,1)S(1)}, u32[]{:S(2)}, u32[]{:S(2)}) collective-permute-start(bf16[1,224,384]{2,1,0:T(8,128)(2,1)} %bitcast.14), channel_id=1, source_target_pairs={{0,4},{1,5},{2,6},{3,7},{4,0},{5,1},{6,2},{7,3},{8,9},{9,8},{10,11... | collective-permute-start | bytes 516104 | tf_op jit(solution)/shard_map/ppermute | solution.py:562
  16.0 6.3 %collective-permute-start.2 = (bf16[4,80,384]{2,1,0:T(8,128)(2,1)S(1)}, bf16[4,80,384]{2,1,0:T(8,128)(2,1)S(1)}, u32[]{:S(2)}, u32[]{:S(2)}) collective-permute-start(bf16[4,80,384]{2,1,0:T(8,128)(2,1)S(1)} %pad_maximum_fusion.2.mine_a), channel_id=1, source_target_pairs={{0,1},{1,0},{2,3},{3,2},{4,5},{5,4},{6,7},{7,6},{8,10},{9,11},{10,... | collective-permute-start | bytes 737288 | tf_op jit(solution)/shard_map/ppermute | solution.py:562
  17.9 6.1 %collective-permute-start.4 = (bf16[4,80,384]{2,1,0:T(8,128)(2,1)S(1)}, bf16[4,80,384]{2,1,0:T(8,128)(2,1)S(1)}, u32[]{:S(2)}, u32[]{:S(2)}) collective-permute-start(bf16[4,80,384]{2,1,0:T(8,128)(2,1)S(1)} %pad_maximum_fusion.2.mine_a), channel_id=1, source_target_pairs={{0,8},{1,9},{2,10},{3,11},{4,12},{5,13},{6,14},{7,15},{8,0},{9,1},... | collective-permute-start | bytes 737288 | tf_op jit(solution)/shard_map/ppermute | solution.py:562
  22.2 1.8 %collective-permute-start.5 = (bf16[4,80,384]{2,1,0:T(8,128)(2,1)S(1)}, bf16[4,80,384]{2,1,0:T(8,128)(2,1)S(1)}, u32[]{:S(2)}, u32[]{:S(2)}) collective-permute-start(bf16[4,80,384]{2,1,0:T(8,128)(2,1)S(1)} %collective-permute-done.2.mine_b), channel_id=1, source_target_pairs={{0,8},{1,9},{2,10},{3,11},{4,12},{5,13},{6,14},{7,15},{8,0},{9,1},... | collective-permute-start | bytes 737288 | tf_op jit(solution)/shard_map/ppermute | solution.py:562
  22.2 10.9 %collective-permute-start.6 = (bf16[2,224,384]{2,1,0:T(8,128)(2,1)S(1)}, bf16[2,224,384]{2,1,0:T(8,128)(2,1)S(1)}, u32[]{:S(2)}, u32[]{:S(2)}) collective-permute-start(bf16[2,224,384]{2,1,0:T(8,128)(2,1)S(1)} %pad_maximum_fusion.1), channel_id=1, source_target_pairs={{0,2},{1,3},{2,0},{3,1},{4,6},{5,7},{6,4},{7,5},{8,12},{9,13},{10,... | collective-permute-start | bytes 1032200 | tf_op jit(solution)/shard_map/ppermute | solution.py:562
  24.0 1.7 %copy-start.6 = (f32[4,384,384]{2,1,0:T(8,128)S(1)}, f32[4,384,384]{2,1,0:T(8,128)}, u32[]{:S(2)}) copy-start(f32[4,384,384]{2,1,0:T(8,128)} %x_ref.7) | copy-start | bytes 7077892
  25.7 9.5 %copy-start.7 = (f32[4,384,384]{2,1,0:T(8,128)S(1)}, f32[4,384,384]{2,1,0:T(8,128)}, u32[]{:S(2)}) copy-start(f32[4,384,384]{2,1,0:T(8,128)} %x_ref.7) | copy-start | bytes 7077892
  33.3 11.0 %collective-permute-start.7 = (bf16[4,224,384]{2,1,0:T(8,128)(2,1)S(1)}, bf16[4,224,384]{2,1,0:T(8,128)(2,1)S(1)}, u32[]{:S(2)}, u32[]{:S(2)}) collective-permute-start(bf16[4,224,384]{2,1,0:T(8,128)(2,1)S(1)} %pad_maximum_fusion.mine_a), channel_id=1, source_target_pairs={{0,1},{1,0},{2,3},{3,2},{4,5},{5,4},{6,7},{7,6},{8,10},{9,11},{10,... | collective-permute-start | bytes 2064392 | tf_op jit(solution)/shard_map/ppermute | solution.py:562
  35.2 12.3 %copy-start.5 = (f32[4,384,384]{2,1,0:T(8,128)S(1)}, f32[4,384,384]{2,1,0:T(8,128)}, u32[]{:S(2)}) copy-start(f32[4,384,384]{2,1,0:T(8,128)} %cot_ref.1) | copy-start | bytes 7077892
  40.1 5.6 %collective-permute-start.8 = (bf16[4,224,384]{2,1,0:T(8,128)(2,1)S(1)}, bf16[4,224,384]{2,1,0:T(8,128)(2,1)S(1)}, u32[]{:S(2)}, u32[]{:S(2)}) collective-permute-start(bf16[4,224,384]{2,1,0:T(8,128)(2,1)S(1)} %pad_maximum_fusion.mine_a), channel_id=1, source_target_pairs={{0,8},{1,9},{2,10},{3,11},{4,12},{5,13},{6,14},{7,15},{8,0},{9,1},... | collective-permute-start | bytes 2064392 | tf_op jit(solution)/shard_map/ppermute | solution.py:562
  44.3 3.3 %collective-permute-start.9 = (bf16[4,224,384]{2,1,0:T(8,128)(2,1)S(1)}, bf16[4,224,384]{2,1,0:T(8,128)(2,1)S(1)}, u32[]{:S(2)}, u32[]{:S(2)}) collective-permute-start(bf16[4,224,384]{2,1,0:T(8,128)(2,1)S(1)} %collective-permute-done.7.mine_b), channel_id=1, source_target_pairs={{0,8},{1,9},{2,10},{3,11},{4,12},{5,13},{6,14},{7,15},{8,0},{9,1},... | collective-permute-start | bytes 2064392 | tf_op jit(solution)/shard_map/ppermute | solution.py:562
  70.4 3.3 %collective-permute-start.10 = (bf16[8,224,384]{2,1,0:T(8,128)(2,1)S(1)}, bf16[8,224,384]{2,1,0:T(8,128)(2,1)S(1)}, u32[]{:S(2)}, u32[]{:S(2)}) collective-permute-start(bf16[8,224,384]{2,1,0:T(8,128)(2,1)S(1)} %get-tuple-element.132), channel_id=1, source_target_pairs={{0,8},{1,9},{2,10},{3,11},{4,12},{5,13},{6,14},{7,15},{8,0},{9,1},... | collective-permute-start | bytes 4128776 | tf_op jit(solution)/shard_map/ppermute | solution.py:562
  74.1 11.0 %collective-permute-start.11 = (bf16[4,224,384]{2,1,0:T(8,128)(2,1)S(1)}, bf16[4,224,384]{2,1,0:T(8,128)(2,1)S(1)}, u32[]{:S(2)}, u32[]{:S(2)}) collective-permute-start(bf16[4,224,384]{2,1,0:T(8,128)(2,1)S(1)} %slice.71), channel_id=1, source_target_pairs={{0,1},{1,0},{2,3},{3,2},{4,5},{5,4},{6,7},{7,6},{8,10},{9,11},{10,... | collective-permute-start | bytes 2064392 | tf_op jit(solution)/shard_map/ppermute | solution.py:562
  84.3 1.9 %collective-permute-start.12 = (bf16[8,80,384]{2,1,0:T(8,128)(2,1)S(1)}, bf16[8,80,384]{2,1,0:T(8,128)(2,1)S(1)}, u32[]{:S(2)}, u32[]{:S(2)}) collective-permute-start(bf16[8,80,384]{2,1,0:T(8,128)(2,1)S(1)} %get-tuple-element.141), channel_id=1, source_target_pairs={{0,8},{1,9},{2,10},{3,11},{4,12},{5,13},{6,14},{7,15},{8,0},{9,1},... | collective-permute-start | bytes 1474568 | tf_op jit(solution)/shard_map/ppermute | solution.py:562
  85.2 7.8 %copy-start.21 = (f32[4,224,384]{2,1,0:T(8,128)}, f32[4,224,384]{2,1,0:T(8,128)S(1)}, u32[]{:S(2)}) copy-start(f32[4,224,384]{2,1,0:T(8,128)S(1)} %convert_add_fusion.1) | copy-start | bytes 4128772
  85.2 3.5 %copy-start.18 = (f32[4,384,384]{2,1,0:T(8,128)S(1)}, f32[4,384,384]{2,1,0:T(8,128)}, u32[]{:S(2)}) copy-start(f32[4,384,384]{2,1,0:T(8,128)} %get-tuple-element.123.dm_ref) | copy-start | bytes 7077892
  86.2 8.3 %slice-start = ((s8[4718592]{0:T(1024)(128)(4,1)}), s8[4194304]{0:T(1024)(128)(4,1)S(1)}, s32[]{:S(2)}) async-start(s8[4718592]{0:T(1024)(128)(4,1)} %bitcast.8), calls=%async_computation | async-start | bytes 8388608
  86.4 6.7 %collective-permute-start.13 = (bf16[4,80,384]{2,1,0:T(8,128)(2,1)S(1)}, bf16[4,80,384]{2,1,0:T(8,128)(2,1)S(1)}, u32[]{:S(2)}, u32[]{:S(2)}) collective-permute-start(bf16[4,80,384]{2,1,0:T(8,128)(2,1)S(1)} %slice.73), channel_id=1, source_target_pairs={{0,1},{1,0},{2,3},{3,2},{4,5},{5,4},{6,7},{7,6},{8,10},{9,11},{10,... | collective-permute-start | bytes 737288 | tf_op jit(solution)/shard_map/ppermute | solution.py:562
  87.9 11.5 %collective-permute-start.14 = (bf16[2,224,384]{2,1,0:T(8,128)(2,1)S(1)}, bf16[2,224,384]{2,1,0:T(8,128)(2,1)S(1)}, u32[]{:S(2)}, u32[]{:S(2)}) collective-permute-start(bf16[2,224,384]{2,1,0:T(8,128)(2,1)S(1)} %slice.72), channel_id=1, source_target_pairs={{0,2},{1,3},{2,0},{3,1},{4,6},{5,7},{6,4},{7,5},{8,12},{9,13},{10,... | collective-permute-start | bytes 1032200 | tf_op jit(solution)/shard_map/ppermute | solution.py:562
  88.7 5.8 %slice-start.1 = ((s8[4718592]{0:T(1024)(128)(4,1)}), s8[524288]{0:T(1024)(128)(4,1)S(1)}, s32[]{:S(2)}) async-start(s8[4718592]{0:T(1024)(128)(4,1)} %bitcast.8), calls=%async_computation.1 | async-start | bytes 1048576
  88.7 5.8 %copy-start.19 = (f32[4,384,384]{2,1,0:T(8,128)S(1)}, f32[4,384,384]{2,1,0:T(8,128)}, u32[]{:S(2)}) copy-start(f32[4,384,384]{2,1,0:T(8,128)} %get-tuple-element.145.mid_ref) | copy-start | bytes 7077892
  88.7 5.8 %copy-start.20 = (bf16[384,1536]{1,0:T(8,128)(2,1)S(1)}, bf16[384,1536]{1,0:T(8,128)(2,1)}, u32[]{:S(2)}) copy-start(bf16[384,1536]{1,0:T(8,128)(2,1)} %get-tuple-element.147.wd_ref) | copy-start | bytes 3538948
  93.1 9.2 %collective-permute-start.15 = (bf16[2,80,384]{2,1,0:T(8,128)(2,1)S(1)}, bf16[2,80,384]{2,1,0:T(8,128)(2,1)S(1)}, u32[]{:S(2)}, u32[]{:S(2)}) collective-permute-start(bf16[2,80,384]{2,1,0:T(8,128)(2,1)S(1)} %slice.75), channel_id=1, source_target_pairs={{0,2},{1,3},{2,0},{3,1},{4,6},{5,7},{6,4},{7,5},{8,12},{9,13},{10,... | collective-permute-start | bytes 368648 | tf_op jit(solution)/shard_map/ppermute | solution.py:562
  94.6 4.8 %slice-start.2 = ((f32[4,224,384]{2,1,0:T(8,128)}), f32[2,224,384]{2,1,0:T(8,128)S(1)}, s32[]{:S(2)}) async-start(f32[4,224,384]{2,1,0:T(8,128)} %copy-done.21), calls=%async_computation.2 | async-start | bytes 1376256 | tf_op jit(solution)/shard_map/slice | solution.py:650
  98.6 20.3 %copy-start.2 = (f32[144,384]{1,0:T(8,128)S(1)}, f32[144,384]{1,0:T(8,128)}, u32[]{:S(2)}) copy-start(f32[144,384]{1,0:T(8,128)} %refs_0_.2) | copy-start | bytes 663556
  98.6 20.3 %copy-start.4 = (f32[576]{0:T(1024)S(1)}, f32[576]{0:T(1024)}, u32[]{:S(2)}) copy-start(f32[576]{0:T(1024)} %refs_3_.2) | copy-start | bytes 6916
  98.6 20.3 %copy-start.12 = (f32[144,384]{1,0:T(8,128)S(1)}, f32[144,384]{1,0:T(8,128)}, u32[]{:S(2)}) copy-start(f32[144,384]{1,0:T(8,128)} %refs_1_.2) | copy-start | bytes 663556
  98.7 20.3 %copy-start.13 = (f32[144,384]{1,0:T(8,128)S(1)}, f32[144,384]{1,0:T(8,128)}, u32[]{:S(2)}) copy-start(f32[144,384]{1,0:T(8,128)} %refs_2_.2) | copy-start | bytes 663556
  98.7 20.3 %copy-start.16 = (f32[576]{0:T(1024)S(1)}, f32[576]{0:T(1024)}, u32[]{:S(2)}) copy-start(f32[576]{0:T(1024)} %refs_4_.2) | copy-start | bytes 6916
  98.7 20.3 %copy-start.17 = (f32[576]{0:T(1024)S(1)}, f32[576]{0:T(1024)}, u32[]{:S(2)}) copy-start(f32[576]{0:T(1024)} %refs_5_.2) | copy-start | bytes 6916
  99.5 8.9 %collective-permute-start.16 = (bf16[1,224,384]{2,1,0:T(8,128)(2,1)S(1)}, bf16[1,224,384]{2,1,0:T(8,128)(2,1)S(1)}, u32[]{:S(2)}, u32[]{:S(2)}) collective-permute-start(bf16[1,224,384]{2,1,0:T(8,128)(2,1)S(1)} %slice.74), channel_id=1, source_target_pairs={{0,4},{1,5},{2,6},{3,7},{4,0},{5,1},{6,2},{7,3},{8,9},{9,8},{10,11... | collective-permute-start | bytes 516104 | tf_op jit(solution)/shard_map/ppermute | solution.py:562
  102.4 7.3 %collective-permute-start.17 = (bf16[1,80,384]{2,1,0:T(8,128)(2,1)S(1)}, bf16[1,80,384]{2,1,0:T(8,128)(2,1)S(1)}, u32[]{:S(2)}, u32[]{:S(2)}) collective-permute-start(bf16[1,80,384]{2,1,0:T(8,128)(2,1)S(1)} %slice.76), channel_id=1, source_target_pairs={{0,4},{1,5},{2,6},{3,7},{4,0},{5,1},{6,2},{7,3},{8,9},{9,8},{10,11... | collective-permute-start | bytes 184328 | tf_op jit(solution)/shard_map/ppermute | solution.py:562
  109.7 4.9 %collective-permute-start.18 = (bf16[80,384]{1,0:T(8,128)(2,1)S(1)}, bf16[80,384]{1,0:T(8,128)(2,1)S(1)}, u32[]{:S(2)}, u32[]{:S(2)}) collective-permute-start(bf16[80,384]{1,0:T(8,128)(2,1)S(1)} %fusion), channel_id=1, source_target_pairs={{0,16},{1,17},{2,18},{3,19},{4,20},{5,21},{6,22},{7,23},{8,24},{9,... | collective-permute-start | bytes 184328 | tf_op jit(solution)/shard_map/ppermute | solution.py:562
  111.3 6.1 %collective-permute-start.19 = (bf16[224,384]{1,0:T(8,128)(2,1)S(1)}, bf16[224,384]{1,0:T(8,128)(2,1)S(1)}, u32[]{:S(2)}, u32[]{:S(2)}) collective-permute-start(bf16[224,384]{1,0:T(8,128)(2,1)S(1)} %bitcast.10), channel_id=1, source_target_pairs={{0,16},{1,17},{2,18},{3,19},{4,20},{5,21},{6,22},{7,23},{8,24},{9,... | collective-permute-start | bytes 516104 | tf_op jit(solution)/shard_map/ppermute | solution.py:562
  117.4 2.7 %copy-start = (f32[192,384]{1,0:T(8,128)S(1)}, f32[192,384]{1,0:T(8,128)}, u32[]{:S(2)}) copy-start(f32[192,384]{1,0:T(8,128)} %refs_3_.3) | copy-start | bytes 884740
  117.5 2.7 %copy-start.1 = (f32[48,1536]{1,0:T(8,128)S(1)}, f32[48,1536]{1,0:T(8,128)}, u32[]{:S(2)}) copy-start(f32[48,1536]{1,0:T(8,128)} %refs_6_.1) | copy-start | bytes 884740
  117.5 2.7 %copy-start.3 = (f32[48,384]{1,0:T(8,128)S(1)}, f32[48,384]{1,0:T(8,128)}, u32[]{:S(2)}) copy-start(f32[48,384]{1,0:T(8,128)} %refs_0_.3) | copy-start | bytes 221188
  117.5 2.7 %copy-start.8 = (f32[192,384]{1,0:T(8,128)S(1)}, f32[192,384]{1,0:T(8,128)}, u32[]{:S(2)}) copy-start(f32[192,384]{1,0:T(8,128)} %refs_4_.3) | copy-start | bytes 884740
  117.5 2.7 %copy-start.9 = (f32[192,384]{1,0:T(8,128)S(1)}, f32[192,384]{1,0:T(8,128)}, u32[]{:S(2)}) copy-start(f32[192,384]{1,0:T(8,128)} %refs_5_.3) | copy-start | bytes 884740
  117.5 2.7 %copy-start.10 = (f32[48,1536]{1,0:T(8,128)S(1)}, f32[48,1536]{1,0:T(8,128)}, u32[]{:S(2)}) copy-start(f32[48,1536]{1,0:T(8,128)} %refs_7_.1) | copy-start | bytes 884740
  117.5 2.7 %copy-start.11 = (f32[48,1536]{1,0:T(8,128)S(1)}, f32[48,1536]{1,0:T(8,128)}, u32[]{:S(2)}) copy-start(f32[48,1536]{1,0:T(8,128)} %refs_8_.1) | copy-start | bytes 884740
  117.5 2.7 %copy-start.14 = (f32[48,384]{1,0:T(8,128)S(1)}, f32[48,384]{1,0:T(8,128)}, u32[]{:S(2)}) copy-start(f32[48,384]{1,0:T(8,128)} %refs_1_.3) | copy-start | bytes 221188
  117.5 2.7 %copy-start.15 = (f32[48,384]{1,0:T(8,128)S(1)}, f32[48,384]{1,0:T(8,128)}, u32[]{:S(2)}) copy-start(f32[48,384]{1,0:T(8,128)} %refs_2_.3) | copy-start | bytes 221188
  117.6 1.4 %collective-permute-start.20 = (f32[80,384]{1,0:T(8,128)S(1)}, f32[80,384]{1,0:T(8,128)S(1)}, u32[]{:S(2)}, u32[]{:S(2)}) collective-permute-start(f32[80,384]{1,0:T(8,128)S(1)} %convert_add_fusion.7.mine_ref), channel_id=1, source_target_pairs={{0,8},{1,9},{2,10},{3,11},{4,12},{5,13},{6,14},{7,15},{8,0},{9,1},... | collective-permute-start | bytes 368648 | tf_op jit(solution)/shard_map/ppermute | solution.py:562
  117.6 2.5 %collective-permute-start.21 = (f32[224,384]{1,0:T(8,128)S(1)}, f32[224,384]{1,0:T(8,128)S(1)}, u32[]{:S(2)}, u32[]{:S(2)}) collective-permute-start(f32[224,384]{1,0:T(8,128)S(1)} %convert_add_fusion.5.mine_ref), channel_id=1, source_target_pairs={{0,8},{1,9},{2,10},{3,11},{4,12},{5,13},{6,14},{7,15},{8,0},{9,1},... | collective-permute-start | bytes 1032200 | tf_op jit(solution)/shard_map/ppermute | solution.py:562
